TPU v7x, 32 devices: a whole 2x2x4 slice. The times are simulated.
32 devices in a mesh: blk: 8 (over z, y), dp: 2 (over core), head: 2 (over x).
Axes of the slice: x: 2, y: 2, z: 4, core: 2. Of those that a mesh axis runs over, the one named last changes fastest.
Arguments:
- tokens: bfloat16 [4, 4096, 1024], P('dp', 'blk'), may hold values from -6 to 6
- doc_ids: int32 [4, 4096], P('dp'), may hold values from 0 to 6, as said below
- w_qkv: bfloat16 [3, 1024, 1024], P(None, None, 'head'), may hold values from -0.1875 to 0.1875
- w_out: bfloat16 [1024, 1024], P('head'), may hold values from -0.75 to 0.75
- slopes: float32 [8], P('head'), may hold values from 0.02 to 1
- w_up: bfloat16 [1024, 4096], P(None, 'head'), may hold values from -0.1875 to 0.1875
- w_down: bfloat16 [4096, 1024], P('head'), may hold values from -0.09375 to 0.09375
- w_comp: bfloat16 [3, 1024, 1024], replicated, may hold values from -0.109375 to 0.109375
- comp_bias: float32 [1024], replicated, may hold values from -1.5 to 1.5
- norm1_gain: float32 [1024], replicated, may hold values from 0.5 to 1.5
- norm1_bias: float32 [1024], replicated, may hold values from -1 to 1
- norm2_gain: float32 [1024], replicated, may hold values from 0.5 to 1.5
- norm2_bias: float32 [1024], replicated, may hold values from -1 to 1
- out_cot: bfloat16 [4, 4096, 1024], P('dp', 'blk'), may hold values from -6 to 6
- recon_cot: float32 [4, 8, 4096], P('dp', 'head', 'blk'), may hold values from -6 to 6
Outputs:
- layer_out: bfloat16 [4, 4096, 1024], P('dp', 'blk')
- recon: float32 [4, 8, 4096], P('dp', 'head', 'blk')
- grad_tokens: bfloat16 [4, 4096, 1024], P('dp', 'blk')
- grad_qkv: float32 [3, 1024, 1024], P(None, ('blk', 'dp'), 'head')
- grad_out: float32 [1024, 1024], P('head', ('blk', 'dp'))
- grad_slopes: float32 [8], P('head')
- grad_up: float32 [1024, 4096], P(('blk', 'dp'), 'head')
- grad_down: float32 [4096, 1024], P('head', ('blk', 'dp'))
- grad_comp: float32 [3, 1024, 1024], P(None, ('blk', 'dp'))
- grad_comp_bias: float32 [1024], replicated
- grad_norm1_gain: float32 [1024], replicated
- grad_norm1_bias: float32 [1024], replicated
- grad_norm2_gain: float32 [1024], replicated
- grad_norm2_bias: float32 [1024], replicated
Inputs may be any that keep to these rules, and one draw needn't show every extreme that they name: `doc_ids`: ids never fall along a sequence and start at 0. In every draw, among the 2 sequences of each index of dp, one chosen by the seed is a single document; each of the others holds exactly 7 documents.
All inputs are finite; a program needn't handle non-finite values.
Results may differ from a plain program's by a relative error of at most 0.015.
Values may be sent and summed in bfloat16 or wider, within the bound.
No kernel may reach another device: no remote copies, remote signals or barrier semaphores. Data moves between devices by JAX's collectives and lax.ppermute only.
A program may use at most 256 MiB of HBM per device.

v0:
```python
import jax
import jax.numpy as jnp
from jax import lax
from jax.sharding import PartitionSpec as P

CSEGS = 3


NEG = -1e30
EPS = 1e-05


def from_behind(x, axis, by):
    devices = lax.axis_size(axis)
    pairs = [(i, i + by) for i in range(devices) if 0 <= i + by < devices]
    return lax.ppermute(x, axis, pairs)


def norm_rows(inputs, gain, bias):
    center = inputs - jnp.mean(inputs, axis=-1, keepdims=True)
    inverse = lax.rsqrt(jnp.mean(center * center, axis=-1, keepdims=True) + EPS)
    return center * inverse * gain + bias


def score_block(queries, key_part, scaling, distance, slopes):
    product = jnp.einsum("sqhe,skhe->shqk", queries, key_part, preferred_element_type=jnp.float32)
    return product * scaling - slopes[None, :, None, None] * distance[None, None]


def masked_scores(queries, key_part, scaling, visible, distance, slopes):
    scores = score_block(queries, key_part, scaling, distance, slopes)
    return jnp.where(visible[:, None], scores, NEG)


def back_weights(
    queries, key_part, value_part, grad_mixed, log_total, scaling, visible, distance, slopes
):
    scores = score_block(queries, key_part, scaling, distance, slopes)
    weights = jnp.where(visible[:, None], jnp.exp(scores - log_total[..., None]), 0.0)
    dweights = jnp.einsum(
        "sqhe,skhe->shqk", grad_mixed, value_part, preferred_element_type=jnp.float32
    )
    return (weights, dweights)


def back_finish(queries, key_part, grad_mixed, weights, dweights, row_dot, scaling, distance):
    score_grad = weights * (dweights - row_dot[..., None])
    dslope = -jnp.sum(score_grad * distance[None, None], axis=(0, 2, 3))
    dscores = score_grad.astype(jnp.bfloat16)
    dquery = (
        jnp.einsum("shqk,skhe->sqhe", dscores, key_part, preferred_element_type=jnp.float32)
        * scaling
    )
    dkey = (
        jnp.einsum("shqk,sqhe->skhe", dscores, queries, preferred_element_type=jnp.float32)
        * scaling
    )
    dvalue = jnp.einsum(
        "shqk,sqhe->skhe",
        weights.astype(jnp.bfloat16),
        grad_mixed,
        preferred_element_type=jnp.float32,
    )
    return (dquery, dkey, dvalue, dslope)


def recon_pass(queries, key_part, value_part, scaling):
    scores = (
        jnp.einsum("sqhe,skhe->shqk", queries, key_part, preferred_element_type=jnp.float32)
        * scaling
    )
    weights = jax.nn.softmax(scores, axis=-1)
    attended = jnp.einsum(
        "shqk,skhe->shqe",
        weights.astype(jnp.bfloat16),
        value_part,
        preferred_element_type=jnp.float32,
    )
    return (weights, attended)


def recon_back(queries, key_part, value_part, weights, grad_low, scaling):
    dweights = jnp.einsum(
        "shqe,skhe->shqk", grad_low, value_part, preferred_element_type=jnp.float32
    )
    row_sum = jnp.sum(weights * dweights, axis=-1)
    dscores = (weights * (dweights - row_sum[..., None])).astype(jnp.bfloat16)
    dquery = (
        jnp.einsum("shqk,skhe->sqhe", dscores, key_part, preferred_element_type=jnp.float32)
        * scaling
    )
    dkey = (
        jnp.einsum("shqk,sqhe->skhe", dscores, queries, preferred_element_type=jnp.float32)
        * scaling
    )
    dvalue = jnp.einsum(
        "shqk,shqe->skhe",
        weights.astype(jnp.bfloat16),
        grad_low,
        preferred_element_type=jnp.float32,
    )
    return (dquery, dkey, dvalue)


def shards(
    tokens,
    doc_ids,
    w_qkv,
    w_out,
    slopes,
    w_up,
    w_down,
    w_comp,
    comp_bias,
    norm1_gain,
    norm1_bias,
    norm2_gain,
    norm2_bias,
    out_cot,
    recon_cot,
):
    seq_count, seg_rows, model_width = tokens.shape
    head_count = slopes.shape[0]
    local_width = w_qkv.shape[2]
    head_dim = local_width // head_count
    slot_rows = seg_rows // 3
    used_rows = 3 * slot_rows
    cycle_size = lax.axis_size("blk")
    position = lax.axis_index("blk")
    scaling = head_dim ** (-0.5)
    memory_slots = CSEGS * slot_rows
    head_shape = (seq_count, seg_rows, head_count, head_dim)
    slot_shape = (seq_count, slot_rows, head_count, head_dim)
    inputs = tokens.astype(jnp.float32)
    normed, norm1_pull = jax.vjp(norm_rows, inputs, norm1_gain, norm1_bias)
    normed_low = normed.astype(jnp.bfloat16)
    projected = jnp.einsum(
        "sgd,tde->tsge", normed_low, w_qkv, preferred_element_type=jnp.float32
    ).astype(jnp.bfloat16)
    queries = projected[0].reshape(head_shape)
    key_rows = projected[1].reshape(head_shape)
    value_rows = projected[2].reshape(head_shape)
    triples = normed_low[:, :used_rows].reshape(seq_count, slot_rows, 3, model_width)
    packed = (
        jnp.einsum("scrd,rde->sce", triples, w_comp, preferred_element_type=jnp.float32) + comp_bias
    )
    packed_low = packed.astype(jnp.bfloat16)
    slot_proj = jnp.einsum(
        "scd,tde->tsce", packed_low, w_qkv[1:], preferred_element_type=jnp.float32
    ).astype(jnp.bfloat16)
    slot_keys = slot_proj[0].reshape(slot_shape)
    slot_values = slot_proj[1].reshape(slot_shape)
    query_pos = position * seg_rows + jnp.arange(seg_rows, dtype=jnp.int32)
    near_pos = position * seg_rows - seg_rows + jnp.arange(2 * seg_rows, dtype=jnp.int32)
    query_doc = lax.dynamic_slice_in_dim(doc_ids, position * seg_rows, seg_rows, 1)
    padded_doc = jnp.concatenate([jnp.full((seq_count, seg_rows), -1, jnp.int32), doc_ids], 1)
    near_doc = lax.dynamic_slice_in_dim(padded_doc, position * seg_rows, 2 * seg_rows, 1)
    near_visible = (
        (near_pos[None, None, :] >= 0)
        & (near_pos[None, None, :] <= query_pos[None, :, None])
        & (near_doc[:, None, :] == query_doc[:, :, None])
    )
    near_distance = jnp.log1p(
        jnp.maximum(query_pos[:, None] - near_pos[None, :], 0).astype(jnp.float32)
    )
    segment_docs = doc_ids.reshape(seq_count, cycle_size, seg_rows)[:, :, 0:used_rows:3]
    segment_docs = jnp.concatenate(
        [jnp.full((seq_count, CSEGS + 1, slot_rows), -1, jnp.int32), segment_docs], 1
    )
    memory_doc = lax.dynamic_slice_in_dim(segment_docs, position, CSEGS, 1).reshape(
        seq_count, memory_slots
    )
    slot_local = jnp.arange(memory_slots, dtype=jnp.int32)
    memory_seg = position - 1 - CSEGS + slot_local // slot_rows
    memory_pos = memory_seg * seg_rows + 3 * (slot_local % slot_rows) + 1
    slot_visible = (memory_seg[None, None, :] >= 0) & (
        memory_doc[:, None, :] == query_doc[:, :, None]
    )
    slot_distance = jnp.log1p(
        jnp.maximum(query_pos[:, None] - memory_pos[None, :], 0).astype(jnp.float32)
    )
    memory_keys, memory_values = from_behind((key_rows, value_rows), "blk", 1)
    near_keys = jnp.concatenate([memory_keys, key_rows], 1)
    near_values = jnp.concatenate([memory_values, value_rows], 1)
    key_list = []
    value_list = []
    for lag in range(CSEGS + 1, 1, -1):
        far_keys, far_values = from_behind((slot_keys, slot_values), "blk", lag)
        key_list.append(far_keys)
        value_list.append(far_values)
    table_keys = jnp.concatenate(key_list, 1)
    table_values = jnp.concatenate(value_list, 1)
    near_scores = masked_scores(queries, near_keys, scaling, near_visible, near_distance, slopes)
    slot_scores = masked_scores(queries, table_keys, scaling, slot_visible, slot_distance, slopes)
    top = jnp.maximum(jnp.max(near_scores, axis=-1), jnp.max(slot_scores, axis=-1))
    near_w = jnp.where(near_visible[:, None], jnp.exp(near_scores - top[..., None]), 0.0)
    slot_w = jnp.where(slot_visible[:, None], jnp.exp(slot_scores - top[..., None]), 0.0)
    weight_sum = jnp.sum(near_w, axis=-1) + jnp.sum(slot_w, axis=-1)
    near_p = (near_w / weight_sum[..., None]).astype(jnp.bfloat16)
    slot_p = (slot_w / weight_sum[..., None]).astype(jnp.bfloat16)
    mixed = jnp.einsum(
        "shqk,skhe->sqhe", near_p, near_values, preferred_element_type=jnp.float32
    ) + jnp.einsum("shqk,skhe->sqhe", slot_p, table_values, preferred_element_type=jnp.float32)
    log_total = top + jnp.log(weight_sum)
    mixed_low = mixed.reshape(seq_count, seg_rows, local_width).astype(jnp.bfloat16)
    attn_part = jnp.einsum("sgd,de->sge", mixed_low, w_out, preferred_element_type=jnp.float32)
    middle = inputs + lax.psum(attn_part, "head")
    normed_two, norm2_pull = jax.vjp(norm_rows, middle, norm2_gain, norm2_bias)
    normed_two_low = normed_two.astype(jnp.bfloat16)
    inner = jnp.einsum("sgd,df->sgf", normed_two_low, w_up, preferred_element_type=jnp.float32)
    hidden, gelu_pull = jax.vjp(jax.nn.gelu, inner)
    hidden_low = hidden.astype(jnp.bfloat16)
    ffn_part = jnp.einsum("sgf,fe->sge", hidden_low, w_down, preferred_element_type=jnp.float32)
    layer_out = (middle + lax.psum(ffn_part, "head")).astype(jnp.bfloat16)
    full_weights, full_out = recon_pass(queries, key_rows, value_rows, scaling)
    comp_weights, comp_out = recon_pass(queries, slot_keys, slot_values, scaling)
    spread = full_out - comp_out
    recon = jnp.sum(spread * spread, axis=-1) / head_dim**0.5
    cotangent = out_cot.astype(jnp.float32)
    dhidden = jnp.einsum("sge,fe->sgf", out_cot, w_down, preferred_element_type=jnp.float32)
    grad_down = jnp.einsum("sgf,sge->fe", hidden_low, out_cot, preferred_element_type=jnp.float32)
    dinner = gelu_pull(dhidden)[0].astype(jnp.bfloat16)
    dnormed_two_part = jnp.einsum("sgf,df->sgd", dinner, w_up, preferred_element_type=jnp.float32)
    grad_up = jnp.einsum("sgd,sgf->df", normed_two_low, dinner, preferred_element_type=jnp.float32)
    dnormed_two = lax.psum(dnormed_two_part, "head")
    dmiddle, dgain_two, dbias_two = norm2_pull(dnormed_two)
    dmiddle = dmiddle + cotangent
    dbranch_low = dmiddle.astype(jnp.bfloat16)
    grad_out = jnp.einsum("sgd,sge->de", mixed_low, dbranch_low, preferred_element_type=jnp.float32)
    dmixed = (
        jnp.einsum("sge,de->sgd", dbranch_low, w_out, preferred_element_type=jnp.float32)
        .astype(jnp.bfloat16)
        .reshape(head_shape)
    )
    near_wt, near_dw = back_weights(
        queries,
        near_keys,
        near_values,
        dmixed,
        log_total,
        scaling,
        near_visible,
        near_distance,
        slopes,
    )
    slot_wt, slot_dw = back_weights(
        queries,
        table_keys,
        table_values,
        dmixed,
        log_total,
        scaling,
        slot_visible,
        slot_distance,
        slopes,
    )
    row_dot = jnp.sum(near_wt * near_dw, axis=-1) + jnp.sum(slot_wt * slot_dw, axis=-1)
    dq_near, dk_near, dv_near, dslope_near = back_finish(
        queries, near_keys, dmixed, near_wt, near_dw, row_dot, scaling, near_distance
    )
    back_keys, back_values = from_behind((dk_near[:, :seg_rows], dv_near[:, :seg_rows]), "blk", -1)
    dq_slots, dk_table, dv_table, dslope_slots = back_finish(
        queries, table_keys, dmixed, slot_wt, slot_dw, row_dot, scaling, slot_distance
    )
    own_dk = jnp.zeros(slot_shape, jnp.float32)
    own_dv = jnp.zeros(slot_shape, jnp.float32)
    for index, lag in enumerate(range(CSEGS + 1, 1, -1)):
        piece_keys = dk_table[:, index * slot_rows : (index + 1) * slot_rows]
        piece_values = dv_table[:, index * slot_rows : (index + 1) * slot_rows]
        got_keys, got_values = from_behind((piece_keys, piece_values), "blk", -lag)
        own_dk = own_dk + got_keys
        own_dv = own_dv + got_values
    dspread = recon_cot[..., None] * 2.0 * spread / head_dim**0.5
    dq_full, dk_full, dv_full = recon_back(
        queries, key_rows, value_rows, full_weights, dspread.astype(jnp.bfloat16), scaling
    )
    dq_comp, dk_comp, dv_comp = recon_back(
        queries, slot_keys, slot_values, comp_weights, (-dspread).astype(jnp.bfloat16), scaling
    )
    dq_total = dq_near + dq_slots + dq_full + dq_comp
    dk_total = dk_near[:, seg_rows:] + back_keys + dk_full
    dv_total = dv_near[:, seg_rows:] + back_values + dv_full
    dslot_k = own_dk + dk_comp
    dslot_v = own_dv + dv_comp
    grads_low = (
        jnp.stack([dq_total, dk_total, dv_total])
        .reshape(3, seq_count, seg_rows, local_width)
        .astype(jnp.bfloat16)
    )
    slot_grads_low = (
        jnp.stack([dslot_k, dslot_v])
        .reshape(2, seq_count, slot_rows, local_width)
        .astype(jnp.bfloat16)
    )
    grad_proj = jnp.einsum(
        "sgd,tsge->tde", normed_low, grads_low, preferred_element_type=jnp.float32
    )
    grad_slot_proj = jnp.einsum(
        "scd,tsce->tde", packed_low, slot_grads_low, preferred_element_type=jnp.float32
    )
    grad_qkv = jnp.concatenate([grad_proj[:1], grad_proj[1:] + grad_slot_proj], 0)
    dnormed_part = jnp.einsum("tsge,tde->sgd", grads_low, w_qkv, preferred_element_type=jnp.float32)
    dpacked_part = jnp.einsum(
        "tsce,tde->scd", slot_grads_low, w_qkv[1:], preferred_element_type=jnp.float32
    )
    dnormed_sum, dpacked_sum = lax.psum((dnormed_part, dpacked_part), "head")
    dpacked_low = dpacked_sum.astype(jnp.bfloat16)
    grad_comp = jnp.einsum(
        "scrd,sce->rde", triples, dpacked_low, preferred_element_type=jnp.float32
    )
    dcomp_bias = jnp.sum(dpacked_low.astype(jnp.float32), axis=(0, 1))
    dtriples = jnp.einsum(
        "sce,rde->scrd", dpacked_low, w_comp, preferred_element_type=jnp.float32
    ).reshape(seq_count, used_rows, model_width)
    dtriples = jnp.concatenate(
        [dtriples, jnp.zeros((seq_count, seg_rows - used_rows, model_width), jnp.float32)], 1
    )
    dinputs, dgain_one, dbias_one = norm1_pull(dnormed_sum + dtriples)
    grad_tokens = (dinputs + dmiddle).astype(jnp.bfloat16)
    dslope_total = dslope_near + dslope_slots
    qkv_sum, out_sum, up_sum, down_sum, comp_sum = (
        lax.psum_scatter(grad_qkv, ("blk", "dp"), scatter_dimension=1, tiled=True),
        lax.psum_scatter(grad_out, ("blk", "dp"), scatter_dimension=1, tiled=True),
        lax.psum_scatter(grad_up, ("blk", "dp"), scatter_dimension=0, tiled=True),
        lax.psum_scatter(grad_down, ("blk", "dp"), scatter_dimension=1, tiled=True),
        lax.psum_scatter(grad_comp, ("blk", "dp"), scatter_dimension=1, tiled=True),
    )
    small_sums = lax.psum(
        (dgain_one, dbias_one, dgain_two, dbias_two, dcomp_bias, dslope_total), ("blk", "dp")
    )
    return (
        layer_out,
        recon,
        grad_tokens,
        qkv_sum,
        out_sum,
        small_sums[5],
        up_sum,
        down_sum,
        comp_sum,
        small_sums[4],
        small_sums[0],
        small_sums[1],
        small_sums[2],
        small_sums[3],
    )


def solution(mesh):
    in_specs = (
        P("dp", "blk", None),
        P("dp", None),
        P(None, None, "head"),
        P("head", None),
        P("head"),
        P(None, "head"),
        P("head", None),
        P(),
        P(),
        P(),
        P(),
        P(),
        P(),
        P("dp", "blk", None),
        P("dp", "head", "blk"),
    )
    out_specs = (
        P("dp", "blk", None),
        P("dp", "head", "blk"),
        P("dp", "blk", None),
        P(None, ("blk", "dp"), "head"),
        P("head", ("blk", "dp")),
        P("head"),
        P(("blk", "dp"), "head"),
        P("head", ("blk", "dp")),
        P(None, ("blk", "dp"), None),
        P(),
        P(),
        P(),
        P(),
        P(),
    )
    return jax.shard_map(shards, mesh=mesh, in_specs=in_specs, out_specs=out_specs, check_vma=False)
```

profile of v0, /device:TPU:0, one launch (start us, length us, event | category | flops | bytes accessed | tf_op | source)
XLA Modules:
  0.0 1622.0 jit_solution(11419179671650933431)
XLA Ops:
  92.7 10.2 select_reduce_fusion
  110.2 10.0 fusion.2
  130.0 14.1 add_convert_fusion.3
  170.0 138.7 %all-reduce.12.cloned.1.call-done = f32[2,512,1024]{2,1,0:T(8,128)} async-done(((f32[2,512,1024]{2,1,0:T(8,128)}), f32[2,512,1024]{2,1,0:T(8,128)}) %all-reduce.12.cloned.1.call-update) | async-done | bytes 4194320 | tf_op jit(solution)/shard_map/psum | solution.py:207
  319.9 9.8 fusion.9
  357.4 88.6 %all-reduce.14.cloned.1.call-done = f32[2,512,1024]{2,1,0:T(8,128)} async-done(((f32[2,512,1024]{2,1,0:T(8,128)}), f32[2,512,1024]{2,1,0:T(8,128)}) %all-reduce.14.cloned.1.call-update) | async-done | bytes 4194320 | tf_op jit(solution)/shard_map/psum | solution.py:225
  459.3 10.1 fusion.64
  484.5 16.8 %multiply_reduce_fusion.1 = (f32[2,4,512]{2,1,0:T(4,128)S(1)}, f32[2,4,512,1024]{3,2,1,0:T(8,128)}) fusion(f32[2,4,512]{2,1,0:T(4,128)S(1)} %bitcast.232, f32[4,512,1024]{2,1,0:T(8,128)} %copy-done.2, f32[2,4,512,1024]{3,2,1,0:T(8,128)} %get-tuple-element.125, pred[2,512,1024]{2,1,0:T(8,128)(4,1)S(1)} %copy-done.13, ...), kind=kOutput, calls=%fused_computation.4 | convolution fusion | flops 1103097856 | bytes 46170112 | tf_op jit(solution)/shard_map/sqhe,skhe->shqk/dot_general | solution.py:40
  501.3 16.3 %multiply_reduce_fusion.3 = (f32[4]{0:T(128)S(1)}, bf16[2,4,512,510]{2,1,3,0:T(4,128)(2,1)}, bf16[2,4,512,510]{2,1,3,0:T(4,128)(2,1)}) fusion(f32[512,510]{0,1:T(8,128)} %copy-done.26, f32[2,4,512]{2,1,0:T(4,128)S(1)} %add.303, f32[2,4,512,510]{2,3,1,0:T(8,128)} %copy-done.8, f32[2,4,512,510]{2,1,3,0:T(4,128)} %get-tuple-element.107, ...), kind=kLoop, calls=%fused_computation.29 | loop fusion | flops 16711676 | bytes 26667024 | tf_op jit(solution)/shard_map/reduce_sum | solution.py:48
  517.6 15.4 multiply_reduce_fusion
  586.3 26.8 %collective-permute-done.10 = f32[2,170,4,128]{3,2,1,0:T(4,128)} collective-permute-done((f32[2,170,4,128]{3,2,1,0:T(4,128)}, f32[2,170,4,128]{3,2,1,0:T(4,128)}, u32[]{:S(2)}, u32[]{:S(2)}) %collective-permute-start.10) | collective-permute-done | bytes 696352 | tf_op jit(solution)/shard_map/ppermute | solution.py:16
  629.3 30.9 %collective-permute-done.13 = f32[2,170,4,128]{3,2,1,0:T(4,128)} collective-permute-done((f32[2,170,4,128]{3,2,1,0:T(4,128)}, f32[2,170,4,128]{3,2,1,0:T(4,128)}, u32[]{:S(2)}, u32[]{:S(2)}) %collective-permute-start.13) | collective-permute-done | bytes 696352 | tf_op jit(solution)/shard_map/ppermute | solution.py:16
  660.1 27.3 %collective-permute-done.15 = f32[2,170,4,128]{3,2,1,0:T(4,128)} collective-permute-done((f32[2,170,4,128]{3,2,1,0:T(4,128)}, f32[2,170,4,128]{3,2,1,0:T(4,128)}, u32[]{:S(2)}, u32[]{:S(2)}) %collective-permute-start.15) | collective-permute-done | bytes 696352 | tf_op jit(solution)/shard_map/ppermute | solution.py:16
  720.0 9.3 copy.339
  729.6 11.8 fusion.36
  752.2 11.5 convolution_bitcast_fusion.1
  765.3 11.3 convolution_bitcast_fusion
  780.5 36.2 %all-reduce.19 = bf16[2,170,1024]{2,1,0:T(8,128)(2,1)S(1)} all-reduce(f32[2,170,1024]{2,1,0:T(8,128)} %fusion.104), channel_id=1, replica_groups=mesh['blk'=8,'dp'=2,'head'=2] {'head'}, use_global_device_ids=true, to_apply=%region_23.24 | all-reduce | flops 348160 | bytes 2088960 | tf_op jit(solution)/shard_map/psum | solution.py:306
  838.5 152.3 %all-reduce.16.cloned.1.call-done = f32[3,1024,512]{2,0,1:T(4,128)} async-done(((f32[3,1024,512]{2,0,1:T(4,128)}), f32[3,1024,512]{2,0,1:T(4,128)}) %all-reduce.16.cloned.1.call-update) | async-done | bytes 6291472
  992.9 198.9 %all-reduce.18.cloned.1.call-done = (f32[2,512,1024]{2,1,0:T(8,128)}, f32[2,512,1024]{2,1,0:T(8,128)}) async-done(((f32[2,512,1024]{2,1,0:T(8,128)}, f32[2,512,1024]{2,1,0:T(8,128)}), (f32[2,512,1024]{2,1,0:T(8,128)}, f32[2,512,1024]{2,1,0:T(8,128)})) %all-reduce.18.cloned.1.call-update) | async-done | bytes 8388624 | tf_op jit(solution)/shard_map/psum | solution.py:214
  1200.3 61.3 %all-reduce.4 = (f32[4]{0:T(128)}, f32[1024]{0:T(1024)}, f32[1024]{0:T(1024)}, f32[1024]{0:T(1024)}, f32[1024]{0:T(1024)}, /*index=5*/f32[1024]{0:T(1024)}) all-reduce(f32[4]{0:T(128)S(1)} %negate_add_fusion, f32[1024]{0:T(1024)S(1)} %convert_reduce_fusion.1, ...), channel_id=1, replica_groups=mesh['blk'=8,'dp'=2,'head'=2] {'blk','dp'}, use_global_device_ids=true, to_apply=%region_30.31 | all-reduce | flops 5124 | bytes 40992 | tf_op jit(solution)/shard_map/psum | solution.py:328
  1271.9 94.8 %reduce-scatter.7.cloned.1.call-done = f32[64,2048]{1,0:T(8,128)} async-done(((f32[1024,2048]{1,0:T(8,128)}), f32[64,2048]{1,0:T(8,128)}) %reduce-scatter.7.cloned.1.call-update) | async-done | bytes 524304 | tf_op jit(solution)/shard_map/reduce_scatter | solution.py:324
  1366.7 109.0 %reduce-scatter.9.cloned.1.call-done = f32[2048,64]{0,1:T(8,128)} async-done(((f32[2048,1024]{0,1:T(8,128)}), f32[2048,64]{0,1:T(8,128)}) %reduce-scatter.9.cloned.1.call-update) | async-done | bytes 524304 | tf_op jit(solution)/shard_map/reduce_scatter | solution.py:325
  1475.7 139.1 %reduce-scatter.11.cloned.1.call-done = f32[3,64,1024]{2,1,0:T(8,128)} async-done(((f32[3,1024,1024]{2,1,0:T(8,128)}), f32[3,64,1024]{2,1,0:T(8,128)}) %reduce-scatter.11.cloned.1.call-update) | async-done | bytes 786448 | tf_op jit(solution)/shard_map/reduce_scatter | solution.py:326
  (357 shorter events, 354.8 us)
Async XLA Ops:
  7.2 301.5 %all-reduce.12.cloned.1.call-start = ((), (), s32[]{:S(2)}) async-start(), calls=%async_computation.4 | async-start | bytes 8388608 | tf_op jit(solution)/shard_map/psum | solution.py:207
  20.2 44.4 %collective-permute-start.2 = (bf16[2,170,4,128]{3,1,2,0:T(8,128)(2,1)}, bf16[2,170,4,128]{3,1,2,0:T(8,128)(2,1)}, u32[]{:S(2)}, u32[]{:S(2)}) collective-permute-start(bf16[2,170,4,128]{3,1,2,0:T(8,128)(2,1)} %copy.280), channel_id=1, source_target_pairs={{0,16},{4,20},{8,24},{12,28},{1,17},{5,21},{9,25},{13,29},{2,18},{... | collective-permute-start | bytes 1044488 | tf_op jit(solution)/shard_map/ppermute | solution.py:16
  26.9 39.8 %collective-permute-start.3 = (bf16[2,170,4,128]{3,1,2,0:T(8,128)(2,1)}, bf16[2,170,4,128]{3,1,2,0:T(8,128)(2,1)}, u32[]{:S(2)}, u32[]{:S(2)}) collective-permute-start(bf16[2,170,4,128]{3,1,2,0:T(8,128)(2,1)} %copy.280), channel_id=1, source_target_pairs={{0,12},{4,16},{8,20},{12,24},{16,28},{1,13},{5,17},{9,21},{13,25},... | collective-permute-start | bytes 1044488 | tf_op jit(solution)/shard_map/ppermute | solution.py:16
  32.1 37.9 %collective-permute-start.4 = (bf16[2,170,4,128]{3,1,2,0:T(8,128)(2,1)}, bf16[2,170,4,128]{3,1,2,0:T(8,128)(2,1)}, u32[]{:S(2)}, u32[]{:S(2)}) collective-permute-start(bf16[2,170,4,128]{3,1,2,0:T(8,128)(2,1)} %copy.280), channel_id=1, source_target_pairs={{0,8},{4,12},{8,16},{12,20},{16,24},{20,28},{1,9},{5,13},{9,17},{1... | collective-permute-start | bytes 1044488 | tf_op jit(solution)/shard_map/ppermute | solution.py:16
  35.1 90.5 %collective-permute-start.5 = (bf16[2,170,4,128]{1,3,2,0:T(8,128)(2,1)}, bf16[2,170,4,128]{1,3,2,0:T(8,128)(2,1)}, u32[]{:S(2)}, u32[]{:S(2)}) collective-permute-start(bf16[2,170,4,128]{1,3,2,0:T(8,128)(2,1)} %bitcast.60), channel_id=1, source_target_pairs={{0,16},{4,20},{8,24},{12,28},{1,17},{5,21},{9,25},{13,29},{2,18},{... | collective-permute-start | bytes 1044488 | tf_op jit(solution)/shard_map/ppermute | solution.py:16
  37.2 88.4 %collective-permute-start.6 = (bf16[2,170,4,128]{1,3,2,0:T(8,128)(2,1)}, bf16[2,170,4,128]{1,3,2,0:T(8,128)(2,1)}, u32[]{:S(2)}, u32[]{:S(2)}) collective-permute-start(bf16[2,170,4,128]{1,3,2,0:T(8,128)(2,1)} %bitcast.60), channel_id=1, source_target_pairs={{0,12},{4,16},{8,20},{12,24},{16,28},{1,13},{5,17},{9,21},{13,25},... | collective-permute-start | bytes 1044488 | tf_op jit(solution)/shard_map/ppermute | solution.py:16
  64.6 61.0 %collective-permute-start.7 = (bf16[2,170,4,128]{1,3,2,0:T(8,128)(2,1)}, bf16[2,170,4,128]{1,3,2,0:T(8,128)(2,1)}, u32[]{:S(2)}, u32[]{:S(2)}) collective-permute-start(bf16[2,170,4,128]{1,3,2,0:T(8,128)(2,1)} %bitcast.60), channel_id=1, source_target_pairs={{0,8},{4,12},{8,16},{12,20},{16,24},{20,28},{1,9},{5,13},{9,17},{1... | collective-permute-start | bytes 1044488 | tf_op jit(solution)/shard_map/ppermute | solution.py:16
  66.7 25.9 %collective-permute-start.1 = (bf16[2,512,4,128]{3,1,2,0:T(8,128)(2,1)S(1)}, bf16[2,512,4,128]{3,1,2,0:T(8,128)(2,1)}, u32[]{:S(2)}, u32[]{:S(2)}) collective-permute-start(bf16[2,512,4,128]{3,1,2,0:T(8,128)(2,1)S(1)} %copy-done.25), channel_id=1, source_target_pairs={{0,4},{4,8},{8,12},{12,16},{16,20},{20,24},{24,28},{1,5},{5,9},{9,... | collective-permute-start | bytes 3145736 | tf_op jit(solution)/shard_map/ppermute | solution.py:16
  70.0 59.9 %collective-permute-start = (bf16[2,512,4,128]{1,3,2,0:T(8,128)(2,1)}, bf16[2,512,4,128]{1,3,2,0:T(8,128)(2,1)}, u32[]{:S(2)}, u32[]{:S(2)}) collective-permute-start(bf16[2,512,4,128]{1,3,2,0:T(8,128)(2,1)} %bitcast.4), channel_id=1, source_target_pairs={{0,4},{4,8},{8,12},{12,16},{16,20},{20,24},{24,28},{1,5},{5,9},{9,... | collective-permute-start | bytes 3145736 | tf_op jit(solution)/shard_map/ppermute | solution.py:16
  148.6 297.4 %all-reduce.14.cloned.1.call-start = ((), (), s32[]{:S(2)}) async-start(), calls=%async_computation.5 | async-start | bytes 8388608 | tf_op jit(solution)/shard_map/psum | solution.py:225
  338.0 652.9 %all-reduce.16.cloned.1.call-start = ((), (), s32[]{:S(2)}) async-start(), calls=%async_computation.10 | async-start | bytes 16777216
  547.9 65.2 %collective-permute-start.10 = (f32[2,170,4,128]{3,2,1,0:T(4,128)}, f32[2,170,4,128]{3,2,1,0:T(4,128)}, u32[]{:S(2)}, u32[]{:S(2)}) collective-permute-start(f32[2,170,4,128]{3,2,1,0:T(4,128)} %copy.317), channel_id=1, source_target_pairs={{16,0},{20,4},{24,8},{28,12},{17,1},{21,5},{25,9},{29,13},{18,2},{... | collective-permute-start | bytes 2088968 | tf_op jit(solution)/shard_map/ppermute | solution.py:16
  551.6 62.8 %collective-permute-start.11 = (f32[2,170,4,128]{3,2,1,0:T(4,128)}, f32[2,170,4,128]{3,2,1,0:T(4,128)}, u32[]{:S(2)}, u32[]{:S(2)}) collective-permute-start(f32[2,170,4,128]{3,2,1,0:T(4,128)} %copy.318), channel_id=1, source_target_pairs={{12,0},{16,4},{20,8},{24,12},{28,16},{13,1},{17,5},{21,9},{25,13},... | collective-permute-start | bytes 2088968 | tf_op jit(solution)/shard_map/ppermute | solution.py:16
  554.1 61.6 %collective-permute-start.12 = (f32[2,170,4,128]{3,2,1,0:T(4,128)}, f32[2,170,4,128]{3,2,1,0:T(4,128)}, u32[]{:S(2)}, u32[]{:S(2)}) collective-permute-start(f32[2,170,4,128]{3,2,1,0:T(4,128)} %copy.321), channel_id=1, source_target_pairs={{8,0},{12,4},{16,8},{20,12},{24,16},{28,20},{9,1},{13,5},{17,9},{2... | collective-permute-start | bytes 2088968 | tf_op jit(solution)/shard_map/ppermute | solution.py:16
  563.3 96.8 %collective-permute-start.13 = (f32[2,170,4,128]{3,2,1,0:T(4,128)}, f32[2,170,4,128]{3,2,1,0:T(4,128)}, u32[]{:S(2)}, u32[]{:S(2)}) collective-permute-start(f32[2,170,4,128]{3,2,1,0:T(4,128)} %copy.326), channel_id=1, source_target_pairs={{16,0},{20,4},{24,8},{28,12},{17,1},{21,5},{25,9},{29,13},{18,2},{... | collective-permute-start | bytes 2088968 | tf_op jit(solution)/shard_map/ppermute | solution.py:16
  577.4 114.7 %collective-permute-start.8 = (f32[2,512,4,128]{1,3,2,0:T(8,128)}, f32[2,512,4,128]{1,3,2,0:T(8,128)}, u32[]{:S(2)}, u32[]{:S(2)}) collective-permute-start(f32[2,512,4,128]{1,3,2,0:T(8,128)} %slice.88), channel_id=1, source_target_pairs={{4,0},{8,4},{12,8},{16,12},{20,16},{24,20},{28,24},{5,1},{9,5},{13... | collective-permute-start | bytes 6291464 | tf_op jit(solution)/shard_map/ppermute | solution.py:16
  613.1 47.0 %collective-permute-start.14 = (f32[2,170,4,128]{3,2,1,0:T(4,128)}, f32[2,170,4,128]{3,2,1,0:T(4,128)}, u32[]{:S(2)}, u32[]{:S(2)}) collective-permute-start(f32[2,170,4,128]{3,2,1,0:T(4,128)} %copy.327), channel_id=1, source_target_pairs={{12,0},{16,4},{20,8},{24,12},{28,16},{13,1},{17,5},{21,9},{25,13},... | collective-permute-start | bytes 2088968 | tf_op jit(solution)/shard_map/ppermute | solution.py:16
  614.4 73.0 %collective-permute-start.15 = (f32[2,170,4,128]{3,2,1,0:T(4,128)}, f32[2,170,4,128]{3,2,1,0:T(4,128)}, u32[]{:S(2)}, u32[]{:S(2)}) collective-permute-start(f32[2,170,4,128]{3,2,1,0:T(4,128)} %copy.330), channel_id=1, source_target_pairs={{8,0},{12,4},{16,8},{20,12},{24,16},{28,20},{9,1},{13,5},{17,9},{2... | collective-permute-start | bytes 2088968 | tf_op jit(solution)/shard_map/ppermute | solution.py:16
  615.8 82.6 %collective-permute-start.9 = (f32[2,512,4,128]{1,3,2,0:T(8,128)}, f32[2,512,4,128]{1,3,2,0:T(8,128)}, u32[]{:S(2)}, u32[]{:S(2)}) collective-permute-start(f32[2,512,4,128]{1,3,2,0:T(8,128)} %slice.90), channel_id=1, source_target_pairs={{4,0},{8,4},{12,8},{16,12},{20,16},{24,20},{28,24},{5,1},{9,5},{13... | collective-permute-start | bytes 6291464 | tf_op jit(solution)/shard_map/ppermute | solution.py:16
  729.4 462.4 %all-reduce.18.cloned.1.call-start = ((), (), s32[]{:S(2)}) async-start(), calls=%async_computation.11 | async-start | bytes 16777216 | tf_op jit(solution)/shard_map/psum | solution.py:214
  746.7 525.2 %reduce-scatter.5.cloned.1.call-start = ((), (), s32[]{:S(2)}) async-start(), calls=%async_computation.6 | async-start | bytes 2228224 | tf_op jit(solution)/shard_map/reduce_scatter | solution.py:323
  752.1 614.6 %reduce-scatter.7.cloned.1.call-start = ((), (), s32[]{:S(2)}) async-start(), calls=%async_computation.7 | async-start | bytes 8912896 | tf_op jit(solution)/shard_map/reduce_scatter | solution.py:324
  763.7 712.0 %reduce-scatter.9.cloned.1.call-start = ((), (), s32[]{:S(2)}) async-start(), calls=%async_computation.8 | async-start | bytes 8912896 | tf_op jit(solution)/shard_map/reduce_scatter | solution.py:325
  776.7 838.1 %reduce-scatter.11.cloned.1.call-start = ((), (), s32[]{:S(2)}) async-start(), calls=%async_computation.9 | async-start | bytes 13369344 | tf_op jit(solution)/shard_map/reduce_scatter | solution.py:326
  (95 other events, 2937.7 us)
Sparse Core Ops, SparseCore 0:
  148.7 160.0 all-reduce.11
  338.1 107.8 all-reduce.13
  729.5 261.3 all-reduce.15
  993.4 198.3 all-reduce.17
  1196.4 62.0 reduce-scatter.4
  1263.0 103.5 reduce-scatter.6
  1371.3 104.3 reduce-scatter.8
  1480.3 134.3 reduce-scatter.10
where the time goes:
time: 1630 us; the launch traced here: 1620 us
  waiting for transfers between devices  1020 us (63%)
  matrix products  242 us (15%)
  other arithmetic  121 us (7%)
  blocking collectives  97.5 us (6%)
  local copies, waits for them, and re-layouts  91.2 us (6%)
  starting transfers between devices  38 us (2%)
  between operations  16.6 us (1%)
    psum x1, waiting for transfers between devices, shards(): layer_out = (middle + lax.psum(ffn_part, 'head')).astype(jnp.bfloat16)  199 us
    unnamed x9, waiting for transfers between devices  152 us
    reduce_scatter x1, waiting for transfers between devices, shards(): lax.psum_scatter(grad_comp, ('blk', 'dp'), scatter_dimension=1, tiled=True)  139 us
    psum x1, waiting for transfers between devices, shards(): middle = inputs + lax.psum(attn_part, 'head')  139 us
    reduce_scatter x1, waiting for transfers between devices, shards(): lax.psum_scatter(grad_down, ('blk', 'dp'), scatter_dimension=1, tiled=True)  109 us
    reduce_scatter x1, waiting for transfers between devices, shards(): lax.psum_scatter(grad_up, ('blk', 'dp'), scatter_dimension=0, tiled=True)  94.8 us
    ppermute x16, waiting for transfers between devices, from_behind(): return lax.ppermute(x, axis, pairs)  94 us
    psum x1, waiting for transfers between devices, shards(): dnormed_two = lax.psum(dnormed_two_part, 'head')  88.6 us
  transfers between devices with their start and end apart: 24, of which 11 were waited for; matrix products, arithmetic and copies ran while one was open for 15% of the time, Pallas kernels for 0%

commit v1 on v0

v1 whole, which is shorter than its diff:
```python
import functools
import math

import jax
import jax.numpy as jnp
from jax import lax
from jax.experimental import pallas as pl
from jax.experimental.pallas import tpu as pltpu
from jax.sharding import PartitionSpec as P

CSEGS = 3
EPS = 1e-05
FAR = 1e30
LOG2E = math.log2(math.e)
BF = jnp.bfloat16
F32 = jnp.float32
TILE = 256
NT = (((1,), (1,)), ((), ()))
GELU_A = math.sqrt(2.0 / math.pi)
GELU_B = 0.044715


def dot(a, b):
    return jnp.dot(a, b, preferred_element_type=F32)


def dot_nt(a, b):
    return lax.dot_general(a, b, NT, preferred_element_type=F32)


def dot_tn(a, b):
    return lax.dot_general(a, b, (((0,), (0,)), ((), ())), preferred_element_type=F32)


def shift(x, axis, by):
    devices = lax.axis_size(axis)
    pairs = [(i, i + by) for i in range(devices) if 0 <= i + by < devices]
    return lax.ppermute(x, axis, pairs)


def swap(x, axis, step=1):
    devices = lax.axis_size(axis)
    return lax.ppermute(x, axis, [(i, i ^ step) for i in range(devices)])


def row_stats(x):
    center = x - jnp.mean(x, axis=-1, keepdims=True)
    inverse = lax.rsqrt(jnp.mean(center * center, axis=-1, keepdims=True) + EPS)
    return center * inverse, inverse


def norm_back(grad, unit, inverse, gain):
    scaled = grad * gain
    mean_one = jnp.mean(scaled, axis=-1, keepdims=True)
    mean_two = jnp.mean(scaled * unit, axis=-1, keepdims=True)
    return inverse * (scaled - mean_one - unit * mean_two)


def forward_kernel(slopes, q, kp, ko, km, vp, vo, vm, far, out, lse, *, rows, scaling):
    head = pl.program_id(0)
    c1 = scaling * LOG2E
    c2 = slopes[head] * LOG2E
    tiles = rows // TILE
    sources = ((kp, vp, 0), (ko, vo, rows), (km, vm, 2 * rows))
    for qi in range(tiles):
        qs = slice(qi * TILE, (qi + 1) * TILE)
        qb = q[0, qs, :]
        scores = []
        for which, (k, v, base) in enumerate(sources):
            for ki in range(tiles):
                if which == 1 and ki > qi:
                    continue
                ks = slice(ki * TILE, (ki + 1) * TILE)
                s = dot_nt(k[0, 0, ks, :], qb) * c1
                s = s - c2 * far[0, base + ki * TILE : base + (ki + 1) * TILE, qs]
                scores.append((s, v, ks))
        top = functools.reduce(
            jnp.maximum, [jnp.max(s, axis=0, keepdims=True) for s, _, _ in scores]
        )
        total = jnp.zeros((1, TILE), F32)
        mixed = jnp.zeros((q.shape[2], TILE), F32)
        for s, v, ks in scores:
            p = jnp.exp2(s - top)
            total = total + jnp.sum(p, axis=0, keepdims=True)
            mixed = mixed + dot(v[0, 0, ks, :].T, p.astype(BF))
        out[0, qs, :] = (mixed / total).T.astype(BF)
        lse[0, :, qs] = top + jnp.log2(total)


def attend_forward(s, slopes, q, kv_prev, kv_own, kv_mem, far, scaling):
    rows, width = q.shape[1], q.shape[2]
    heads = slopes.shape[0]
    hd = width // heads
    part = lambda i: pl.BlockSpec((1, 1, rows, hd), lambda h: (i, s, 0, h))
    return pl.pallas_call(
        functools.partial(forward_kernel, rows=rows, scaling=scaling),
        grid=(heads,),
        in_specs=[
            pl.BlockSpec(memory_space=pltpu.SMEM),
            pl.BlockSpec((1, rows, hd), lambda h: (s, 0, h)),
            part(0), part(0), part(0), part(1), part(1), part(1),
            pl.BlockSpec((1, 3 * rows, rows), lambda h: (s, 0, 0)),
        ],
        out_specs=[
            pl.BlockSpec((1, rows, hd), lambda h: (0, 0, h)),
            pl.BlockSpec((1, 1, rows), lambda h: (h, 0, 0)),
        ],
        out_shape=[
            jax.ShapeDtypeStruct((1, rows, width), BF),
            jax.ShapeDtypeStruct((heads, 1, rows), F32),
        ],
        compiler_params=pltpu.CompilerParams(vmem_limit_bytes=40 << 20),
        cost_estimate=pl.CostEstimate(
            flops=4 * heads * rows * rows * 3 * hd, bytes_accessed=8 << 20,
            transcendentals=3 * heads * rows * rows),
        name="attend_forward",
    )(slopes, q, kv_prev, kv_own, kv_mem, kv_prev, kv_own, kv_mem, far)


def backward_kernel(
    slopes, q, do, lse, dot_row, far, *refs, rows, scaling, parts, own, extra
):
    head = pl.program_id(0)
    c1 = scaling * LOG2E
    c2 = slopes[head] * LOG2E
    tiles = rows // TILE
    kv = refs[: 2 * parts]
    extras = refs[2 * parts : 2 * parts + extra]
    dq, dkv, dslope = refs[2 * parts + extra], refs[2 * parts + extra + 1 : -1], refs[-1]
    hd = q.shape[2]
    dqs = [jnp.zeros((hd, TILE), F32) for _ in range(tiles)]
    zero = jnp.zeros((8, TILE), F32)
    sums = [[zero, zero, zero] for _ in range(tiles)]
    for part in range(parts):
        k, v = kv[2 * part], kv[2 * part + 1]
        for ki in range(tiles):
            ks = slice(ki * TILE, (ki + 1) * TILE)
            kb, vb = k[0, 0, ks, :], v[0, 0, ks, :]
            kt = kb.T
            dk = jnp.zeros((TILE, hd), F32)
            dv = jnp.zeros((TILE, hd), F32)
            for qi in range(tiles):
                if own and ki > qi:
                    continue
                qs = slice(qi * TILE, (qi + 1) * TILE)
                qb, db = q[0, qs, :], do[0, qs, :]
                base = part * rows + ki * TILE
                dist = far[0, base : base + TILE, qs]
                s = dot_nt(kb, qb) * c1 - c2 * dist
                p = jnp.exp2(s - lse[0, :, qs])
                dp = dot_nt(vb, db)
                weighted = p * dp
                away = p * dist
                ds = weighted - p * dot_row[0, :, qs]
                for index, value in enumerate((weighted, away, away * dp)):
                    value = jnp.sum(value.reshape(TILE // 8, 8, TILE), axis=0)
                    sums[qi][index] = sums[qi][index] + value
                p = p.astype(BF)
                ds = ds.astype(BF)
                dv = dv + dot(p, db)
                dk = dk + dot(ds, qb)
                dqs[qi] = dqs[qi] + dot(kt, ds)
            dk = dk * scaling
            if own:
                dk = dk + extras[2][0, ks, :]
                dv = dv + extras[3][0, ks, :]
            dkv[part][0, ks, :] = dk.astype(dkv[part].dtype)
            dkv[part][1, ks, :] = dv.astype(dkv[part].dtype)
    for qi in range(tiles):
        qs = slice(qi * TILE, (qi + 1) * TILE)
        value = dqs[qi].T * scaling
        if own:
            value = value + extras[0][0, qs, :] + extras[1][0, qs, :]
        dq[0, qs, :] = value.astype(dq.dtype)
        for index in range(3):
            rows_sum = jnp.sum(sums[qi][index], axis=0, keepdims=True)
            dslope[0, index : index + 1, qs] = rows_sum


def attend_backward(s, slopes, q, do, lse, dot_row, far, kvs, own, extras, scaling):
    rows, width = q.shape[1], q.shape[2]
    heads = slopes.shape[0]
    hd = width // heads
    parts = len(kvs)
    part = lambda i: pl.BlockSpec((1, 1, rows, hd), lambda h: (i, s, 0, h))
    plain = pl.BlockSpec((1, rows, hd), lambda h: (0, 0, h))
    lane = pl.BlockSpec((1, 1, rows), lambda h: (h, 0, 0))
    dtype = F32 if own else BF
    operands = [slopes, q, do, lse, dot_row, far]
    specs = [
        pl.BlockSpec(memory_space=pltpu.SMEM),
        pl.BlockSpec((1, rows, hd), lambda h: (s, 0, h)),
        plain, lane, lane,
        pl.BlockSpec((1, parts * rows, rows), lambda h: (s, 0, 0)),
    ]
    for kv in kvs:
        operands += [kv, kv]
        specs += [part(0), part(1)]
    operands += extras
    specs += [plain] * len(extras)
    pair = pl.BlockSpec((2, rows, hd), lambda h: (0, 0, h))
    return pl.pallas_call(
        functools.partial(
            backward_kernel, rows=rows, scaling=scaling, parts=parts, own=own, extra=len(extras)
        ),
        grid=(heads,),
        in_specs=specs,
        out_specs=[plain] + [pair] * parts + [pl.BlockSpec((1, 8, rows), lambda h: (h, 0, 0))],
        out_shape=[jax.ShapeDtypeStruct((1, rows, width), BF if own else F32)]
        + [jax.ShapeDtypeStruct((2, rows, width), dtype)] * parts
        + [jax.ShapeDtypeStruct((heads, 8, rows), F32)],
        compiler_params=pltpu.CompilerParams(vmem_limit_bytes=48 << 20),
        cost_estimate=pl.CostEstimate(
            flops=10 * heads * rows * rows * parts * hd, bytes_accessed=8 << 20,
            transcendentals=parts * heads * rows * rows),
        name="attend_backward_own" if own else "attend_backward_far",
    )(*operands)


def recon_kernel(
    q, ko, vo, kc, vc, cot, recon, dq, dk, dv, dkc, dvc, *, rows, slots, scaling
):
    hd = q.shape[2]
    c1 = scaling * LOG2E
    tiles = rows // TILE
    comp_rows = kc.shape[2]
    dkt = [jnp.zeros((TILE, hd), F32) for _ in range(tiles)]
    dvt = [jnp.zeros((TILE, hd), F32) for _ in range(tiles)]
    dkct = jnp.zeros((comp_rows, hd), F32)
    dvct = jnp.zeros((comp_rows, hd), F32)
    live = lax.broadcasted_iota(jnp.int32, (comp_rows, TILE), 0) < slots
    kct, vct = kc[0, 0].T, vc[0, 0].T
    for qi in range(tiles):
        qs = slice(qi * TILE, (qi + 1) * TILE)
        qb = q[0, qs, :]
        full_s = [dot_nt(ko[0, 0, ki * TILE : (ki + 1) * TILE, :], qb) * c1 for ki in range(tiles)]
        top = functools.reduce(
            jnp.maximum, [jnp.max(s, axis=0, keepdims=True) for s in full_s]
        )
        full_p = [jnp.exp2(s - top) for s in full_s]
        total = functools.reduce(jnp.add, [jnp.sum(p, axis=0, keepdims=True) for p in full_p])
        inverse = 1.0 / total
        full_p = [p * inverse for p in full_p]
        full_low = [p.astype(BF) for p in full_p]
        full = functools.reduce(
            jnp.add,
            [dot(vo[0, 0, ki * TILE : (ki + 1) * TILE, :].T, full_low[ki]) for ki in range(tiles)],
        )
        comp_s = jnp.where(live, dot_nt(kc[0, 0], qb) * c1, -FAR)
        comp_p = jnp.exp2(comp_s - jnp.max(comp_s, axis=0, keepdims=True))
        comp_p = comp_p * (1.0 / jnp.sum(comp_p, axis=0, keepdims=True))
        comp_low = comp_p.astype(BF)
        comp = dot(vct, comp_low)
        spread = full - comp
        recon[0, :, qs] = jnp.sum(spread * spread, axis=0, keepdims=True) / hd**0.5
        dfull = spread * (cot[0, :, qs] * (2.0 / hd**0.5))
        dfull_low = dfull.astype(BF)
        dcomp_low = (-dfull).astype(BF)
        dqt = jnp.zeros((hd, TILE), F32)
        dws = [dot(vo[0, 0, ki * TILE : (ki + 1) * TILE, :], dfull_low) for ki in range(tiles)]
        row = functools.reduce(
            jnp.add, [jnp.sum(p * d, axis=0, keepdims=True) for p, d in zip(full_p, dws)]
        )
        for ki in range(tiles):
            ds = (full_p[ki] * (dws[ki] - row)).astype(BF)
            dkt[ki] = dkt[ki] + dot(ds, qb)
            dvt[ki] = dvt[ki] + dot_nt(full_low[ki], dfull_low)
            dqt = dqt + dot(ko[0, 0, ki * TILE : (ki + 1) * TILE, :].T, ds)
        dw = dot(vc[0, 0], dcomp_low)
        row = jnp.sum(comp_p * dw, axis=0, keepdims=True)
        ds = (comp_p * (dw - row)).astype(BF)
        dkct = dkct + dot(ds, qb)
        dvct = dvct + dot_nt(comp_low, dcomp_low)
        dqt = dqt + dot(kct, ds)
        dq[0, qs, :] = dqt.T * scaling
    for ki in range(tiles):
        dk[0, ki * TILE : (ki + 1) * TILE, :] = dkt[ki] * scaling
        dv[0, ki * TILE : (ki + 1) * TILE, :] = dvt[ki]
    dkc[0] = dkct * scaling
    dvc[0] = dvct


def recon_both(s, q, kv_own, kv_slot, cot, slots, heads, scaling):
    rows, width = q.shape[1], q.shape[2]
    hd = width // heads
    comp_rows = kv_slot.shape[2]
    part = lambda i: pl.BlockSpec((1, 1, rows, hd), lambda h: (i, s, 0, h))
    slot = lambda i: pl.BlockSpec((1, 1, comp_rows, hd), lambda h: (i, s, 0, h))
    plain = pl.BlockSpec((1, rows, hd), lambda h: (0, 0, h))
    small = pl.BlockSpec((1, comp_rows, hd), lambda h: (0, 0, h))
    lane = pl.BlockSpec((1, 1, rows), lambda h: (h, 0, 0))
    big = jax.ShapeDtypeStruct((1, rows, width), F32)
    little = jax.ShapeDtypeStruct((1, comp_rows, width), F32)
    return pl.pallas_call(
        functools.partial(recon_kernel, rows=rows, slots=slots, scaling=scaling),
        grid=(heads,),
        in_specs=[
            pl.BlockSpec((1, rows, hd), lambda h: (s, 0, h)),
            part(0), part(1), slot(0), slot(1),
            pl.BlockSpec((1, 1, rows), lambda h: (s * heads + h, 0, 0)),
        ],
        out_specs=[lane, plain, plain, plain, small, small],
        out_shape=[jax.ShapeDtypeStruct((heads, 1, rows), F32), big, big, big, little, little],
        compiler_params=pltpu.CompilerParams(vmem_limit_bytes=40 << 20),
        cost_estimate=pl.CostEstimate(
            flops=12 * heads * rows * (rows + comp_rows) * hd, bytes_accessed=8 << 20,
            transcendentals=heads * rows * (rows + comp_rows)),
        name="recon_both",
    )(q, kv_own, kv_own, kv_slot, kv_slot, cot)


def reduce_rows(part, dp_index):
    blocks, cores = lax.axis_size("blk"), lax.axis_size("dp")
    rows = part.shape[0] // (blocks * cores)
    split = part.astype(BF).reshape(blocks, cores, rows, part.shape[1])
    away = lax.dynamic_index_in_dim(split, 1 - dp_index, 1, keepdims=False)
    here = lax.dynamic_index_in_dim(split, dp_index, 1, keepdims=False)
    total = here + swap(away, "dp")
    total = total.reshape(blocks * rows, part.shape[1])
    return lax.psum_scatter(total, "blk", scatter_dimension=0, tiled=True).astype(F32)


def butterfly(x):
    x = x + swap(x, "dp")
    step = 1
    while step < lax.axis_size("blk"):
        x = x + swap(x, "blk", step)
        step *= 2
    return x


def shards(
    tokens, doc_ids, w_qkv, w_out, slopes, w_up, w_down, w_comp, comp_bias,
    norm1_gain, norm1_bias, norm2_gain, norm2_bias, out_cot, recon_cot,
):
    seqs, rows, model = tokens.shape
    heads = slopes.shape[0]
    width = w_qkv.shape[2]
    hd = width // heads
    slots = rows // 3
    used = 3 * slots
    slot_pad = -(-slots // 16) * 16
    position = lax.axis_index("blk")
    dp_index = lax.axis_index("dp")
    head_index = lax.axis_index("head")
    scaling = hd ** (-0.5)
    memory = CSEGS * slots
    half = model // lax.axis_size("head")

    w_out_other = swap(w_out, "head")

    inputs = tokens.astype(F32)
    unit1, inverse1 = row_stats(inputs)
    normed = (unit1 * norm1_gain + norm1_bias).astype(BF)
    kv_own = jnp.einsum("sgd,tde->tsge", normed, w_qkv[1:], preferred_element_type=F32).astype(BF)
    kv_prev = shift(kv_own, "blk", 1)
    triples = normed[:, :used].reshape(seqs, slots, 3, model)
    packed = jnp.einsum("scrd,rde->sce", triples, w_comp, preferred_element_type=F32) + comp_bias
    packed = packed.astype(BF)
    kv_slot = jnp.einsum("scd,tde->tsce", packed, w_qkv[1:], preferred_element_type=F32).astype(BF)
    kv_mem = jnp.concatenate(
        [shift(kv_slot, "blk", lag) for lag in range(CSEGS + 1, 1, -1)]
        + [jnp.zeros((2, seqs, rows - memory, width), BF)],
        2,
    )
    kv_slot_pad = jnp.pad(kv_slot, ((0, 0), (0, 0), (0, slot_pad - slots), (0, 0)))
    q = jnp.einsum("sgd,de->sge", normed, w_qkv[0], preferred_element_type=F32).astype(BF)

    local = jnp.arange(rows, dtype=jnp.int32)
    query_pos = position * rows + local
    mem_seg = position - 1 - CSEGS + local // slots
    mem_pos = mem_seg * rows + 3 * (local % slots) + 1
    key_pos = jnp.concatenate([query_pos - rows, query_pos, mem_pos])
    key_live = jnp.concatenate(
        [query_pos - rows >= 0, query_pos >= 0, (mem_seg >= 0) & (local < memory)]
    )
    query_doc = lax.dynamic_slice_in_dim(doc_ids, position * rows, rows, 1)
    lead = jnp.full((seqs, (CSEGS + 1) * rows), -1, jnp.int32)
    padded_doc = jnp.concatenate([lead, doc_ids], 1)
    window = lax.dynamic_slice_in_dim(padded_doc, position * rows, (CSEGS + 2) * rows, 1)
    window = window.reshape(seqs, CSEGS + 2, rows)
    mem_doc = window[:, :CSEGS, 0:used:3].reshape(seqs, memory)
    mem_doc = jnp.pad(mem_doc, ((0, 0), (0, rows - memory)), constant_values=-1)
    key_doc = jnp.concatenate([window[:, CSEGS], window[:, CSEGS + 1], mem_doc], 1)
    apart = query_pos[None, :] - key_pos[:, None]
    seen = (
        key_live[None, :, None]
        & (apart >= 0)[None]
        & (key_doc[:, :, None] == query_doc[:, None, :])
    )
    far = jnp.where(seen, jnp.log((1 + jnp.maximum(apart, 0)).astype(F32))[None], FAR)

    cot_rows = recon_cot.reshape(seqs * heads, 1, rows)
    recon_parts = [
        recon_both(s, q, kv_own, kv_slot_pad, cot_rows, slots, heads, scaling)
        for s in range(seqs)
    ]
    recon = jnp.stack([part[0].reshape(heads, rows) for part in recon_parts])

    dhidden = jnp.einsum("sge,fe->sgf", out_cot, w_down, preferred_element_type=F32).astype(BF)

    attended, lses, others = [], [], []
    for s in range(seqs):
        out, lse = attend_forward(s, slopes, q, kv_prev, kv_own, kv_mem, far, scaling)
        attended.append(out)
        lses.append(lse)
        others.append(swap(out, "head"))

    middles, units2, inverses2, normed2s, hiddens, dinners, dn2s = [], [], [], [], [], [], []
    ffn_parts = []
    for s in range(seqs):
        branch = dot(attended[s][0], w_out) + dot(others[s][0], w_out_other)
        middle = inputs[s] + branch
        unit2, inverse2 = row_stats(middle)
        normed2 = (unit2 * norm2_gain + norm2_bias).astype(BF)
        inner = dot(normed2, w_up)
        inside = jnp.tanh(GELU_A * (inner + GELU_B * inner * inner * inner))
        hidden = (0.5 * inner * (1.0 + inside)).astype(BF)
        slope = 0.5 * (1.0 + inside) + 0.5 * inner * (1.0 - inside * inside) * GELU_A * (
            1.0 + 3.0 * GELU_B * inner * inner
        )
        dinner = (dhidden[s].astype(F32) * slope).astype(BF)
        dn2 = dot_nt(dinner, w_up).astype(BF)
        middles.append(middle)
        units2.append(unit2)
        inverses2.append(inverse2)
        normed2s.append(normed2)
        hiddens.append(hidden)
        dinners.append(dinner)
        dn2s.append((dn2, swap(dn2, "head")))
        ffn_parts.append(dot(hidden, w_down).astype(BF))
    normed2 = jnp.concatenate(normed2s, 0)
    hidden = jnp.concatenate(hiddens, 0)
    dinner = jnp.concatenate(dinners, 0)
    flat_cot = out_cot.reshape(seqs * rows, model)
    grad_up = dot_tn(normed2, dinner)
    grad_down = dot_tn(flat_cot, hidden)
    up_down = reduce_rows(jnp.concatenate([grad_up, grad_down], 1), dp_index)
    ffn_part = jnp.stack(ffn_parts)
    ffn_other = swap(ffn_part, "head")
    layer_out = jnp.stack(middles) + (ffn_part.astype(F32) + ffn_other.astype(F32))
    layer_out = layer_out.astype(BF)

    dmiddles, dbranches, dmixeds, dot_rows = [], [], [], []
    dgain2 = jnp.zeros((model,), F32)
    dbias2 = jnp.zeros((model,), F32)
    far_parts = []
    for s in range(seqs):
        dn2 = dn2s[s][0].astype(F32) + dn2s[s][1].astype(F32)
        dgain2 = dgain2 + jnp.sum(dn2 * units2[s], axis=0)
        dbias2 = dbias2 + jnp.sum(dn2, axis=0)
        dmiddle = out_cot[s].astype(F32) + norm_back(dn2, units2[s], inverses2[s], norm2_gain)
        dbranch = dmiddle.astype(BF)
        dmixed = dot_nt(dbranch, w_out).astype(BF)
        product = dmixed.astype(F32) * attended[s][0].astype(F32)
        dot_row = jnp.sum(product.reshape(rows, heads, hd), axis=-1).T.reshape(heads, 1, rows)
        dmiddles.append(dmiddle)
        dbranches.append(dbranch)
        dmixeds.append(dmixed[None])
        dot_rows.append(dot_row)
        far_parts.append(
            attend_backward(
                s, slopes, q, dmixed[None], lses[s], dot_row,
                jnp.concatenate([far[:, :rows], far[:, 2 * rows :]], 1),
                [kv_prev, kv_mem], False, [], scaling,
            )
        )
    back_kv = [shift(part[1], "blk", -1) for part in far_parts]
    dmem = jnp.stack([part[2] for part in far_parts], 1)
    dslot = jnp.stack(
        [
            jnp.stack([part[4][0, :slots], part[5][0, :slots]]) for part in recon_parts
        ],
        1,
    )
    for index, lag in enumerate(range(CSEGS + 1, 1, -1)):
        got = shift(dmem[:, :, index * slots : (index + 1) * slots], "blk", -lag)
        dslot = dslot + got.astype(F32)
    dslot = dslot.astype(BF)
    dpacked_part = jnp.einsum("tsce,tde->scd", dslot, w_qkv[1:], preferred_element_type=F32)
    dpacked_part = dpacked_part.astype(BF)
    away = lax.dynamic_slice_in_dim(dpacked_part, (1 - head_index) * half, half, 2)
    here = lax.dynamic_slice_in_dim(dpacked_part, head_index * half, half, 2)
    dpacked = (here.astype(F32) + swap(away, "head").astype(F32)).astype(BF)
    w_comp_half = lax.dynamic_slice_in_dim(w_comp, head_index * half, half, 2)
    grad_comp = jnp.einsum("scrd,sce->dre", triples, dpacked, preferred_element_type=F32)
    dcomp_bias = jnp.sum(dpacked.astype(F32), axis=(0, 1))
    dtriples = jnp.einsum("sce,rde->scrd", dpacked, w_comp_half, preferred_element_type=F32)
    dtriples = dtriples.reshape(seqs, used, model)
    dtriples = jnp.pad(dtriples, ((0, 0), (0, rows - used), (0, 0)))

    grad_out = dot_tn(
        jnp.concatenate(dbranches, 0), jnp.concatenate([a[0] for a in attended], 0)
    )

    own_parts = []
    for s in range(seqs):
        own_parts.append(
            attend_backward(
                s, slopes, q, dmixeds[s], lses[s], dot_rows[s], far[:, rows : 2 * rows],
                [kv_own], True,
                [far_parts[s][0], recon_parts[s][1], recon_parts[s][2], recon_parts[s][3]],
                scaling,
            )
        )
    dn1s, dqs, dkvs = [], [], []
    for s in range(seqs):
        dq = own_parts[s][0][0]
        dkv = (own_parts[s][1] + back_kv[s].astype(F32)).astype(BF)
        dn1 = dot_nt(dq, w_qkv[0]) + dot_nt(dkv[0], w_qkv[1]) + dot_nt(dkv[1], w_qkv[2])
        dn1 = (dn1 + dtriples[s]).astype(BF)
        dn1s.append((dn1, swap(dn1, "head")))
        dqs.append(dq)
        dkvs.append(dkv)
    flat_normed = normed.reshape(seqs * rows, model)
    flat_packed = packed.reshape(seqs * slots, model)
    dq_all = jnp.concatenate(dqs, 0)
    dkv_all = jnp.concatenate(dkvs, 1)
    flat_slot = dslot.reshape(2, seqs * slots, width)
    grad_q = dot_tn(flat_normed, dq_all)
    grad_k = dot_tn(flat_normed, dkv_all[0]) + dot_tn(flat_packed, flat_slot[0])
    grad_v = dot_tn(flat_normed, dkv_all[1]) + dot_tn(flat_packed, flat_slot[1])
    late = reduce_rows(
        jnp.concatenate([grad_q, grad_k, grad_v, grad_out, grad_comp.reshape(model, 3 * half)], 1),
        dp_index,
    )
    share = late.shape[0]
    comp_mine = late[:, 4 * width :].reshape(share, 3, half)
    comp_all = lax.all_gather(comp_mine, "head", axis=2, tiled=True)

    grad_tokens = []
    dgain1 = jnp.zeros((model,), F32)
    dbias1 = jnp.zeros((model,), F32)
    for s in range(seqs):
        dn1 = dn1s[s][0].astype(F32) + dn1s[s][1].astype(F32)
        dgain1 = dgain1 + jnp.sum(dn1 * unit1[s], axis=0)
        dbias1 = dbias1 + jnp.sum(dn1, axis=0)
        grad = dmiddles[s] + norm_back(dn1, unit1[s], inverse1[s], norm1_gain)
        grad_tokens.append(grad.astype(BF))
    dslopes = jnp.zeros((heads,), F32)
    for s in range(seqs):
        sums = far_parts[s][-1] + own_parts[s][-1]
        dslopes = dslopes - jnp.sum(sums[:, 2] - sums[:, 0] * sums[:, 1], axis=1)
    comp_bias_all = jnp.zeros((model,), F32)
    comp_bias_all = lax.dynamic_update_slice_in_dim(comp_bias_all, dcomp_bias, head_index * half, 0)
    small = jnp.concatenate([dgain1, dbias1, dgain2, dbias2, comp_bias_all, jnp.pad(dslopes, (0, 128 - heads))])
    small = butterfly(small.reshape(-1, 128)).reshape(-1)
    comp_bias_sum = small[4 * model : 5 * model]
    comp_bias_sum = comp_bias_sum + swap(comp_bias_sum, "head")
    return (
        layer_out,
        recon,
        jnp.stack(grad_tokens),
        jnp.transpose(late[:, : 3 * width].reshape(share, 3, width), (1, 0, 2)),
        late[:, 3 * width : 4 * width].T,
        small[5 * model : 5 * model + heads],
        up_down[:, : w_up.shape[1]],
        up_down[:, w_up.shape[1] :].T,
        jnp.transpose(comp_all, (1, 0, 2)),
        comp_bias_sum,
        small[:model],
        small[model : 2 * model],
        small[2 * model : 3 * model],
        small[3 * model : 4 * model],
    )


def solution(mesh):
    in_specs = (
        P("dp", "blk", None),
        P("dp", None),
        P(None, None, "head"),
        P("head", None),
        P("head"),
        P(None, "head"),
        P("head", None),
        P(),
        P(),
        P(),
        P(),
        P(),
        P(),
        P("dp", "blk", None),
        P("dp", "head", "blk"),
    )
    out_specs = (
        P("dp", "blk", None),
        P("dp", "head", "blk"),
        P("dp", "blk", None),
        P(None, ("blk", "dp"), "head"),
        P("head", ("blk", "dp")),
        P("head"),
        P(("blk", "dp"), "head"),
        P("head", ("blk", "dp")),
        P(None, ("blk", "dp"), None),
        P(),
        P(),
        P(),
        P(),
        P(),
    )
    return jax.shard_map(shards, mesh=mesh, in_specs=in_specs, out_specs=out_specs, check_vma=False)
```

time: 1630 us -> 638 us (0.39)
  waiting for transfers between devices: 1020 us -> 204 us
  matrix products: 242 us -> 97.5 us
  blocking collectives: 97.5 us -> 14.2 us
  Pallas kernels: 0 us -> 79.2 us
  other arithmetic: 121 us -> 65.9 us
  starting transfers between devices: 38 us -> 67.5 us
    psum x3 -> x0, waiting for transfers between devices: 426 us -> none  [the longest x1 199 us: shards(): layer_out = (middle + lax.psum(ffn_part, 'head')).astype(jnp.bfloat16)]
    reduce_scatter x4 -> x2, waiting for transfers between devices: 343 us -> 4.63 us  [reduce_rows(): lax.psum_scatter(total, 'blk', scatter_dimension=0, tiled=True).astype(F32)]
    unnamed x9 -> x2, waiting for transfers between devices: 152 us -> 0.03 us
    dot_general x40 -> x34, matrix products: 232 us -> 97.5 us  [the longest x8 24.9 us: dot_tn(): lax.dot_general(a, b, (((0,), (0,)), ((), ())), preferred_element_type=F32)]
    ppermute x16 -> x25, waiting for transfers between devices: 94 us -> 199 us  [the longest x16 108 us: swap(): return lax.ppermute(x, axis, [(i, i ^ step) for i in range(devices)])]
    psum x2 -> x0, blocking collectives: 97.5 us -> none  [the longest x1 61.3 us: shards(): lax.psum((dgain_one, dbias_one, dgain_two, dbias_two, dcomp_bias, dslope_...]
    pallas_call x0 -> x8, Pallas kernels: none -> 79.2 us  [the longest x4 37.8 us: attend_backward(): pl.pallas_call(functools.partial(backward_kernel, rows=rows, scaling=scal...]
    reduce_sum x14 -> x11, other arithmetic: 78 us -> 13.3 us  [the longest x1 3.88 us: shards(): dgain1 = dgain1 + jnp.sum(dn1 * unit1[s], axis=0)]
  transfers between devices with their start and end apart: 24 -> 27, of which waited for: 11 -> 14; matrix products, arithmetic and copies ran while one was open for 15% -> 29% of each run, Pallas kernels for 0% -> 13%
where the time goes in v1:
time: 638 us; the launch traced here: 628 us
  waiting for transfers between devices  204 us (32%)
  matrix products  97.5 us (15%)
  local copies, waits for them, and re-layouts  83.7 us (13%)
  Pallas kernels  79.2 us (12%)
  starting transfers between devices  67.5 us (11%)
  other arithmetic  65.9 us (10%)
  between operations  15.9 us (2%)
  blocking collectives  14.2 us (2%)
    ppermute x16, waiting for transfers between devices, swap(): return lax.ppermute(x, axis, [(i, i ^ step) for i in range(devices)])  108 us
    ppermute x9, waiting for transfers between devices, shift(): return lax.ppermute(x, axis, pairs)  90.9 us
    ppermute x16, starting transfers between devices, swap(): return lax.ppermute(x, axis, [(i, i ^ step) for i in range(devices)])  42.8 us
    pallas_call x4, Pallas kernels, attend_backward(): pl.pallas_call(functools.partial(backward_kernel, rows=rows, scaling=scal...  37.8 us
    unnamed x192, local copies, waits for them, and re-layouts  27.7 us
    dot_general x8, matrix products, dot_tn(): lax.dot_general(a, b, (((0,), (0,)), ((), ())), preferred_element_type=F32)  24.9 us
    dot_general x8, matrix products, dot(): return jnp.dot(a, b, preferred_element_type=F32)  24.8 us
    ppermute x9, starting transfers between devices, shift(): return lax.ppermute(x, axis, pairs)  24.6 us
  transfers between devices with their start and end apart: 27, of which 14 were waited for; matrix products, arithmetic and copies ran while one was open for 29% of the time, Pallas kernels for 13%

profile of v1, /device:TPU:0, one launch (start us, length us, event | category | flops | bytes accessed | tf_op | source)
XLA Modules:
  0.0 627.7 jit_solution(8858650967391661962)
XLA Ops:
  22.2 6.9 %collective-permute-start.1 = (bf16[2,2,170,512]{3,1,2,0:T(2,128)(2,1)}, bf16[2,2,170,512]{3,1,2,0:T(2,128)(2,1)}, u32[]{:S(2)}, u32[]{:S(2)}) collective-permute-start(bf16[2,2,170,512]{3,1,2,0:T(2,128)(2,1)} %copy.92), channel_id=1, source_target_pairs={{0,16},{4,20},{8,24},{12,28},{1,17},{5,21},{9,25},{13,29},{2,18},{... | collective-permute-start | bytes 2088968 | tf_op jit(solution)/shard_map/ppermute | solution.py:38
  49.0 9.5 %fusion.38 = bf16[2,512,2048]{2,1,0:T(8,128)(2,1)} fusion(bf16[2,512,1024]{2,1,0:T(8,128)(2,1)} %param.28, bf16[2048,1024]{1,0:T(8,128)(2,1)} %param.21), kind=kOutput, calls=%fused_computation.55 | convolution fusion | flops 4297064448 | bytes 10485760 | tf_op jit(solution)/shard_map/sge,fe->sgf/dot_general | solution.py:400
  64.6 12.2 %recon_both.2 = (f32[4,1,512]{2,1,0:T(1,128)S(1)}, f32[1,512,512]{2,1,0:T(8,128)S(1)}, f32[1,512,512]{2,1,0:T(8,128)S(1)}, f32[1,512,512]{2,1,0:T(8,128)S(1)}, f...) custom-call(bf16[2,512,512]{2,1,0:T(8,128)(2,1)S(1)} %convolution_convert_fusion.1.q, ...), custom_call_target="tpu_custom_call" | custom-call | flops 2164260864 | bytes 8388608 | tf_op jit(solution)/shard_map/recon_both/pallas_call | solution.py:294
  87.2 8.7 %attend_forward.3 = (bf16[1,512,512]{2,1,0:T(8,128)(2,1)}, f32[4,1,512]{2,1,0:T(1,128)S(1)}) custom-call(f32[4]{0:T(128)S(1)} %copy-done.22, bf16[2,512,512]{2,1,0:T(8,128)(2,1)S(1)} %convolution_convert_fusion.1.q, bf16[2,2,512,512]{3,2,1,0:T(8,128)(2,1)} %collective-permute-done.kp.vp.refs_0_.refs_1_, ...), custom_call_target="tpu_custom_call" | custom-call | flops 1610612736 | bytes 8388608 | tf_op jit(solution)/shard_map/attend_forward/pallas_call | solution.py:95
  97.4 12.2 %recon_both.3 = (f32[4,1,512]{2,1,0:T(1,128)S(1)}, f32[1,512,512]{2,1,0:T(8,128)S(1)}, f32[1,512,512]{2,1,0:T(8,128)S(1)}, f32[1,512,512]{2,1,0:T(8,128)S(1)}, f...) custom-call(bf16[2,512,512]{2,1,0:T(8,128)(2,1)S(1)} %convolution_convert_fusion.1.q, ...), custom_call_target="tpu_custom_call" | custom-call | flops 2164260864 | bytes 8388608 | tf_op jit(solution)/shard_map/recon_both/pallas_call | solution.py:294
  132.0 8.2 %attend_forward.2 = (bf16[1,512,512]{2,1,0:T(8,128)(2,1)S(1)}, f32[4,1,512]{2,1,0:T(1,128)S(1)}) custom-call(f32[4]{0:T(128)S(1)} %copy-done.22, bf16[2,512,512]{2,1,0:T(8,128)(2,1)S(1)} %convolution_convert_fusion.1.q, bf16[2,2,512,512]{3,2,1,0:T(8,128)(2,1)} %collective-permute-done.kp.vp.refs_0_.refs_1_, ...), custom_call_target="tpu_custom_call" | custom-call | flops 1610612736 | bytes 8388608 | tf_op jit(solution)/shard_map/attend_forward/pallas_call | solution.py:95
  145.5 6.7 %collective-permute-done.4 = bf16[1,512,512]{2,1,0:T(8,128)(2,1)S(1)} collective-permute-done((bf16[1,512,512]{2,1,0:T(8,128)(2,1)S(1)}, bf16[1,512,512]{2,1,0:T(8,128)(2,1)S(1)}, u32[]{:S(2)}, u32[]{:S(2)}) %collective-permute-start.4) | collective-permute-done | bytes 524320 | tf_op jit(solution)/shard_map/ppermute | solution.py:43
  161.4 9.4 %fusion.10 = (bf16[512,2048]{1,0:T(8,128)(2,1)S(1)}, bf16[512,2048]{1,0:T(8,128)(2,1)S(1)}, bf16[512,2048]{1,0:T(8,128)(2,1)S(1)}, bf16[512,2048]{1,0:T(8,128)(2,1)}) fusion(bf16[2,512,2048]{2,1,0:T(8,128)(2,1)S(1)} %copy-done.86, f32[512,2048]{1,0:T(8,128)S(1)} %fusion.204, bf16[512,1024]{1,0:T(8,128)(2,1)S(1)} %get-tuple-element.181, ...), kind=kOutput, calls=%fused_computation.22 | convolution fusion | flops 2193620992 | bytes 22020096 | tf_op jit(solution)/shard_map/dot_general | solution.py:24
  182.6 6.6 %fusion.32 = bf16[2048,1024]{0,1:T(8,128)(2,1)S(1)} fusion(bf16[1024,1024]{1,0:T(8,128)(2,1)S(1)} %bitcast.349, bf16[512,2048]{1,0:T(8,128)(2,1)S(1)} %get-tuple-element.161, bf16[512,2048]{1,0:T(8,128)(2,1)} %get-tuple-element.162), kind=kOutput, calls=%fused_computation.53 | convolution fusion | flops 4305453056 | bytes 10485760 | tf_op jit(solution)/shard_map/dot_general | solution.py:32
  192.5 14.2 %collective-permute-done.10 = bf16[512,1024]{1,0:T(8,128)(2,1)S(1)} collective-permute-done((bf16[512,1024]{1,0:T(8,128)(2,1)S(1)}, bf16[512,1024]{1,0:T(8,128)(2,1)S(1)}, u32[]{:S(2)}, u32[]{:S(2)}) %collective-permute-start.10) | collective-permute-done | bytes 1048608 | tf_op jit(solution)/shard_map/ppermute | solution.py:43
  206.6 18.6 %collective-permute-done.8 = bf16[512,1024]{1,0:T(8,128)(2,1)S(1)} collective-permute-done((bf16[512,1024]{1,0:T(8,128)(2,1)S(1)}, bf16[512,1024]{1,0:T(8,128)(2,1)S(1)}, u32[]{:S(2)}, u32[]{:S(2)}) %collective-permute-start.8) | collective-permute-done | bytes 1048608 | tf_op jit(solution)/shard_map/ppermute | solution.py:43
  244.6 11.4 %attend_backward_far.3 = (f32[1,512,512]{2,1,0:T(8,128)S(1)}, bf16[2,512,512]{2,1,0:T(8,128)(2,1)S(1)}, bf16[2,512,512]{2,1,0:T(8,128)(2,1)S(1)}, f32[4,8,512]{2,1,0:T(8,128)S(1)}) custom-call(f32[4]{0:T(128)S(1)} %copy-done.22, bf16[2,512,512]{2,1,0:T(8,128)(2,1)S(1)} %convolution_convert_fusion.1.q, bf16[1,512,512]{2,1,0:T(8,128)(2,1)S(1)} %bitcast.316, ...), custom_call_target="tpu_custom_call" | custom-call | flops 2684354560 | bytes 8388608 | tf_op jit(solution)/shard_map/attend_backward_far/pallas_call | solution.py:202
  257.4 11.9 %attend_backward_far.2 = (f32[1,512,512]{2,1,0:T(8,128)S(1)}, bf16[2,512,512]{2,1,0:T(8,128)(2,1)}, bf16[2,512,512]{2,1,0:T(8,128)(2,1)S(1)}, f32[4,8,512]{2,1,0:T(8,128)S(1)}) custom-call(f32[4]{0:T(128)S(1)} %copy-done.22, bf16[2,512,512]{2,1,0:T(8,128)(2,1)S(1)} %convolution_convert_fusion.1.q, bf16[1,512,512]{2,1,0:T(8,128)(2,1)S(1)} %bitcast.318, ...), custom_call_target="tpu_custom_call" | custom-call | flops 2684354560 | bytes 8388608 | tf_op jit(solution)/shard_map/attend_backward_far/pallas_call | solution.py:202
  276.0 7.1 %attend_backward_own.2 = (bf16[1,512,512]{2,1,0:T(8,128)(2,1)S(1)}, f32[2,512,512]{2,1,0:T(8,128)}, f32[4,8,512]{2,1,0:T(8,128)S(1)}) custom-call(f32[4]{0:T(128)S(1)} %copy-done.22, bf16[2,512,512]{2,1,0:T(8,128)(2,1)S(1)} %convolution_convert_fusion.1.q, bf16[1,512,512]{2,1,0:T(8,128)(2,1)S(1)} %bitcast.319, f32[4,1,512]{2,1,0:T(1,128)S(1)} %get-tuple-element.48.lse, ...), custom_call_target="tpu_custom_call" | custom-call | flops 1342177280 | bytes 8388608 | tf_op jit(solution)/shard_map/attend_backward_own/pallas_call | solution.py:202
  283.2 7.3 %attend_backward_own.3 = (bf16[1,512,512]{2,1,0:T(8,128)(2,1)S(1)}, f32[2,512,512]{2,1,0:T(8,128)}, f32[4,8,512]{2,1,0:T(8,128)S(1)}) custom-call(f32[4]{0:T(128)S(1)} %copy-done.22, bf16[2,512,512]{2,1,0:T(8,128)(2,1)S(1)} %convolution_convert_fusion.1.q, bf16[1,512,512]{2,1,0:T(8,128)(2,1)S(1)} %bitcast.317, f32[4,1,512]{2,1,0:T(1,128)S(1)} %get-tuple-element.61.lse, ...), custom_call_target="tpu_custom_call" | custom-call | flops 1342177280 | bytes 8388608 | tf_op jit(solution)/shard_map/attend_backward_own/pallas_call | solution.py:202
  296.3 88.5 %collective-permute-done.11 = bf16[2,2,170,512]{3,1,2,0:T(2,128)(2,1)S(1)} collective-permute-done((bf16[2,2,170,512]{3,1,2,0:T(2,128)(2,1)S(1)}, bf16[2,2,170,512]{3,1,2,0:T(2,128)(2,1)S(1)}, u32[]{:S(2)}, u32[]{:S(2)}) %collective-permute-start.11) | collective-permute-done | bytes 696352 | tf_op jit(solution)/shard_map/ppermute | solution.py:38
  409.0 7.6 %copy.113 = bf16[1024,3,512]{2,1,0:T(4,128)(2,1)} copy(bf16[1024,3,512]{0,2,1:T(8,128)(2,1)} %fusion.44) | data formatting | bytes 6291456 | tf_op jit(solution)/shard_map/scrd,sce->dre/transpose | solution.py:486
  416.6 9.8 %concatenate.78 = bf16[8,2,64,1536]{3,2,1,0:T(8,128)(2,1)} reshape(bf16[1024,3,512]{2,1,0:T(4,128)(2,1)} %copy.113) | data formatting | bytes 6291456 | tf_op jit(solution)/shard_map/concatenate | solution.py:524
  475.6 23.4 %collective-permute-done.7 = bf16[2,512,1024]{2,1,0:T(8,128)(2,1)} collective-permute-done((bf16[2,512,1024]{2,1,0:T(8,128)(2,1)}, bf16[2,512,1024]{2,1,0:T(8,128)(2,1)}, u32[]{:S(2)}, u32[]{:S(2)}) %collective-permute-start.7) | collective-permute-done | bytes 2097184 | tf_op jit(solution)/shard_map/ppermute | solution.py:43
  504.5 16.9 %collective-permute-done.17 = bf16[512,1024]{1,0:T(8,128)(2,1)} collective-permute-done((bf16[512,1024]{1,0:T(8,128)(2,1)S(1)}, bf16[512,1024]{1,0:T(8,128)(2,1)}, u32[]{:S(2)}, u32[]{:S(2)}) %collective-permute-start.17) | collective-permute-done | bytes 1048608 | tf_op jit(solution)/shard_map/ppermute | solution.py:43
  521.5 20.8 %collective-permute-done.15 = bf16[512,1024]{1,0:T(8,128)(2,1)} collective-permute-done((bf16[512,1024]{1,0:T(8,128)(2,1)}, bf16[512,1024]{1,0:T(8,128)(2,1)}, u32[]{:S(2)}, u32[]{:S(2)}) %collective-permute-start.15) | collective-permute-done | bytes 1048608 | tf_op jit(solution)/shard_map/ppermute | solution.py:43
  547.5 15.4 %collective-permute-start.20 = (f32[41,128]{1,0:T(8,128)S(1)}, f32[41,128]{1,0:T(8,128)S(1)}, u32[]{:S(2)}, u32[]{:S(2)}) collective-permute-start(f32[41,128]{1,0:T(8,128)S(1)} %bitcast_add_fusion.1), channel_id=1, source_target_pairs={{0,4},{4,0},{8,12},{12,8},{16,20},{20,16},{24,28},{28,24},{1,5},{5... | collective-permute-start | bytes 62984 | tf_op jit(solution)/shard_map/ppermute | solution.py:43
  564.7 16.0 %collective-permute-start.21 = (f32[41,128]{1,0:T(8,128)S(1)}, f32[41,128]{1,0:T(8,128)S(1)}, u32[]{:S(2)}, u32[]{:S(2)}) collective-permute-start(f32[41,128]{1,0:T(8,128)S(1)} %fusion.238), channel_id=1, source_target_pairs={{0,8},{4,12},{8,0},{12,4},{16,24},{20,28},{24,16},{28,20},{1,9},{5... | collective-permute-start | bytes 62984 | tf_op jit(solution)/shard_map/ppermute | solution.py:43
  603.0 14.2 %all_gather.3 = f32[64,3,1024]{2,1,0:T(4,128)S(1)} all-gather(f32[64,3,512]{2,1,0:T(4,128)S(1)} %reshape.307), channel_id=1, replica_groups=mesh['blk'=8,'dp'=2,'head'=2] {'head'}, dimensions={2}, use_global_device_ids=true | all-gather | bytes 1179648 | tf_op jit(solution)/shard_map/all_gather | solution.py:529
  (386 shorter events, 248.0 us)
Async XLA Ops:
  7.2 586.1 %reduce-scatter.5.cloned.1.call-start = ((), (), s32[]{:S(2)}) async-start(), calls=%async_computation.3 | async-start | bytes 4718592 | tf_op jit(solution)/shard_map/reduce_scatter | solution.py:320
  22.2 58.3 %collective-permute-start.1 = (bf16[2,2,170,512]{3,1,2,0:T(2,128)(2,1)}, bf16[2,2,170,512]{3,1,2,0:T(2,128)(2,1)}, u32[]{:S(2)}, u32[]{:S(2)}) collective-permute-start(bf16[2,2,170,512]{3,1,2,0:T(2,128)(2,1)} %copy.92), channel_id=1, source_target_pairs={{0,16},{4,20},{8,24},{12,28},{1,17},{5,21},{9,25},{13,29},{2,18},{... | collective-permute-start | bytes 2088968 | tf_op jit(solution)/shard_map/ppermute | solution.py:38
  29.1 52.6 %collective-permute-start.2 = (bf16[2,2,170,512]{3,1,2,0:T(2,128)(2,1)}, bf16[2,2,170,512]{3,1,2,0:T(2,128)(2,1)}, u32[]{:S(2)}, u32[]{:S(2)}) collective-permute-start(bf16[2,2,170,512]{3,1,2,0:T(2,128)(2,1)} %copy.92), channel_id=1, source_target_pairs={{0,12},{4,16},{8,20},{12,24},{16,28},{1,13},{5,17},{9,21},{13,25},... | collective-permute-start | bytes 2088968 | tf_op jit(solution)/shard_map/ppermute | solution.py:38
  34.4 48.5 %collective-permute-start.3 = (bf16[2,2,170,512]{3,1,2,0:T(2,128)(2,1)}, bf16[2,2,170,512]{3,1,2,0:T(2,128)(2,1)}, u32[]{:S(2)}, u32[]{:S(2)}) collective-permute-start(bf16[2,2,170,512]{3,1,2,0:T(2,128)(2,1)} %copy.92), channel_id=1, source_target_pairs={{0,8},{4,12},{8,16},{12,20},{16,24},{20,28},{1,9},{5,13},{9,17},{1... | collective-permute-start | bytes 2088968 | tf_op jit(solution)/shard_map/ppermute | solution.py:38
  40.3 46.9 %collective-permute-start = (bf16[2,2,512,512]{3,2,1,0:T(8,128)(2,1)}, bf16[2,2,512,512]{3,2,1,0:T(8,128)(2,1)}, u32[]{:S(2)}, u32[]{:S(2)}) collective-permute-start(bf16[2,2,512,512]{3,2,1,0:T(8,128)(2,1)} %convert_bitcast_fusion.ko.vo.refs_0_.refs_1_), channel_id=1, source_target_pairs={{0,4},{4,8},{8,12},{12,16},{16,20},{20,24},{24,28},{1,5},{5,9},{9,... | collective-permute-start | bytes 6291464 | tf_op jit(solution)/shard_map/ppermute | solution.py:38
  43.9 96.9 %collective-permute-start.5 = (bf16[512,1024]{1,0:T(8,128)(2,1)}, bf16[512,1024]{1,0:T(8,128)(2,1)}, u32[]{:S(2)}, u32[]{:S(2)}) collective-permute-start(bf16[512,1024]{1,0:T(8,128)(2,1)} %param.18), channel_id=1, source_target_pairs={{0,1},{1,0},{2,3},{3,2},{4,5},{5,4},{6,7},{7,6},{8,9},{9,8},{10,11... | collective-permute-start | bytes 3145736 | tf_op jit(solution)/shard_map/ppermute | solution.py:43
  95.9 45.0 %collective-permute-start.6 = (bf16[1,512,512]{2,1,0:T(8,128)(2,1)}, bf16[1,512,512]{2,1,0:T(8,128)(2,1)}, u32[]{:S(2)}, u32[]{:S(2)}) collective-permute-start(bf16[1,512,512]{2,1,0:T(8,128)(2,1)} %get-tuple-element.45), channel_id=1, source_target_pairs={{0,1},{1,0},{2,3},{3,2},{4,5},{5,4},{6,7},{7,6},{8,9},{9,8},{10,11... | collective-permute-start | bytes 1572872 | tf_op jit(solution)/shard_map/ppermute | solution.py:43
  140.2 11.9 %collective-permute-start.4 = (bf16[1,512,512]{2,1,0:T(8,128)(2,1)S(1)}, bf16[1,512,512]{2,1,0:T(8,128)(2,1)S(1)}, u32[]{:S(2)}, u32[]{:S(2)}) collective-permute-start(bf16[1,512,512]{2,1,0:T(8,128)(2,1)S(1)} %get-tuple-element.44), channel_id=1, source_target_pairs={{0,1},{1,0},{2,3},{3,2},{4,5},{5,4},{6,7},{7,6},{8,9},{9,8},{10,11... | collective-permute-start | bytes 1572872 | tf_op jit(solution)/shard_map/ppermute | solution.py:43
  180.5 26.2 %collective-permute-start.10 = (bf16[512,1024]{1,0:T(8,128)(2,1)S(1)}, bf16[512,1024]{1,0:T(8,128)(2,1)S(1)}, u32[]{:S(2)}, u32[]{:S(2)}) collective-permute-start(bf16[512,1024]{1,0:T(8,128)(2,1)S(1)} %convolution_convert_fusion.2), channel_id=1, source_target_pairs={{0,1},{1,0},{2,3},{3,2},{4,5},{5,4},{6,7},{7,6},{8,9},{9,8},{10,11... | collective-permute-start | bytes 3145736 | tf_op jit(solution)/shard_map/ppermute | solution.py:43
  181.2 43.9 %collective-permute-start.8 = (bf16[512,1024]{1,0:T(8,128)(2,1)S(1)}, bf16[512,1024]{1,0:T(8,128)(2,1)S(1)}, u32[]{:S(2)}, u32[]{:S(2)}) collective-permute-start(bf16[512,1024]{1,0:T(8,128)(2,1)S(1)} %convolution_convert_fusion.3), channel_id=1, source_target_pairs={{0,1},{1,0},{2,3},{3,2},{4,5},{5,4},{6,7},{7,6},{8,9},{9,8},{10,11... | collective-permute-start | bytes 3145736 | tf_op jit(solution)/shard_map/ppermute | solution.py:43
  192.5 204.1 %collective-permute-start.23 = (bf16[8,64,4096]{2,1,0:T(8,128)(2,1)}, bf16[8,64,4096]{2,1,0:T(8,128)(2,1)}, u32[]{:S(2)}, u32[]{:S(2)}) collective-permute-start(bf16[8,64,4096]{2,1,0:T(8,128)(2,1)} %fusion.17), channel_id=1, source_target_pairs={{0,2},{2,0},{1,3},{3,1},{4,6},{6,4},{5,7},{7,5},{8,10},{10,8},{9,1... | collective-permute-start | bytes 12582920 | tf_op jit(solution)/shard_map/ppermute | solution.py:43
  256.1 170.4 %collective-permute-start.16 = (bf16[2,512,512]{2,1,0:T(8,128)(2,1)S(1)}, bf16[2,512,512]{2,1,0:T(8,128)(2,1)}, u32[]{:S(2)}, u32[]{:S(2)}) collective-permute-start(bf16[2,512,512]{2,1,0:T(8,128)(2,1)S(1)} %get-tuple-element.69), channel_id=1, source_target_pairs={{4,0},{8,4},{12,8},{16,12},{20,16},{24,20},{28,24},{5,1},{9,5},{13... | collective-permute-start | bytes 3145736 | tf_op jit(solution)/shard_map/ppermute | solution.py:38
  270.4 114.4 %collective-permute-start.11 = (bf16[2,2,170,512]{3,1,2,0:T(2,128)(2,1)S(1)}, bf16[2,2,170,512]{3,1,2,0:T(2,128)(2,1)S(1)}, u32[]{:S(2)}, u32[]{:S(2)}) collective-permute-start(bf16[2,2,170,512]{3,1,2,0:T(2,128)(2,1)S(1)} %copy.103), channel_id=1, source_target_pairs={{16,0},{20,4},{24,8},{28,12},{17,1},{21,5},{25,9},{29,13},{18,2},{... | collective-permute-start | bytes 2088968 | tf_op jit(solution)/shard_map/ppermute | solution.py:38
  272.5 113.7 %collective-permute-start.12 = (bf16[2,2,170,512]{3,1,2,0:T(2,128)(2,1)S(1)}, bf16[2,2,170,512]{3,1,2,0:T(2,128)(2,1)S(1)}, u32[]{:S(2)}, u32[]{:S(2)}) collective-permute-start(bf16[2,2,170,512]{3,1,2,0:T(2,128)(2,1)S(1)} %copy.105), channel_id=1, source_target_pairs={{12,0},{16,4},{20,8},{24,12},{28,16},{13,1},{17,5},{21,9},{25,13},... | collective-permute-start | bytes 2088968 | tf_op jit(solution)/shard_map/ppermute | solution.py:38
  274.7 111.5 %collective-permute-start.13 = (bf16[2,2,170,512]{3,1,2,0:T(2,128)(2,1)S(1)}, bf16[2,2,170,512]{3,1,2,0:T(2,128)(2,1)S(1)}, u32[]{:S(2)}, u32[]{:S(2)}) collective-permute-start(bf16[2,2,170,512]{3,1,2,0:T(2,128)(2,1)S(1)} %copy.107), channel_id=1, source_target_pairs={{8,0},{12,4},{16,8},{20,12},{24,16},{28,20},{9,1},{13,5},{17,9},{2... | collective-permute-start | bytes 2088968 | tf_op jit(solution)/shard_map/ppermute | solution.py:38
  384.8 44.0 %collective-permute-start.9 = (bf16[2,512,512]{2,1,0:T(8,128)(2,1)}, bf16[2,512,512]{2,1,0:T(8,128)(2,1)}, u32[]{:S(2)}, u32[]{:S(2)}) collective-permute-start(bf16[2,512,512]{2,1,0:T(8,128)(2,1)} %get-tuple-element.55), channel_id=1, source_target_pairs={{4,0},{8,4},{12,8},{16,12},{20,16},{24,20},{28,24},{5,1},{9,5},{13... | collective-permute-start | bytes 3145736 | tf_op jit(solution)/shard_map/ppermute | solution.py:38
  389.8 14.5 %collective-permute-start.14 = (bf16[2,170,512]{2,1,0:T(8,128)(2,1)}, bf16[2,170,512]{2,1,0:T(8,128)(2,1)}, u32[]{:S(2)}, u32[]{:S(2)}) collective-permute-start(bf16[2,170,512]{2,1,0:T(8,128)(2,1)} %constant_dynamic-slice_fusion), channel_id=1, source_target_pairs={{0,1},{1,0},{2,3},{3,2},{4,5},{5,4},{6,7},{7,6},{8,9},{9,8},{10,11... | collective-permute-start | bytes 1044488 | tf_op jit(solution)/shard_map/ppermute | solution.py:43
  402.2 199.5 %reduce-scatter.3.cloned.1.call-start = ((), (), s32[]{:S(2)}) async-start(), calls=%async_computation.2 | async-start | bytes 4128768 | tf_op jit(solution)/shard_map/reduce_scatter | solution.py:320
  441.0 14.7 %collective-permute-start.18 = (bf16[8,64,3584]{2,1,0:T(8,128)(2,1)S(1)}, bf16[8,64,3584]{2,1,0:T(8,128)(2,1)S(1)}, u32[]{:S(2)}, u32[]{:S(2)}) collective-permute-start(bf16[8,64,3584]{2,1,0:T(8,128)(2,1)S(1)} %dynamic-slice_bitcast_fusion), channel_id=1, source_target_pairs={{0,2},{2,0},{1,3},{3,1},{4,6},{6,4},{5,7},{7,5},{8,10},{10,8},{9,1... | collective-permute-start | bytes 11010056 | tf_op jit(solution)/shard_map/ppermute | solution.py:43
  450.1 48.9 %collective-permute-start.7 = (bf16[2,512,1024]{2,1,0:T(8,128)(2,1)}, bf16[2,512,1024]{2,1,0:T(8,128)(2,1)}, u32[]{:S(2)}, u32[]{:S(2)}) collective-permute-start(bf16[2,512,1024]{2,1,0:T(8,128)(2,1)} %pad_maximum_fusion.1), channel_id=1, source_target_pairs={{0,1},{1,0},{2,3},{3,2},{4,5},{5,4},{6,7},{7,6},{8,9},{9,8},{10,11... | collective-permute-start | bytes 6291464 | tf_op jit(solution)/shard_map/ppermute | solution.py:43
  470.2 51.2 %collective-permute-start.17 = (bf16[512,1024]{1,0:T(8,128)(2,1)S(1)}, bf16[512,1024]{1,0:T(8,128)(2,1)}, u32[]{:S(2)}, u32[]{:S(2)}) collective-permute-start(bf16[512,1024]{1,0:T(8,128)(2,1)S(1)} %fusion.56), channel_id=1, source_target_pairs={{0,1},{1,0},{2,3},{3,2},{4,5},{5,4},{6,7},{7,6},{8,9},{9,8},{10,11... | collective-permute-start | bytes 3145736 | tf_op jit(solution)/shard_map/ppermute | solution.py:43
  473.8 68.5 %collective-permute-start.15 = (bf16[512,1024]{1,0:T(8,128)(2,1)}, bf16[512,1024]{1,0:T(8,128)(2,1)}, u32[]{:S(2)}, u32[]{:S(2)}) collective-permute-start(bf16[512,1024]{1,0:T(8,128)(2,1)} %fusion.53), channel_id=1, source_target_pairs={{0,1},{1,0},{2,3},{3,2},{4,5},{5,4},{6,7},{7,6},{8,9},{9,8},{10,11... | collective-permute-start | bytes 3145736 | tf_op jit(solution)/shard_map/ppermute | solution.py:43
  547.5 17.2 %collective-permute-start.20 = (f32[41,128]{1,0:T(8,128)S(1)}, f32[41,128]{1,0:T(8,128)S(1)}, u32[]{:S(2)}, u32[]{:S(2)}) collective-permute-start(f32[41,128]{1,0:T(8,128)S(1)} %bitcast_add_fusion.1), channel_id=1, source_target_pairs={{0,4},{4,0},{8,12},{12,8},{16,20},{20,16},{24,28},{28,24},{1,5},{5... | collective-permute-start | bytes 62984 | tf_op jit(solution)/shard_map/ppermute | solution.py:43
  564.7 17.8 %collective-permute-start.21 = (f32[41,128]{1,0:T(8,128)S(1)}, f32[41,128]{1,0:T(8,128)S(1)}, u32[]{:S(2)}, u32[]{:S(2)}) collective-permute-start(f32[41,128]{1,0:T(8,128)S(1)} %fusion.238), channel_id=1, source_target_pairs={{0,8},{4,12},{8,0},{12,4},{16,24},{20,28},{24,16},{28,20},{1,9},{5... | collective-permute-start | bytes 62984 | tf_op jit(solution)/shard_map/ppermute | solution.py:43
  (95 other events, 1079.9 us)
Sparse Core Ops, SparseCore 0:
  402.3 113.1 reduce-scatter.4
  519.6 81.9 reduce-scatter.2

commit v2 on v0

v2 whole, which is shorter than its diff:
```python
import functools
import math

import jax
import jax.numpy as jnp
from jax import lax
from jax.experimental import pallas as pl
from jax.experimental.pallas import tpu as pltpu
from jax.sharding import PartitionSpec as P

CSEGS = 3
EPS = 1e-05
FAR = 1e30
LOG2E = math.log2(math.e)
BF = jnp.bfloat16
F32 = jnp.float32
TILE = 256
NT = (((1,), (1,)), ((), ()))
GELU_A = math.sqrt(2.0 / math.pi)
GELU_B = 0.044715


def dot(a, b):
    return jnp.dot(a, b, preferred_element_type=F32)


def dot_nt(a, b):
    return lax.dot_general(a, b, NT, preferred_element_type=F32)


def dot_tn(a, b):
    return lax.dot_general(a, b, (((0,), (0,)), ((), ())), preferred_element_type=F32)


def shift(x, axis, by):
    devices = lax.axis_size(axis)
    pairs = [(i, i + by) for i in range(devices) if 0 <= i + by < devices]
    return lax.ppermute(x, axis, pairs)


def swap(x, axis, step=1):
    devices = lax.axis_size(axis)
    return lax.ppermute(x, axis, [(i, i ^ step) for i in range(devices)])


def row_stats(x):
    center = x - jnp.mean(x, axis=-1, keepdims=True)
    inverse = lax.rsqrt(jnp.mean(center * center, axis=-1, keepdims=True) + EPS)
    return center * inverse, inverse


def norm_back(grad, unit, inverse, gain):
    scaled = grad * gain
    mean_one = jnp.mean(scaled, axis=-1, keepdims=True)
    mean_two = jnp.mean(scaled * unit, axis=-1, keepdims=True)
    return inverse * (scaled - mean_one - unit * mean_two)


def front_kernel(me, own, other, gain, bias, normed, tri_own, tri_other, unit, *, slots):
    rows, model = own.shape
    padded = tri_own.shape[0]
    for source, tri in ((own, tri_own), (other, tri_other)):
        for start in range(0, rows, 128):
            part = slice(start, start + 128)
            x, _ = row_stats(source[part, :].astype(F32))
            x = x * gain[...] + bias[...]
            for lane in range(model // 128):
                unit[lane, part, :] = x[:, lane * 128 : (lane + 1) * 128]
            if source is own:
                normed[part, :] = x.astype(BF)
        live = lax.broadcasted_iota(jnp.int32, (padded, 128), 0) < slots
        for lane in range(model // 128):
            unit[lane, rows:, :] = jnp.zeros((unit.shape[1] - rows, 128), F32)
            for tap in range(3):
                at = tap * model + lane * 128
                rows_of = unit[lane, pl.ds(tap, padded, stride=3), :]
                tri[:, at : at + 128] = jnp.where(live, rows_of, 0.0).astype(BF)


def front(me, tokens, gain, bias, slots, padded):
    _, rows, model = tokens.shape
    tri = jax.ShapeDtypeStruct((padded, 3 * model), BF)
    fixed = lambda shape: pl.BlockSpec(shape, lambda i, m: (0, 0))
    pick = lambda turn: pl.BlockSpec((None, rows, model), lambda i, m: ((m[0] + turn) % 2, 0, 0))
    return pl.pallas_call(
        functools.partial(front_kernel, slots=slots),
        grid_spec=pltpu.PrefetchScalarGridSpec(
            num_scalar_prefetch=1,
            grid=(1,),
            in_specs=[pick(0), pick(1), fixed((1, model)), fixed((1, model))],
            out_specs=[fixed((rows, model)), fixed((padded, 3 * model)), fixed((padded, 3 * model))],
            scratch_shapes=[pltpu.VMEM((model // 128, 3 * padded + 8, 128), F32)],
        ),
        out_shape=[jax.ShapeDtypeStruct((rows, model), BF), tri, tri],
        compiler_params=pltpu.CompilerParams(vmem_limit_bytes=20 << 20),
        cost_estimate=pl.CostEstimate(
            flops=40 * rows * model, bytes_accessed=6 << 20, transcendentals=0),
        name="front",
    )(me, tokens, tokens, gain.reshape(1, model), bias.reshape(1, model))


def distant_kernel(halo, mem, w, kf, vf):
    rows = halo.shape[0]
    for index, out in ((1, kf), (2, vf)):
        out[:rows, :] = dot(halo[...], w[index]).astype(BF)
        out[rows:, :] = dot(mem[...], w[index]).astype(BF)


def project_distant(halo, mem, w):
    rows, model = halo.shape
    width = w.shape[2]
    shape = jax.ShapeDtypeStruct((2 * rows, width), BF)
    return pl.pallas_call(
        distant_kernel,
        out_shape=[shape, shape],
        compiler_params=pltpu.CompilerParams(vmem_limit_bytes=20 << 20),
        cost_estimate=pl.CostEstimate(
            flops=8 * model * width * rows, bytes_accessed=6 << 20, transcendentals=0),
        name="project_distant",
    )(halo, mem, w)


def far_kernel(place, docs, query, out, mem, *, slots, rows):
    position = place[0]
    for seg in range(CSEGS):
        mem[seg * slots : (seg + 1) * slots, :] = docs[pl.ds(seg * rows, slots, stride=3), :]
    mem[CSEGS * slots :, :] = jnp.full((rows - CSEGS * slots, 128), -1, jnp.int32)
    column = lax.broadcasted_iota(jnp.int32, (1, rows), 1)
    step = 64
    for start in range(0, 3 * rows, step):
        local = lax.broadcasted_iota(jnp.int32, (step, 1), 0) + start % rows
        if start < rows:
            doc = docs[CSEGS * rows + start : CSEGS * rows + start + step, :1]
            where, live = local - rows, position > 0
        elif start < 2 * rows:
            doc = mem[start - rows : start - rows + step, :1]
            lead = sum((local >= seg * slots).astype(jnp.int32) for seg in range(1, CSEGS + 1))
            where = (lead - 1 - CSEGS) * rows + 3 * (local - lead * slots) + 1
            live = position - 1 - CSEGS + lead >= 0
        else:
            at = (CSEGS + 1) * rows + start - 2 * rows
            doc = docs[at : at + step, :1]
            where, live = local, position >= 0
        doc = jnp.where(live, doc, -2)
        apart = column - where
        seen = (apart >= 0) & (doc == query[...])
        value = jnp.log((1 + jnp.maximum(apart, 0)).astype(F32))
        out[start : start + step, :] = jnp.where(seen, value, FAR)


def far_log(place, docs, query, slots):
    rows = query.shape[1]
    return pl.pallas_call(
        functools.partial(far_kernel, slots=slots, rows=rows),
        in_specs=[
            pl.BlockSpec(memory_space=pltpu.SMEM),
            pl.BlockSpec(memory_space=pltpu.VMEM),
            pl.BlockSpec(memory_space=pltpu.VMEM),
        ],
        out_shape=jax.ShapeDtypeStruct((3 * rows, rows), F32),
        scratch_shapes=[pltpu.VMEM((rows, 128), jnp.int32)],
        compiler_params=pltpu.CompilerParams(vmem_limit_bytes=20 << 20),
        cost_estimate=pl.CostEstimate(
            flops=60 * rows * rows, bytes_accessed=5 << 20, transcendentals=3 * rows * rows),
        name="far_log",
    )(place, docs, query)


def project_kernel(normed, packed, w, q, k, v, kc, vc):
    for index, out in enumerate((q, k, v)):
        out[...] = dot(normed[...], w[index]).astype(BF)
    kc[...] = dot(packed[...], w[1]).astype(BF)
    vc[...] = dot(packed[...], w[2]).astype(BF)


def project(normed, packed, w):
    rows, model = normed.shape
    padded, width = packed.shape[0], w.shape[2]
    near = jax.ShapeDtypeStruct((rows, width), BF)
    little = jax.ShapeDtypeStruct((padded, width), BF)
    return pl.pallas_call(
        project_kernel,
        out_shape=[near, near, near, little, little],
        compiler_params=pltpu.CompilerParams(vmem_limit_bytes=20 << 20),
        cost_estimate=pl.CostEstimate(
            flops=2 * model * width * (3 * rows + 2 * padded), bytes_accessed=6 << 20,
            transcendentals=0),
        name="project",
    )(normed, packed, w)


def forward_kernel(slopes, q, kf, vf, ko, vo, far, out, lse, *, scaling):
    head = pl.program_id(0)
    c1 = scaling * LOG2E
    c2 = slopes[head] * LOG2E
    rows, reach = q.shape[0], kf.shape[0]
    vft, vot = vf[...].T, vo[...].T
    for qi in range(rows // TILE):
        qs = slice(qi * TILE, (qi + 1) * TILE)
        until = (qi + 1) * TILE
        qb = q[qs, :]
        near = dot_nt(ko[:until, :], qb) * c1 - c2 * far[reach : reach + until, qs]
        away = dot_nt(kf[...], qb) * c1 - c2 * far[:reach, qs]
        top = jnp.maximum(
            jnp.max(near, axis=0, keepdims=True), jnp.max(away, axis=0, keepdims=True)
        )
        near = jnp.exp2(near - top)
        away = jnp.exp2(away - top)
        total = jnp.sum(near, axis=0, keepdims=True) + jnp.sum(away, axis=0, keepdims=True)
        mixed = dot(vot[:, :until], near.astype(BF)) + dot(vft, away.astype(BF))
        out[qs, :] = (mixed / total).T.astype(BF)
        lse[0, :, qs] = top + jnp.log2(total)


def attend_forward(slopes, q, kf, vf, ko, vo, far, scaling):
    rows, width = q.shape
    reach = kf.shape[0]
    heads = slopes.shape[0]
    hd = width // heads
    near = pl.BlockSpec((rows, hd), lambda h: (0, h))
    wide = pl.BlockSpec((reach, hd), lambda h: (0, h))
    return pl.pallas_call(
        functools.partial(forward_kernel, scaling=scaling),
        grid=(heads,),
        in_specs=[
            pl.BlockSpec(memory_space=pltpu.SMEM), near, wide, wide, near, near,
            pl.BlockSpec((reach + rows, rows), lambda h: (0, 0)),
        ],
        out_specs=[near, pl.BlockSpec((1, 1, rows), lambda h: (h, 0, 0))],
        out_shape=[
            jax.ShapeDtypeStruct((rows, width), BF),
            jax.ShapeDtypeStruct((heads, 1, rows), F32),
        ],
        compiler_params=pltpu.CompilerParams(vmem_limit_bytes=20 << 20),
        cost_estimate=pl.CostEstimate(
            flops=8 * heads * rows * (reach + rows) * hd, bytes_accessed=8 << 20,
            transcendentals=heads * rows * (reach + rows)),
        name="attend_forward",
    )(slopes, q, kf, vf, ko, vo, far)


def backward_kernel(slopes, q, do, lse, dot_row, far, k, v, *refs, scaling, own):
    head = pl.program_id(0)
    c1 = scaling * LOG2E
    c2 = slopes[head] * LOG2E
    extras = refs[:-4]
    dq, dk_out, dv_out, sums_out = refs[-4:]
    rows, hd = q.shape
    keys = k.shape[0]
    tall = rows
    for ki in range(keys // tall):
        base = ki * tall
        kt = k[base : base + tall, :].T
        dks, dvs = [], []
        for qi in range(rows // TILE):
            qs = slice(qi * TILE, (qi + 1) * TILE)
            until = (qi + 1) * TILE if own else tall
            ks = slice(base, base + until)
            qb, db = q[qs, :], do[qs, :]
            dist = far[ks, qs]
            s = dot_nt(k[ks, :], qb) * c1 - c2 * dist
            p = jnp.exp2(s - lse[0, :, qs])
            dp = dot_nt(v[ks, :], db)
            ds = p * (dp - dot_row[0, :, qs])
            for index, value in enumerate((ds, p * dist, ds * dist)):
                value = jnp.sum(value, axis=0, keepdims=True)
                if ki > 0:
                    value = value + sums_out[0, index : index + 1, qs]
                sums_out[0, index : index + 1, qs] = value
            p = p.astype(BF)
            ds = ds.astype(BF)
            dvs.append(dot(p, db))
            dks.append(dot(ds, qb))
            value = dot(kt[:, :until], ds).T * scaling
            if own:
                value = value + extras[0][qs, :] + extras[1][qs, :]
            if ki > 0:
                value = value + dq[qs, :]
            dq[qs, :] = value.astype(dq.dtype)
        for start in range(0, tall, TILE):
            ks = slice(base + start, base + start + TILE)
            dk = sum(d[start : start + TILE, :] for d in dks if d.shape[0] > start) * scaling
            dv = sum(d[start : start + TILE, :] for d in dvs if d.shape[0] > start)
            if own:
                dk = dk + extras[2][ks, :]
                dv = dv + extras[3][ks, :]
            dk_out[ks, :] = dk.astype(BF)
            dv_out[ks, :] = dv.astype(BF)


def attend_backward(slopes, q, do, lse, dot_row, far, k, v, own, extras, scaling):
    rows, width = q.shape
    keys = k.shape[0]
    heads = slopes.shape[0]
    hd = width // heads
    near = pl.BlockSpec((rows, hd), lambda h: (0, h))
    wide = pl.BlockSpec((keys, hd), lambda h: (0, h))
    lane = pl.BlockSpec((1, 1, rows), lambda h: (h, 0, 0))
    place = far.shape[0] // keys - 1 if own else 0
    return pl.pallas_call(
        functools.partial(backward_kernel, scaling=scaling, own=own),
        grid=(heads,),
        in_specs=[
            pl.BlockSpec(memory_space=pltpu.SMEM), near, near, lane, lane,
            pl.BlockSpec((keys, rows), lambda h: (place, 0)), wide, wide,
        ]
        + [near] * len(extras),
        out_specs=[near, wide, wide, pl.BlockSpec((1, 8, rows), lambda h: (h, 0, 0))],
        out_shape=[
            jax.ShapeDtypeStruct((rows, width), BF if own else F32),
            jax.ShapeDtypeStruct((keys, width), BF),
            jax.ShapeDtypeStruct((keys, width), BF),
            jax.ShapeDtypeStruct((heads, 8, rows), F32),
        ],
        compiler_params=pltpu.CompilerParams(vmem_limit_bytes=30 << 20),
        cost_estimate=pl.CostEstimate(
            flops=12 * heads * rows * keys * hd, bytes_accessed=8 << 20,
            transcendentals=heads * rows * keys),
        name="attend_backward_own" if own else "attend_backward_far",
    )(slopes, q, do, lse, dot_row, far, k, v, *extras)


def recon_kernel(q, ko, vo, kc, vc, cot, recon, dq, dk, dv, dkc, dvc, *, slots, scaling):
    rows, hd = q.shape
    c1 = scaling * LOG2E
    comp_rows = kc.shape[0]
    live = lax.broadcasted_iota(jnp.int32, (comp_rows, TILE), 0) < slots
    kct, vct, kot, vot = kc[...].T, vc[...].T, ko[...].T, vo[...].T
    for qi in range(rows // TILE):
        qs = slice(qi * TILE, (qi + 1) * TILE)
        qb = q[qs, :]
        full_s = dot_nt(ko[...], qb) * c1
        full_p = jnp.exp2(full_s - jnp.max(full_s, axis=0, keepdims=True))
        full_p = full_p * (1.0 / jnp.sum(full_p, axis=0, keepdims=True))
        full_low = full_p.astype(BF)
        comp_s = jnp.where(live, dot_nt(kc[...], qb) * c1, -FAR)
        comp_p = jnp.exp2(comp_s - jnp.max(comp_s, axis=0, keepdims=True))
        comp_p = comp_p * (1.0 / jnp.sum(comp_p, axis=0, keepdims=True))
        comp_low = comp_p.astype(BF)
        full, comp = dot(vot, full_low), dot(vct, comp_low)
        spread = full - comp
        recon[0, :, qs] = jnp.sum(spread * spread, axis=0, keepdims=True) / hd**0.5
        dfull = spread * (cot[0, :, qs] * (2.0 / hd**0.5))
        dfull_low = dfull.astype(BF)
        dfull_rows = dfull_low.T
        full_dw = dot(vo[...], dfull_low)
        comp_dw = dot(vc[...], dfull_low)
        row = jnp.sum(full_p * full_dw, axis=0, keepdims=True)
        full_ds = (full_p * (full_dw - row)).astype(BF)
        row = jnp.sum(comp_p * comp_dw, axis=0, keepdims=True)
        comp_ds = (comp_p * (row - comp_dw)).astype(BF)
        dq[qs, :] = (dot(kot, full_ds) + dot(kct, comp_ds)).T * scaling
        values = (
            (dk, dot(full_ds, qb) * scaling),
            (dv, dot(full_low, dfull_rows)),
            (dkc, dot(comp_ds, qb) * scaling),
            (dvc, -dot(comp_low, dfull_rows)),
        )
        for ref, value in values:
            if qi > 0:
                value = value + ref[...]
            ref[...] = value


def recon_both(q, ko, vo, kc, vc, cot, slots, scaling):
    rows, width = q.shape
    heads = cot.shape[0]
    hd = width // heads
    comp_rows = kc.shape[0]
    near = pl.BlockSpec((rows, hd), lambda h: (0, h))
    small = pl.BlockSpec((comp_rows, hd), lambda h: (0, h))
    lane = pl.BlockSpec((1, 1, rows), lambda h: (h, 0, 0))
    big = jax.ShapeDtypeStruct((rows, width), F32)
    little = jax.ShapeDtypeStruct((comp_rows, width), F32)
    return pl.pallas_call(
        functools.partial(recon_kernel, slots=slots, scaling=scaling),
        grid=(heads,),
        in_specs=[near, near, near, small, small, lane],
        out_specs=[lane, near, near, near, small, small],
        out_shape=[jax.ShapeDtypeStruct((heads, 1, rows), F32), big, big, big, little, little],
        compiler_params=pltpu.CompilerParams(vmem_limit_bytes=20 << 20),
        cost_estimate=pl.CostEstimate(
            flops=24 * heads * rows * (rows + comp_rows) * hd, bytes_accessed=8 << 20,
            transcendentals=heads * rows * (rows + comp_rows)),
        name="recon_both",
    )(q, ko, vo, kc, vc, cot)


def middle_kernel(me, tokens, a_one, a_two, w_one, w_two, gain, bias, middle, normed):
    value = tokens[...].astype(F32) + (dot(a_one[...], w_one[...]) + dot(a_two[...], w_two[...]))
    middle[...] = value
    unit, _ = row_stats(value)
    normed[...] = (unit * gain[...] + bias[...]).astype(BF)


def middle_norm(me, tokens, a_one, a_two, w_one, w_two, gain, bias):
    _, rows, model = tokens.shape
    width = a_one.shape[1]
    tall = pl.BlockSpec((TILE, model), lambda i, m: (i, 0))
    part = pl.BlockSpec((TILE, width), lambda i, m: (i, 0))
    fixed = lambda shape: pl.BlockSpec(shape, lambda i, m: (0, 0))
    return pl.pallas_call(
        middle_kernel,
        grid_spec=pltpu.PrefetchScalarGridSpec(
            num_scalar_prefetch=1,
            grid=(rows // TILE,),
            in_specs=[pl.BlockSpec((None, TILE, model), lambda i, m: (m[0], i, 0)), part, part,
                      fixed((width, model)), fixed((width, model)), fixed((1, model)),
                      fixed((1, model))],
            out_specs=[tall, tall],
        ),
        out_shape=[jax.ShapeDtypeStruct((rows, model), F32), jax.ShapeDtypeStruct((rows, model), BF)],
        compiler_params=pltpu.CompilerParams(vmem_limit_bytes=20 << 20),
        cost_estimate=pl.CostEstimate(
            flops=4 * rows * width * model, bytes_accessed=8 << 20, transcendentals=0),
        name="middle_norm",
    )(me, tokens, a_one, a_two, w_one, w_two, gain.reshape(1, model), bias.reshape(1, model))


def mlp_kernel(which, normed, cot, w_up, w_down, hidden, dinner, dnormed, branch, dn_sum, br_sum):
    step = pl.program_id(0)
    rows = normed.shape[0]
    for start in range(0, rows, rows):
        part = slice(start, start + rows)
        inner = dot(normed[part, :], w_up[...])
        dhidden = dot_nt(cot[part, :], w_down[...])
        square = inner * inner
        inside = jnp.tanh(inner * (GELU_A + (GELU_A * GELU_B) * square))
        bent = 0.5 * (1.0 + inside)
        low = (inner * bent).astype(BF)
        slope = bent + inner * (0.5 - 0.5 * inside * inside) * (
            GELU_A + (3.0 * GELU_A * GELU_B) * square
        )
        dlow = (dhidden * slope).astype(BF)
        hidden[part, :] = low
        dinner[part, :] = dlow
        dn = dot_nt(dlow, w_up[...])
        br = dot(low, w_down[...])

        @pl.when(step == 0)
        def _():
            dn_sum[part, :] = dn
            br_sum[part, :] = br

        @pl.when(step > 0)
        def _():
            dn_sum[part, :] += dn
            br_sum[part, :] += br

    @pl.when(step == pl.num_programs(0) - 1)
    def _():
        dnormed[...] = dn_sum[...].astype(dnormed.dtype)
        branch[...] = br_sum[...].astype(branch.dtype)


def mlp(which, normed, cot, w_up, w_down, dtype):
    rows, model = normed.shape
    units = w_up.shape[1]
    step = 512
    tall = pl.BlockSpec((rows, model), lambda f, m: (0, 0))
    act = pl.BlockSpec((rows, step), lambda f, m: (0, f))
    return pl.pallas_call(
        mlp_kernel,
        grid_spec=pltpu.PrefetchScalarGridSpec(
            num_scalar_prefetch=1,
            grid=(units // step,),
            in_specs=[tall, pl.BlockSpec((None, rows, model), lambda f, m: (m[0], 0, 0)),
                      pl.BlockSpec((model, step), lambda f, m: (0, f)),
                      pl.BlockSpec((step, model), lambda f, m: (f, 0))],
            out_specs=[act, act, tall, tall],
            scratch_shapes=[pltpu.VMEM((rows, model), F32)] * 2,
        ),
        out_shape=[jax.ShapeDtypeStruct((rows, units), BF)] * 2
        + [jax.ShapeDtypeStruct((rows, model), dtype)] * 2,
        compiler_params=pltpu.CompilerParams(vmem_limit_bytes=30 << 20),
        cost_estimate=pl.CostEstimate(
            flops=8 * rows * units * model, bytes_accessed=16 << 20, transcendentals=rows * units),
        name="mlp",
    )(which, normed, cot, w_up, w_down)


def turn_kernel(
    me, dn_own, dn_got, middle, cot, a_one, a_two, w_one, w_two, gain,
    dmiddle, dbranch, da_one, da_two, row_one, row_two, sums,
):
    step = pl.program_id(0)
    dn = dn_own[...] + dn_got[...].astype(F32)
    unit, inverse = row_stats(middle[...])
    value = cot[...].astype(F32) + norm_back(dn, unit, inverse, gain[...])
    dmiddle[...] = value
    low = value.astype(BF)
    dbranch[...] = low
    for a, w, da, row in ((a_one, w_one, da_one, row_one), (a_two, w_two, da_two, row_two)):
        grad = dot_nt(low, w[...]).astype(BF)
        da[...] = grad
        product = (grad.astype(F32) * a[...].astype(F32)).T
        heads = row.shape[0]
        row[:, 0, :] = jnp.sum(product.reshape(heads, -1, TILE), axis=1)

    @pl.when(step == 0)
    def _():
        sums[...] = jnp.zeros_like(sums)

    sums[0:1, :] += jnp.sum(dn * unit, axis=0, keepdims=True)
    sums[1:2, :] += jnp.sum(dn, axis=0, keepdims=True)


def turn(me, dn_own, dn_got, middle, cot, a_one, a_two, w_one, w_two, gain, heads):
    rows, model = middle.shape
    width = a_one.shape[1]
    tall = pl.BlockSpec((TILE, model), lambda i, m: (i, 0))
    part = pl.BlockSpec((TILE, width), lambda i, m: (i, 0))
    lane = pl.BlockSpec((heads, 1, TILE), lambda i, m: (0, 0, i))
    fixed = lambda shape: pl.BlockSpec(shape, lambda i, m: (0, 0))
    return pl.pallas_call(
        turn_kernel,
        grid_spec=pltpu.PrefetchScalarGridSpec(
            num_scalar_prefetch=1,
            grid=(rows // TILE,),
            in_specs=[tall, tall, tall,
                      pl.BlockSpec((None, TILE, model), lambda i, m: (m[0], i, 0)),
                      part, part, fixed((width, model)), fixed((width, model)), fixed((1, model))],
            out_specs=[tall, tall, part, part, lane, lane, fixed((8, model))],
        ),
        out_shape=[
            jax.ShapeDtypeStruct((rows, model), F32),
            jax.ShapeDtypeStruct((rows, model), BF),
            jax.ShapeDtypeStruct((rows, width), BF),
            jax.ShapeDtypeStruct((rows, width), BF),
            jax.ShapeDtypeStruct((heads, 1, rows), F32),
            jax.ShapeDtypeStruct((heads, 1, rows), F32),
            jax.ShapeDtypeStruct((8, model), F32),
        ],
        compiler_params=pltpu.CompilerParams(vmem_limit_bytes=30 << 20),
        cost_estimate=pl.CostEstimate(
            flops=4 * rows * width * model, bytes_accessed=12 << 20, transcendentals=0),
        name="turn",
    )(me, dn_own, dn_got, middle, cot, a_one, a_two, w_one, w_two, gain.reshape(1, model))


def finish_kernel(
    me, base, back, dpacked, w_comp, tokens, dmiddle, gain, grad, sums, total, *, rows
):
    model = base.shape[1]
    padded = dpacked.shape[0]
    for lane in range(model // 128):
        wide = slice(lane * 128, (lane + 1) * 128)
        total[lane, :rows, :] = base[:, wide] + back[:, wide].astype(F32)
        total[lane, rows:, :] = jnp.zeros((total.shape[1] - rows, 128), F32)
    for tap in range(3):
        place = pl.ds(tap, padded, stride=3)
        term = dot_nt(dpacked[...], w_comp[tap])
        for lane in range(model // 128):
            value = total[lane, place, :] + term[:, lane * 128 : (lane + 1) * 128]
            total[lane, place, :] = value
    one = jnp.zeros((1, model), F32)
    two = jnp.zeros((1, model), F32)
    for start in range(0, rows, 128):
        part = slice(start, start + 128)
        dn = jnp.concatenate([total[lane, part, :] for lane in range(model // 128)], 1)
        unit, inverse = row_stats(tokens[part, :].astype(F32))
        value = dmiddle[part, :] + norm_back(dn, unit, inverse, gain[...])
        grad[part, :] = value.astype(BF)
        one = one + jnp.sum(dn * unit, axis=0, keepdims=True)
        two = two + jnp.sum(dn, axis=0, keepdims=True)
    sums[0:1, :] = one
    sums[1:2, :] = two


def finish(me, base, back, dpacked, w_comp, tokens, dmiddle, gain):
    rows, model = base.shape
    padded = dpacked.shape[0]
    fixed = lambda *shape: pl.BlockSpec(shape, lambda i, m: (0,) * len(shape))
    return pl.pallas_call(
        functools.partial(finish_kernel, rows=rows),
        grid_spec=pltpu.PrefetchScalarGridSpec(
            num_scalar_prefetch=1,
            grid=(1,),
            in_specs=[fixed(rows, model), fixed(rows, model), fixed(padded, model),
                      fixed(*w_comp.shape),
                      pl.BlockSpec((None, rows, model), lambda i, m: (m[0], 0, 0)),
                      fixed(rows, model), fixed(1, model)],
            out_specs=[fixed(rows, model), fixed(8, model)],
            scratch_shapes=[pltpu.VMEM((model // 128, 3 * padded + 8, 128), F32)],
        ),
        out_shape=[
            jax.ShapeDtypeStruct((rows, model), BF),
            jax.ShapeDtypeStruct((8, model), F32),
        ],
        compiler_params=pltpu.CompilerParams(vmem_limit_bytes=36 << 20),
        cost_estimate=pl.CostEstimate(
            flops=6 * padded * model * model, bytes_accessed=16 << 20, transcendentals=0),
        name="finish",
    )(me, base, back, dpacked, w_comp, tokens, dmiddle, gain.reshape(1, model))


def weight_kernel(core, *refs, plan, block, share):
    if share:
        operands, (keep, send, held) = refs[:-3], refs[-3:]
    else:
        operands, held = refs[:-1], refs[-1]
    tall = held.shape[0]
    at = 0
    for pairs, columns in plan:
        for start in range(0, columns, block):
            wide = slice(start, min(start + block, columns))
            value = None
            for a, b in pairs:
                term = lax.dot_general(
                    operands[a][...], operands[b][:, wide], (((0,), (0,)), ((), ())),
                    preferred_element_type=F32,
                )
                value = term if value is None else value + term
            held[:, at + start : at + wide.stop] = value.astype(BF)
        at += columns
    if not share:
        return
    mine = core[0]
    for index in range(tall // (2 * share)):
        here = slice(index * share, (index + 1) * share)
        keep[here, :] = held[pl.ds(index * 2 * share + mine * share, share), :]
        send[here, :] = held[pl.ds(index * 2 * share + (1 - mine) * share, share), :]


def weight_grads(scalars, sections, share, model, name, tall=512):
    operands, specs, plan, total = [], [], [], 0
    known = {}

    def place(array, kind, at, columns, depth):
        key = (id(array), kind, at, columns)
        if key not in known:
            known[key] = len(operands)
            operands.append(array)
            if kind == "b":
                col, row = at
                spec = pl.BlockSpec(
                    (depth, columns), lambda i, c, f=col // columns, r=row // depth: (r, f)
                )
            elif array.ndim == 3:
                spec = pl.BlockSpec((None, depth, tall), lambda i, c, t=at: ((c[1] + t) % 2, 0, i))
            else:
                spec = pl.BlockSpec((depth, tall), lambda i, c, f=at // tall: (0, f + i))
            specs.append(spec)
        return known[key]

    for pairs in sections:
        columns = pairs[0][4]
        plan.append(
            (
                [
                    (
                        place(a, "a", pa, 0, a.shape[-2]),
                        place(b, "b", pb, columns, a.shape[-2]),
                    )
                    for a, pa, b, pb, _ in pairs
                ],
                columns,
            )
        )
        total += columns
    tile = tall // 2 if share else tall
    out = [pl.BlockSpec((tile, total), lambda i, c: (i, 0))] * (2 if share else 1)
    shape = [jax.ShapeDtypeStruct((tile * (model // tall), total), BF)] * len(out)
    flops = sum(2 * model * p[4] * p[0].shape[-2] for pairs in sections for p in pairs)
    return pl.pallas_call(
        functools.partial(weight_kernel, plan=tuple(plan), block=512, share=share),
        grid_spec=pltpu.PrefetchScalarGridSpec(
            num_scalar_prefetch=1,
            grid=(model // tall,),
            in_specs=specs,
            out_specs=out,
            scratch_shapes=[pltpu.VMEM((tall, total), BF)] if share else [],
        ),
        out_shape=shape,
        compiler_params=pltpu.CompilerParams(vmem_limit_bytes=40 << 20),
        cost_estimate=pl.CostEstimate(flops=flops, bytes_accessed=16 << 20, transcendentals=0),
        name=name,
    )(scalars, *operands)


def after(x, *others):
    return lax.optimization_barrier((x,) + others)[0]


def halve_blocks(x, bits, position):
    blocks = lax.axis_size("blk")
    count = blocks.bit_length() - 1
    x = x.reshape((2,) * count + (x.shape[0] // blocks, x.shape[1]))
    left = list(range(count - 1, -1, -1))
    for bit in bits:
        axis = left.index(bit)
        mine = (position >> bit) & 1
        away = lax.dynamic_index_in_dim(x, 1 - mine, axis, keepdims=False)
        here = lax.dynamic_index_in_dim(x, mine, axis, keepdims=False)
        x = here + swap(away, "blk", 1 << bit)
        left.remove(bit)
    return x


def reduce_blocks(x):
    return lax.psum_scatter(x, "blk", scatter_dimension=0, tiled=True)


def butterfly(x):
    x = x + swap(x, "dp")
    step = 1
    while step < lax.axis_size("blk"):
        x = x + swap(x, "blk", step)
        step *= 2
    return x + swap(x, "head")


def in_order(mine, first, second, axis):
    return jnp.where(
        mine == 0, jnp.concatenate([first, second], axis), jnp.concatenate([second, first], axis)
    )


def pick(x, index, axis=0):
    return lax.dynamic_index_in_dim(x, index, axis, keepdims=False)


def shards(
    tokens, doc_ids, w_qkv, w_out, slopes, w_up, w_down, w_comp, comp_bias,
    norm1_gain, norm1_bias, norm2_gain, norm2_bias, out_cot, recon_cot,
):
    seqs, rows, model = tokens.shape
    heads = slopes.shape[0]
    width = w_qkv.shape[2]
    hd = width // heads
    slots = rows // 3
    used = 3 * slots
    padded = -(-slots // 16) * 16
    memory = CSEGS * slots
    position = lax.axis_index("blk")
    core = lax.axis_index("dp")
    me = lax.axis_index("head")
    ot = 1 - me
    scaling = hd ** (-0.5)
    half = model // 2
    share = model // (lax.axis_size("blk") * lax.axis_size("dp"))
    bits = lax.axis_size("blk").bit_length() - 1
    rising = list(range(bits))
    falling = [1, 0] + rising[2:]
    scalars = jnp.stack([core, me]).astype(jnp.int32)
    me_arg, ot_arg = me.reshape(1).astype(jnp.int32), ot.reshape(1).astype(jnp.int32)

    small = jnp.concatenate(
        [pick(recon_cot, ot), jnp.pad(slopes, (0, rows - heads)).reshape(1, rows)], 0
    )
    small_got = swap(small, "head")
    half_rows = model // 2
    qkv_part = lax.dynamic_slice_in_dim(after(w_qkv, small), core * half_rows, half_rows, 1)
    far_qkv = swap(qkv_part, "head")
    groups = ("own", "oth")

    normed, tri_own, tri_oth = front(
        me_arg, after(tokens, qkv_part), norm1_gain, norm1_bias, slots, padded
    )
    halo = shift(normed, "blk", 1)
    packed = dot(tri_own, w_comp.reshape(3 * model, model)) + comp_bias
    packed = packed.astype(BF)
    parity = position % 2
    lag2 = shift(packed, "blk", 2)

    out_part = lax.dynamic_slice_in_dim(
        after(w_out, packed), core * (width // 2), width // 2, 0
    )
    far_out = swap(out_part, "head")

    docs = pick(doc_ids, me)
    query_doc = lax.dynamic_slice_in_dim(docs, position * rows, rows, 0).reshape(1, rows)
    padded_doc = jnp.concatenate([jnp.full(((CSEGS + 1) * rows,), -1, jnp.int32), docs])
    window = lax.dynamic_slice_in_dim(padded_doc, position * rows, (CSEGS + 2) * rows, 0)
    window = jnp.broadcast_to(window[:, None], ((CSEGS + 2) * rows, 128))
    far = far_log(position.reshape(1).astype(jnp.int32), window, after(query_doc, out_part), slots)

    weights, outs = {"own": w_qkv}, {"own": w_out}
    cots = {"own": pick(recon_cot, me).reshape(heads, 1, rows)}
    slope = {"own": slopes}
    q, ko, vo, kc, vc, rec, kf, vf, att, lse = ({} for _ in range(10))
    q["own"], ko["own"], vo["own"], kc["own"], vc["own"] = project(
        normed, after(packed, far), w_qkv
    )
    lag2 = after(lag2, q["own"])
    lag4 = shift(lag2, "blk", 2)
    small_got = after(small_got, q["own"])
    cots["oth"] = small_got[:heads].reshape(heads, 1, rows)
    slope["oth"] = small_got[heads, :heads]
    rec["own"] = recon_both(
        after(q["own"], small_got), ko["own"], vo["own"], kc["own"], vc["own"], cots["own"],
        slots, scaling,
    )
    lag4 = after(lag4, rec["own"][0])
    lag3 = swap(jnp.where(parity == 0, lag2, lag4), "blk", 1)
    far_qkv = after(far_qkv, rec["own"][0])
    near_qkv = swap(far_qkv, "dp")
    mem = jnp.zeros((rows, model), BF)
    for index, lag in enumerate((lag4, lag3, lag2)):
        place = (index * slots, rows - (index + 1) * slots)
        mem = mem + jnp.pad(lag[:slots], (place, (0, 0)))
    for g in groups:
        if g == "oth":
            near_qkv = after(near_qkv, att["own"])
            weights[g] = in_order(core, far_qkv, near_qkv, 1)
            outs[g] = in_order(core, far_out, after(near_out, att["own"]), 0)
            q[g], ko[g], vo[g], kc[g], vc[g] = project(normed, packed, weights[g])
        kf[g], vf[g] = project_distant(halo, after(mem, q[g], far_qkv), weights[g])
        if g == "own":
            far_out = after(far_out, kf[g])
            near_out = swap(far_out, "dp")
        att[g], lse[g] = attend_forward(
            slope[g], q[g], after(kf[g], far_out), vf[g], ko[g], vo[g], far, scaling
        )

    middle, n2_own = middle_norm(
        me_arg, tokens, att["own"], att["oth"], w_out, outs["oth"], norm2_gain, norm2_bias
    )
    n2_oth = swap(n2_own, "head")
    rec["oth"] = recon_both(
        after(q["oth"], n2_own), ko["oth"], vo["oth"], kc["oth"], vc["oth"], cots["oth"], slots,
        scaling,
    )
    hid_own, din_own, dn_own, ffn_own = mlp(
        me_arg, after(n2_own, rec["oth"][0]), out_cot, w_up, w_down, F32
    )
    hid_oth, din_oth, dn_oth, ffn_oth = mlp(
        ot_arg, after(n2_oth, dn_own), out_cot, w_up, w_down, BF
    )
    dn_got = swap(dn_oth, "head")
    units = w_up.shape[1]
    (up_down_part,) = weight_grads(
        scalars,
        [
            [(n2_own, 0, din_own, (0, 0), units), (n2_oth, 0, din_oth, (0, 0), units)],
            [(out_cot, 0, hid_own, (0, 0), units), (out_cot, 1, hid_oth, (0, 0), units)],
        ],
        0, model, "mlp_grads",
    )
    up_down = lax.psum_scatter(up_down_part, ("blk", "dp"), scatter_dimension=0, tiled=True)
    dn_got = after(dn_got, up_down_part)
    ffn_got = swap(after(ffn_oth, dn_got), "head")

    dmiddle, dbranch, datt_own, datt_oth, row_own, row_oth, sums2 = turn(
        me_arg, dn_own, dn_got, middle, out_cot, att["own"], att["oth"], w_out, outs["oth"],
        norm2_gain, heads,
    )
    datt = {"own": datt_own, "oth": datt_oth}
    row = {"own": row_own, "oth": row_oth}
    back, near, grads = {}, {}, {}

    def far_back(g, first):
        back[g] = attend_backward(
            slope[g], q[g], after(datt[g], first), lse[g], row[g], far, kf[g], vf[g], False, [],
            scaling,
        )

    def near_back(g, first):
        r = rec[g]
        near[g] = attend_backward(
            slope[g], q[g], after(datt[g], first), lse[g], row[g], far, ko[g], vo[g], True,
            [back[g][0], r[1], r[2], r[3]], scaling,
        )

    def group_grads(g, first):
        r = rec[g]
        sections = [[(normed, 0, near[g][0], (0, 0), width)]]
        for i in (1, 2):
            sections.append(
                [
                    (normed, 0, near[g][i], (0, 0), width),
                    (packed, 0, r[3 + i], (0, 0), width),
                    (halo, 0, back[g][i], (0, 0), width),
                    (mem, 0, back[g][i], (0, rows), width),
                ]
            )
        sections.append([(after(dbranch, first), 0, att[g], (0, 0), width)])
        grads[g] = weight_grads(scalars, sections, share, model, "attention_grads")

    far_back("oth", dbranch)
    far_back("own", back["oth"][0])
    ffn_got = after(ffn_got, back["own"][0])
    lo_own = (middle + (ffn_own + ffn_got.astype(F32))).astype(BF)
    lo_got = swap(lo_own, "head")
    ddistant = sum(
        dot_nt(after(back[g][1], lo_own), weights[g][1]) + dot_nt(back[g][2], weights[g][2])
        for g in groups
    ).astype(BF)
    halo_back = shift(ddistant[:rows], "blk", -1)
    back4 = ddistant[rows : rows + slots]
    back3 = ddistant[rows + slots : rows + 2 * slots]
    back2 = ddistant[rows + 2 * slots : rows + memory]
    got3 = swap(back3, "blk", 1)
    near_back("oth", ddistant)
    group_grads("oth", near["oth"][0])
    cross_got = swap(grads["oth"][1], "dp")
    got3 = after(got3, grads["oth"][1])
    nothing = jnp.zeros_like(got3)
    back4 = back4 + jnp.where(parity == 1, got3, nothing)
    back2 = back2 + jnp.where(parity == 0, got3, nothing)
    got4 = shift(back4, "blk", -2)
    near_back("own", back4)
    cross = grads["oth"][0] + after(cross_got, near["own"][0], lo_got)
    cross_one = swap(cross[:, : 2 * width], "head")
    back2 = back2 + after(got4, near["own"][0])
    slot_back = shift(back2, "blk", -2)
    group_grads("own", after(back2, cross))
    own_got = swap(grads["own"][1], "dp")
    base = sum(
        dot_nt(after(near[g][i], grads["own"][1]), weights[g][i]) for g in groups for i in range(3)
    )
    slot_base = sum(
        dot_nt(rec[g][3 + i].astype(BF), weights[g][i]) for g in groups for i in (1, 2)
    )
    dpacked = slot_base + jnp.pad(
        after(slot_back, base), ((0, padded - slots), (0, 0))
    ).astype(F32)
    dpacked = dpacked.astype(BF)
    dp_mine = lax.dynamic_slice_in_dim(dpacked, me * half, half, 1)
    dp_got = swap(lax.dynamic_slice_in_dim(dpacked, ot * half, half, 1), "head")
    late = grads["own"][0] + after(own_got, dpacked)
    cross_one = after(cross_one, late)
    cross_two = swap(after(cross[:, 2 * width :], cross_one), "head")
    late_one = late[:, : 2 * width] + cross_one
    late_qk = halve_blocks(late_one, rising, position)
    grad_own, sums1 = finish(
        me_arg, base, halo_back, dpacked, w_comp, tokens, after(dmiddle, late_one), norm1_gain
    )
    dp_got = after(dp_got, grad_own)
    keep, send = weight_grads(
        scalars,
        [
            [
                (tri_own, tap * model, dp_mine, (0, 0), half),
                (tri_oth, tap * model, dp_got, (0, 0), half),
            ]
            for tap in range(3)
        ],
        share, model, "pack_grads",
    )
    comp_got = swap(send, "dp")
    cross_two = after(cross_two, keep)
    grad_got = swap(after(grad_own, cross_two), "head")
    late_vo = halve_blocks(late[:, 2 * width :] + cross_two, falling, position)
    comp = halve_blocks(keep + comp_got, falling, position)
    comp_got = swap(comp, "head")
    comp_all = in_order(
        me, comp.reshape(share, 3, half), comp_got.reshape(share, 3, half), 2
    ).astype(F32)

    dslopes = {}
    for g in groups:
        total = back[g][3] + near[g][3]
        dslopes[g] = -jnp.sum(total[:, 2] - total[:, 0] * total[:, 1], axis=1)
    both = in_order(me, dslopes["own"], dslopes["oth"], 0)
    dcomp_bias = jnp.sum(dpacked.astype(F32), axis=0)
    vector = jnp.concatenate(
        [sums1[0], sums1[1], sums2[0], sums2[1], dcomp_bias, jnp.pad(both, (0, 128 - 2 * heads))]
    )
    vector = butterfly(vector.reshape(-1, 128)).reshape(-1)
    slope_sum = lax.dynamic_slice_in_dim(vector, 5 * model + me * heads, heads, 0)

    recon_own = rec["own"][0].reshape(heads, rows)
    recon_got = swap(rec["oth"][0].reshape(heads, rows), "head")
    recon = in_order(me, recon_own[None], recon_got[None], 0)
    layer_out = in_order(me, lo_own[None], lo_got[None], 0)
    grad_tokens = in_order(me, grad_own[None], grad_got[None], 0)
    late = jnp.concatenate([late_qk, late_vo], 1).astype(F32)
    up_down = up_down.astype(F32)
    return (
        layer_out,
        recon,
        grad_tokens,
        jnp.transpose(late[:, : 3 * width].reshape(share, 3, width), (1, 0, 2)),
        late[:, 3 * width :].T,
        slope_sum,
        up_down[:, :units],
        up_down[:, units:].T,
        jnp.transpose(comp_all, (1, 0, 2)),
        vector[4 * model : 5 * model],
        vector[:model],
        vector[model : 2 * model],
        vector[2 * model : 3 * model],
        vector[3 * model : 4 * model],
    )


def solution(mesh):
    in_specs = (
        P("dp", "blk", None),
        P("dp", None),
        P(None, None, "head"),
        P("head", None),
        P("head"),
        P(None, "head"),
        P("head", None),
        P(),
        P(),
        P(),
        P(),
        P(),
        P(),
        P("dp", "blk", None),
        P("dp", "head", "blk"),
    )
    out_specs = (
        P("dp", "blk", None),
        P("dp", "head", "blk"),
        P("dp", "blk", None),
        P(None, ("blk", "dp"), "head"),
        P("head", ("blk", "dp")),
        P("head"),
        P(("blk", "dp"), "head"),
        P("head", ("blk", "dp")),
        P(None, ("blk", "dp"), None),
        P(),
        P(),
        P(),
        P(),
        P(),
    )
    return jax.shard_map(shards, mesh=mesh, in_specs=in_specs, out_specs=out_specs, check_vma=False)
```

time: 1630 us -> 477 us (0.29)
  waiting for transfers between devices: 1020 us -> 123 us
  matrix products: 242 us -> 22.2 us
  Pallas kernels: 0 us -> 152 us
  blocking collectives: 97.5 us -> 0 us
  other arithmetic: 121 us -> 28.2 us
    psum x3 -> x0, waiting for transfers between devices: 426 us -> none  [the longest x1 199 us: shards(): layer_out = (middle + lax.psum(ffn_part, 'head')).astype(jnp.bfloat16)]
    reduce_scatter x4 -> x1, waiting for transfers between devices: 343 us -> 0.01 us  [shards(): lax.psum_scatter(up_down_part, ('blk', 'dp'), scatter_dimension=0, tiled=...]
    dot_general x40 -> x15, matrix products: 232 us -> 22.2 us  [the longest x14 17.4 us: dot_nt(): return lax.dot_general(a, b, NT, preferred_element_type=F32)]
    unnamed x9 -> x1, waiting for transfers between devices: 152 us -> 0.02 us
    pallas_call x0 -> x23, Pallas kernels: none -> 152 us  [the longest x4 32.4 us: weight_grads(): pl.pallas_call(functools.partial(weight_kernel, plan=tuple(plan), block=5...]
    psum x2 -> x0, blocking collectives: 97.5 us -> none  [the longest x1 61.3 us: shards(): lax.psum((dgain_one, dbias_one, dgain_two, dbias_two, dcomp_bias, dslope_...]
    reduce_sum x14 -> x2, other arithmetic: 78 us -> 0.24 us  [shards(): dslopes[g] = -jnp.sum(total[:, 2] - total[:, 0] * total[:, 1], axis=1)]
    ppermute x16 -> x40, waiting for transfers between devices: 94 us -> 123 us  [the longest x34 115 us: swap(): return lax.ppermute(x, axis, [(i, i ^ step) for i in range(devices)])]
  transfers between devices with their start and end apart: 24 -> 41, of which waited for: 11 -> 15; matrix products, arithmetic and copies ran while one was open for 15% -> 14% of each run, Pallas kernels for 0% -> 26%
where the time goes in v2:
time: 477 us; the launch traced here: 470 us
  Pallas kernels  152 us (32%)
  waiting for transfers between devices  123 us (26%)
  local copies, waits for them, and re-layouts  74.9 us (16%)
  starting transfers between devices  53.9 us (11%)
  other arithmetic  28.2 us (6%)
  matrix products  22.2 us (5%)
  between operations  16.3 us (3%)
    ppermute x34, waiting for transfers between devices, swap(): return lax.ppermute(x, axis, [(i, i ^ step) for i in range(devices)])  115 us
    unnamed x319, local copies, waits for them, and re-layouts  55.9 us
    ppermute x34, starting transfers between devices, swap(): return lax.ppermute(x, axis, [(i, i ^ step) for i in range(devices)])  38.7 us
    pallas_call x4, Pallas kernels, weight_grads(): pl.pallas_call(functools.partial(weight_kernel, plan=tuple(plan), block=5...  32.4 us
    pallas_call x4, Pallas kernels, attend_backward(): pl.pallas_call(functools.partial(backward_kernel, scaling=scaling, own=ow...  28.2 us
    pallas_call x2, Pallas kernels, mlp(): pl.pallas_call(mlp_kernel, grid_spec=pltpu.PrefetchScalarGridSpec(num_sca...  25.4 us
    pallas_call x2, Pallas kernels, recon_both(): pl.pallas_call(functools.partial(recon_kernel, slots=slots, scaling=scali...  22.5 us
    dot_general x14, matrix products, dot_nt(): return lax.dot_general(a, b, NT, preferred_element_type=F32)  17.4 us
  transfers between devices with their start and end apart: 41, of which 15 were waited for; matrix products, arithmetic and copies ran while one was open for 14% of the time, Pallas kernels for 26%

profile of v2, /device:TPU:0, one launch (start us, length us, event | category | flops | bytes accessed | tf_op | source)
XLA Modules:
  0.0 469.7 jit_solution(14309335987140213917)
XLA Ops:
  53.9 11.4 %recon_both.2 = (f32[4,1,512]{2,1,0:T(1,128)S(1)}, f32[512,512]{1,0:T(8,128)S(1)}, f32[512,512]{1,0:T(8,128)S(1)}, f32[512,512]{1,0:T(8,128)S(1)}, f32[176,512]{1,0:T(8,128)S(1)}, /*index=5*/f32[176,512]{1,0:T(8,128)S(1)}) custom-call(bf16[512,512]{1,0:T(8,128)(2,1)S(1)} %copy-done.56, bf16[512,512]{1,0:T(8,128)(2,1)S(1)} %copy-done.60, ...), custom_call_target="tpu_custom_call" | custom-call | flops 4328521728 | bytes 8388608 | tf_op jit(solution)/shard_map/recon_both/pallas_call | solution.py:375
  68.8 6.4 %collective-permute-done.4 = bf16[176,1024]{1,0:T(8,128)(2,1)S(1)} collective-permute-done((bf16[176,1024]{1,0:T(8,128)(2,1)S(1)}, bf16[176,1024]{1,0:T(8,128)(2,1)S(1)}, u32[]{:S(2)}, u32[]{:S(2)}) %collective-permute-start.4) | collective-permute-done | bytes 360480 | tf_op jit(solution)/shard_map/ppermute | solution.py:43
  81.3 7.6 %attend_forward.2 = (bf16[512,512]{1,0:T(8,128)(2,1)S(1)}, f32[4,1,512]{2,1,0:T(1,128)S(1)}) custom-call(f32[4]{0:T(128)S(1)} %copy-done.107, bf16[512,512]{1,0:T(8,128)(2,1)S(1)} %copy-done.57, bf16[1024,512]{1,0:T(8,128)(2,1)S(1)} %get-tuple-element.156.kf.k, bf16[1024,512]{1,0:T(8,128)(2,1)S(1)} %get-tuple-element.157.vf.v, ...), custom_call_target="tpu_custom_call" | custom-call | flops 3221225472 | bytes 8388608 | tf_op jit(solution)/shard_map/attend_forward/pallas_call | solution.py:222
  100.0 7.6 %attend_forward.3 = (bf16[512,512]{1,0:T(8,128)(2,1)S(1)}, f32[4,1,512]{2,1,0:T(1,128)S(1)}) custom-call(f32[4]{0:T(128)S(1)} %slice_bitcast_fusion.20.slopes, bf16[512,512]{1,0:T(8,128)(2,1)S(1)} %get-tuple-element.171.q, bf16[1024,512]{1,0:T(8,128)(2,1)S(1)} %get-tuple-element.163.kf.k, bf16[1024,512]{1,0:T(8,128)(2,1)S(1)} %get-tuple-element.164.vf.v, ...), custom_call_target="tpu_custom_call" | custom-call | flops 3221225472 | bytes 8388608 | tf_op jit(solution)/shard_map/attend_forward/pallas_call | solution.py:222
  112.7 11.1 %recon_both.3 = (f32[4,1,512]{2,1,0:T(1,128)S(1)}, f32[512,512]{1,0:T(8,128)S(1)}, f32[512,512]{1,0:T(8,128)S(1)}, f32[512,512]{1,0:T(8,128)S(1)}, f32[176,512]{1,0:T(8,128)S(1)}, /*index=5*/f32[176,512]{1,0:T(8,128)S(1)}) custom-call(bf16[512,512]{1,0:T(8,128)(2,1)S(1)} %get-tuple-element.171.q, bf16[512,512]{1,0:T(8,128)(2,1)S(1)} %get-tuple-element.165.ko.k, ...), custom_call_target="tpu_custom_call" | custom-call | flops 4328521728 | bytes 8388608 | tf_op jit(solution)/shard_map/recon_both/pallas_call | solution.py:375
  128.2 12.3 %mlp.2 = (bf16[512,2048]{1,0:T(8,128)(2,1)S(1)}, bf16[512,2048]{1,0:T(8,128)(2,1)S(1)}, f32[512,1024]{1,0:T(8,128)S(1)}, f32[512,1024]{1,0:T(8,128)S(1)}) custom-call(s32[1]{0:T(128)} %bitcast.me.which, bf16[512,1024]{1,0:T(8,128)(2,1)S(1)} %get-tuple-element.175.normed.refs_0_, bf16[2,512,1024]{2,1,0:T(8,128)(2,1)S(1)} %copy-done.19, ...), custom_call_target="tpu_custom_call" | custom-call | flops 8589934592 | bytes 16777216 | tf_op jit(solution)/shard_map/mlp/pallas_call | solution.py:462
  141.8 13.2 %mlp.3 = (bf16[512,2048]{1,0:T(8,128)(2,1)S(1)}, bf16[512,2048]{1,0:T(8,128)(2,1)S(1)}, bf16[512,1024]{1,0:T(8,128)(2,1)}, bf16[512,1024]{1,0:T(8,128)(2,1)S(1)}) custom-call(s32[1]{0:T(128)} %bitcast.11.which, bf16[512,1024]{1,0:T(8,128)(2,1)S(1)} %collective-permute-done.9.normed.refs_2_, bf16[2,512,1024]{2,1,0:T(8,128)(2,1)S(1)} %copy-done.19, ...), custom_call_target="tpu_custom_call" | custom-call | flops 8589934592 | bytes 16777216 | tf_op jit(solution)/shard_map/mlp/pallas_call | solution.py:462
  157.9 12.4 %mlp_grads.1 = bf16[1024,4096]{1,0:T(8,128)(2,1)} custom-call(s32[2]{0:T(128)S(1)} %copy-done.109, bf16[512,1024]{1,0:T(8,128)(2,1)S(1)} %get-tuple-element.175.normed.refs_0_, bf16[512,2048]{1,0:T(8,128)(2,1)S(1)} %get-tuple-element.181.refs_1_, bf16[512,1024]{1,0:T(8,128)(2,1)S(1)} %collective-permute-done.9.normed.refs_2_, ...), custom_call_target="tpu_custom_call" | custom-call | flops 8589934592 | bytes 16777216 | tf_op jit(solution)/shard_map/mlp_grads/pallas_call | solution.py:665
  170.3 10.3 %collective-permute-done.10.dn_got = bf16[512,1024]{1,0:T(8,128)(2,1)} collective-permute-done((bf16[512,1024]{1,0:T(8,128)(2,1)}, bf16[512,1024]{1,0:T(8,128)(2,1)}, u32[]{:S(2)}, u32[]{:S(2)}) %collective-permute-start.10) | collective-permute-done | bytes 1048608 | tf_op jit(solution)/shard_map/ppermute | solution.py:43
  198.5 9.0 %attend_backward_far.2 = (f32[512,512]{1,0:T(8,128)S(1)}, bf16[1024,512]{1,0:T(8,128)(2,1)S(1)}, bf16[1024,512]{1,0:T(8,128)(2,1)S(1)}, f32[4,8,512]{2,1,0:T(8,128)S(1)}) custom-call(f32[4]{0:T(128)S(1)} %copy-done.112, bf16[512,512]{1,0:T(8,128)(2,1)S(1)} %copy-done.68, bf16[512,512]{1,0:T(8,128)(2,1)S(1)} %get-tuple-element.205.do, ...), custom_call_target="tpu_custom_call" | custom-call | flops 3221225472 | bytes 8388608 | tf_op jit(solution)/shard_map/attend_backward_far/pallas_call | solution.py:300
  208.3 9.2 %attend_backward_far.3 = (f32[512,512]{1,0:T(8,128)S(1)}, bf16[1024,512]{1,0:T(8,128)(2,1)S(1)}, bf16[1024,512]{1,0:T(8,128)(2,1)S(1)}, f32[4,8,512]{2,1,0:T(8,128)S(1)}) custom-call(f32[4]{0:T(128)S(1)} %copy-done.108, bf16[512,512]{1,0:T(8,128)(2,1)S(1)} %copy-done.58, bf16[512,512]{1,0:T(8,128)(2,1)S(1)} %get-tuple-element.217.do, ...), custom_call_target="tpu_custom_call" | custom-call | flops 3221225472 | bytes 8388608 | tf_op jit(solution)/shard_map/attend_backward_far/pallas_call | solution.py:300
  232.3 5.0 %attend_backward_own.2 = (bf16[512,512]{1,0:T(8,128)(2,1)S(1)}, bf16[512,512]{1,0:T(8,128)(2,1)S(1)}, bf16[512,512]{1,0:T(8,128)(2,1)S(1)}, f32[4,8,512]{2,1,0:T(8,128)S(1)}) custom-call(f32[4]{0:T(128)S(1)} %copy-done.112, bf16[512,512]{1,0:T(8,128)(2,1)S(1)} %copy-done.68, bf16[512,512]{1,0:T(8,128)(2,1)S(1)} %get-tuple-element.205.do, ...), custom_call_target="tpu_custom_call" | custom-call | flops 1610612736 | bytes 8388608 | tf_op jit(solution)/shard_map/attend_backward_own/pallas_call | solution.py:300
  242.8 8.2 %attention_grads.2 = (bf16[512,2048]{1,0:T(8,128)(2,1)S(1)}, bf16[512,2048]{1,0:T(8,128)(2,1)}) custom-call(s32[2]{0:T(128)S(1)} %copy-done.110, bf16[512,1024]{1,0:T(8,128)(2,1)S(1)} %copy-done.118, bf16[512,512]{1,0:T(8,128)(2,1)S(1)} %get-tuple-element.230.refs_1_, bf16[512,512]{1,0:T(8,128)(2,1)S(1)} %get-tuple-element.231.refs_2_, ...), custom_call_target="tpu_custom_call" | custom-call | flops 4664066048 | bytes 16777216 | tf_op jit(solution)/shard_map/attention_grads/pallas_call | solution.py:665
  251.1 21.5 %collective-permute-done.14 = bf16[170,1024]{1,0:T(8,128)(2,1)} collective-permute-done((bf16[170,1024]{1,0:T(8,128)(2,1)}, bf16[170,1024]{1,0:T(8,128)(2,1)}, u32[]{:S(2)}, u32[]{:S(2)}) %collective-permute-start.14) | collective-permute-done | bytes 348192 | tf_op jit(solution)/shard_map/ppermute | solution.py:43
  280.7 5.0 %attend_backward_own.3 = (bf16[512,512]{1,0:T(8,128)(2,1)S(1)}, bf16[512,512]{1,0:T(8,128)(2,1)S(1)}, bf16[512,512]{1,0:T(8,128)(2,1)S(1)}, f32[4,8,512]{2,1,0:T(8,128)S(1)}) custom-call(f32[4]{0:T(128)S(1)} %copy-done.108, bf16[512,512]{1,0:T(8,128)(2,1)S(1)} %copy-done.58, bf16[512,512]{1,0:T(8,128)(2,1)S(1)} %copy-done.74, ...), custom_call_target="tpu_custom_call" | custom-call | flops 1610612736 | bytes 8388608 | tf_op jit(solution)/shard_map/attend_backward_own/pallas_call | solution.py:300
  295.3 8.6 %attention_grads.3 = (bf16[512,2048]{1,0:T(8,128)(2,1)S(1)}, bf16[512,2048]{1,0:T(8,128)(2,1)}) custom-call(s32[2]{0:T(128)S(1)} %copy-done.110, bf16[512,1024]{1,0:T(8,128)(2,1)S(1)} %copy-done.118, bf16[512,512]{1,0:T(8,128)(2,1)S(1)} %copy-done.80, bf16[512,512]{1,0:T(8,128)(2,1)S(1)} %copy-done.84, bf16[176,1024]{1,0:T(8,128)(2,1)S(1)} %copy-done.124, ...), custom_call_target="tpu_custom_call" | custom-call | flops 4664066048 | bytes 16777216 | tf_op jit(solution)/shard_map/attention_grads/pallas_call | solution.py:665
  310.0 5.3 %collective-permute-done.16 = bf16[170,1024]{1,0:T(8,128)(2,1)S(1)} collective-permute-done((bf16[170,1024]{1,0:T(8,128)(2,1)S(1)}, bf16[170,1024]{1,0:T(8,128)(2,1)S(1)}, u32[]{:S(2)}, u32[]{:S(2)}) %collective-permute-start.16) | collective-permute-done | bytes 348192 | tf_op jit(solution)/shard_map/ppermute | solution.py:38
  330.8 16.0 %collective-permute-done.20 = bf16[512,1024]{1,0:T(8,128)(2,1)S(1)} collective-permute-done((bf16[512,1024]{1,0:T(8,128)(2,1)S(1)}, bf16[512,1024]{1,0:T(8,128)(2,1)S(1)}, u32[]{:S(2)}, u32[]{:S(2)}) %collective-permute-start.20) | collective-permute-done | bytes 1048608 | tf_op jit(solution)/shard_map/ppermute | solution.py:43
  375.8 6.7 %collective-permute-done.34 = f32[41,128]{1,0:T(8,128)S(1)} collective-permute-done((f32[41,128]{1,0:T(8,128)S(1)}, f32[41,128]{1,0:T(8,128)S(1)}, u32[]{:S(2)}, u32[]{:S(2)}) %collective-permute-start.34) | collective-permute-done | bytes 21024 | tf_op jit(solution)/shard_map/ppermute | solution.py:43
  391.4 7.7 %collective-permute-done.27 = bf16[2,2,64,1024]{3,2,1,0:T(8,128)(2,1)S(1)} collective-permute-done((bf16[2,2,64,1024]{3,2,1,0:T(8,128)(2,1)S(1)}, bf16[2,2,64,1024]{3,2,1,0:T(8,128)(2,1)S(1)}, u32[]{:S(2)}, u32[]{:S(2)}) %collective-permute-start.27) | collective-permute-done | bytes 524320 | tf_op jit(solution)/shard_map/ppermute | solution.py:43
  407.9 17.9 %collective-permute-done.36 = bf16[2,2,64,1536]{3,2,1,0:T(8,128)(2,1)S(1)} collective-permute-done((bf16[2,2,64,1536]{3,2,1,0:T(8,128)(2,1)S(1)}, bf16[2,2,64,1536]{3,2,1,0:T(8,128)(2,1)S(1)}, u32[]{:S(2)}, u32[]{:S(2)}) %collective-permute-start.36) | collective-permute-done | bytes 786464 | tf_op jit(solution)/shard_map/ppermute | solution.py:43
  429.6 7.2 %collective-permute-done.37 = bf16[2,64,1536]{2,1,0:T(8,128)(2,1)S(1)} collective-permute-done((bf16[2,64,1536]{2,1,0:T(8,128)(2,1)S(1)}, bf16[2,64,1536]{2,1,0:T(8,128)(2,1)S(1)}, u32[]{:S(2)}, u32[]{:S(2)}) %collective-permute-start.37) | collective-permute-done | bytes 393248 | tf_op jit(solution)/shard_map/ppermute | solution.py:43
  438.9 7.2 %collective-permute-done.38 = bf16[64,1536]{1,0:T(8,128)(2,1)S(1)} collective-permute-done((bf16[64,1536]{1,0:T(8,128)(2,1)S(1)}, bf16[64,1536]{1,0:T(8,128)(2,1)S(1)}, u32[]{:S(2)}, u32[]{:S(2)}) %collective-permute-start.38) | collective-permute-done | bytes 196640 | tf_op jit(solution)/shard_map/ppermute | solution.py:43
  447.0 7.6 %collective-permute-done.23 = bf16[512,1024]{1,0:T(8,128)(2,1)} collective-permute-done((bf16[512,1024]{1,0:T(8,128)(2,1)S(1)}, bf16[512,1024]{1,0:T(8,128)(2,1)}, u32[]{:S(2)}, u32[]{:S(2)}) %collective-permute-start.23) | collective-permute-done | bytes 1048608 | tf_op jit(solution)/shard_map/ppermute | solution.py:43
  (495 shorter events, 219.2 us)
Async XLA Ops:
  7.2 452.6 %reduce-scatter.2.cloned.1.call-start = ((), (), s32[]{:S(2)}) async-start(), calls=%async_computation.1 | async-start | bytes 8912896 | tf_op jit(solution)/shard_map/reduce_scatter | solution.py:840
  10.0 37.1 %collective-permute-start.3 = (f32[5,512]{1,0:T(8,128)}, f32[5,512]{1,0:T(8,128)}, u32[]{:S(2)}, u32[]{:S(2)}) collective-permute-start(f32[5,512]{1,0:T(8,128)} %pad_maximum_fusion), channel_id=1, source_target_pairs={{0,1},{1,0},{2,3},{3,2},{4,5},{5,4},{6,7},{7,6},{8,9},{9,8},{10,11... | collective-permute-start | bytes 30728 | tf_op jit(solution)/shard_map/ppermute | solution.py:43
  15.6 51.4 %collective-permute-start.5 = (bf16[3,512,512]{2,1,0:T(8,128)(2,1)}, bf16[3,512,512]{2,1,0:T(8,128)(2,1)}, u32[]{:S(2)}, u32[]{:S(2)}) collective-permute-start(bf16[3,512,512]{2,1,0:T(8,128)(2,1)} %constant_dynamic-slice_fusion.5), channel_id=1, source_target_pairs={{0,1},{1,0},{2,3},{3,2},{4,5},{5,4},{6,7},{7,6},{8,9},{9,8},{10,11... | collective-permute-start | bytes 4718600 | tf_op jit(solution)/shard_map/ppermute | solution.py:43
  22.4 24.7 %collective-permute-start.1 = (bf16[176,1024]{1,0:T(8,128)(2,1)S(1)}, bf16[176,1024]{1,0:T(8,128)(2,1)}, u32[]{:S(2)}, u32[]{:S(2)}) collective-permute-start(bf16[176,1024]{1,0:T(8,128)(2,1)S(1)} %fusion.packed.refs_3_), channel_id=1, source_target_pairs={{0,8},{4,12},{8,16},{12,20},{16,24},{20,28},{1,9},{5,13},{9,17},{1... | collective-permute-start | bytes 1081352 | tf_op jit(solution)/shard_map/ppermute | solution.py:38
  29.0 51.5 %collective-permute-start.6 = (bf16[256,1024]{1,0:T(8,128)(2,1)}, bf16[256,1024]{1,0:T(8,128)(2,1)}, u32[]{:S(2)}, u32[]{:S(2)}) collective-permute-start(bf16[256,1024]{1,0:T(8,128)(2,1)} %constant_dynamic-slice_fusion.3), channel_id=1, source_target_pairs={{0,1},{1,0},{2,3},{3,2},{4,5},{5,4},{6,7},{7,6},{8,9},{9,8},{10,11... | collective-permute-start | bytes 1572872 | tf_op jit(solution)/shard_map/ppermute | solution.py:43
  30.5 45.9 %collective-permute-start = (bf16[512,1024]{1,0:T(8,128)(2,1)}, bf16[512,1024]{1,0:T(8,128)(2,1)}, u32[]{:S(2)}, u32[]{:S(2)}) collective-permute-start(bf16[512,1024]{1,0:T(8,128)(2,1)} %copy-done.115), channel_id=1, source_target_pairs={{0,4},{4,8},{8,12},{12,16},{16,20},{20,24},{24,28},{1,5},{5,9},{9,... | collective-permute-start | bytes 3145736 | tf_op jit(solution)/shard_map/ppermute | solution.py:38
  47.1 18.2 %collective-permute-start.2 = (bf16[176,1024]{1,0:T(8,128)(2,1)}, bf16[176,1024]{1,0:T(8,128)(2,1)S(1)}, u32[]{:S(2)}, u32[]{:S(2)}) collective-permute-start(bf16[176,1024]{1,0:T(8,128)(2,1)} %collective-permute-done.1), channel_id=1, source_target_pairs={{0,8},{4,12},{8,16},{12,20},{16,24},{20,28},{1,9},{5,13},{9,17},{1... | collective-permute-start | bytes 1081352 | tf_op jit(solution)/shard_map/ppermute | solution.py:38
  67.0 23.9 %collective-permute-start.7 = (bf16[3,512,512]{2,1,0:T(8,128)(2,1)}, bf16[3,512,512]{2,1,0:T(8,128)(2,1)S(1)}, u32[]{:S(2)}, u32[]{:S(2)}) collective-permute-start(bf16[3,512,512]{2,1,0:T(8,128)(2,1)} %collective-permute-done.5), channel_id=1, source_target_pairs={{0,2},{2,0},{1,3},{3,1},{4,6},{6,4},{5,7},{7,5},{8,10},{10,8},{9,1... | collective-permute-start | bytes 4718600 | tf_op jit(solution)/shard_map/ppermute | solution.py:43
  112.2 29.6 %collective-permute-start.9 = (bf16[512,1024]{1,0:T(8,128)(2,1)S(1)}, bf16[512,1024]{1,0:T(8,128)(2,1)S(1)}, u32[]{:S(2)}, u32[]{:S(2)}) collective-permute-start(bf16[512,1024]{1,0:T(8,128)(2,1)S(1)} %get-tuple-element.175.normed.refs_0_), channel_id=1, source_target_pairs={{0,1},{1,0},{2,3},{3,2},{4,5},{5,4},{6,7},{7,6},{8,9},{9,8},{10,11... | collective-permute-start | bytes 3145736 | tf_op jit(solution)/shard_map/ppermute | solution.py:43
  155.0 25.6 %collective-permute-start.10 = (bf16[512,1024]{1,0:T(8,128)(2,1)}, bf16[512,1024]{1,0:T(8,128)(2,1)}, u32[]{:S(2)}, u32[]{:S(2)}) collective-permute-start(bf16[512,1024]{1,0:T(8,128)(2,1)} %get-tuple-element.180), channel_id=1, source_target_pairs={{0,1},{1,0},{2,3},{3,2},{4,5},{5,4},{6,7},{7,6},{8,9},{9,8},{10,11... | collective-permute-start | bytes 3145736 | tf_op jit(solution)/shard_map/ppermute | solution.py:43
  180.6 38.3 %collective-permute-start.11 = (bf16[512,1024]{1,0:T(8,128)(2,1)}, bf16[512,1024]{1,0:T(8,128)(2,1)S(1)}, u32[]{:S(2)}, u32[]{:S(2)}) collective-permute-start(bf16[512,1024]{1,0:T(8,128)(2,1)} %copy-done.121), channel_id=1, source_target_pairs={{0,1},{1,0},{2,3},{3,2},{4,5},{5,4},{6,7},{7,6},{8,9},{9,8},{10,11... | collective-permute-start | bytes 3145736 | tf_op jit(solution)/shard_map/ppermute | solution.py:43
  222.6 95.2 %collective-permute-start.12 = (bf16[512,1024]{1,0:T(8,128)(2,1)}, bf16[512,1024]{1,0:T(8,128)(2,1)}, u32[]{:S(2)}, u32[]{:S(2)}) collective-permute-start(bf16[512,1024]{1,0:T(8,128)(2,1)} %add_convert_fusion.1), channel_id=1, source_target_pairs={{0,1},{1,0},{2,3},{3,2},{4,5},{5,4},{6,7},{7,6},{8,9},{9,8},{10,11... | collective-permute-start | bytes 3145736 | tf_op jit(solution)/shard_map/ppermute | solution.py:43
  240.0 32.7 %collective-permute-start.14 = (bf16[170,1024]{1,0:T(8,128)(2,1)}, bf16[170,1024]{1,0:T(8,128)(2,1)}, u32[]{:S(2)}, u32[]{:S(2)}) collective-permute-start(bf16[170,1024]{1,0:T(8,128)(2,1)} %slice.184), channel_id=1, source_target_pairs={{0,4},{4,0},{8,12},{12,8},{16,20},{20,16},{24,28},{28,24},{1,5},{5... | collective-permute-start | bytes 1044488 | tf_op jit(solution)/shard_map/ppermute | solution.py:43
  240.5 107.4 %collective-permute-start.15 = (bf16[512,1024]{1,0:T(8,128)(2,1)}, bf16[512,1024]{1,0:T(8,128)(2,1)}, u32[]{:S(2)}, u32[]{:S(2)}) collective-permute-start(bf16[512,1024]{1,0:T(8,128)(2,1)} %slice.186), channel_id=1, source_target_pairs={{4,0},{8,4},{12,8},{16,12},{20,16},{24,20},{28,24},{5,1},{9,5},{13... | collective-permute-start | bytes 3145736 | tf_op jit(solution)/shard_map/ppermute | solution.py:38
  251.0 66.8 %collective-permute-start.19 = (bf16[512,2048]{1,0:T(8,128)(2,1)}, bf16[512,2048]{1,0:T(8,128)(2,1)}, u32[]{:S(2)}, u32[]{:S(2)}) collective-permute-start(bf16[512,2048]{1,0:T(8,128)(2,1)} %get-tuple-element.215), channel_id=1, source_target_pairs={{0,2},{2,0},{1,3},{3,1},{4,6},{6,4},{5,7},{7,5},{8,10},{10,8},{9,1... | collective-permute-start | bytes 6291464 | tf_op jit(solution)/shard_map/ppermute | solution.py:43
  305.6 24.3 %collective-permute-start.18 = (bf16[512,2048]{1,0:T(8,128)(2,1)}, bf16[512,2048]{1,0:T(8,128)(2,1)S(1)}, u32[]{:S(2)}, u32[]{:S(2)}) collective-permute-start(bf16[512,2048]{1,0:T(8,128)(2,1)} %get-tuple-element.226), channel_id=1, source_target_pairs={{0,2},{2,0},{1,3},{3,1},{4,6},{6,4},{5,7},{7,5},{8,10},{10,8},{9,1... | collective-permute-start | bytes 6291464 | tf_op jit(solution)/shard_map/ppermute | solution.py:43
  321.5 25.3 %collective-permute-start.20 = (bf16[512,1024]{1,0:T(8,128)(2,1)S(1)}, bf16[512,1024]{1,0:T(8,128)(2,1)S(1)}, u32[]{:S(2)}, u32[]{:S(2)}) collective-permute-start(bf16[512,1024]{1,0:T(8,128)(2,1)S(1)} %get-tuple-element.271), channel_id=1, source_target_pairs={{0,1},{1,0},{2,3},{3,2},{4,5},{5,4},{6,7},{7,6},{8,9},{9,8},{10,11... | collective-permute-start | bytes 3145736 | tf_op jit(solution)/shard_map/ppermute | solution.py:43
  328.2 28.3 %collective-permute-start.22 = (bf16[176,512]{1,0:T(8,128)(2,1)}, bf16[176,512]{1,0:T(8,128)(2,1)S(1)}, u32[]{:S(2)}, u32[]{:S(2)}) collective-permute-start(bf16[176,512]{1,0:T(8,128)(2,1)} %get-tuple-element.272), channel_id=1, source_target_pairs={{0,1},{1,0},{2,3},{3,2},{4,5},{5,4},{6,7},{7,6},{8,9},{9,8},{10,11... | collective-permute-start | bytes 540680 | tf_op jit(solution)/shard_map/ppermute | solution.py:43
  356.5 27.2 %collective-permute-start.21 = (bf16[512,1024]{1,0:T(8,128)(2,1)}, bf16[512,1024]{1,0:T(8,128)(2,1)S(1)}, u32[]{:S(2)}, u32[]{:S(2)}) collective-permute-start(bf16[512,1024]{1,0:T(8,128)(2,1)} %get-tuple-element.243), channel_id=1, source_target_pairs={{0,1},{1,0},{2,3},{3,2},{4,5},{5,4},{6,7},{7,6},{8,9},{9,8},{10,11... | collective-permute-start | bytes 3145736 | tf_op jit(solution)/shard_map/ppermute | solution.py:43
  364.3 26.0 %collective-permute-start.35 = (bf16[512,1536]{1,0:T(8,128)(2,1)S(1)}, bf16[512,1536]{1,0:T(8,128)(2,1)S(1)}, u32[]{:S(2)}, u32[]{:S(2)}) collective-permute-start(bf16[512,1536]{1,0:T(8,128)(2,1)S(1)} %get-tuple-element.255), channel_id=1, source_target_pairs={{0,2},{2,0},{1,3},{3,1},{4,6},{6,4},{5,7},{7,5},{8,10},{10,8},{9,1... | collective-permute-start | bytes 4718600 | tf_op jit(solution)/shard_map/ppermute | solution.py:43
  390.8 35.0 %collective-permute-start.36 = (bf16[2,2,64,1536]{3,2,1,0:T(8,128)(2,1)S(1)}, bf16[2,2,64,1536]{3,2,1,0:T(8,128)(2,1)S(1)}, u32[]{:S(2)}, u32[]{:S(2)}) collective-permute-start(bf16[2,2,64,1536]{3,2,1,0:T(8,128)(2,1)S(1)} %dynamic-slice_bitcast_fusion), channel_id=1, source_target_pairs={{0,8},{4,12},{8,0},{12,4},{16,24},{20,28},{24,16},{28,20},{1,9},{5... | collective-permute-start | bytes 2359304 | tf_op jit(solution)/shard_map/ppermute | solution.py:43
  404.7 24.0 %collective-permute-start.26 = (bf16[64,1024]{1,0:T(8,128)(2,1)S(1)}, bf16[64,1024]{1,0:T(8,128)(2,1)S(1)}, u32[]{:S(2)}, u32[]{:S(2)}) collective-permute-start(bf16[64,1024]{1,0:T(8,128)(2,1)S(1)} %dynamic-slice_bitcast_fusion.8), channel_id=1, source_target_pairs={{0,16},{4,20},{8,24},{12,28},{16,0},{20,4},{24,8},{28,12},{1,17},{... | collective-permute-start | bytes 393224 | tf_op jit(solution)/shard_map/ppermute | solution.py:43
  406.5 23.0 %collective-permute-start.29 = (bf16[64,1024]{1,0:T(8,128)(2,1)S(1)}, bf16[64,1024]{1,0:T(8,128)(2,1)S(1)}, u32[]{:S(2)}, u32[]{:S(2)}) collective-permute-start(bf16[64,1024]{1,0:T(8,128)(2,1)S(1)} %dynamic-slice_bitcast_fusion.7), channel_id=1, source_target_pairs={{0,16},{4,20},{8,24},{12,28},{16,0},{20,4},{24,8},{28,12},{1,17},{... | collective-permute-start | bytes 393224 | tf_op jit(solution)/shard_map/ppermute | solution.py:43
  428.8 25.8 %collective-permute-start.23 = (bf16[512,1024]{1,0:T(8,128)(2,1)S(1)}, bf16[512,1024]{1,0:T(8,128)(2,1)}, u32[]{:S(2)}, u32[]{:S(2)}) collective-permute-start(bf16[512,1024]{1,0:T(8,128)(2,1)S(1)} %copy-done.36), channel_id=1, source_target_pairs={{0,1},{1,0},{2,3},{3,2},{4,5},{5,4},{6,7},{7,6},{8,9},{9,8},{10,11... | collective-permute-start | bytes 3145736 | tf_op jit(solution)/shard_map/ppermute | solution.py:43
  (172 other events, 1291.1 us)
Sparse Core Ops, SparseCore 0:
  170.4 126.4 reduce-scatter.1

commit v3 on v2

v3 whole, which is shorter than its diff:
```python
import functools
import math

import jax
import jax.numpy as jnp
from jax import lax
from jax.experimental import pallas as pl
from jax.experimental.pallas import tpu as pltpu
from jax.sharding import PartitionSpec as P

CSEGS = 3
EPS = 1e-05
FAR = 1e30
LOG2E = math.log2(math.e)
BF = jnp.bfloat16
F32 = jnp.float32
TILE = 256
SHARE = 1 << 24
TAIL = 1.0


LIMITS = {"recon_both": 10.3, "mlp": 20.7, "mlp_grads": 27.7, "branches": 23.3, "turn": 17.4, "attention_grads": 26.4, "spread": 17.4, "pack_grads": 19.1, "finish": 21.1}


def limit(name):
    return int(LIMITS.get(name, 14.0) * (1 << 20))


def cost(us):
    return pl.CostEstimate(flops=int(us * SHARE), bytes_accessed=1 << 10, transcendentals=0)

NT = (((1,), (1,)), ((), ()))
GELU_A = math.sqrt(2.0 / math.pi)
GELU_B = 0.044715


def dot(a, b):
    return jnp.dot(a, b, preferred_element_type=F32)


def dot_nt(a, b):
    return lax.dot_general(a, b, NT, preferred_element_type=F32)


def dot_tn(a, b):
    return lax.dot_general(a, b, (((0,), (0,)), ((), ())), preferred_element_type=F32)


def shift(x, axis, by):
    devices = lax.axis_size(axis)
    pairs = [(i, i + by) for i in range(devices) if 0 <= i + by < devices]
    return lax.ppermute(x, axis, pairs)


def trade(x):
    return lax.all_to_all(x, "dp", 0, 0)


def swap(x, axis, step=1):
    devices = lax.axis_size(axis)
    return lax.ppermute(x, axis, [(i, i ^ step) for i in range(devices)])


def call(
    kernel, deps=(), gates=(), prefetch=0, in_specs=None, from_hbm=False, to_hbm=False, **rest
):
    def run(*operands):
        count = len(operands)
        if from_hbm:
            operands = operands[:prefetch] + tuple(
                pltpu.with_memory_space_constraint(x, pltpu.HBM)
                if spec.memory_space is None else x
                for x, spec in zip(operands[prefetch:], in_specs)
            )
        passed = len(deps) + len(gates)
        specs = in_specs or [pl.BlockSpec(memory_space=pltpu.VMEM)] * count
        far = pl.BlockSpec(memory_space=pltpu.HBM)
        specs = list(specs) + [far] * passed

        def body(*refs):
            refs = refs[:count] + refs[count + passed :]
            results = count + len(rest_out)
            kernel(*refs[:results], *refs[results + len(gates) :])

        rest_out = list(rest["out_shape"])
        if to_hbm:
            rest_out = [pltpu.HBM(x.shape, x.dtype) for x in rest_out]
        settings = dict(rest)
        settings["out_shape"] = rest_out + [jax.ShapeDtypeStruct(g.shape, g.dtype) for g in gates]
        if gates:
            plain = [pl.BlockSpec(memory_space=pltpu.VMEM)] * len(rest_out)
            settings["out_specs"] = list(rest.get("out_specs", plain)) + [far] * len(gates)
            settings["input_output_aliases"] = {
                count + len(deps) + i: len(rest_out) + i for i in range(len(gates))
            }
        if prefetch:
            grid = {
                key: settings.pop(key)
                for key in ("grid", "out_specs", "scratch_shapes") if key in settings
            }
            settings["grid_spec"] = pltpu.PrefetchScalarGridSpec(
                num_scalar_prefetch=prefetch, in_specs=specs, **grid
            )
        else:
            settings["in_specs"] = specs
        return pl.pallas_call(body, **settings)(*operands, *deps, *gates)

    return run


def still(shape, index_map):
    return pl.BlockSpec(shape, index_map, pipeline_mode=pl.Buffered(1))


def row_stats(x):
    center = x - jnp.mean(x, axis=-1, keepdims=True)
    inverse = lax.rsqrt(jnp.mean(center * center, axis=-1, keepdims=True) + EPS)
    return center * inverse, inverse


def norm_back(grad, unit, inverse, gain):
    scaled = grad * gain
    mean_one = jnp.mean(scaled, axis=-1, keepdims=True)
    mean_two = jnp.mean(scaled * unit, axis=-1, keepdims=True)
    return inverse * (scaled - mean_one - unit * mean_two)


def front_kernel(me, own, other, gain, bias, normed, tri_own, tri_other, unit, *, slots):
    rows, model = own.shape
    padded = tri_own.shape[0]
    for source, tri in ((own, tri_own), (other, tri_other)):
        for start in range(0, rows, 128):
            part = slice(start, start + 128)
            x, _ = row_stats(source[part, :].astype(F32))
            x = x * gain[...] + bias[...]
            for lane in range(model // 128):
                unit[lane, part, :] = x[:, lane * 128 : (lane + 1) * 128]
            if source is own:
                normed[part, :] = x.astype(BF)
        live = lax.broadcasted_iota(jnp.int32, (padded, 128), 0) < slots
        for lane in range(model // 128):
            unit[lane, rows:, :] = jnp.zeros((unit.shape[1] - rows, 128), F32)
            for tap in range(3):
                at = tap * model + lane * 128
                rows_of = unit[lane, pl.ds(tap, padded, stride=3), :]
                tri[:, at : at + 128] = jnp.where(live, rows_of, 0.0).astype(BF)


def front(me, tokens, gain, bias, slots, padded, deps=(), gates=()):
    _, rows, model = tokens.shape
    tri = jax.ShapeDtypeStruct((padded, 3 * model), BF)
    fixed = lambda shape: still(shape, lambda i, m: (0, 0))
    pick = lambda turn: still((None, rows, model), lambda i, m: ((m[0] + turn) % 2, 0, 0))
    return call(
        functools.partial(front_kernel, slots=slots),
        deps=deps,
        gates=gates,
        **dict(
            prefetch=1,
            grid=(1,),
            in_specs=[pick(0), pick(1), fixed((1, model)), fixed((1, model))],
            out_specs=[fixed((rows, model)), fixed((padded, 3 * model)), fixed((padded, 3 * model))],
            scratch_shapes=[pltpu.VMEM((model // 128, 3 * padded + 8, 128), F32)],
        ),
        out_shape=[jax.ShapeDtypeStruct((rows, model), BF), tri, tri],
        compiler_params=pltpu.CompilerParams(vmem_limit_bytes=limit("front")),
        cost_estimate=cost(0.02),
        name="front",
    )(me, tokens, tokens, gain.reshape(1, model), bias.reshape(1, model))


def distant_kernel(halo, mem, w, kf, vf):
    rows = halo.shape[0]
    for index, out in ((1, kf), (2, vf)):
        out[:rows, :] = dot(halo[...], w[index]).astype(BF)
        out[rows:, :] = dot(mem[...], w[index]).astype(BF)


def project_distant(halo, mem, w, deps=(), gates=()):
    rows, model = halo.shape
    width = w.shape[2]
    shape = jax.ShapeDtypeStruct((2 * rows, width), BF)
    return call(
        distant_kernel,
        deps=deps,
        gates=gates,
        out_shape=[shape, shape],
        compiler_params=pltpu.CompilerParams(vmem_limit_bytes=limit("project_distant")),
        cost_estimate=cost(2.1),
        name="project_distant",
    )(halo, mem, w)


def far_kernel(place, docs, query, out, mem, *, slots, rows):
    position = place[0]
    for seg in range(CSEGS):
        mem[seg * slots : (seg + 1) * slots, :] = docs[pl.ds(seg * rows, slots, stride=3), :]
    mem[CSEGS * slots :, :] = jnp.full((rows - CSEGS * slots, 128), -1, jnp.int32)
    column = lax.broadcasted_iota(jnp.int32, (1, rows), 1)
    step = 64
    for start in range(0, 3 * rows, step):
        local = lax.broadcasted_iota(jnp.int32, (step, 1), 0) + start % rows
        if start < rows:
            doc = docs[CSEGS * rows + start : CSEGS * rows + start + step, :1]
            where, live = local - rows, position > 0
        elif start < 2 * rows:
            doc = mem[start - rows : start - rows + step, :1]
            lead = sum((local >= seg * slots).astype(jnp.int32) for seg in range(1, CSEGS + 1))
            where = (lead - 1 - CSEGS) * rows + 3 * (local - lead * slots) + 1
            live = position - 1 - CSEGS + lead >= 0
        else:
            at = (CSEGS + 1) * rows + start - 2 * rows
            doc = docs[at : at + step, :1]
            where, live = local, position >= 0
        doc = jnp.where(live, doc, -2)
        apart = column - where
        seen = (apart >= 0) & (doc == query[...])
        value = jnp.log((1 + jnp.maximum(apart, 0)).astype(F32))
        out[start : start + step, :] = jnp.where(seen, value, FAR)


def far_log(place, docs, query, slots, deps=(), gates=()):
    rows = query.shape[1]
    return call(
        functools.partial(far_kernel, slots=slots, rows=rows),
        deps=deps,
        gates=gates,
        in_specs=[
            pl.BlockSpec(memory_space=pltpu.SMEM),
            pl.BlockSpec(memory_space=pltpu.VMEM),
            pl.BlockSpec(memory_space=pltpu.VMEM),
        ],
        out_shape=[jax.ShapeDtypeStruct((3 * rows, rows), F32)],
        scratch_shapes=[pltpu.VMEM((rows, 128), jnp.int32)],
        compiler_params=pltpu.CompilerParams(vmem_limit_bytes=limit("far_log")),
        cost_estimate=cost(0.02),
        name="far_log",
    )(place, docs, query)


def project_kernel(normed, packed, w, q, k, v, kc, vc):
    for index, out in enumerate((q, k, v)):
        out[...] = dot(normed[...], w[index]).astype(BF)
    kc[...] = dot(packed[...], w[1]).astype(BF)
    vc[...] = dot(packed[...], w[2]).astype(BF)


def project(normed, packed, w, deps=(), gates=()):
    rows, model = normed.shape
    padded, width = packed.shape[0], w.shape[2]
    near = jax.ShapeDtypeStruct((rows, width), BF)
    little = jax.ShapeDtypeStruct((padded, width), BF)
    return call(
        project_kernel,
        deps=deps,
        gates=gates,
        out_shape=[near, near, near, little, little],
        compiler_params=pltpu.CompilerParams(vmem_limit_bytes=limit("project")),
        cost_estimate=cost(2.0),
        name="project",
    )(normed, packed, w)


def forward_kernel(slopes, q, kf, vf, ko, vo, far, out, lse, *, scaling):
    head = pl.program_id(0)
    c1 = scaling * LOG2E
    c2 = slopes[head] * LOG2E
    rows, reach = q.shape[0], kf.shape[0]
    vft, vot = vf[...].T, vo[...].T
    for qi in range(rows // TILE):
        qs = slice(qi * TILE, (qi + 1) * TILE)
        until = (qi + 1) * TILE
        qb = q[qs, :]
        near = dot_nt(ko[:until, :], qb) * c1 - c2 * far[reach : reach + until, qs]
        away = dot_nt(kf[...], qb) * c1 - c2 * far[:reach, qs]
        top = jnp.maximum(
            jnp.max(near, axis=0, keepdims=True), jnp.max(away, axis=0, keepdims=True)
        )
        near = jnp.exp2(near - top)
        away = jnp.exp2(away - top)
        total = jnp.sum(near, axis=0, keepdims=True) + jnp.sum(away, axis=0, keepdims=True)
        mixed = dot(vot[:, :until], near.astype(BF)) + dot(vft, away.astype(BF))
        out[qs, :] = (mixed / total).T.astype(BF)
        lse[0, :, qs] = top + jnp.log2(total)


def attend_forward(slopes, q, kf, vf, ko, vo, far, scaling, deps=(), gates=()):
    rows, width = q.shape
    reach = kf.shape[0]
    heads = slopes.shape[0]
    hd = width // heads
    near = pl.BlockSpec((rows, hd), lambda h: (0, h))
    wide = pl.BlockSpec((reach, hd), lambda h: (0, h))
    return call(
        functools.partial(forward_kernel, scaling=scaling),
        deps=deps,
        gates=gates,
        grid=(heads,),
        in_specs=[
            pl.BlockSpec(memory_space=pltpu.SMEM), near, wide, wide, near, near,
            still((reach + rows, rows), lambda h: (0, 0)),
        ],
        out_specs=[near, pl.BlockSpec((1, 1, rows), lambda h: (h, 0, 0))],
        out_shape=[
            jax.ShapeDtypeStruct((rows, width), BF),
            jax.ShapeDtypeStruct((heads, 1, rows), F32),
        ],
        compiler_params=pltpu.CompilerParams(vmem_limit_bytes=limit("attend_forward")),
        cost_estimate=cost(3.2),
        name="attend_forward",
    )(slopes, q, kf, vf, ko, vo, far)


def backward_kernel(slopes, q, do, lse, dot_row, far, k, v, *refs, scaling, own):
    head = pl.program_id(0)
    c1 = scaling * LOG2E
    c2 = slopes[head] * LOG2E
    extras = refs[:-4]
    dq, dk_out, dv_out, sums_out = refs[-4:]
    rows, hd = q.shape
    keys = k.shape[0]
    tall = rows
    dqs = [None] * (rows // TILE)
    for ki in range(keys // tall):
        base = ki * tall
        kt = k[base : base + tall, :].T
        dks, dvs = [], []
        for qi in range(rows // TILE):
            qs = slice(qi * TILE, (qi + 1) * TILE)
            until = (qi + 1) * TILE if own else tall
            ks = slice(base, base + until)
            qb, db = q[qs, :], do[qs, :]
            dist = far[ks, qs]
            s = dot_nt(k[ks, :], qb) * c1 - c2 * dist
            p = jnp.exp2(s - lse[0, :, qs])
            dp = dot_nt(v[ks, :], db)
            ds = p * (dp - dot_row[0, :, qs])
            for index, value in enumerate((ds, p * dist, ds * dist)):
                value = jnp.sum(value, axis=0, keepdims=True)
                if ki > 0:
                    value = value + sums_out[0, index : index + 1, qs]
                sums_out[0, index : index + 1, qs] = value
            p = p.astype(BF)
            ds = ds.astype(BF)
            dvs.append(dot(p, db))
            dks.append(dot(ds, qb))
            value = dot(kt[:, :until], ds)
            if ki > 0:
                value = value + dqs[qi]
            dqs[qi] = value
            if ki == keys // tall - 1:
                value = value.T * scaling
                if own:
                    value = value + extras[0][qs, :].astype(F32) + extras[1][qs, :].astype(F32)
                dq[qs, :] = value.astype(BF)
        for start in range(0, tall, TILE):
            ks = slice(base + start, base + start + TILE)
            dk = sum(d[start : start + TILE, :] for d in dks if d.shape[0] > start) * scaling
            dv = sum(d[start : start + TILE, :] for d in dvs if d.shape[0] > start)
            if own:
                dk = dk + extras[2][ks, :].astype(F32)
                dv = dv + extras[3][ks, :].astype(F32)
            dk_out[ks, :] = dk.astype(BF)
            dv_out[ks, :] = dv.astype(BF)


def attend_backward(
    slopes, q, do, lse, dot_row, far, k, v, own, extras, scaling, deps=(), gates=(), late=False
):
    rows, width = q.shape
    keys = k.shape[0]
    heads = slopes.shape[0]
    hd = width // heads
    near = pl.BlockSpec((rows, hd), lambda h: (0, h))
    wide = pl.BlockSpec((keys, hd), lambda h: (0, h))
    lane = pl.BlockSpec((1, 1, rows), lambda h: (h, 0, 0))
    place = far.shape[0] // keys - 1 if own else 0
    return call(
        functools.partial(backward_kernel, scaling=scaling, own=own),
        deps=deps,
        gates=gates,
        grid=(heads,),
        in_specs=[
            pl.BlockSpec(memory_space=pltpu.SMEM), near, near, lane, lane,
            still((keys, rows), lambda h: (place, 0)), wide, wide,
        ]
        + [near] * len(extras),
        out_specs=[near, wide, wide, pl.BlockSpec((1, 8, rows), lambda h: (h, 0, 0))],
        out_shape=[
            jax.ShapeDtypeStruct((rows, width), BF),
            jax.ShapeDtypeStruct((keys, width), BF),
            jax.ShapeDtypeStruct((keys, width), BF),
            jax.ShapeDtypeStruct((heads, 8, rows), F32),
        ],
        compiler_params=pltpu.CompilerParams(vmem_limit_bytes=limit("far" if not own else "own")),
        cost_estimate=cost(TAIL * (5 if own else 9)),
        from_hbm=late,
        to_hbm=own,
        name="attend_backward_own" if own else "attend_backward_far",
    )(slopes, q, do, lse, dot_row, far, k, v, *extras)


def recon_kernel(q, ko, vo, kc, vc, cot, recon, dq, dk, dv, dkc, dvc, *, slots, scaling):
    rows, hd = q.shape
    c1 = scaling * LOG2E
    comp_rows = kc.shape[0]
    live = lax.broadcasted_iota(jnp.int32, (comp_rows, TILE), 0) < slots
    kct, vct, kot, vot = kc[...].T, vc[...].T, ko[...].T, vo[...].T
    for qi in range(rows // TILE):
        qs = slice(qi * TILE, (qi + 1) * TILE)
        qb = q[qs, :]
        full_s = dot_nt(ko[...], qb) * c1
        full_p = jnp.exp2(full_s - jnp.max(full_s, axis=0, keepdims=True))
        full_p = full_p * (1.0 / jnp.sum(full_p, axis=0, keepdims=True))
        full_low = full_p.astype(BF)
        comp_s = jnp.where(live, dot_nt(kc[...], qb) * c1, -FAR)
        comp_p = jnp.exp2(comp_s - jnp.max(comp_s, axis=0, keepdims=True))
        comp_p = comp_p * (1.0 / jnp.sum(comp_p, axis=0, keepdims=True))
        comp_low = comp_p.astype(BF)
        full, comp = dot(vot, full_low), dot(vct, comp_low)
        spread = full - comp
        recon[0, :, qs] = jnp.sum(spread * spread, axis=0, keepdims=True) / hd**0.5
        dfull = spread * (cot[0, :, qs] * (2.0 / hd**0.5))
        dfull_low = dfull.astype(BF)
        dfull_rows = dfull_low.T
        full_dw = dot(vo[...], dfull_low)
        comp_dw = dot(vc[...], dfull_low)
        row = jnp.sum(full_p * full_dw, axis=0, keepdims=True)
        full_ds = (full_p * (full_dw - row)).astype(BF)
        row = jnp.sum(comp_p * comp_dw, axis=0, keepdims=True)
        comp_ds = (comp_p * (row - comp_dw)).astype(BF)
        dq[qs, :] = ((dot(kot, full_ds) + dot(kct, comp_ds)).T * scaling).astype(BF)
        terms = (
            dot(full_ds, qb) * scaling, dot(full_low, dfull_rows),
            dot(comp_ds, qb) * scaling, -dot(comp_low, dfull_rows),
        )
        values = terms if qi == 0 else [a + b for a, b in zip(values, terms)]
    for ref, value in zip((dk, dv, dkc, dvc), values):
        ref[...] = value.astype(ref.dtype)


def recon_both(q, ko, vo, kc, vc, cot, slots, scaling, deps=(), gates=()):
    rows, width = q.shape
    heads = cot.shape[0]
    hd = width // heads
    comp_rows = kc.shape[0]
    near = pl.BlockSpec((rows, hd), lambda h: (0, h))
    small = pl.BlockSpec((comp_rows, hd), lambda h: (0, h))
    lane = pl.BlockSpec((1, 1, rows), lambda h: (h, 0, 0))
    big = jax.ShapeDtypeStruct((rows, width), BF)
    little = jax.ShapeDtypeStruct((comp_rows, width), BF)
    return call(
        functools.partial(recon_kernel, slots=slots, scaling=scaling),
        deps=deps,
        gates=gates,
        grid=(heads,),
        in_specs=[near, near, near, small, small, lane],
        out_specs=[lane, near, near, near, small, small],
        out_shape=[jax.ShapeDtypeStruct((heads, 1, rows), F32), big, big, big, little, little],
        compiler_params=pltpu.CompilerParams(vmem_limit_bytes=limit("recon_both")),
        cost_estimate=cost(4.3),
        to_hbm=True,
        name="recon_both",
    )(q, ko, vo, kc, vc, cot)


def middle_kernel(me, tokens, a_one, a_two, w_one, w_two, gain, bias, middle, normed):
    value = tokens[...].astype(F32) + (dot(a_one[...], w_one[...]) + dot(a_two[...], w_two[...]))
    middle[...] = value
    unit, _ = row_stats(value)
    normed[...] = (unit * gain[...] + bias[...]).astype(BF)


def middle_norm(me, tokens, a_one, a_two, w_one, w_two, gain, bias, deps=(), gates=()):
    _, rows, model = tokens.shape
    width = a_one.shape[1]
    tall = pl.BlockSpec((TILE, model), lambda i, m: (i, 0))
    part = pl.BlockSpec((TILE, width), lambda i, m: (i, 0))
    fixed = lambda shape: still(shape, lambda i, m: (0, 0))
    return call(
        middle_kernel,
        deps=deps,
        gates=gates,
        **dict(
            prefetch=1,
            grid=(rows // TILE,),
            in_specs=[pl.BlockSpec((None, TILE, model), lambda i, m: (m[0], i, 0)), part, part,
                      fixed((width, model)), fixed((width, model)), fixed((1, model)),
                      fixed((1, model))],
            out_specs=[tall, tall],
        ),
        out_shape=[jax.ShapeDtypeStruct((rows, model), F32), jax.ShapeDtypeStruct((rows, model), BF)],
        compiler_params=pltpu.CompilerParams(vmem_limit_bytes=limit("middle_norm")),
        cost_estimate=cost(1.1),
        name="middle_norm",
    )(me, tokens, a_one, a_two, w_one, w_two, gain.reshape(1, model), bias.reshape(1, model))


def mlp_kernel(which, normed, cot, w_up, w_down, hidden, dinner, dnormed, dn_sum):
    step = pl.program_id(0)
    inner = dot(normed[...], w_up[...])
    dhidden = dot_nt(cot[...], w_down[...])
    square = inner * inner
    inside = jnp.tanh(inner * (GELU_A + (GELU_A * GELU_B) * square))
    bent = 0.5 * (1.0 + inside)
    hidden[...] = (inner * bent).astype(BF)
    slope = bent + inner * (0.5 - 0.5 * inside * inside) * (
        GELU_A + (3.0 * GELU_A * GELU_B) * square
    )
    dlow = (dhidden * slope).astype(BF)
    dinner[...] = dlow
    dn = dot_nt(dlow, w_up[...])

    @pl.when(step == 0)
    def _():
        dn_sum[...] = dn

    @pl.when(step > 0)
    def _():
        dn_sum[...] += dn

    @pl.when(step == pl.num_programs(0) - 1)
    def _():
        dnormed[...] = dn_sum[...].astype(dnormed.dtype)


def mlp(which, normed, cot, w_up, w_down, dtype, deps=(), gates=()):
    rows, model = normed.shape
    units = w_up.shape[1]
    step = 512
    tall = still((rows, model), lambda f, m: (0, 0))
    act = pl.BlockSpec((rows, step), lambda f, m: (0, f))
    return call(
        mlp_kernel,
        deps=deps,
        gates=gates,
        **dict(
            prefetch=1,
            grid=(units // step,),
            in_specs=[tall, still((None, rows, model), lambda f, m: (m[0], 0, 0)),
                      pl.BlockSpec((model, step), lambda f, m: (0, f)),
                      pl.BlockSpec((step, model), lambda f, m: (f, 0))],
            out_specs=[act, act, tall],
            scratch_shapes=[pltpu.VMEM((rows, model), F32)],
        ),
        out_shape=[jax.ShapeDtypeStruct((rows, units), BF)] * 2
        + [jax.ShapeDtypeStruct((rows, model), dtype)],
        compiler_params=pltpu.CompilerParams(vmem_limit_bytes=limit("mlp")),
        cost_estimate=cost(6.4),
        name="mlp",
    )(which, normed, cot, w_up, w_down)


def branch_kernel(own, oth, w_down, out_own, out_oth, sum_own, sum_oth):
    step = pl.program_id(0)
    for source, total, out in ((own, sum_own, out_own), (oth, sum_oth, out_oth)):
        part = dot(source[...], w_down[...])

        @pl.when(step == 0)
        def _():
            total[...] = part

        @pl.when(step > 0)
        def _():
            total[...] += part

        @pl.when(step == pl.num_programs(0) - 1)
        def _():
            out[...] = total[...].astype(out.dtype)


def branches(own, oth, w_down, deps=(), gates=()):
    rows, units = own.shape
    model = w_down.shape[1]
    step = 512
    tall = still((rows, model), lambda f: (0, 0))
    act = pl.BlockSpec((rows, step), lambda f: (0, f))
    return call(
        branch_kernel,
        deps=deps,
        gates=gates,
        grid=(units // step,),
        in_specs=[act, act, pl.BlockSpec((step, model), lambda f: (f, 0))],
        out_specs=[tall, tall],
        out_shape=[jax.ShapeDtypeStruct((rows, model), BF)] * 2,
        scratch_shapes=[pltpu.VMEM((rows, model), F32)] * 2,
        compiler_params=pltpu.CompilerParams(vmem_limit_bytes=limit("branches")),
        cost_estimate=cost(TAIL * 6),
        name="branches",
    )(own, oth, w_down)


def turn_kernel(
    me, dn_own, dn_got, middle, cot, a_one, a_two, w_one, w_two, gain,
    dbranch, da_one, da_two, row_one, row_two, sums,
):
    step = pl.program_id(0)
    dn = dn_own[...].astype(F32) + dn_got[...].astype(F32)
    unit, inverse = row_stats(middle[...])
    value = cot[...].astype(F32) + norm_back(dn, unit, inverse, gain[...])
    low = value.astype(BF)
    dbranch[...] = low
    for a, w, da, row in ((a_one, w_one, da_one, row_one), (a_two, w_two, da_two, row_two)):
        grad = dot_nt(low, w[...]).astype(BF)
        da[...] = grad
        product = (grad.astype(F32) * a[...].astype(F32)).T
        heads = row.shape[0]
        row[:, 0, :] = jnp.sum(product.reshape(heads, -1, TILE), axis=1)

    @pl.when(step == 0)
    def _():
        sums[...] = jnp.zeros_like(sums)

    sums[0:1, :] += jnp.sum(dn * unit, axis=0, keepdims=True)
    sums[1:2, :] += jnp.sum(dn, axis=0, keepdims=True)


def turn(me, dn_own, dn_got, middle, cot, a_one, a_two, w_one, w_two, gain, heads, deps=(), gates=()):
    rows, model = middle.shape
    width = a_one.shape[1]
    tall = pl.BlockSpec((TILE, model), lambda i, m: (i, 0))
    part = pl.BlockSpec((TILE, width), lambda i, m: (i, 0))
    lane = pl.BlockSpec((heads, 1, TILE), lambda i, m: (0, 0, i))
    fixed = lambda shape: still(shape, lambda i, m: (0, 0))
    return call(
        turn_kernel,
        deps=deps,
        gates=gates,
        **dict(
            prefetch=1,
            grid=(rows // TILE,),
            in_specs=[tall, tall, tall,
                      pl.BlockSpec((None, TILE, model), lambda i, m: (m[0], i, 0)),
                      part, part, fixed((width, model)), fixed((width, model)), fixed((1, model))],
            out_specs=[tall, part, part, lane, lane, fixed((8, model))],
        ),
        out_shape=[
            jax.ShapeDtypeStruct((rows, model), BF),
            jax.ShapeDtypeStruct((rows, width), BF),
            jax.ShapeDtypeStruct((rows, width), BF),
            jax.ShapeDtypeStruct((heads, 1, rows), F32),
            jax.ShapeDtypeStruct((heads, 1, rows), F32),
            jax.ShapeDtypeStruct((8, model), F32),
        ],
        compiler_params=pltpu.CompilerParams(vmem_limit_bytes=limit("turn")),
        cost_estimate=cost(TAIL * 5),
        name="turn",
    )(me, dn_own, dn_got, middle, cot, a_one, a_two, w_one, w_two, gain.reshape(1, model))


def spread_kernel(ka, va, kb, vb, wka, wva, wkb, wvb, near, four, three, two, held, *, slots):
    step = pl.program_id(0)
    value = dot_nt(ka[...], wka[...]) + dot_nt(va[...], wva[...])
    value = value + dot_nt(kb[...], wkb[...]) + dot_nt(vb[...], wvb[...])

    @pl.when(step == 0)
    def _():
        near[...] = value.astype(BF)

    @pl.when(step == 1)
    def _():
        rows = value.shape[0]
        held[:rows, :] = value
        held[rows:, :] = jnp.zeros((held.shape[0] - rows, value.shape[1]), F32)
        padded = four.shape[0]
        live = lax.broadcasted_iota(jnp.int32, four.shape, 0) < slots
        for index, out in enumerate((four, three, two)):
            part = held[index * slots : index * slots + padded, :]
            out[...] = jnp.where(live, part, 0.0).astype(BF)


def spread(ka, va, kb, vb, wa, wb, slots, padded, deps=(), gates=()):
    rows, width = ka.shape[0] // 2, ka.shape[1]
    model = wa.shape[1]
    part = pl.BlockSpec((rows, width), lambda i: (i, 0))
    weight = lambda t: still((None, model, width), lambda i: (t, 0, 0))
    fixed = lambda *shape: still(shape, lambda i: (0, 0))
    little = jax.ShapeDtypeStruct((padded, model), BF)
    return call(
        functools.partial(spread_kernel, slots=slots),
        deps=deps,
        gates=gates,
        grid=(2,),
        in_specs=[part] * 4 + [weight(1), weight(2)] * 2,
        out_specs=[fixed(rows, model)] + [fixed(padded, model)] * 3,
        out_shape=[jax.ShapeDtypeStruct((rows, model), BF), little, little, little],
        scratch_shapes=[pltpu.VMEM((rows + 16, model), F32)],
        compiler_params=pltpu.CompilerParams(vmem_limit_bytes=limit("spread")),
        cost_estimate=cost(TAIL * 6),
        name="spread",
    )(ka, va, kb, vb, wa, wa, wb, wb)


def base_kernel(q, k, v, kc, vc, w, *refs, more):
    before, slot_before = refs[:2] if more else (None, None)
    base, slot_base, total, slot_total = refs[-4:]
    step = pl.program_id(0)
    for index, part in enumerate((q, k, v)):

        @pl.when(step == index)
        def _():
            value = dot_nt(part[...], w[...])
            if index > 0:
                value = value + total[...]
            elif more:
                value = value + before[...].astype(F32)
            if index == 2:
                base[...] = value.astype(BF)
            else:
                total[...] = value

    for index, part in enumerate((kc, vc)):

        @pl.when(step == index + 1)
        def _():
            value = dot_nt(part[...], w[...])
            if index > 0:
                value = value + slot_total[...]
            elif more:
                value = value + slot_before[...].astype(F32)
            if index == 1:
                slot_base[...] = value.astype(BF)
            else:
                slot_total[...] = value


def base_rows(near, slot, w, before, deps=(), gates=()):
    rows, width = near[0].shape
    padded = slot[0].shape[0]
    model = w.shape[1]
    fixed = lambda *shape: still(shape, lambda i: (0, 0))
    outs = [fixed(rows, model), fixed(padded, model)]
    return call(
        functools.partial(base_kernel, more=bool(before)),
        deps=deps,
        gates=gates,
        grid=(3,),
        in_specs=[fixed(rows, width)] * 3 + [fixed(padded, width)] * 2
        + [pl.BlockSpec((None, model, width), lambda i: (i, 0, 0))]
        + outs[: len(before)],
        out_specs=outs,
        out_shape=[
            jax.ShapeDtypeStruct((rows, model), BF),
            jax.ShapeDtypeStruct((padded, model), BF),
        ],
        scratch_shapes=[pltpu.VMEM((rows, model), F32), pltpu.VMEM((padded, model), F32)],
        compiler_params=pltpu.CompilerParams(vmem_limit_bytes=limit("base_rows")),
        cost_estimate=cost(TAIL * 3),
        from_hbm=True,
        name="base_rows",
    )(*near, *slot, w, *before)


def packed_kernel(me, base, *refs):
    gots, (dpacked, mine, away, bias) = refs[:-4], refs[-4:]
    value = sum(part[...].astype(F32) for part in (base, *gots)).astype(BF)
    dpacked[...] = value
    half = mine.shape[1]
    first, second = value[:, :half], value[:, half:]
    low = me[0] == 0
    mine[...] = jnp.where(low, first, second)
    away[...] = jnp.where(low, second, first)
    bias[0:1, :] = jnp.sum(value.astype(F32), axis=0, keepdims=True)


def packed_back(me, base, gots, deps=(), gates=()):
    padded, model = base.shape
    whole = pl.BlockSpec(memory_space=pltpu.VMEM)
    little = jax.ShapeDtypeStruct((padded, model // 2), BF)
    return call(
        packed_kernel,
        deps=deps,
        gates=gates,
        in_specs=[pl.BlockSpec(memory_space=pltpu.SMEM), whole] + [whole] * len(gots),
        out_shape=[jax.ShapeDtypeStruct((padded, model), BF), little, little,
                   jax.ShapeDtypeStruct((8, model), F32)],
        compiler_params=pltpu.CompilerParams(vmem_limit_bytes=limit("packed_back")),
        cost_estimate=cost(TAIL * 400),
        name="packed_back",
    )(me, base, *gots)


def finish_kernel(
    me, base, back, dpacked, w_comp, tokens, dmiddle, gain, grad, sums, total, *, rows
):
    model = base.shape[1]
    padded = dpacked.shape[0]
    for lane in range(model // 128):
        wide = slice(lane * 128, (lane + 1) * 128)
        total[lane, :rows, :] = base[:, wide].astype(F32) + back[:, wide].astype(F32)
        total[lane, rows:, :] = jnp.zeros((total.shape[1] - rows, 128), F32)
    for tap in range(3):
        place = pl.ds(tap, padded, stride=3)
        term = dot_nt(dpacked[...], w_comp[tap])
        for lane in range(model // 128):
            value = total[lane, place, :] + term[:, lane * 128 : (lane + 1) * 128]
            total[lane, place, :] = value
    one = jnp.zeros((1, model), F32)
    two = jnp.zeros((1, model), F32)
    for start in range(0, rows, 128):
        part = slice(start, start + 128)
        dn = jnp.concatenate([total[lane, part, :] for lane in range(model // 128)], 1)
        unit, inverse = row_stats(tokens[part, :].astype(F32))
        value = dmiddle[part, :].astype(F32) + norm_back(dn, unit, inverse, gain[...])
        grad[part, :] = value.astype(BF)
        one = one + jnp.sum(dn * unit, axis=0, keepdims=True)
        two = two + jnp.sum(dn, axis=0, keepdims=True)
    sums[0:1, :] = one
    sums[1:2, :] = two


def finish(me, base, back, dpacked, w_comp, tokens, dmiddle, gain, deps=(), gates=()):
    rows, model = base.shape
    padded = dpacked.shape[0]
    fixed = lambda *shape: still(shape, lambda i, m: (0,) * len(shape))
    return call(
        functools.partial(finish_kernel, rows=rows),
        deps=deps,
        gates=gates,
        **dict(
            prefetch=1,
            grid=(1,),
            in_specs=[fixed(rows, model), fixed(rows, model), fixed(padded, model),
                      fixed(*w_comp.shape),
                      still((None, rows, model), lambda i, m: (m[0], 0, 0)),
                      fixed(rows, model), fixed(1, model)],
            out_specs=[fixed(rows, model), fixed(8, model)],
            scratch_shapes=[pltpu.VMEM((model // 128, 3 * padded + 8, 128), F32)],
        ),
        out_shape=[
            jax.ShapeDtypeStruct((rows, model), BF),
            jax.ShapeDtypeStruct((8, model), F32),
        ],
        compiler_params=pltpu.CompilerParams(vmem_limit_bytes=limit("finish")),
        cost_estimate=cost(TAIL * 4),
        name="finish",
    )(me, base, back, dpacked, w_comp, tokens, dmiddle, gain.reshape(1, model))


def weight_kernel(core, *refs, plan, block, share):
    if share:
        operands, (parts, token, held) = refs[:-3], refs[-3:]
    else:
        operands, (held, token) = refs[:-2], refs[-2:]
    token[...] = jnp.zeros_like(token)
    tall = held.shape[0]
    at = 0
    for pairs, columns in plan:
        for start in range(0, columns, block):
            wide = slice(start, min(start + block, columns))
            value = None
            for a, b in pairs:
                term = lax.dot_general(
                    operands[a][...], operands[b][:, wide], (((0,), (0,)), ((), ())),
                    preferred_element_type=F32,
                )
                value = term if value is None else value + term
            held[:, at + start : at + wide.stop] = value.astype(BF)
        at += columns
    if not share:
        return
    for index in range(tall // (2 * share)):
        for side in range(2):
            here = (2 * index + side) * share
            parts[side, index * share : (index + 1) * share, :] = held[here : here + share, :]


def weight_grads(scalars, sections, share, model, name, tall=512, deps=(), gates=()):
    operands, specs, plan, total = [], [], [], 0
    known = {}

    def place(array, kind, at, columns, depth):
        key = (id(array), kind, at, columns)
        if key not in known:
            known[key] = len(operands)
            operands.append(array)
            if kind == "b":
                col, row = at
                spec = still(
                    (depth, columns), lambda i, c, f=col // columns, r=row // depth: (r, f)
                )
            elif array.ndim == 3:
                spec = pl.BlockSpec((None, depth, tall), lambda i, c, t=at: ((c[1] + t) % 2, 0, i))
            else:
                spec = pl.BlockSpec((depth, tall), lambda i, c, f=at // tall: (0, f + i))
            specs.append(spec)
        return known[key]

    for pairs in sections:
        columns = pairs[0][4]
        plan.append(
            (
                [
                    (
                        place(a, "a", pa, 0, a.shape[-2]),
                        place(b, "b", pb, columns, a.shape[-2]),
                    )
                    for a, pa, b, pb, _ in pairs
                ],
                columns,
            )
        )
        total += columns
    tile = tall // 2 if share else tall
    if share:
        out = [pl.BlockSpec((2, tile, total), lambda i, c: (0, i, 0))]
        shape = [jax.ShapeDtypeStruct((2, tile * (model // tall), total), BF)]
    else:
        out = [pl.BlockSpec((tile, total), lambda i, c: (i, 0))]
        shape = [jax.ShapeDtypeStruct((model, total), BF)]
    out.append(pl.BlockSpec((8, 128), lambda i, c: (0, 0)))
    shape.append(jax.ShapeDtypeStruct((8, 128), F32))
    flops = sum(2 * model * p[4] * p[0].shape[-2] for pairs in sections for p in pairs)
    return call(
        functools.partial(weight_kernel, plan=tuple(plan), block=512, share=share),
        deps=deps,
        gates=gates,
        **dict(
            prefetch=1,
            grid=(model // tall,),
            in_specs=specs,
            out_specs=out,
            scratch_shapes=[pltpu.VMEM((tall, total), BF)] if share else [],
        ),
        out_shape=shape,
        compiler_params=pltpu.CompilerParams(vmem_limit_bytes=limit(name)),
        cost_estimate=cost(TAIL * flops * 1.4e-9),
        to_hbm=True,
        name=name,
    )(scalars, *operands)


def sum_kernel(*refs, split):
    terms, outs = refs[:-split], refs[-split:]
    total = sum(term[...].astype(F32) for term in terms)
    wide = total.shape[1] // split
    for index, out in enumerate(outs):
        out[...] = total[:, index * wide : (index + 1) * wide].astype(out.dtype)


def add(terms, split, name, deps=(), gates=()):
    rows, columns = terms[0].shape[-2:]
    wide = columns // split
    tile = 128 if rows % 128 == 0 else rows
    blocks, operands = [], []
    for term in terms:
        if term.ndim == 3:
            for t in range(term.shape[0]):
                blocks.append(pl.BlockSpec((None, tile, columns), lambda i, t=t: (t, i, 0)))
                operands.append(term)
        else:
            blocks.append(pl.BlockSpec((tile, columns), lambda i: (i, 0)))
            operands.append(term)
    return call(
        functools.partial(sum_kernel, split=split),
        deps=deps,
        gates=gates,
        grid=(rows // tile,),
        in_specs=blocks,
        out_specs=[pl.BlockSpec((tile, wide), lambda i: (i, 0))] * split,
        out_shape=[jax.ShapeDtypeStruct((rows, wide), BF)] * split,
        compiler_params=pltpu.CompilerParams(vmem_limit_bytes=limit(name)),
        cost_estimate=cost(TAIL * 2),
        from_hbm=True,
        name=name,
    )(*operands)


def halve_kernel(bit, *refs, blocks, stride, terms):
    parts, outs = refs[:terms], refs[terms:]
    rows = parts[0].shape[0] // blocks
    mine = bit[0]
    if len(outs) == 1:
        outs[0][...] = sum(part[...].astype(F32) for part in parts).astype(outs[0].dtype)
        return
    for out, side in zip(outs, (mine, 1 - mine)):
        for j in range(blocks // 2):
            at = (j // stride * 2 * stride + j % stride) * rows + side * (stride * rows)
            place = pl.ds(pl.multiple_of(at, rows), rows)
            total = sum(part[place, :].astype(F32) for part in parts)
            out[j * rows : (j + 1) * rows, :] = total.astype(BF)


def halve(bit, parts, blocks, stride, columns, deps=(), gates=()):
    rows = parts[0][0].shape[-2]
    last = blocks == 1
    shape = jax.ShapeDtypeStruct((rows if last else rows // 2, columns), F32 if last else BF)
    return call(
        functools.partial(halve_kernel, blocks=blocks, stride=stride, terms=len(parts)),
        deps=deps,
        gates=gates,
        **dict(
            prefetch=1,
            grid=(1,),
            in_specs=[
                still((rows, columns), lambda i, m, f=part[1] // columns: (0, f))
                if len(part) == 2
                else still(
                    (None, rows, columns), lambda i, m, f=part[1] // columns, t=part[2]: (t, 0, f)
                )
                for part in parts
            ],
            out_specs=[still(shape.shape, lambda i, m: (0, 0))] * (1 if last else 2),
        ),
        out_shape=[shape] * (1 if last else 2),
        compiler_params=pltpu.CompilerParams(vmem_limit_bytes=limit("halve")),
        cost_estimate=cost(TAIL * 3),
        name="halve",
    )(bit, *[part[0] for part in parts])


class Halving:
    def __init__(self, parts, columns, order, position):
        self.parts, self.columns, self.order = parts, columns, list(order)
        self.position = position
        self.blocks = lax.axis_size("blk")
        self.left = list(range(self.blocks.bit_length() - 2, -1, -1))

    def step(self, *deps, gates=()):
        bit = self.order.pop(0)
        place = len(self.left) - 1 - self.left.index(bit)
        mine = scalar((self.position >> bit) & 1)
        keep, away, *rest = halve(
            mine, self.parts, self.blocks, 1 << place, self.columns, deps, gates
        )
        self.parts = [(keep, 0), (swap(away, "blk", 1 << bit), 0)]
        self.left.remove(bit)
        self.blocks //= 2
        return (away, *rest) if rest else away

    def last(self, *deps):
        while self.order:
            self.step(*deps)
        return halve(scalar(self.position), self.parts, 1, 1, self.columns, deps)[0]


def scalar(x):
    return x.reshape(1).astype(jnp.int32)


def total_kernel(one, two, out):
    out[...] = one[...] + two[...]


def butterfly_steps():
    blocks = lax.axis_size("blk")
    return [("dp", 1)] + [("blk", 1 << i) for i in range(blocks.bit_length() - 1)] + [("head", 1)]


def butterfly_add(x, got, deps=()):
    whole = pl.BlockSpec(memory_space=pltpu.VMEM)
    return call(
        total_kernel,
        deps=deps,
        in_specs=[whole, whole],
        out_shape=[jax.ShapeDtypeStruct(x.shape, F32)],
        cost_estimate=cost(TAIL),
        name="small_sum",
    )(x, got)[0]


def in_order(mine, first, second, axis):
    return jnp.where(
        mine == 0, jnp.concatenate([first, second], axis), jnp.concatenate([second, first], axis)
    )


def pick(x, index, axis=0):
    return lax.dynamic_index_in_dim(x, index, axis, keepdims=False)


def shards(
    tokens, doc_ids, w_qkv, w_out, slopes, w_up, w_down, w_comp, comp_bias,
    norm1_gain, norm1_bias, norm2_gain, norm2_bias, out_cot, recon_cot,
):
    seqs, rows, model = tokens.shape
    heads = slopes.shape[0]
    width = w_qkv.shape[2]
    hd = width // heads
    slots = rows // 3
    used = 3 * slots
    padded = -(-slots // 16) * 16
    memory = CSEGS * slots
    position = lax.axis_index("blk")
    core = lax.axis_index("dp")
    me = lax.axis_index("head")
    ot = 1 - me
    scaling = hd ** (-0.5)
    half = model // 2
    share = model // (lax.axis_size("blk") * lax.axis_size("dp"))
    bits = lax.axis_size("blk").bit_length() - 1
    rising = list(range(bits))
    falling = [1, 0] + rising[2:]
    scalars = jnp.stack([core, me]).astype(jnp.int32)
    me_arg, ot_arg = me.reshape(1).astype(jnp.int32), ot.reshape(1).astype(jnp.int32)

    small = jnp.concatenate(
        [pick(recon_cot, ot), jnp.pad(slopes, (0, rows - heads)).reshape(1, rows)], 0
    )
    small_got = swap(small, "head")
    half_rows = model // 2
    qkv_part = lax.dynamic_slice_in_dim(w_qkv, core * half_rows, half_rows, 1)
    out_part = lax.dynamic_slice_in_dim(w_out, core * half_rows, half_rows, 1)
    far_part = jnp.concatenate([qkv_part, out_part[None]], 0)
    far_got = swap(far_part, "head")
    groups = ("own", "oth")

    normed, tri_own, tri_oth = front(
        me_arg, tokens, norm1_gain, norm1_bias, slots, padded, deps=(far_part, small)
    )
    halo = shift(normed, "blk", 1)
    packed = dot(tri_own, w_comp.reshape(3 * model, model)) + comp_bias
    packed = packed.astype(BF)
    lag2, lag3 = shift(packed, "blk", 2), shift(packed, "blk", 3)

    docs = pick(doc_ids, me)
    query_doc = lax.dynamic_slice_in_dim(docs, position * rows, rows, 0).reshape(1, rows)
    padded_doc = jnp.concatenate([jnp.full(((CSEGS + 1) * rows,), -1, jnp.int32), docs])
    window = lax.dynamic_slice_in_dim(padded_doc, position * rows, (CSEGS + 2) * rows, 0)
    window = jnp.broadcast_to(window[:, None], ((CSEGS + 2) * rows, 128))
    (far,) = far_log(
        position.reshape(1).astype(jnp.int32), window, query_doc, slots, deps=(packed,)
    )

    weights, outs = {"own": w_qkv}, {"own": w_out}
    cots = {"own": pick(recon_cot, me).reshape(heads, 1, rows)}
    slope = {"own": slopes}
    q, ko, vo, kc, vc, rec, kf, vf, att, lse = ({} for _ in range(10))
    q["own"], ko["own"], vo["own"], kc["own"], vc["own"], lag2 = project(
        normed, packed, w_qkv, deps=(far,), gates=(lag2,)
    )
    lag4 = shift(lag2, "blk", 2)
    cots["oth"] = small_got[:heads].reshape(heads, 1, rows)
    slope["oth"] = small_got[heads, :heads]
    rec["own"] = recon_both(
        q["own"], ko["own"], vo["own"], kc["own"], vc["own"], cots["own"], slots, scaling,
    )
    mem = jnp.zeros((rows, model), BF)
    for index, lag in enumerate((lag4, lag3, lag2)):
        place = (index * slots, rows - (index + 1) * slots)
        mem = mem + jnp.pad(lag[:slots], (place, (0, 0)))
    kf["own"], vf["own"], far_got = project_distant(
        halo, mem, w_qkv, deps=(rec["own"][0],), gates=(far_got,)
    )
    near_got = swap(far_got, "dp")
    att["own"], lse["own"] = attend_forward(
        slope["own"], q["own"], kf["own"], vf["own"], ko["own"], vo["own"], far, scaling
    )
    weights["oth"] = in_order(core, far_got[:3], near_got[:3], 1)
    outs["oth"] = in_order(core, far_got[3], near_got[3], 1)
    q["oth"], ko["oth"], vo["oth"], kc["oth"], vc["oth"] = project(
        normed, packed, weights["oth"], deps=(att["own"],)
    )
    kf["oth"], vf["oth"] = project_distant(halo, mem, weights["oth"], deps=(q["oth"],))
    att["oth"], lse["oth"] = attend_forward(
        slope["oth"], q["oth"], kf["oth"], vf["oth"], ko["oth"], vo["oth"], far, scaling
    )

    middle, n2_own = middle_norm(
        me_arg, tokens, att["own"], att["oth"], w_out, outs["oth"], norm2_gain, norm2_bias
    )
    n2_oth = swap(n2_own, "head")
    rec["oth"] = recon_both(
        q["oth"], ko["oth"], vo["oth"], kc["oth"], vc["oth"], cots["oth"], slots, scaling,
        deps=(n2_own,),
    )
    hid_own, din_own, dn_own = mlp(
        me_arg, n2_own, out_cot, w_up, w_down, BF, deps=(rec["oth"][0],)
    )
    hid_oth, din_oth, dn_oth = mlp(
        ot_arg, n2_oth, out_cot, w_up, w_down, BF, deps=(dn_own,)
    )
    dn_got = swap(dn_oth, "head")
    units = w_up.shape[1]
    up_down, token = weight_grads(
        scalars,
        [
            [(n2_own, 0, din_own, (0, 0), units), (n2_oth, 0, din_oth, (0, 0), units)],
            [(out_cot, 0, hid_own, (0, 0), units), (out_cot, 1, hid_oth, (0, 0), units)],
        ],
        0, model, "mlp_grads", deps=(dn_oth,),
    )
    ffn_own, ffn_oth = branches(hid_own, hid_oth, w_down, deps=(token,))
    up_down = lax.psum_scatter(up_down, ("blk", "dp"), scatter_dimension=0, tiled=True)
    (
        dbranch, datt_own, datt_oth, row_own, row_oth, sums2,
        ffn_oth, recon_oth,
    ) = turn(
        me_arg, dn_own, dn_got, middle, out_cot, att["own"], att["oth"], w_out, outs["oth"],
        norm2_gain, heads, gates=(ffn_oth, rec["oth"][0]),
    )
    ffn_got = swap(ffn_oth, "head")
    recon_got = swap(recon_oth.reshape(heads, rows), "head")
    datt = {"own": datt_own, "oth": datt_oth}
    row = {"own": row_own, "oth": row_oth}
    back, near, grads = {}, {}, {}

    def far_back(g, *deps):
        back[g] = attend_backward(
            slope[g], q[g], datt[g], lse[g], row[g], far, kf[g], vf[g], False, [], scaling,
            deps=deps, late=g == "own",
        )

    def near_back(g, *deps, gates=()):
        r = rec[g]
        near[g] = attend_backward(
            slope[g], q[g], datt[g], lse[g], row[g], far, ko[g], vo[g], True,
            [back[g][0], r[1], r[2], r[3]], scaling, deps=deps, gates=gates, late=g == "own",
        )

    def group_grads(g, *deps, gates=()):
        r = rec[g]
        sections = [[(normed, 0, near[g][0], (0, 0), width)]]
        for i in (1, 2):
            sections.append(
                [
                    (normed, 0, near[g][i], (0, 0), width),
                    (packed, 0, r[3 + i], (0, 0), width),
                    (halo, 0, back[g][i], (0, 0), width),
                    (mem, 0, back[g][i], (0, rows), width),
                ]
            )
        sections.append([(dbranch, 0, att[g], (0, 0), width)])
        grads[g] = weight_grads(
            scalars, sections, share, model, "attention_grads", deps=deps, gates=gates
        )

    far_back("oth", dbranch)
    near_back("oth")
    group_grads("oth")
    cross = trade(grads["oth"][0])
    far_back("own", grads["oth"][1])
    (lo_own,) = add((middle, ffn_own, ffn_got), 1, "layer_sum", deps=(back["own"][3],))
    (cross,) = add((cross,), 1, "cross_sum", deps=(lo_own,))
    cross_got = swap(cross, "head")
    halo_part, back4, back3, back2 = spread(
        back["oth"][1], back["oth"][2], back["own"][1], back["own"][2], weights["oth"], w_qkv,
        slots, padded, deps=(cross,),
    )
    slot_gots = [
        shift(part, "blk", -lag)
        for part, lag in zip((back4, back3, back2), range(CSEGS + 1, 1, -1))
    ]
    near_back("own", halo_part)
    group_grads("own")
    own = trade(grads["own"][0])
    base_oth = base_rows(
        near["oth"][:3], rec["oth"][4:6], weights["oth"], [], deps=(grads["own"][1],)
    )
    base, slot_base = base_rows(near["own"][:3], rec["own"][4:6], w_qkv, base_oth)
    wide = 2 * width
    late_qk = Halving([(own, 0, 0), (own, 0, 1), (cross_got, 0)], wide, rising, position)
    late_vo = Halving([(own, wide, 0), (own, wide, 1), (cross_got, wide)], wide, falling, position)
    moved = late_qk.step(base)
    moved = late_vo.step(moved)
    dpacked, dp_mine, dp_away, bias_sum, halo_part, lo_own = packed_back(
        me_arg, slot_base, slot_gots, deps=(moved,), gates=(halo_part, lo_own)
    )
    dp_got = swap(dp_away, "head")
    halo_back = shift(halo_part, "blk", -1)
    lo_got = swap(lo_own, "head")
    send, token = weight_grads(
        scalars,
        [
            [
                (tri_own, tap * model, dp_mine, (0, 0), half),
                (tri_oth, tap * model, dp_got, (0, 0), half),
            ]
            for tap in range(3)
        ],
        share, model, "pack_grads",
    )
    comp = trade(send)
    comp = Halving([(comp, 0, 0), (comp, 0, 1)], 3 * half, falling, position)
    moved = comp.step(token)
    moved = late_qk.step(moved)
    moved = late_vo.step(moved)
    grad_own, sums1 = finish(
        me_arg, base, halo_back, dpacked, w_comp, tokens, dbranch, norm1_gain,
        deps=(recon_got, moved),
    )
    dslopes = {}
    for g in groups:
        total = back[g][3] + near[g][3]
        dslopes[g] = -jnp.sum(total[:, 2] - total[:, 0] * total[:, 1], axis=1)
    both = in_order(me, dslopes["own"], dslopes["oth"], 0)
    vector = jnp.concatenate(
        [sums1[0], sums1[1], sums2[0], sums2[1], bias_sum[0], jnp.pad(both, (0, 128 - 2 * heads))]
    ).reshape(-1, 128)
    rounds = butterfly_steps()
    vector_got = swap(vector, *rounds.pop(0))
    moved, grad_away = comp.step(sums1, gates=(grad_own,))
    grad_got = swap(grad_away, "head")
    vector = butterfly_add(vector, vector_got, deps=(moved,))
    vector_got = swap(vector, *rounds.pop(0))
    moved = vector
    while late_qk.order or comp.order:
        if late_qk.order:
            moved = late_qk.step(moved)
            moved = late_vo.step(moved)
        if comp.order:
            moved = comp.step(moved)
        vector = butterfly_add(vector, vector_got, deps=(moved,))
        vector_got = swap(vector, *rounds.pop(0))
        moved = vector
    late_qk = late_qk.last(moved)
    late_vo = late_vo.last(late_qk)
    while len(rounds) > 1:
        vector = butterfly_add(vector, vector_got, deps=(late_vo,))
        vector_got = swap(vector, *rounds.pop(0))
    vector = butterfly_add(vector, vector_got, deps=(late_vo,))
    vector_got = swap(vector, *rounds.pop(0))
    comp = comp.last(vector)
    vector = (vector + vector_got).reshape(-1)
    comp = comp.astype(BF)
    comp_got = swap(comp, "head")
    comp_all = in_order(
        me, comp.reshape(share, 3, half), comp_got.reshape(share, 3, half), 2
    ).astype(F32)

    slope_sum = lax.dynamic_slice_in_dim(vector, 5 * model + me * heads, heads, 0)

    recon_own = rec["own"][0].reshape(heads, rows)
    recon = in_order(me, recon_own[None], recon_got[None], 0)
    layer_out = in_order(me, lo_own[None], lo_got[None], 0)
    grad_tokens = in_order(me, grad_own[None], grad_got[None], 0)
    late = jnp.concatenate([late_qk, late_vo], 1)
    return (
        layer_out,
        recon,
        grad_tokens,
        jnp.transpose(late[:, : 3 * width].reshape(share, 3, width), (1, 0, 2)),
        late[:, 3 * width :].T,
        slope_sum,
        up_down[:, :units].astype(F32),
        up_down[:, units:].astype(F32).T,
        jnp.transpose(comp_all, (1, 0, 2)),
        vector[4 * model : 5 * model],
        vector[:model],
        vector[model : 2 * model],
        vector[2 * model : 3 * model],
        vector[3 * model : 4 * model],
    )


def solution(mesh):
    in_specs = (
        P("dp", "blk", None),
        P("dp", None),
        P(None, None, "head"),
        P("head", None),
        P("head"),
        P(None, "head"),
        P("head", None),
        P(),
        P(),
        P(),
        P(),
        P(),
        P(),
        P("dp", "blk", None),
        P("dp", "head", "blk"),
    )
    out_specs = (
        P("dp", "blk", None),
        P("dp", "head", "blk"),
        P("dp", "blk", None),
        P(None, ("blk", "dp"), "head"),
        P("head", ("blk", "dp")),
        P("head"),
        P(("blk", "dp"), "head"),
        P("head", ("blk", "dp")),
        P(None, ("blk", "dp"), None),
        P(),
        P(),
        P(),
        P(),
        P(),
    )
    return jax.shard_map(shards, mesh=mesh, in_specs=in_specs, out_specs=out_specs, check_vma=False)
```

time: 477 us -> 454 us (0.952)
  waiting for transfers between devices: 123 us -> 51.9 us
  Pallas kernels: 152 us -> 205 us
  starting transfers between devices: 53.9 us -> 83.6 us
  matrix products: 22.2 us -> 1.32 us
  local copies, waits for them, and re-layouts: 74.9 us -> 62.7 us
  other arithmetic: 28.2 us -> 17.6 us
  blocking collectives: 0 us -> 7.92 us
    ppermute x34 -> x26, waiting for transfers between devices: 115 us -> 50.9 us  [swap(): return lax.ppermute(x, axis, [(i, i ^ step) for i in range(devices)])]
    pallas_call x23 -> x46, Pallas kernels: 152 us -> 205 us  [run(): return pl.pallas_call(body, **settings)(*operands, *deps, *gates)]
    dot_general x14 -> x0, matrix products: 17.4 us -> none  [dot_nt(): return lax.dot_general(a, b, NT, preferred_element_type=F32)]
    ppermute x34 -> x26, starting transfers between devices: 38.7 us -> 52.1 us  [swap(): return lax.ppermute(x, axis, [(i, i ^ step) for i in range(devices)])]
    all_to_all x0 -> x2, starting transfers between devices: none -> 11.7 us  [trade(): return lax.all_to_all(x, 'dp', 0, 0)]
    unnamed x319 -> x296, local copies, waits for them, and re-layouts: 55.9 us -> 47.8 us
    all_to_all x0 -> x1, blocking collectives: none -> 7.92 us  [trade(): return lax.all_to_all(x, 'dp', 0, 0)]
    add x21 -> x1, other arithmetic: 7.39 us -> 0.01 us  [shards(): vector = (vector + vector_got).reshape(-1)]
  transfers between devices with their start and end apart: 41 -> 37, of which waited for: 15 -> 12; matrix products, arithmetic and copies ran while one was open for 14% -> 7% of each run, Pallas kernels for 26% -> 36%
where the time goes in v3:
time: 454 us; the launch traced here: 446 us
  Pallas kernels  205 us (45%)
  starting transfers between devices  83.6 us (18%)
  local copies, waits for them, and re-layouts  62.7 us (14%)
  waiting for transfers between devices  51.9 us (11%)
  other arithmetic  17.6 us (4%)
  between operations  16.3 us (4%)
  blocking collectives  7.92 us (2%)
    pallas_call x46, Pallas kernels, run(): return pl.pallas_call(body, **settings)(*operands, *deps, *gates)  205 us
    ppermute x26, starting transfers between devices, swap(): return lax.ppermute(x, axis, [(i, i ^ step) for i in range(devices)])  52.1 us
    ppermute x26, waiting for transfers between devices, swap(): return lax.ppermute(x, axis, [(i, i ^ step) for i in range(devices)])  50.9 us
    unnamed x296, local copies, waits for them, and re-layouts  47.8 us
    ppermute x8, starting transfers between devices, shift(): return lax.ppermute(x, axis, pairs)  19.8 us
    all_to_all x2, starting transfers between devices, trade(): return lax.all_to_all(x, 'dp', 0, 0)  11.7 us
    select_n x6, other arithmetic, in_order(): jnp.where(mine == 0, jnp.concatenate([first, second], axis), jnp.concaten...  9.22 us
  transfers between devices with their start and end apart: 37, of which 12 were waited for; matrix products, arithmetic and copies ran while one was open for 7% of the time, Pallas kernels for 36%

profile of v3, /device:TPU:0, one launch (start us, length us, event | category | flops | bytes accessed | tf_op | source)
XLA Modules:
  0.0 445.9 jit_solution(449356118467369485)
XLA Ops:
  39.3 11.9 %recon_both.2 = (f32[4,1,512]{2,1,0:T(1,128)}, bf16[512,512]{1,0:T(8,128)(2,1)}, bf16[512,512]{1,0:T(8,128)(2,1)}, bf16[512,512]{1,0:T(8,128)(2,1)}, bf16[176,512]{1,0:T(8,128)(2,1)}, /*index=5*/bf16[176,512]{1,0:T(8,128)(2,1)}) custom-call(bf16[512,512]{1,0:T(8,128)(2,1)S(1)} %get-tuple-element.128.refs_0_.refs_1_, ...), custom_call_target="tpu_custom_call" | custom-call | flops 72142032 | bytes 1024 | tf_op jit(solution)/shard_map/recon_both/pallas_call | solution.py:106
  52.6 6.8 %collective-permute-done.4.refs_4_ = bf16[4,512,512]{2,1,0:T(8,128)(2,1)} collective-permute-done((bf16[4,512,512]{2,1,0:T(8,128)(2,1)}, bf16[4,512,512]{2,1,0:T(8,128)(2,1)}, u32[]{:S(2)}, u32[]{:S(2)}) %collective-permute-start.4) | collective-permute-done | bytes 2097184 | tf_op jit(solution)/shard_map/ppermute | solution.py:61
  72.2 7.6 %attend_forward.2 = (bf16[512,512]{1,0:T(8,128)(2,1)S(1)}, f32[4,1,512]{2,1,0:T(1,128)S(1)}) custom-call(f32[4]{0:T(128)S(1)} %copy-done.125, bf16[512,512]{1,0:T(8,128)(2,1)S(1)} %copy-done.43, bf16[1024,512]{1,0:T(8,128)(2,1)S(1)} %copy-done.67, bf16[1024,512]{1,0:T(8,128)(2,1)S(1)} %copy-done.69, bf16[512,512]{1,0:T(8,128)(2,1)S(1)} %copy-done.55, ...), custom_call_target="tpu_custom_call" | custom-call | flops 53687092 | bytes 1024 | tf_op jit(solution)/shard_map/attend_forward/pallas_call | solution.py:106
  94.0 7.6 %attend_forward.3 = (bf16[512,512]{1,0:T(8,128)(2,1)S(1)}, f32[4,1,512]{2,1,0:T(1,128)S(1)}) custom-call(f32[4]{0:T(128)S(1)} %slice_bitcast_fusion.8.refs_0_, bf16[512,512]{1,0:T(8,128)(2,1)S(1)} %get-tuple-element.139.refs_3_.refs_1_.refs_0_, bf16[1024,512]{1,0:T(8,128)(2,1)S(1)} %get-tuple-element.140.refs_2_.refs_6_, ...), custom_call_target="tpu_custom_call" | custom-call | flops 53687092 | bytes 1024 | tf_op jit(solution)/shard_map/attend_forward/pallas_call | solution.py:106
  107.6 12.3 %recon_both.3 = (f32[4,1,512]{2,1,0:T(1,128)}, bf16[512,512]{1,0:T(8,128)(2,1)}, bf16[512,512]{1,0:T(8,128)(2,1)}, bf16[512,512]{1,0:T(8,128)(2,1)}, bf16[176,512]{1,0:T(8,128)(2,1)}, /*index=5*/bf16[176,512]{1,0:T(8,128)(2,1)}) custom-call(bf16[512,512]{1,0:T(8,128)(2,1)S(1)} %get-tuple-element.139.refs_3_.refs_1_.refs_0_, ...), custom_call_target="tpu_custom_call" | custom-call | flops 72142032 | bytes 1024 | tf_op jit(solution)/shard_map/recon_both/pallas_call | solution.py:106
  120.7 8.8 %mlp.2 = (bf16[512,2048]{1,0:T(8,128)(2,1)S(1)}, bf16[512,2048]{1,0:T(8,128)(2,1)S(1)}, bf16[512,1024]{1,0:T(8,128)(2,1)S(1)}) custom-call(s32[1]{0:T(128)} %bitcast.refs_0_, bf16[512,1024]{1,0:T(8,128)(2,1)S(1)} %get-tuple-element.145.refs_6_.refs_1_, bf16[2,512,1024]{2,1,0:T(8,128)(2,1)S(1)} %copy-done.5, bf16[1024,2048]{1,0:T(8,128)(2,1)S(1)} %copy-done.16, ...), custom_call_target="tpu_custom_call" | custom-call | flops 107374184 | bytes 1024 | tf_op jit(solution)/shard_map/mlp/pallas_call | solution.py:106
  129.5 8.8 %mlp.3 = (bf16[512,2048]{1,0:T(8,128)(2,1)S(1)}, bf16[512,2048]{1,0:T(8,128)(2,1)S(1)}, bf16[512,1024]{1,0:T(8,128)(2,1)S(1)}) custom-call(s32[1]{0:T(128)} %bitcast.14.refs_0_, bf16[512,1024]{1,0:T(8,128)(2,1)S(1)} %collective-permute-done.7.refs_1_.refs_3_, bf16[2,512,1024]{2,1,0:T(8,128)(2,1)S(1)} %copy-done.5, bf16[1024,2048]{1,0:T(8,128)(2,1)S(1)} %copy-done.16, ...), custom_call_target="tpu_custom_call" | custom-call | flops 107374184 | bytes 1024 | tf_op jit(solution)/shard_map/mlp/pallas_call | solution.py:106
  138.3 12.1 %mlp_grads.1 = (bf16[1024,4096]{1,0:T(8,128)(2,1)}, f32[8,128]{1,0:T(8,128)}) custom-call(s32[2]{0:T(128)S(1)} %pad_add_fusion.1.refs_0_, bf16[512,1024]{1,0:T(8,128)(2,1)S(1)} %get-tuple-element.145.refs_6_.refs_1_, bf16[512,2048]{1,0:T(8,128)(2,1)S(1)} %get-tuple-element.154.refs_2_, bf16[512,1024]{1,0:T(8,128)(2,1)S(1)} %collective-permute-done.7.refs_1_.refs_3_, ...), custom_call_target="tpu_custom_call" | custom-call | flops 201761264 | bytes 1024 | tf_op jit(solution)/shard_map/mlp_grads/pallas_call | solution.py:106
  157.6 8.6 %branches.1 = (bf16[512,1024]{1,0:T(8,128)(2,1)S(1)}, bf16[512,1024]{1,0:T(8,128)(2,1)}) custom-call(bf16[512,2048]{1,0:T(8,128)(2,1)S(1)} %copy-done.36, bf16[512,2048]{1,0:T(8,128)(2,1)S(1)} %copy-done.38, bf16[2048,1024]{1,0:T(8,128)(2,1)S(1)} %copy-done.8, f32[8,128]{1,0:T(8,128)S(1)} %copy-done.127), custom_call_target="tpu_custom_call" | custom-call | flops 100663296 | bytes 1024 | tf_op jit(solution)/shard_map/branches/pallas_call | solution.py:106
  167.3 7.6 %collective-permute-done.8.refs_2_ = bf16[512,1024]{1,0:T(8,128)(2,1)S(1)} collective-permute-done((bf16[512,1024]{1,0:T(8,128)(2,1)}, bf16[512,1024]{1,0:T(8,128)(2,1)S(1)}, u32[]{:S(2)}, u32[]{:S(2)}) %collective-permute-start.8) | collective-permute-done | bytes 1048608 | tf_op jit(solution)/shard_map/ppermute | solution.py:61
  180.0 8.7 %attend_backward_far.2 = (bf16[512,512]{1,0:T(8,128)(2,1)S(1)}, bf16[1024,512]{1,0:T(8,128)(2,1)S(1)}, bf16[1024,512]{1,0:T(8,128)(2,1)S(1)}, f32[4,8,512]{2,1,0:T(8,128)S(1)}) custom-call(f32[4]{0:T(128)S(1)} %slice_bitcast_fusion.8.refs_0_, bf16[512,512]{1,0:T(8,128)(2,1)S(1)} %copy-done.20, bf16[512,512]{1,0:T(8,128)(2,1)S(1)} %get-tuple-element.161.refs_2_, ...), custom_call_target="tpu_custom_call" | custom-call | flops 150994944 | bytes 1024 | tf_op jit(solution)/shard_map/attend_backward_far/pallas_call | solution.py:106
  198.0 8.4 %attention_grads.2 = (bf16[2,512,2048]{2,1,0:T(8,128)(2,1)}, f32[8,128]{1,0:T(8,128)}) custom-call(s32[2]{0:T(128)S(1)} %pad_add_fusion.1.refs_0_, bf16[512,1024]{1,0:T(8,128)(2,1)} %get-tuple-element.126.refs_0_.refs_1_, bf16[512,512]{1,0:T(8,128)(2,1)S(1)} %copy-done.76, bf16[512,512]{1,0:T(8,128)(2,1)S(1)} %copy-done.77, ...), custom_call_target="tpu_custom_call" | custom-call | flops 109550064 | bytes 1024 | tf_op jit(solution)/shard_map/attention_grads/pallas_call | solution.py:106
  206.4 5.8 %all-to-all-start = ((bf16[2,512,2048]{2,1,0:T(8,128)(2,1)}), bf16[2,512,2048]{2,1,0:T(8,128)(2,1)}, u32[]{:S(2)}, u32[]{:S(2)}) async-start(bf16[2,512,2048]{2,1,0:T(8,128)(2,1)} %get-tuple-element.183), calls=%async_computation | async-start | bytes 8388608 | tf_op jit(solution)/shard_map/all_to_all | solution.py:56
  212.3 9.9 %attend_backward_far.3 = (bf16[512,512]{1,0:T(8,128)(2,1)S(1)}, bf16[1024,512]{1,0:T(8,128)(2,1)S(1)}, bf16[1024,512]{1,0:T(8,128)(2,1)S(1)}, f32[4,8,512]{2,1,0:T(8,128)S(1)}) custom-call(f32[4]{0:T(128)S(1)} %copy-done.125, bf16[512,512]{1,0:T(8,128)(2,1)} %copy-done.42, bf16[512,512]{1,0:T(8,128)(2,1)} %copy-done.79, f32[4,1,512]{2,1,0:T(1,128)} %copy-done.120, ...), custom_call_target="tpu_custom_call" | custom-call | flops 150994944 | bytes 1024 | tf_op jit(solution)/shard_map/attend_backward_far/pallas_call | solution.py:106
  233.2 6.5 %spread.1 = (bf16[512,1024]{1,0:T(8,128)(2,1)}, bf16[176,1024]{1,0:T(8,128)(2,1)}, bf16[176,1024]{1,0:T(8,128)(2,1)}, bf16[176,1024]{1,0:T(8,128)(2,1)}) custom-call(bf16[1024,512]{1,0:T(8,128)(2,1)S(1)} %copy-done.32, bf16[1024,512]{1,0:T(8,128)(2,1)S(1)} %copy-done.34, bf16[1024,512]{1,0:T(8,128)(2,1)S(1)} %get-tuple-element.181.refs_2_.refs_7_.refs_9_, ...), custom_call_target="tpu_custom_call" | custom-call | flops 100663296 | bytes 1024 | tf_op jit(solution)/shard_map/spread/pallas_call | solution.py:106
  243.6 7.1 %attend_backward_own.3 = (bf16[512,512]{1,0:T(8,128)(2,1)}, bf16[512,512]{1,0:T(8,128)(2,1)}, bf16[512,512]{1,0:T(8,128)(2,1)}, f32[4,8,512]{2,1,0:T(8,128)}) custom-call(f32[4]{0:T(128)S(1)} %copy-done.125, bf16[512,512]{1,0:T(8,128)(2,1)} %copy-done.42, bf16[512,512]{1,0:T(8,128)(2,1)} %copy-done.79, f32[4,1,512]{2,1,0:T(1,128)} %copy-done.120, ...), custom_call_target="tpu_custom_call" | custom-call | flops 83886080 | bytes 1024 | tf_op jit(solution)/shard_map/attend_backward_own/pallas_call | solution.py:106
  254.0 8.4 %attention_grads.3 = (bf16[2,512,2048]{2,1,0:T(8,128)(2,1)}, f32[8,128]{1,0:T(8,128)}) custom-call(s32[2]{0:T(128)S(1)} %pad_add_fusion.1.refs_0_, bf16[512,1024]{1,0:T(8,128)(2,1)} %get-tuple-element.126.refs_0_.refs_1_, bf16[512,512]{1,0:T(8,128)(2,1)S(1)} %copy-done.80, bf16[512,512]{1,0:T(8,128)(2,1)S(1)} %copy-done.81, ...), custom_call_target="tpu_custom_call" | custom-call | flops 109550064 | bytes 1024 | tf_op jit(solution)/shard_map/attention_grads/pallas_call | solution.py:106
  262.4 5.8 %all-to-all-start.1 = ((bf16[2,512,2048]{2,1,0:T(8,128)(2,1)}), bf16[2,512,2048]{2,1,0:T(8,128)(2,1)}, u32[]{:S(2)}, u32[]{:S(2)}) async-start(bf16[2,512,2048]{2,1,0:T(8,128)(2,1)} %get-tuple-element.200), calls=%async_computation.1 | async-start | bytes 8388608 | tf_op jit(solution)/shard_map/all_to_all | solution.py:56
  275.1 5.5 %base_rows.3 = (bf16[512,1024]{1,0:T(8,128)(2,1)S(1)}, bf16[176,1024]{1,0:T(8,128)(2,1)S(1)}) custom-call(bf16[512,512]{1,0:T(8,128)(2,1)} %get-tuple-element.188.refs_2_.refs_0_, bf16[512,512]{1,0:T(8,128)(2,1)} %get-tuple-element.189.refs_3_.refs_1_, bf16[512,512]{1,0:T(8,128)(2,1)} %get-tuple-element.190.refs_10_.refs_2_, ...), custom_call_target="tpu_custom_call" | custom-call | flops 50331648 | bytes 1024 | tf_op jit(solution)/shard_map/base_rows/pallas_call | solution.py:106
  303.2 7.9 %all_to_all.15.refs_1_.refs_2_ = bf16[2,512,1536]{2,1,0:T(8,128)(2,1)S(1)} all-to-all(bf16[2,512,1536]{2,1,0:T(8,128)(2,1)} %get-tuple-element.213), channel_id=1, replica_groups=mesh['blk'=8,'dp'=2,'head'=2] {'dp'}, dimensions={0} | all-to-all | bytes 6291456 | tf_op jit(solution)/shard_map/all_to_all | solution.py:56
  313.1 17.4 %collective-permute-start.20 = (bf16[256,1536]{1,0:T(8,128)(2,1)}, bf16[256,1536]{1,0:T(8,128)(2,1)}, u32[]{:S(2)}, u32[]{:S(2)}) collective-permute-start(bf16[256,1536]{1,0:T(8,128)(2,1)} %get-tuple-element.215.refs_3_), channel_id=1, source_target_pairs={{0,8},{4,12},{8,0},{12,4},{16,24},{20,28},{24,16},{28,20},{1,9},{5... | collective-permute-start | bytes 2359304 | tf_op jit(solution)/shard_map/ppermute | solution.py:61
  339.3 8.3 %collective-permute-done.18.refs_2_ = bf16[256,1024]{1,0:T(8,128)(2,1)S(1)} collective-permute-done((bf16[256,1024]{1,0:T(8,128)(2,1)}, bf16[256,1024]{1,0:T(8,128)(2,1)S(1)}, u32[]{:S(2)}, u32[]{:S(2)}) %collective-permute-start.18) | collective-permute-done | bytes 524320 | tf_op jit(solution)/shard_map/ppermute | solution.py:61
  351.1 10.5 %collective-permute-done.17.refs_2_ = bf16[256,1024]{1,0:T(8,128)(2,1)S(1)} collective-permute-done((bf16[256,1024]{1,0:T(8,128)(2,1)}, bf16[256,1024]{1,0:T(8,128)(2,1)S(1)}, u32[]{:S(2)}, u32[]{:S(2)}) %collective-permute-start.17) | collective-permute-done | bytes 524320 | tf_op jit(solution)/shard_map/ppermute | solution.py:61
  392.3 5.9 %collective-permute-start.24 = (bf16[64,1024]{1,0:T(8,128)(2,1)}, bf16[64,1024]{1,0:T(8,128)(2,1)S(1)}, u32[]{:S(2)}, u32[]{:S(2)}) collective-permute-start(bf16[64,1024]{1,0:T(8,128)(2,1)} %get-tuple-element.230.refs_3_), channel_id=1, source_target_pairs={{0,16},{4,20},{8,24},{12,28},{16,0},{20,4},{24,8},{28,12},{1,17},{... | collective-permute-start | bytes 393224 | tf_op jit(solution)/shard_map/ppermute | solution.py:61
  (442 shorter events, 221.5 us)
Async XLA Ops:
  7.2 429.4 %reduce-scatter.2.cloned.1.call-start = ((), (), s32[]{:S(2)}) async-start(), calls=%async_computation.4 | async-start | bytes 8912896 | tf_op jit(solution)/shard_map/reduce_scatter | solution.py:1184
  10.5 48.9 %collective-permute-start.4 = (bf16[4,512,512]{2,1,0:T(8,128)(2,1)}, bf16[4,512,512]{2,1,0:T(8,128)(2,1)}, u32[]{:S(2)}, u32[]{:S(2)}) collective-permute-start(bf16[4,512,512]{2,1,0:T(8,128)(2,1)} %pad_maximum_fusion.refs_5_), channel_id=1, source_target_pairs={{0,1},{1,0},{2,3},{3,2},{4,5},{5,4},{6,7},{7,6},{8,9},{9,8},{10,11... | collective-permute-start | bytes 6291464 | tf_op jit(solution)/shard_map/ppermute | solution.py:61
  22.6 28.6 %collective-permute-start.3 = (bf16[176,1024]{1,0:T(8,128)(2,1)S(1)}, bf16[176,1024]{1,0:T(8,128)(2,1)}, u32[]{:S(2)}, u32[]{:S(2)}) collective-permute-start(bf16[176,1024]{1,0:T(8,128)(2,1)S(1)} %fusion.refs_3_.refs_1_.refs_4_), channel_id=1, source_target_pairs={{0,12},{4,16},{8,20},{12,24},{16,28},{1,13},{5,17},{9,21},{13,25},... | collective-permute-start | bytes 1081352 | tf_op jit(solution)/shard_map/ppermute | solution.py:52
  27.1 25.5 %collective-permute-start.1 = (bf16[512,1024]{1,0:T(8,128)(2,1)}, bf16[512,1024]{1,0:T(8,128)(2,1)}, u32[]{:S(2)}, u32[]{:S(2)}) collective-permute-start(bf16[512,1024]{1,0:T(8,128)(2,1)} %get-tuple-element.126.refs_0_.refs_1_), channel_id=1, source_target_pairs={{0,4},{4,8},{8,12},{12,16},{16,20},{20,24},{24,28},{1,5},{5,9},{9,... | collective-permute-start | bytes 3145736 | tf_op jit(solution)/shard_map/ppermute | solution.py:52
  105.0 24.4 %collective-permute-start.7 = (bf16[512,1024]{1,0:T(8,128)(2,1)S(1)}, bf16[512,1024]{1,0:T(8,128)(2,1)S(1)}, u32[]{:S(2)}, u32[]{:S(2)}) collective-permute-start(bf16[512,1024]{1,0:T(8,128)(2,1)S(1)} %get-tuple-element.145.refs_6_.refs_1_), channel_id=1, source_target_pairs={{0,1},{1,0},{2,3},{3,2},{4,5},{5,4},{6,7},{7,6},{8,9},{9,8},{10,11... | collective-permute-start | bytes 3145736 | tf_op jit(solution)/shard_map/ppermute | solution.py:61
  150.4 24.4 %collective-permute-start.8 = (bf16[512,1024]{1,0:T(8,128)(2,1)}, bf16[512,1024]{1,0:T(8,128)(2,1)S(1)}, u32[]{:S(2)}, u32[]{:S(2)}) collective-permute-start(bf16[512,1024]{1,0:T(8,128)(2,1)} %copy-done.83), channel_id=1, source_target_pairs={{0,1},{1,0},{2,3},{3,2},{4,5},{5,4},{6,7},{7,6},{8,9},{9,8},{10,11... | collective-permute-start | bytes 3145736 | tf_op jit(solution)/shard_map/ppermute | solution.py:61
  178.8 44.2 %collective-permute-start.9 = (bf16[512,1024]{1,0:T(8,128)(2,1)}, bf16[512,1024]{1,0:T(8,128)(2,1)}, u32[]{:S(2)}, u32[]{:S(2)}) collective-permute-start(bf16[512,1024]{1,0:T(8,128)(2,1)} %get-tuple-element.185), channel_id=1, source_target_pairs={{0,1},{1,0},{2,3},{3,2},{4,5},{5,4},{6,7},{7,6},{8,9},{9,8},{10,11... | collective-permute-start | bytes 3145736 | tf_op jit(solution)/shard_map/ppermute | solution.py:61
  206.4 20.6 %all-to-all-start = ((bf16[2,512,2048]{2,1,0:T(8,128)(2,1)}), bf16[2,512,2048]{2,1,0:T(8,128)(2,1)}, u32[]{:S(2)}, u32[]{:S(2)}) async-start(bf16[2,512,2048]{2,1,0:T(8,128)(2,1)} %get-tuple-element.183), calls=%async_computation | async-start | bytes 8388608 | tf_op jit(solution)/shard_map/all_to_all | solution.py:56
  232.3 49.0 %collective-permute-start.13 = (bf16[512,2048]{1,0:T(8,128)(2,1)}, bf16[512,2048]{1,0:T(8,128)(2,1)}, u32[]{:S(2)}, u32[]{:S(2)}) collective-permute-start(bf16[512,2048]{1,0:T(8,128)(2,1)} %cross_sum.1.refs_8_), channel_id=1, source_target_pairs={{0,1},{1,0},{2,3},{3,2},{4,5},{5,4},{6,7},{7,6},{8,9},{9,8},{10,11... | collective-permute-start | bytes 6291464 | tf_op jit(solution)/shard_map/ppermute | solution.py:61
  239.7 49.4 %collective-permute-start.10 = (bf16[176,1024]{1,0:T(8,128)(2,1)}, bf16[176,1024]{1,0:T(8,128)(2,1)}, u32[]{:S(2)}, u32[]{:S(2)}) collective-permute-start(bf16[176,1024]{1,0:T(8,128)(2,1)} %get-tuple-element.197), channel_id=1, source_target_pairs={{16,0},{20,4},{24,8},{28,12},{17,1},{21,5},{25,9},{29,13},{18,2},{... | collective-permute-start | bytes 1081352 | tf_op jit(solution)/shard_map/ppermute | solution.py:52
  241.0 48.1 %collective-permute-start.11 = (bf16[176,1024]{1,0:T(8,128)(2,1)}, bf16[176,1024]{1,0:T(8,128)(2,1)}, u32[]{:S(2)}, u32[]{:S(2)}) collective-permute-start(bf16[176,1024]{1,0:T(8,128)(2,1)} %get-tuple-element.198), channel_id=1, source_target_pairs={{12,0},{16,4},{20,8},{24,12},{28,16},{13,1},{17,5},{21,9},{25,13},... | collective-permute-start | bytes 1081352 | tf_op jit(solution)/shard_map/ppermute | solution.py:52
  242.3 46.8 %collective-permute-start.12 = (bf16[176,1024]{1,0:T(8,128)(2,1)}, bf16[176,1024]{1,0:T(8,128)(2,1)}, u32[]{:S(2)}, u32[]{:S(2)}) collective-permute-start(bf16[176,1024]{1,0:T(8,128)(2,1)} %get-tuple-element.199), channel_id=1, source_target_pairs={{8,0},{12,4},{16,8},{20,12},{24,16},{28,20},{9,1},{13,5},{17,9},{2... | collective-permute-start | bytes 1081352 | tf_op jit(solution)/shard_map/ppermute | solution.py:52
  262.4 19.0 %all-to-all-start.1 = ((bf16[2,512,2048]{2,1,0:T(8,128)(2,1)}), bf16[2,512,2048]{2,1,0:T(8,128)(2,1)}, u32[]{:S(2)}, u32[]{:S(2)}) async-start(bf16[2,512,2048]{2,1,0:T(8,128)(2,1)} %get-tuple-element.200), calls=%async_computation.1 | async-start | bytes 8388608 | tf_op jit(solution)/shard_map/all_to_all | solution.py:56
  291.4 76.5 %collective-permute-start.16 = (bf16[512,1024]{1,0:T(8,128)(2,1)}, bf16[512,1024]{1,0:T(8,128)(2,1)}, u32[]{:S(2)}, u32[]{:S(2)}) collective-permute-start(bf16[512,1024]{1,0:T(8,128)(2,1)} %get-tuple-element.206), channel_id=1, source_target_pairs={{4,0},{8,4},{12,8},{16,12},{20,16},{24,20},{28,24},{5,1},{9,5},{13... | collective-permute-start | bytes 3145736 | tf_op jit(solution)/shard_map/ppermute | solution.py:52
  313.1 62.4 %collective-permute-start.20 = (bf16[256,1536]{1,0:T(8,128)(2,1)}, bf16[256,1536]{1,0:T(8,128)(2,1)}, u32[]{:S(2)}, u32[]{:S(2)}) collective-permute-start(bf16[256,1536]{1,0:T(8,128)(2,1)} %get-tuple-element.215.refs_3_), channel_id=1, source_target_pairs={{0,8},{4,12},{8,0},{12,4},{16,24},{20,28},{24,16},{28,20},{1,9},{5... | collective-permute-start | bytes 2359304 | tf_op jit(solution)/shard_map/ppermute | solution.py:61
  335.4 26.2 %collective-permute-start.17 = (bf16[256,1024]{1,0:T(8,128)(2,1)}, bf16[256,1024]{1,0:T(8,128)(2,1)S(1)}, u32[]{:S(2)}, u32[]{:S(2)}) collective-permute-start(bf16[256,1024]{1,0:T(8,128)(2,1)} %copy-done.134), channel_id=1, source_target_pairs={{0,8},{4,12},{8,0},{12,4},{16,24},{20,28},{24,16},{28,20},{1,9},{5... | collective-permute-start | bytes 1572872 | tf_op jit(solution)/shard_map/ppermute | solution.py:61
  335.6 28.5 %collective-permute-start.15 = (f32[4,512]{1,0:T(4,128)S(1)}, f32[4,512]{1,0:T(4,128)S(1)}, u32[]{:S(2)}, u32[]{:S(2)}) collective-permute-start(f32[4,512]{1,0:T(4,128)S(1)} %bitcast.84), channel_id=1, source_target_pairs={{0,1},{1,0},{2,3},{3,2},{4,5},{5,4},{6,7},{7,6},{8,9},{9,8},{10,11... | collective-permute-start | bytes 24584 | tf_op jit(solution)/shard_map/ppermute | solution.py:61
  347.6 56.1 %collective-permute-start.14 = (bf16[512,1024]{1,0:T(8,128)(2,1)}, bf16[512,1024]{1,0:T(8,128)(2,1)}, u32[]{:S(2)}, u32[]{:S(2)}) collective-permute-start(bf16[512,1024]{1,0:T(8,128)(2,1)} %copy-done.25), channel_id=1, source_target_pairs={{0,1},{1,0},{2,3},{3,2},{4,5},{5,4},{6,7},{7,6},{8,9},{9,8},{10,11... | collective-permute-start | bytes 3145736 | tf_op jit(solution)/shard_map/ppermute | solution.py:61
  361.6 26.7 %collective-permute-start.22 = (bf16[128,1024]{1,0:T(8,128)(2,1)}, bf16[128,1024]{1,0:T(8,128)(2,1)}, u32[]{:S(2)}, u32[]{:S(2)}) collective-permute-start(bf16[128,1024]{1,0:T(8,128)(2,1)} %get-tuple-element.216.refs_3_), channel_id=1, source_target_pairs={{0,8},{4,12},{8,0},{12,4},{16,24},{20,28},{24,16},{28,20},{1,9},{5... | collective-permute-start | bytes 786440 | tf_op jit(solution)/shard_map/ppermute | solution.py:61
  364.1 28.2 %collective-permute-start.27 = (bf16[128,1024]{1,0:T(8,128)(2,1)}, bf16[128,1024]{1,0:T(8,128)(2,1)}, u32[]{:S(2)}, u32[]{:S(2)}) collective-permute-start(bf16[128,1024]{1,0:T(8,128)(2,1)} %get-tuple-element.217.refs_9_), channel_id=1, source_target_pairs={{0,4},{4,0},{8,12},{12,8},{16,20},{20,16},{24,28},{28,24},{1,5},{5... | collective-permute-start | bytes 786440 | tf_op jit(solution)/shard_map/ppermute | solution.py:61
  378.3 21.8 %collective-permute-start.26 = (bf16[128,1536]{1,0:T(8,128)(2,1)S(1)}, bf16[128,1536]{1,0:T(8,128)(2,1)S(1)}, u32[]{:S(2)}, u32[]{:S(2)}) collective-permute-start(bf16[128,1536]{1,0:T(8,128)(2,1)S(1)} %get-tuple-element.228.refs_2_), channel_id=1, source_target_pairs={{0,4},{4,0},{8,12},{12,8},{16,20},{20,16},{24,28},{28,24},{1,5},{5... | collective-permute-start | bytes 1179656 | tf_op jit(solution)/shard_map/ppermute | solution.py:61
  388.3 45.1 %collective-permute-start.21 = (bf16[512,1024]{1,0:T(8,128)(2,1)S(1)}, bf16[512,1024]{1,0:T(8,128)(2,1)}, u32[]{:S(2)}, u32[]{:S(2)}) collective-permute-start(bf16[512,1024]{1,0:T(8,128)(2,1)S(1)} %get-tuple-element.221), channel_id=1, source_target_pairs={{0,1},{1,0},{2,3},{3,2},{4,5},{5,4},{6,7},{7,6},{8,9},{9,8},{10,11... | collective-permute-start | bytes 3145736 | tf_op jit(solution)/shard_map/ppermute | solution.py:61
  392.3 17.2 %collective-permute-start.24 = (bf16[64,1024]{1,0:T(8,128)(2,1)}, bf16[64,1024]{1,0:T(8,128)(2,1)S(1)}, u32[]{:S(2)}, u32[]{:S(2)}) collective-permute-start(bf16[64,1024]{1,0:T(8,128)(2,1)} %get-tuple-element.230.refs_3_), channel_id=1, source_target_pairs={{0,16},{4,20},{8,24},{12,28},{16,0},{20,4},{24,8},{28,12},{1,17},{... | collective-permute-start | bytes 393224 | tf_op jit(solution)/shard_map/ppermute | solution.py:61
  407.0 18.7 %collective-permute-start.32 = (bf16[64,1536]{1,0:T(8,128)(2,1)S(1)}, bf16[64,1536]{1,0:T(8,128)(2,1)S(1)}, u32[]{:S(2)}, u32[]{:S(2)}) collective-permute-start(bf16[64,1536]{1,0:T(8,128)(2,1)S(1)} %copy-done.112), channel_id=1, source_target_pairs={{0,16},{4,20},{8,24},{12,28},{16,0},{20,4},{24,8},{28,12},{1,17},{... | collective-permute-start | bytes 589832 | tf_op jit(solution)/shard_map/ppermute | solution.py:61
  (156 other events, 1298.4 us)
Sparse Core Ops, SparseCore 0:
  150.6 140.8 reduce-scatter.1

commit v4 on v3

--- a/solution.py
+++ b/solution.py
@@ -167,6 +167,29 @@
         cost_estimate=cost(0.02),
         name="front",
     )(me, tokens, tokens, gain.reshape(1, model), bias.reshape(1, model))
+
+
+def norm_kernel(rows, gain, bias, normed):
+    unit, _ = row_stats(rows[...].astype(F32))
+    normed[...] = (unit * gain[...] + bias[...]).astype(BF)
+
+
+def norm_halo(rows, gain, bias, deps=(), gates=()):
+    count, model = rows.shape
+    tall = pl.BlockSpec((TILE, model), lambda i: (i, 0))
+    fixed = pl.BlockSpec((1, model), lambda i: (0, 0))
+    return call(
+        norm_kernel,
+        deps=deps,
+        gates=gates,
+        grid=(count // TILE,),
+        in_specs=[tall, fixed, fixed],
+        out_specs=[tall],
+        out_shape=[jax.ShapeDtypeStruct((count, model), BF)],
+        compiler_params=pltpu.CompilerParams(vmem_limit_bytes=limit("norm_halo")),
+        cost_estimate=cost(2),
+        name="norm_halo",
+    )(rows, gain.reshape(1, model), bias.reshape(1, model))
 
 
 def distant_kernel(halo, mem, w, kf, vf):
@@ -395,7 +418,6 @@
         compiler_params=pltpu.CompilerParams(vmem_limit_bytes=limit("far" if not own else "own")),
         cost_estimate=cost(TAIL * (5 if own else 9)),
         from_hbm=late,
-        to_hbm=own,
         name="attend_backward_own" if own else "attend_backward_far",
     )(slopes, q, do, lse, dot_row, far, k, v, *extras)
 
@@ -586,6 +608,7 @@
         scratch_shapes=[pltpu.VMEM((rows, model), F32)] * 2,
         compiler_params=pltpu.CompilerParams(vmem_limit_bytes=limit("branches")),
         cost_estimate=cost(TAIL * 6),
+        from_hbm=True,
         name="branches",
     )(own, oth, w_down)
 
@@ -941,7 +964,7 @@
 def add(terms, split, name, deps=(), gates=()):
     rows, columns = terms[0].shape[-2:]
     wide = columns // split
-    tile = 128 if rows % 128 == 0 else rows
+    tile = TILE if rows % TILE == 0 else rows
     blocks, operands = [], []
     for term in terms:
         if term.ndim == 3:
@@ -1105,10 +1128,10 @@
     far_got = swap(far_part, "head")
     groups = ("own", "oth")
 
+    halo_raw = shift(pick(tokens, me), "blk", 1)
     normed, tri_own, tri_oth = front(
         me_arg, tokens, norm1_gain, norm1_bias, slots, padded, deps=(far_part, small)
     )
-    halo = shift(normed, "blk", 1)
     packed = dot(tri_own, w_comp.reshape(3 * model, model)) + comp_bias
     packed = packed.astype(BF)
     lag2, lag3 = shift(packed, "blk", 2), shift(packed, "blk", 3)
@@ -1139,9 +1162,8 @@
     for index, lag in enumerate((lag4, lag3, lag2)):
         place = (index * slots, rows - (index + 1) * slots)
         mem = mem + jnp.pad(lag[:slots], (place, (0, 0)))
-    kf["own"], vf["own"], far_got = project_distant(
-        halo, mem, w_qkv, deps=(rec["own"][0],), gates=(far_got,)
-    )
+    halo = norm_halo(halo_raw, norm1_gain, norm1_bias, deps=(rec["own"][0],))[0]
+    kf["own"], vf["own"], far_got = project_distant(halo, mem, w_qkv, gates=(far_got,))
     near_got = swap(far_got, "dp")
     att["own"], lse["own"] = attend_forward(
         slope["own"], q["own"], kf["own"], vf["own"], ko["own"], vo["own"], far, scaling
@@ -1249,10 +1271,8 @@
     )
     base, slot_base = base_rows(near["own"][:3], rec["own"][4:6], w_qkv, base_oth)
     wide = 2 * width
-    late_qk = Halving([(own, 0, 0), (own, 0, 1), (cross_got, 0)], wide, rising, position)
-    late_vo = Halving([(own, wide, 0), (own, wide, 1), (cross_got, wide)], wide, falling, position)
-    moved = late_qk.step(base)
-    moved = late_vo.step(moved)
+    late = Halving([(own, 0, 0), (own, 0, 1), (cross_got, 0)], 2 * wide, rising, position)
+    moved = late.step(base)
     dpacked, dp_mine, dp_away, bias_sum, halo_part, lo_own = packed_back(
         me_arg, slot_base, slot_gots, deps=(moved,), gates=(halo_part, lo_own)
     )
@@ -1273,8 +1293,7 @@
     comp = trade(send)
     comp = Halving([(comp, 0, 0), (comp, 0, 1)], 3 * half, falling, position)
     moved = comp.step(token)
-    moved = late_qk.step(moved)
-    moved = late_vo.step(moved)
+    moved = late.step(moved)
     grad_own, sums1 = finish(
         me_arg, base, halo_back, dpacked, w_comp, tokens, dbranch, norm1_gain,
         deps=(recon_got, moved),
@@ -1294,23 +1313,26 @@
     vector = butterfly_add(vector, vector_got, deps=(moved,))
     vector_got = swap(vector, *rounds.pop(0))
     moved = vector
-    while late_qk.order or comp.order:
-        if late_qk.order:
-            moved = late_qk.step(moved)
-            moved = late_vo.step(moved)
+    while late.order or comp.order:
+        if late.order:
+            moved = late.step(moved)
         if comp.order:
             moved = comp.step(moved)
         vector = butterfly_add(vector, vector_got, deps=(moved,))
         vector_got = swap(vector, *rounds.pop(0))
         moved = vector
-    late_qk = late_qk.last(moved)
-    late_vo = late_vo.last(late_qk)
+    up_sum, down_sum = up_down[:, :units].astype(F32), up_down[:, units:].astype(F32).T
+    vector = butterfly_add(vector, vector_got, deps=(moved, up_sum, down_sum))
+    vector_got = swap(vector, *rounds.pop(0))
+    late = late.last(vector)
     while len(rounds) > 1:
-        vector = butterfly_add(vector, vector_got, deps=(late_vo,))
+        vector = butterfly_add(vector, vector_got, deps=(late,))
         vector_got = swap(vector, *rounds.pop(0))
-    vector = butterfly_add(vector, vector_got, deps=(late_vo,))
-    vector_got = swap(vector, *rounds.pop(0))
-    comp = comp.last(vector)
+    if rounds:
+        vector = butterfly_add(vector, vector_got, deps=(late,))
+        vector_got = swap(vector, *rounds.pop(0))
+    grad_tokens = in_order(me, grad_own[None], grad_got[None], 0)
+    comp = comp.last(vector, grad_tokens)
     vector = (vector + vector_got).reshape(-1)
     comp = comp.astype(BF)
     comp_got = swap(comp, "head")
@@ -1323,8 +1345,6 @@
     recon_own = rec["own"][0].reshape(heads, rows)
     recon = in_order(me, recon_own[None], recon_got[None], 0)
     layer_out = in_order(me, lo_own[None], lo_got[None], 0)
-    grad_tokens = in_order(me, grad_own[None], grad_got[None], 0)
-    late = jnp.concatenate([late_qk, late_vo], 1)
     return (
         layer_out,
         recon,
@@ -1332,8 +1352,8 @@
         jnp.transpose(late[:, : 3 * width].reshape(share, 3, width), (1, 0, 2)),
         late[:, 3 * width :].T,
         slope_sum,
-        up_down[:, :units].astype(F32),
-        up_down[:, units:].astype(F32).T,
+        up_sum,
+        down_sum,
         jnp.transpose(comp_all, (1, 0, 2)),
         vector[4 * model : 5 * model],
         vector[:model],

time: 454 us -> 431 us (0.949)
  waiting for transfers between devices: 51.9 us -> 33.7 us
  Pallas kernels: 205 us -> 195 us
  starting transfers between devices: 83.6 us -> 92.5 us
    ppermute x26 -> x23, waiting for transfers between devices: 50.9 us -> 32.9 us  [swap(): return lax.ppermute(x, axis, [(i, i ^ step) for i in range(devices)])]
    pallas_call x46 -> x43, Pallas kernels: 205 us -> 195 us  [run(): return pl.pallas_call(body, **settings)(*operands, *deps, *gates)]
    ppermute x26 -> x23, starting transfers between devices: 52.1 us -> 61.2 us  [swap(): return lax.ppermute(x, axis, [(i, i ^ step) for i in range(devices)])]
    unnamed x296 -> x318, local copies, waits for them, and re-layouts: 47.8 us -> 42.4 us
  transfers between devices with their start and end apart: 37 -> 34, of which waited for: 12 -> 11; matrix products, arithmetic and copies ran while one was open for 7% -> 8% of each run, Pallas kernels for 36% -> 37%
where the time goes in v4:
time: 431 us; the launch traced here: 424 us
  Pallas kernels  195 us (45%)
  starting transfers between devices  92.5 us (21%)
  local copies, waits for them, and re-layouts  59.1 us (14%)
  waiting for transfers between devices  33.7 us (8%)
  other arithmetic  17.6 us (4%)
  between operations  16.5 us (4%)
  blocking collectives  7.96 us (2%)
    pallas_call x43, Pallas kernels, run(): return pl.pallas_call(body, **settings)(*operands, *deps, *gates)  195 us
    ppermute x23, starting transfers between devices, swap(): return lax.ppermute(x, axis, [(i, i ^ step) for i in range(devices)])  61.2 us
    unnamed x318, local copies, waits for them, and re-layouts  42.4 us
    ppermute x23, waiting for transfers between devices, swap(): return lax.ppermute(x, axis, [(i, i ^ step) for i in range(devices)])  32.9 us
    ppermute x8, starting transfers between devices, shift(): return lax.ppermute(x, axis, pairs)  19.7 us
    all_to_all x2, starting transfers between devices, trade(): return lax.all_to_all(x, 'dp', 0, 0)  11.5 us
    select_n x6, other arithmetic, in_order(): jnp.where(mine == 0, jnp.concatenate([first, second], axis), jnp.concaten...  9.25 us
  transfers between devices with their start and end apart: 34, of which 11 were waited for; matrix products, arithmetic and copies ran while one was open for 8% of the time, Pallas kernels for 37%

profile of v4, /device:TPU:0, one launch (start us, length us, event | category | flops | bytes accessed | tf_op | source)
XLA Modules:
  0.0 423.6 jit_solution(17158762935125011778)
XLA Ops:
  40.3 11.9 %recon_both.2 = (f32[4,1,512]{2,1,0:T(1,128)}, bf16[512,512]{1,0:T(8,128)(2,1)}, bf16[512,512]{1,0:T(8,128)(2,1)}, bf16[512,512]{1,0:T(8,128)(2,1)}, bf16[176,512]{1,0:T(8,128)(2,1)}, /*index=5*/bf16[176,512]{1,0:T(8,128)(2,1)}) custom-call(bf16[512,512]{1,0:T(8,128)(2,1)S(1)} %get-tuple-element.122.refs_0_.refs_1_, ...), custom_call_target="tpu_custom_call" | custom-call | flops 72142032 | bytes 1024 | tf_op jit(solution)/shard_map/recon_both/pallas_call | solution.py:106
  71.0 7.6 %attend_forward.2 = (bf16[512,512]{1,0:T(8,128)(2,1)S(1)}, f32[4,1,512]{2,1,0:T(1,128)S(1)}) custom-call(f32[4]{0:T(128)S(1)} %copy-done.132, bf16[512,512]{1,0:T(8,128)(2,1)S(1)} %copy-done.56, bf16[1024,512]{1,0:T(8,128)(2,1)S(1)} %copy-done.81, bf16[1024,512]{1,0:T(8,128)(2,1)S(1)} %copy-done.83, bf16[512,512]{1,0:T(8,128)(2,1)S(1)} %copy-done.68, ...), custom_call_target="tpu_custom_call" | custom-call | flops 53687092 | bytes 1024 | tf_op jit(solution)/shard_map/attend_forward/pallas_call | solution.py:106
  89.5 7.6 %attend_forward.3 = (bf16[512,512]{1,0:T(8,128)(2,1)S(1)}, f32[4,1,512]{2,1,0:T(1,128)S(1)}) custom-call(f32[4]{0:T(128)S(1)} %slice_bitcast_fusion.8.refs_0_, bf16[512,512]{1,0:T(8,128)(2,1)S(1)} %get-tuple-element.133.refs_3_.refs_1_.refs_0_, bf16[1024,512]{1,0:T(8,128)(2,1)S(1)} %get-tuple-element.134.refs_2_.refs_6_, ...), custom_call_target="tpu_custom_call" | custom-call | flops 53687092 | bytes 1024 | tf_op jit(solution)/shard_map/attend_forward/pallas_call | solution.py:106
  103.5 11.9 %recon_both.3 = (f32[4,1,512]{2,1,0:T(1,128)}, bf16[512,512]{1,0:T(8,128)(2,1)}, bf16[512,512]{1,0:T(8,128)(2,1)}, bf16[512,512]{1,0:T(8,128)(2,1)}, bf16[176,512]{1,0:T(8,128)(2,1)}, /*index=5*/bf16[176,512]{1,0:T(8,128)(2,1)}) custom-call(bf16[512,512]{1,0:T(8,128)(2,1)S(1)} %get-tuple-element.133.refs_3_.refs_1_.refs_0_, ...), custom_call_target="tpu_custom_call" | custom-call | flops 72142032 | bytes 1024 | tf_op jit(solution)/shard_map/recon_both/pallas_call | solution.py:106
  116.1 8.8 %mlp.2 = (bf16[512,2048]{1,0:T(8,128)(2,1)S(1)}, bf16[512,2048]{1,0:T(8,128)(2,1)S(1)}, bf16[512,1024]{1,0:T(8,128)(2,1)S(1)}) custom-call(s32[1]{0:T(128)} %bitcast.refs_0_, bf16[512,1024]{1,0:T(8,128)(2,1)S(1)} %get-tuple-element.139.refs_6_.refs_1_, bf16[2,512,1024]{2,1,0:T(8,128)(2,1)S(1)} %copy-done.5, bf16[1024,2048]{1,0:T(8,128)(2,1)S(1)} %copy-done.19, ...), custom_call_target="tpu_custom_call" | custom-call | flops 107374184 | bytes 1024 | tf_op jit(solution)/shard_map/mlp/pallas_call | solution.py:106
  125.4 8.8 %mlp.3 = (bf16[512,2048]{1,0:T(8,128)(2,1)S(1)}, bf16[512,2048]{1,0:T(8,128)(2,1)S(1)}, bf16[512,1024]{1,0:T(8,128)(2,1)S(1)}) custom-call(s32[1]{0:T(128)} %bitcast.15.refs_0_, bf16[512,1024]{1,0:T(8,128)(2,1)S(1)} %collective-permute-done.7.refs_1_.refs_3_, bf16[2,512,1024]{2,1,0:T(8,128)(2,1)S(1)} %copy-done.5, bf16[1024,2048]{1,0:T(8,128)(2,1)S(1)} %copy-done.19, ...), custom_call_target="tpu_custom_call" | custom-call | flops 107374184 | bytes 1024 | tf_op jit(solution)/shard_map/mlp/pallas_call | solution.py:106
  134.2 12.2 %mlp_grads.1 = (bf16[1024,4096]{1,0:T(8,128)(2,1)}, f32[8,128]{1,0:T(8,128)}) custom-call(s32[2]{0:T(128)S(1)} %pad_add_fusion.1.refs_0_, bf16[512,1024]{1,0:T(8,128)(2,1)S(1)} %get-tuple-element.139.refs_6_.refs_1_, bf16[512,2048]{1,0:T(8,128)(2,1)S(1)} %get-tuple-element.148.refs_2_, bf16[512,1024]{1,0:T(8,128)(2,1)S(1)} %collective-permute-done.7.refs_1_.refs_3_, ...), custom_call_target="tpu_custom_call" | custom-call | flops 201761264 | bytes 1024 | tf_op jit(solution)/shard_map/mlp_grads/pallas_call | solution.py:106
  148.3 10.2 %branches.1 = (bf16[512,1024]{1,0:T(8,128)(2,1)S(1)}, bf16[512,1024]{1,0:T(8,128)(2,1)}) custom-call(bf16[512,2048]{1,0:T(8,128)(2,1)} %copy-done.50, bf16[512,2048]{1,0:T(8,128)(2,1)} %copy-done.51, bf16[2048,1024]{1,0:T(8,128)(2,1)} %refs_2_.11, f32[8,128]{1,0:T(8,128)S(1)} %copy-done.135), custom_call_target="tpu_custom_call" | custom-call | flops 100663296 | bytes 1024 | tf_op jit(solution)/shard_map/branches/pallas_call | solution.py:106
  159.4 11.0 %collective-permute-done.8.refs_2_ = bf16[512,1024]{1,0:T(8,128)(2,1)S(1)} collective-permute-done((bf16[512,1024]{1,0:T(8,128)(2,1)}, bf16[512,1024]{1,0:T(8,128)(2,1)S(1)}, u32[]{:S(2)}, u32[]{:S(2)}) %collective-permute-start.8) | collective-permute-done | bytes 1048608 | tf_op jit(solution)/shard_map/ppermute | solution.py:61
  175.9 8.7 %attend_backward_far.2 = (bf16[512,512]{1,0:T(8,128)(2,1)S(1)}, bf16[1024,512]{1,0:T(8,128)(2,1)S(1)}, bf16[1024,512]{1,0:T(8,128)(2,1)S(1)}, f32[4,8,512]{2,1,0:T(8,128)S(1)}) custom-call(f32[4]{0:T(128)S(1)} %copy-done.134, bf16[512,512]{1,0:T(8,128)(2,1)S(1)} %copy-done.28, bf16[512,512]{1,0:T(8,128)(2,1)S(1)} %get-tuple-element.155.refs_2_, ...), custom_call_target="tpu_custom_call" | custom-call | flops 150994944 | bytes 1024 | tf_op jit(solution)/shard_map/attend_backward_far/pallas_call | solution.py:106
  190.9 7.6 %attention_grads.2 = (bf16[2,512,2048]{2,1,0:T(8,128)(2,1)}, f32[8,128]{1,0:T(8,128)}) custom-call(s32[2]{0:T(128)S(1)} %pad_add_fusion.1.refs_0_, bf16[512,1024]{1,0:T(8,128)(2,1)S(1)} %copy-done.23, bf16[512,512]{1,0:T(8,128)(2,1)S(1)} %get-tuple-element.163.refs_2_.refs_0_, bf16[512,512]{1,0:T(8,128)(2,1)S(1)} %get-tuple-element.164.refs_3_.refs_1_, ...), custom_call_target="tpu_custom_call" | custom-call | flops 109550064 | bytes 1024 | tf_op jit(solution)/shard_map/attention_grads/pallas_call | solution.py:106
  198.5 5.8 %all-to-all-start = ((bf16[2,512,2048]{2,1,0:T(8,128)(2,1)}), bf16[2,512,2048]{2,1,0:T(8,128)(2,1)}, u32[]{:S(2)}, u32[]{:S(2)}) async-start(bf16[2,512,2048]{2,1,0:T(8,128)(2,1)} %get-tuple-element.177), calls=%async_computation | async-start | bytes 8388608 | tf_op jit(solution)/shard_map/all_to_all | solution.py:56
  204.3 10.1 %attend_backward_far.3 = (bf16[512,512]{1,0:T(8,128)(2,1)S(1)}, bf16[1024,512]{1,0:T(8,128)(2,1)S(1)}, bf16[1024,512]{1,0:T(8,128)(2,1)S(1)}, f32[4,8,512]{2,1,0:T(8,128)S(1)}) custom-call(f32[4]{0:T(128)S(1)} %copy-done.132, bf16[512,512]{1,0:T(8,128)(2,1)} %copy-done.55, bf16[512,512]{1,0:T(8,128)(2,1)} %copy-done.93, f32[4,1,512]{2,1,0:T(1,128)} %copy-done.128, ...), custom_call_target="tpu_custom_call" | custom-call | flops 150994944 | bytes 1024 | tf_op jit(solution)/shard_map/attend_backward_far/pallas_call | solution.py:106
  227.3 6.5 %spread.1 = (bf16[512,1024]{1,0:T(8,128)(2,1)}, bf16[176,1024]{1,0:T(8,128)(2,1)}, bf16[176,1024]{1,0:T(8,128)(2,1)}, bf16[176,1024]{1,0:T(8,128)(2,1)}) custom-call(bf16[1024,512]{1,0:T(8,128)(2,1)S(1)} %copy-done.46, bf16[1024,512]{1,0:T(8,128)(2,1)S(1)} %copy-done.48, bf16[1024,512]{1,0:T(8,128)(2,1)S(1)} %copy-done.40, bf16[1024,512]{1,0:T(8,128)(2,1)S(1)} %copy-done.43, ...), custom_call_target="tpu_custom_call" | custom-call | flops 100663296 | bytes 1024 | tf_op jit(solution)/shard_map/spread/pallas_call | solution.py:106
  237.8 6.3 %attend_backward_own.3 = (bf16[512,512]{1,0:T(8,128)(2,1)S(1)}, bf16[512,512]{1,0:T(8,128)(2,1)S(1)}, bf16[512,512]{1,0:T(8,128)(2,1)S(1)}, f32[4,8,512]{2,1,0:T(8,128)S(1)}) custom-call(f32[4]{0:T(128)S(1)} %copy-done.132, bf16[512,512]{1,0:T(8,128)(2,1)} %copy-done.55, bf16[512,512]{1,0:T(8,128)(2,1)} %copy-done.93, f32[4,1,512]{2,1,0:T(1,128)} %copy-done.128, ...), custom_call_target="tpu_custom_call" | custom-call | flops 83886080 | bytes 1024 | tf_op jit(solution)/shard_map/attend_backward_own/pallas_call | solution.py:106
  244.8 7.6 %attention_grads.3 = (bf16[2,512,2048]{2,1,0:T(8,128)(2,1)}, f32[8,128]{1,0:T(8,128)}) custom-call(s32[2]{0:T(128)S(1)} %pad_add_fusion.1.refs_0_, bf16[512,1024]{1,0:T(8,128)(2,1)S(1)} %copy-done.24, bf16[512,512]{1,0:T(8,128)(2,1)S(1)} %get-tuple-element.182.refs_2_.refs_0_, bf16[512,512]{1,0:T(8,128)(2,1)S(1)} %get-tuple-element.183.refs_3_.refs_1_, ...), custom_call_target="tpu_custom_call" | custom-call | flops 109550064 | bytes 1024 | tf_op jit(solution)/shard_map/attention_grads/pallas_call | solution.py:106
  252.4 5.7 %all-to-all-start.1 = ((bf16[2,512,2048]{2,1,0:T(8,128)(2,1)}), bf16[2,512,2048]{2,1,0:T(8,128)(2,1)}, u32[]{:S(2)}, u32[]{:S(2)}) async-start(bf16[2,512,2048]{2,1,0:T(8,128)(2,1)} %get-tuple-element.194), calls=%async_computation.1 | async-start | bytes 8388608 | tf_op jit(solution)/shard_map/all_to_all | solution.py:56
  258.2 5.3 %base_rows.2 = (bf16[512,1024]{1,0:T(8,128)(2,1)S(1)}, bf16[176,1024]{1,0:T(8,128)(2,1)S(1)}) custom-call(bf16[512,512]{1,0:T(8,128)(2,1)} %copy-done.90, bf16[512,512]{1,0:T(8,128)(2,1)} %copy-done.91, bf16[512,512]{1,0:T(8,128)(2,1)} %copy-done.92, bf16[176,512]{1,0:T(8,128)(2,1)} %get-tuple-element.165.refs_5_.refs_3_, ...), custom_call_target="tpu_custom_call" | custom-call | flops 50331648 | bytes 1024 | tf_op jit(solution)/shard_map/base_rows/pallas_call | solution.py:106
  265.3 5.5 %base_rows.3 = (bf16[512,1024]{1,0:T(8,128)(2,1)S(1)}, bf16[176,1024]{1,0:T(8,128)(2,1)S(1)}) custom-call(bf16[512,512]{1,0:T(8,128)(2,1)} %copy-done.94, bf16[512,512]{1,0:T(8,128)(2,1)} %copy-done.95, bf16[512,512]{1,0:T(8,128)(2,1)} %copy-done.96, bf16[176,512]{1,0:T(8,128)(2,1)} %get-tuple-element.185.refs_5_.refs_3_, ...), custom_call_target="tpu_custom_call" | custom-call | flops 50331648 | bytes 1024 | tf_op jit(solution)/shard_map/base_rows/pallas_call | solution.py:106
  279.0 12.8 %collective-permute-start.17 = (bf16[256,2048]{1,0:T(8,128)(2,1)}, bf16[256,2048]{1,0:T(8,128)(2,1)}, u32[]{:S(2)}, u32[]{:S(2)}) collective-permute-start(bf16[256,2048]{1,0:T(8,128)(2,1)} %get-tuple-element.196.refs_5_), channel_id=1, source_target_pairs={{0,4},{4,0},{8,12},{12,8},{16,20},{20,16},{24,28},{28,24},{1,5},{5... | collective-permute-start | bytes 3145736 | tf_op jit(solution)/shard_map/ppermute | solution.py:61
  297.2 5.1 %collective-permute-done.18.refs_4_ = bf16[176,512]{1,0:T(8,128)(2,1)S(1)} collective-permute-done((bf16[176,512]{1,0:T(8,128)(2,1)S(1)}, bf16[176,512]{1,0:T(8,128)(2,1)S(1)}, u32[]{:S(2)}, u32[]{:S(2)}) %collective-permute-start.18) | collective-permute-done | bytes 180256 | tf_op jit(solution)/shard_map/ppermute | solution.py:61
  307.6 8.0 %all_to_all.15.refs_1_.refs_2_ = bf16[2,512,1536]{2,1,0:T(8,128)(2,1)S(1)} all-to-all(bf16[2,512,1536]{2,1,0:T(8,128)(2,1)} %get-tuple-element.205), channel_id=1, replica_groups=mesh['blk'=8,'dp'=2,'head'=2] {'dp'}, dimensions={0} | all-to-all | bytes 6291456 | tf_op jit(solution)/shard_map/all_to_all | solution.py:56
  317.6 10.9 %collective-permute-start.19 = (bf16[256,1536]{1,0:T(8,128)(2,1)}, bf16[256,1536]{1,0:T(8,128)(2,1)}, u32[]{:S(2)}, u32[]{:S(2)}) collective-permute-start(bf16[256,1536]{1,0:T(8,128)(2,1)} %get-tuple-element.207.refs_3_), channel_id=1, source_target_pairs={{0,8},{4,12},{8,0},{12,4},{16,24},{20,28},{24,16},{28,20},{1,9},{5... | collective-permute-start | bytes 2359304 | tf_op jit(solution)/shard_map/ppermute | solution.py:61
  342.0 9.7 %collective-permute-start.21 = (bf16[128,2048]{1,0:T(8,128)(2,1)}, bf16[128,2048]{1,0:T(8,128)(2,1)}, u32[]{:S(2)}, u32[]{:S(2)}) collective-permute-start(bf16[128,2048]{1,0:T(8,128)(2,1)} %get-tuple-element.208.refs_9_), channel_id=1, source_target_pairs={{0,8},{4,12},{8,0},{12,4},{16,24},{20,28},{24,16},{28,20},{1,9},{5... | collective-permute-start | bytes 1572872 | tf_op jit(solution)/shard_map/ppermute | solution.py:61
  (458 shorter events, 201.7 us)
Async XLA Ops:
  7.2 374.5 %reduce-scatter.4.cloned.1.call-start = ((), (), s32[]{:S(2)}) async-start(), calls=%async_computation.4 | async-start | bytes 8912896 | tf_op jit(solution)/shard_map/reduce_scatter | solution.py:1206
  10.5 48.9 %collective-permute-start.4 = (bf16[4,512,512]{2,1,0:T(8,128)(2,1)}, bf16[4,512,512]{2,1,0:T(8,128)(2,1)}, u32[]{:S(2)}, u32[]{:S(2)}) collective-permute-start(bf16[4,512,512]{2,1,0:T(8,128)(2,1)} %pad_maximum_fusion.refs_5_), channel_id=1, source_target_pairs={{0,1},{1,0},{2,3},{3,2},{4,5},{5,4},{6,7},{7,6},{8,9},{9,8},{10,11... | collective-permute-start | bytes 6291464 | tf_op jit(solution)/shard_map/ppermute | solution.py:61
  19.3 15.8 %collective-permute-start = (bf16[176,1024]{1,0:T(8,128)(2,1)S(1)}, bf16[176,1024]{1,0:T(8,128)(2,1)}, u32[]{:S(2)}, u32[]{:S(2)}) collective-permute-start(bf16[176,1024]{1,0:T(8,128)(2,1)S(1)} %fusion.refs_3_.refs_1_.refs_4_), channel_id=1, source_target_pairs={{0,8},{4,12},{8,16},{12,20},{16,24},{20,28},{1,9},{5,13},{9,17},{1... | collective-permute-start | bytes 1081352 | tf_op jit(solution)/shard_map/ppermute | solution.py:52
  23.6 28.6 %collective-permute-start.3 = (bf16[176,1024]{1,0:T(8,128)(2,1)S(1)}, bf16[176,1024]{1,0:T(8,128)(2,1)}, u32[]{:S(2)}, u32[]{:S(2)}) collective-permute-start(bf16[176,1024]{1,0:T(8,128)(2,1)S(1)} %fusion.refs_3_.refs_1_.refs_4_), channel_id=1, source_target_pairs={{0,12},{4,16},{8,20},{12,24},{16,28},{1,13},{5,17},{9,21},{13,25},... | collective-permute-start | bytes 1081352 | tf_op jit(solution)/shard_map/ppermute | solution.py:52
  29.1 25.3 %collective-permute-start.1 = (bf16[512,1024]{1,0:T(8,128)(2,1)}, bf16[512,1024]{1,0:T(8,128)(2,1)}, u32[]{:S(2)}, u32[]{:S(2)}) collective-permute-start(bf16[512,1024]{1,0:T(8,128)(2,1)} %dynamic-slice_bitcast_fusion), channel_id=1, source_target_pairs={{0,4},{4,8},{8,12},{12,16},{16,20},{20,24},{24,28},{1,5},{5,9},{9,... | collective-permute-start | bytes 3145736 | tf_op jit(solution)/shard_map/ppermute | solution.py:52
  63.7 16.2 %collective-permute-start.6 = (bf16[4,512,512]{2,1,0:T(8,128)(2,1)}, bf16[4,512,512]{2,1,0:T(8,128)(2,1)}, u32[]{:S(2)}, u32[]{:S(2)}) collective-permute-start(bf16[4,512,512]{2,1,0:T(8,128)(2,1)} %get-tuple-element.132), channel_id=1, source_target_pairs={{0,2},{2,0},{1,3},{3,1},{4,6},{6,4},{5,7},{7,5},{8,10},{10,8},{9,1... | collective-permute-start | bytes 6291464 | tf_op jit(solution)/shard_map/ppermute | solution.py:61
  100.9 24.4 %collective-permute-start.7 = (bf16[512,1024]{1,0:T(8,128)(2,1)S(1)}, bf16[512,1024]{1,0:T(8,128)(2,1)S(1)}, u32[]{:S(2)}, u32[]{:S(2)}) collective-permute-start(bf16[512,1024]{1,0:T(8,128)(2,1)S(1)} %get-tuple-element.139.refs_6_.refs_1_), channel_id=1, source_target_pairs={{0,1},{1,0},{2,3},{3,2},{4,5},{5,4},{6,7},{7,6},{8,9},{9,8},{10,11... | collective-permute-start | bytes 3145736 | tf_op jit(solution)/shard_map/ppermute | solution.py:61
  146.4 24.0 %collective-permute-start.8 = (bf16[512,1024]{1,0:T(8,128)(2,1)}, bf16[512,1024]{1,0:T(8,128)(2,1)S(1)}, u32[]{:S(2)}, u32[]{:S(2)}) collective-permute-start(bf16[512,1024]{1,0:T(8,128)(2,1)} %copy-done.99), channel_id=1, source_target_pairs={{0,1},{1,0},{2,3},{3,2},{4,5},{5,4},{6,7},{7,6},{8,9},{9,8},{10,11... | collective-permute-start | bytes 3145736 | tf_op jit(solution)/shard_map/ppermute | solution.py:61
  174.3 42.1 %collective-permute-start.9 = (bf16[512,1024]{1,0:T(8,128)(2,1)}, bf16[512,1024]{1,0:T(8,128)(2,1)}, u32[]{:S(2)}, u32[]{:S(2)}) collective-permute-start(bf16[512,1024]{1,0:T(8,128)(2,1)} %get-tuple-element.179), channel_id=1, source_target_pairs={{0,1},{1,0},{2,3},{3,2},{4,5},{5,4},{6,7},{7,6},{8,9},{9,8},{10,11... | collective-permute-start | bytes 3145736 | tf_op jit(solution)/shard_map/ppermute | solution.py:61
  198.5 21.5 %all-to-all-start = ((bf16[2,512,2048]{2,1,0:T(8,128)(2,1)}), bf16[2,512,2048]{2,1,0:T(8,128)(2,1)}, u32[]{:S(2)}, u32[]{:S(2)}) async-start(bf16[2,512,2048]{2,1,0:T(8,128)(2,1)} %get-tuple-element.177), calls=%async_computation | async-start | bytes 8388608 | tf_op jit(solution)/shard_map/all_to_all | solution.py:56
  224.8 48.3 %collective-permute-start.13 = (bf16[512,2048]{1,0:T(8,128)(2,1)}, bf16[512,2048]{1,0:T(8,128)(2,1)}, u32[]{:S(2)}, u32[]{:S(2)}) collective-permute-start(bf16[512,2048]{1,0:T(8,128)(2,1)} %cross_sum.1.refs_8_), channel_id=1, source_target_pairs={{0,1},{1,0},{2,3},{3,2},{4,5},{5,4},{6,7},{7,6},{8,9},{9,8},{10,11... | collective-permute-start | bytes 6291464 | tf_op jit(solution)/shard_map/ppermute | solution.py:61
  233.8 58.0 %collective-permute-start.10 = (bf16[176,1024]{1,0:T(8,128)(2,1)}, bf16[176,1024]{1,0:T(8,128)(2,1)}, u32[]{:S(2)}, u32[]{:S(2)}) collective-permute-start(bf16[176,1024]{1,0:T(8,128)(2,1)} %get-tuple-element.191), channel_id=1, source_target_pairs={{16,0},{20,4},{24,8},{28,12},{17,1},{21,5},{25,9},{29,13},{18,2},{... | collective-permute-start | bytes 1081352 | tf_op jit(solution)/shard_map/ppermute | solution.py:52
  235.1 56.7 %collective-permute-start.11 = (bf16[176,1024]{1,0:T(8,128)(2,1)}, bf16[176,1024]{1,0:T(8,128)(2,1)}, u32[]{:S(2)}, u32[]{:S(2)}) collective-permute-start(bf16[176,1024]{1,0:T(8,128)(2,1)} %get-tuple-element.192), channel_id=1, source_target_pairs={{12,0},{16,4},{20,8},{24,12},{28,16},{13,1},{17,5},{21,9},{25,13},... | collective-permute-start | bytes 1081352 | tf_op jit(solution)/shard_map/ppermute | solution.py:52
  236.4 55.4 %collective-permute-start.12 = (bf16[176,1024]{1,0:T(8,128)(2,1)}, bf16[176,1024]{1,0:T(8,128)(2,1)}, u32[]{:S(2)}, u32[]{:S(2)}) collective-permute-start(bf16[176,1024]{1,0:T(8,128)(2,1)} %get-tuple-element.193), channel_id=1, source_target_pairs={{8,0},{12,4},{16,8},{20,12},{24,16},{28,20},{9,1},{13,5},{17,9},{2... | collective-permute-start | bytes 1081352 | tf_op jit(solution)/shard_map/ppermute | solution.py:52
  252.4 20.1 %all-to-all-start.1 = ((bf16[2,512,2048]{2,1,0:T(8,128)(2,1)}), bf16[2,512,2048]{2,1,0:T(8,128)(2,1)}, u32[]{:S(2)}, u32[]{:S(2)}) async-start(bf16[2,512,2048]{2,1,0:T(8,128)(2,1)} %get-tuple-element.194), calls=%async_computation.1 | async-start | bytes 8388608 | tf_op jit(solution)/shard_map/all_to_all | solution.py:56
  279.0 58.8 %collective-permute-start.17 = (bf16[256,2048]{1,0:T(8,128)(2,1)}, bf16[256,2048]{1,0:T(8,128)(2,1)}, u32[]{:S(2)}, u32[]{:S(2)}) collective-permute-start(bf16[256,2048]{1,0:T(8,128)(2,1)} %get-tuple-element.196.refs_5_), channel_id=1, source_target_pairs={{0,4},{4,0},{8,12},{12,8},{16,20},{20,16},{24,28},{28,24},{1,5},{5... | collective-permute-start | bytes 3145736 | tf_op jit(solution)/shard_map/ppermute | solution.py:61
  294.4 57.3 %collective-permute-start.16 = (bf16[512,1024]{1,0:T(8,128)(2,1)}, bf16[512,1024]{1,0:T(8,128)(2,1)}, u32[]{:S(2)}, u32[]{:S(2)}) collective-permute-start(bf16[512,1024]{1,0:T(8,128)(2,1)} %get-tuple-element.199), channel_id=1, source_target_pairs={{4,0},{8,4},{12,8},{16,12},{20,16},{24,20},{28,24},{5,1},{9,5},{13... | collective-permute-start | bytes 3145736 | tf_op jit(solution)/shard_map/ppermute | solution.py:52
  317.6 42.6 %collective-permute-start.19 = (bf16[256,1536]{1,0:T(8,128)(2,1)}, bf16[256,1536]{1,0:T(8,128)(2,1)}, u32[]{:S(2)}, u32[]{:S(2)}) collective-permute-start(bf16[256,1536]{1,0:T(8,128)(2,1)} %get-tuple-element.207.refs_3_), channel_id=1, source_target_pairs={{0,8},{4,12},{8,0},{12,4},{16,24},{20,28},{24,16},{28,20},{1,9},{5... | collective-permute-start | bytes 2359304 | tf_op jit(solution)/shard_map/ppermute | solution.py:61
  329.6 22.0 %collective-permute-start.15 = (f32[4,512]{1,0:T(4,128)S(1)}, f32[4,512]{1,0:T(4,128)S(1)}, u32[]{:S(2)}, u32[]{:S(2)}) collective-permute-start(f32[4,512]{1,0:T(4,128)S(1)} %bitcast.91), channel_id=1, source_target_pairs={{0,1},{1,0},{2,3},{3,2},{4,5},{5,4},{6,7},{7,6},{8,9},{9,8},{10,11... | collective-permute-start | bytes 24584 | tf_op jit(solution)/shard_map/ppermute | solution.py:61
  333.0 36.1 %collective-permute-start.14 = (bf16[512,1024]{1,0:T(8,128)(2,1)}, bf16[512,1024]{1,0:T(8,128)(2,1)}, u32[]{:S(2)}, u32[]{:S(2)}) collective-permute-start(bf16[512,1024]{1,0:T(8,128)(2,1)} %copy-done.36), channel_id=1, source_target_pairs={{0,1},{1,0},{2,3},{3,2},{4,5},{5,4},{6,7},{7,6},{8,9},{9,8},{10,11... | collective-permute-start | bytes 3145736 | tf_op jit(solution)/shard_map/ppermute | solution.py:61
  342.0 31.1 %collective-permute-start.21 = (bf16[128,2048]{1,0:T(8,128)(2,1)}, bf16[128,2048]{1,0:T(8,128)(2,1)}, u32[]{:S(2)}, u32[]{:S(2)}) collective-permute-start(bf16[128,2048]{1,0:T(8,128)(2,1)} %get-tuple-element.208.refs_9_), channel_id=1, source_target_pairs={{0,8},{4,12},{8,0},{12,4},{16,24},{20,28},{24,16},{28,20},{1,9},{5... | collective-permute-start | bytes 1572872 | tf_op jit(solution)/shard_map/ppermute | solution.py:61
  365.6 26.8 %collective-permute-start.20 = (bf16[512,1024]{1,0:T(8,128)(2,1)}, bf16[512,1024]{1,0:T(8,128)(2,1)}, u32[]{:S(2)}, u32[]{:S(2)}) collective-permute-start(bf16[512,1024]{1,0:T(8,128)(2,1)} %get-tuple-element.212), channel_id=1, source_target_pairs={{0,1},{1,0},{2,3},{3,2},{4,5},{5,4},{6,7},{7,6},{8,9},{9,8},{10,11... | collective-permute-start | bytes 3145736 | tf_op jit(solution)/shard_map/ppermute | solution.py:61
  374.3 21.3 %collective-permute-start.23 = (bf16[64,2048]{1,0:T(8,128)(2,1)S(1)}, bf16[64,2048]{1,0:T(8,128)(2,1)}, u32[]{:S(2)}, u32[]{:S(2)}) collective-permute-start(bf16[64,2048]{1,0:T(8,128)(2,1)S(1)} %get-tuple-element.221.refs_3_), channel_id=1, source_target_pairs={{0,16},{4,20},{8,24},{12,28},{16,0},{20,4},{24,8},{28,12},{1,17},{... | collective-permute-start | bytes 786440 | tf_op jit(solution)/shard_map/ppermute | solution.py:61
  377.0 31.4 %collective-permute-start.29 = (bf16[64,1536]{1,0:T(8,128)(2,1)S(1)}, bf16[64,1536]{1,0:T(8,128)(2,1)S(1)}, u32[]{:S(2)}, u32[]{:S(2)}) collective-permute-start(bf16[64,1536]{1,0:T(8,128)(2,1)S(1)} %get-tuple-element.223.refs_2_), channel_id=1, source_target_pairs={{0,16},{4,20},{8,24},{12,28},{16,0},{20,4},{24,8},{28,12},{1,17},{... | collective-permute-start | bytes 589832 | tf_op jit(solution)/shard_map/ppermute | solution.py:61
  (164 other events, 1343.7 us)
Sparse Core Ops, SparseCore 0:
  146.5 141.8 reduce-scatter.3

commit v5 on v4

--- a/solution.py
+++ b/solution.py
@@ -15,15 +15,15 @@
 BF = jnp.bfloat16
 F32 = jnp.float32
 TILE = 256
+GROUP = 2
+OWN, OTH = 0, 1
+BLK, DP, HEAD = "blk", "dp", "head"
 SHARE = 1 << 24
 TAIL = 1.0
 
 
-LIMITS = {"recon_both": 10.3, "mlp": 20.7, "mlp_grads": 27.7, "branches": 23.3, "turn": 17.4, "attention_grads": 26.4, "spread": 17.4, "pack_grads": 19.1, "finish": 21.1}
-
-
-def limit(name):
-    return int(LIMITS.get(name, 14.0) * (1 << 20))
+def mib(count):
+    return int(count * (1 << 20))
 
 
 def cost(us):
@@ -53,7 +53,7 @@
 
 
 def trade(x):
-    return lax.all_to_all(x, "dp", 0, 0)
+    return lax.all_to_all(x, DP, 0, 0)
 
 
 def swap(x, axis, step=1):
@@ -108,6 +108,23 @@
     return run
 
 
+def by_heads(kernel, count, width):
+    def body(*refs):
+        for index in range(count):
+            columns = slice(index * width, (index + 1) * width)
+            views = []
+            for ref in refs:
+                if len(ref.shape) == 3:
+                    views.append(ref.at[index : index + 1])
+                elif len(ref.shape) == 2 and ref.dtype == BF:
+                    views.append(ref.at[:, columns])
+                else:
+                    views.append(ref)
+            kernel(pl.program_id(0) * count + index, *views)
+
+    return body
+
+
 def still(shape, index_map):
     return pl.BlockSpec(shape, index_map, pipeline_mode=pl.Buffered(1))
 
@@ -163,9 +180,8 @@
             scratch_shapes=[pltpu.VMEM((model // 128, 3 * padded + 8, 128), F32)],
         ),
         out_shape=[jax.ShapeDtypeStruct((rows, model), BF), tri, tri],
-        compiler_params=pltpu.CompilerParams(vmem_limit_bytes=limit("front")),
+        compiler_params=pltpu.CompilerParams(vmem_limit_bytes=mib(14.0)),
         cost_estimate=cost(0.02),
-        name="front",
     )(me, tokens, tokens, gain.reshape(1, model), bias.reshape(1, model))
 
 
@@ -186,9 +202,8 @@
         in_specs=[tall, fixed, fixed],
         out_specs=[tall],
         out_shape=[jax.ShapeDtypeStruct((count, model), BF)],
-        compiler_params=pltpu.CompilerParams(vmem_limit_bytes=limit("norm_halo")),
+        compiler_params=pltpu.CompilerParams(vmem_limit_bytes=mib(14.0)),
         cost_estimate=cost(2),
-        name="norm_halo",
     )(rows, gain.reshape(1, model), bias.reshape(1, model))
 
 
@@ -208,9 +223,8 @@
         deps=deps,
         gates=gates,
         out_shape=[shape, shape],
-        compiler_params=pltpu.CompilerParams(vmem_limit_bytes=limit("project_distant")),
+        compiler_params=pltpu.CompilerParams(vmem_limit_bytes=mib(14.0)),
         cost_estimate=cost(2.1),
-        name="project_distant",
     )(halo, mem, w)
 
 
@@ -255,9 +269,8 @@
         ],
         out_shape=[jax.ShapeDtypeStruct((3 * rows, rows), F32)],
         scratch_shapes=[pltpu.VMEM((rows, 128), jnp.int32)],
-        compiler_params=pltpu.CompilerParams(vmem_limit_bytes=limit("far_log")),
+        compiler_params=pltpu.CompilerParams(vmem_limit_bytes=mib(14.0)),
         cost_estimate=cost(0.02),
-        name="far_log",
     )(place, docs, query)
 
 
@@ -278,14 +291,12 @@
         deps=deps,
         gates=gates,
         out_shape=[near, near, near, little, little],
-        compiler_params=pltpu.CompilerParams(vmem_limit_bytes=limit("project")),
+        compiler_params=pltpu.CompilerParams(vmem_limit_bytes=mib(14.0)),
         cost_estimate=cost(2.0),
-        name="project",
     )(normed, packed, w)
 
 
-def forward_kernel(slopes, q, kf, vf, ko, vo, far, out, lse, *, scaling):
-    head = pl.program_id(0)
+def forward_kernel(head, slopes, q, kf, vf, ko, vo, far, out, lse, *, scaling):
     c1 = scaling * LOG2E
     c2 = slopes[head] * LOG2E
     rows, reach = q.shape[0], kf.shape[0]
@@ -312,30 +323,28 @@
     reach = kf.shape[0]
     heads = slopes.shape[0]
     hd = width // heads
-    near = pl.BlockSpec((rows, hd), lambda h: (0, h))
-    wide = pl.BlockSpec((reach, hd), lambda h: (0, h))
-    return call(
-        functools.partial(forward_kernel, scaling=scaling),
-        deps=deps,
-        gates=gates,
-        grid=(heads,),
+    near = pl.BlockSpec((rows, GROUP * hd), lambda h: (0, h))
+    wide = pl.BlockSpec((reach, GROUP * hd), lambda h: (0, h))
+    return call(
+        by_heads(functools.partial(forward_kernel, scaling=scaling), GROUP, hd),
+        deps=deps,
+        gates=gates,
+        grid=(heads // GROUP,),
         in_specs=[
             pl.BlockSpec(memory_space=pltpu.SMEM), near, wide, wide, near, near,
             still((reach + rows, rows), lambda h: (0, 0)),
         ],
-        out_specs=[near, pl.BlockSpec((1, 1, rows), lambda h: (h, 0, 0))],
+        out_specs=[near, pl.BlockSpec((GROUP, 1, rows), lambda h: (h, 0, 0))],
         out_shape=[
             jax.ShapeDtypeStruct((rows, width), BF),
             jax.ShapeDtypeStruct((heads, 1, rows), F32),
         ],
-        compiler_params=pltpu.CompilerParams(vmem_limit_bytes=limit("attend_forward")),
+        compiler_params=pltpu.CompilerParams(vmem_limit_bytes=mib(14.0)),
         cost_estimate=cost(3.2),
-        name="attend_forward",
     )(slopes, q, kf, vf, ko, vo, far)
 
 
-def backward_kernel(slopes, q, do, lse, dot_row, far, k, v, *refs, scaling, own):
-    head = pl.program_id(0)
+def backward_kernel(head, slopes, q, do, lse, dot_row, far, k, v, *refs, scaling, own):
     c1 = scaling * LOG2E
     c2 = slopes[head] * LOG2E
     extras = refs[:-4]
@@ -394,35 +403,34 @@
     keys = k.shape[0]
     heads = slopes.shape[0]
     hd = width // heads
-    near = pl.BlockSpec((rows, hd), lambda h: (0, h))
-    wide = pl.BlockSpec((keys, hd), lambda h: (0, h))
-    lane = pl.BlockSpec((1, 1, rows), lambda h: (h, 0, 0))
+    near = pl.BlockSpec((rows, GROUP * hd), lambda h: (0, h))
+    wide = pl.BlockSpec((keys, GROUP * hd), lambda h: (0, h))
+    lane = pl.BlockSpec((GROUP, 1, rows), lambda h: (h, 0, 0))
     place = far.shape[0] // keys - 1 if own else 0
     return call(
-        functools.partial(backward_kernel, scaling=scaling, own=own),
-        deps=deps,
-        gates=gates,
-        grid=(heads,),
+        by_heads(functools.partial(backward_kernel, scaling=scaling, own=own), GROUP, hd),
+        deps=deps,
+        gates=gates,
+        grid=(heads // GROUP,),
         in_specs=[
             pl.BlockSpec(memory_space=pltpu.SMEM), near, near, lane, lane,
             still((keys, rows), lambda h: (place, 0)), wide, wide,
         ]
         + [near] * len(extras),
-        out_specs=[near, wide, wide, pl.BlockSpec((1, 8, rows), lambda h: (h, 0, 0))],
+        out_specs=[near, wide, wide, pl.BlockSpec((GROUP, 8, rows), lambda h: (h, 0, 0))],
         out_shape=[
             jax.ShapeDtypeStruct((rows, width), BF),
             jax.ShapeDtypeStruct((keys, width), BF),
             jax.ShapeDtypeStruct((keys, width), BF),
             jax.ShapeDtypeStruct((heads, 8, rows), F32),
         ],
-        compiler_params=pltpu.CompilerParams(vmem_limit_bytes=limit("far" if not own else "own")),
+        compiler_params=pltpu.CompilerParams(vmem_limit_bytes=mib(14.0)),
         cost_estimate=cost(TAIL * (5 if own else 9)),
         from_hbm=late,
-        name="attend_backward_own" if own else "attend_backward_far",
     )(slopes, q, do, lse, dot_row, far, k, v, *extras)
 
 
-def recon_kernel(q, ko, vo, kc, vc, cot, recon, dq, dk, dv, dkc, dvc, *, slots, scaling):
+def recon_kernel(head, q, ko, vo, kc, vc, cot, recon, dq, dk, dv, dkc, dvc, *, slots, scaling):
     rows, hd = q.shape
     c1 = scaling * LOG2E
     comp_rows = kc.shape[0]
@@ -466,23 +474,22 @@
     heads = cot.shape[0]
     hd = width // heads
     comp_rows = kc.shape[0]
-    near = pl.BlockSpec((rows, hd), lambda h: (0, h))
-    small = pl.BlockSpec((comp_rows, hd), lambda h: (0, h))
-    lane = pl.BlockSpec((1, 1, rows), lambda h: (h, 0, 0))
+    near = pl.BlockSpec((rows, GROUP * hd), lambda h: (0, h))
+    small = pl.BlockSpec((comp_rows, GROUP * hd), lambda h: (0, h))
+    lane = pl.BlockSpec((GROUP, 1, rows), lambda h: (h, 0, 0))
     big = jax.ShapeDtypeStruct((rows, width), BF)
     little = jax.ShapeDtypeStruct((comp_rows, width), BF)
     return call(
-        functools.partial(recon_kernel, slots=slots, scaling=scaling),
-        deps=deps,
-        gates=gates,
-        grid=(heads,),
+        by_heads(functools.partial(recon_kernel, slots=slots, scaling=scaling), GROUP, hd),
+        deps=deps,
+        gates=gates,
+        grid=(heads // GROUP,),
         in_specs=[near, near, near, small, small, lane],
         out_specs=[lane, near, near, near, small, small],
         out_shape=[jax.ShapeDtypeStruct((heads, 1, rows), F32), big, big, big, little, little],
-        compiler_params=pltpu.CompilerParams(vmem_limit_bytes=limit("recon_both")),
+        compiler_params=pltpu.CompilerParams(vmem_limit_bytes=mib(10.3)),
         cost_estimate=cost(4.3),
         to_hbm=True,
-        name="recon_both",
     )(q, ko, vo, kc, vc, cot)
 
 
@@ -512,9 +519,8 @@
             out_specs=[tall, tall],
         ),
         out_shape=[jax.ShapeDtypeStruct((rows, model), F32), jax.ShapeDtypeStruct((rows, model), BF)],
-        compiler_params=pltpu.CompilerParams(vmem_limit_bytes=limit("middle_norm")),
+        compiler_params=pltpu.CompilerParams(vmem_limit_bytes=mib(14.0)),
         cost_estimate=cost(1.1),
-        name="middle_norm",
     )(me, tokens, a_one, a_two, w_one, w_two, gain.reshape(1, model), bias.reshape(1, model))
 
 
@@ -567,9 +573,8 @@
         ),
         out_shape=[jax.ShapeDtypeStruct((rows, units), BF)] * 2
         + [jax.ShapeDtypeStruct((rows, model), dtype)],
-        compiler_params=pltpu.CompilerParams(vmem_limit_bytes=limit("mlp")),
+        compiler_params=pltpu.CompilerParams(vmem_limit_bytes=mib(20.7)),
         cost_estimate=cost(6.4),
-        name="mlp",
     )(which, normed, cot, w_up, w_down)
 
 
@@ -606,10 +611,9 @@
         out_specs=[tall, tall],
         out_shape=[jax.ShapeDtypeStruct((rows, model), BF)] * 2,
         scratch_shapes=[pltpu.VMEM((rows, model), F32)] * 2,
-        compiler_params=pltpu.CompilerParams(vmem_limit_bytes=limit("branches")),
+        compiler_params=pltpu.CompilerParams(vmem_limit_bytes=mib(23.3)),
         cost_estimate=cost(TAIL * 6),
         from_hbm=True,
-        name="branches",
     )(own, oth, w_down)
 
 
@@ -665,9 +669,8 @@
             jax.ShapeDtypeStruct((heads, 1, rows), F32),
             jax.ShapeDtypeStruct((8, model), F32),
         ],
-        compiler_params=pltpu.CompilerParams(vmem_limit_bytes=limit("turn")),
+        compiler_params=pltpu.CompilerParams(vmem_limit_bytes=mib(17.4)),
         cost_estimate=cost(TAIL * 5),
-        name="turn",
     )(me, dn_own, dn_got, middle, cot, a_one, a_two, w_one, w_two, gain.reshape(1, model))
 
 
@@ -708,9 +711,8 @@
         out_specs=[fixed(rows, model)] + [fixed(padded, model)] * 3,
         out_shape=[jax.ShapeDtypeStruct((rows, model), BF), little, little, little],
         scratch_shapes=[pltpu.VMEM((rows + 16, model), F32)],
-        compiler_params=pltpu.CompilerParams(vmem_limit_bytes=limit("spread")),
+        compiler_params=pltpu.CompilerParams(vmem_limit_bytes=mib(17.4)),
         cost_estimate=cost(TAIL * 6),
-        name="spread",
     )(ka, va, kb, vb, wa, wa, wb, wb)
 
 
@@ -767,10 +769,9 @@
             jax.ShapeDtypeStruct((padded, model), BF),
         ],
         scratch_shapes=[pltpu.VMEM((rows, model), F32), pltpu.VMEM((padded, model), F32)],
-        compiler_params=pltpu.CompilerParams(vmem_limit_bytes=limit("base_rows")),
+        compiler_params=pltpu.CompilerParams(vmem_limit_bytes=mib(14.0)),
         cost_estimate=cost(TAIL * 3),
         from_hbm=True,
-        name="base_rows",
     )(*near, *slot, w, *before)
 
 
@@ -797,9 +798,8 @@
         in_specs=[pl.BlockSpec(memory_space=pltpu.SMEM), whole] + [whole] * len(gots),
         out_shape=[jax.ShapeDtypeStruct((padded, model), BF), little, little,
                    jax.ShapeDtypeStruct((8, model), F32)],
-        compiler_params=pltpu.CompilerParams(vmem_limit_bytes=limit("packed_back")),
+        compiler_params=pltpu.CompilerParams(vmem_limit_bytes=mib(14.0)),
         cost_estimate=cost(TAIL * 400),
-        name="packed_back",
     )(me, base, *gots)
 
 
@@ -854,9 +854,8 @@
             jax.ShapeDtypeStruct((rows, model), BF),
             jax.ShapeDtypeStruct((8, model), F32),
         ],
-        compiler_params=pltpu.CompilerParams(vmem_limit_bytes=limit("finish")),
+        compiler_params=pltpu.CompilerParams(vmem_limit_bytes=mib(21.1)),
         cost_estimate=cost(TAIL * 4),
-        name="finish",
     )(me, base, back, dpacked, w_comp, tokens, dmiddle, gain.reshape(1, model))
 
 
@@ -888,7 +887,7 @@
             parts[side, index * share : (index + 1) * share, :] = held[here : here + share, :]
 
 
-def weight_grads(scalars, sections, share, model, name, tall=512, deps=(), gates=()):
+def weight_grads(scalars, sections, share, model, limit, tall=512, deps=(), gates=()):
     operands, specs, plan, total = [], [], [], 0
     known = {}
 
@@ -946,10 +945,9 @@
             scratch_shapes=[pltpu.VMEM((tall, total), BF)] if share else [],
         ),
         out_shape=shape,
-        compiler_params=pltpu.CompilerParams(vmem_limit_bytes=limit(name)),
+        compiler_params=pltpu.CompilerParams(vmem_limit_bytes=mib(limit)),
         cost_estimate=cost(TAIL * flops * 1.4e-9),
         to_hbm=True,
-        name=name,
     )(scalars, *operands)
 
 
@@ -961,7 +959,7 @@
         out[...] = total[:, index * wide : (index + 1) * wide].astype(out.dtype)
 
 
-def add(terms, split, name, deps=(), gates=()):
+def add(terms, split, deps=(), gates=()):
     rows, columns = terms[0].shape[-2:]
     wide = columns // split
     tile = TILE if rows % TILE == 0 else rows
@@ -982,10 +980,9 @@
         in_specs=blocks,
         out_specs=[pl.BlockSpec((tile, wide), lambda i: (i, 0))] * split,
         out_shape=[jax.ShapeDtypeStruct((rows, wide), BF)] * split,
-        compiler_params=pltpu.CompilerParams(vmem_limit_bytes=limit(name)),
+        compiler_params=pltpu.CompilerParams(vmem_limit_bytes=mib(14)),
         cost_estimate=cost(TAIL * 2),
         from_hbm=True,
-        name=name,
     )(*operands)
 
 
@@ -1026,9 +1023,8 @@
             out_specs=[still(shape.shape, lambda i, m: (0, 0))] * (1 if last else 2),
         ),
         out_shape=[shape] * (1 if last else 2),
-        compiler_params=pltpu.CompilerParams(vmem_limit_bytes=limit("halve")),
+        compiler_params=pltpu.CompilerParams(vmem_limit_bytes=mib(14.0)),
         cost_estimate=cost(TAIL * 3),
-        name="halve",
     )(bit, *[part[0] for part in parts])
 
 
@@ -1036,7 +1032,7 @@
     def __init__(self, parts, columns, order, position):
         self.parts, self.columns, self.order = parts, columns, list(order)
         self.position = position
-        self.blocks = lax.axis_size("blk")
+        self.blocks = lax.axis_size(BLK)
         self.left = list(range(self.blocks.bit_length() - 2, -1, -1))
 
     def step(self, *deps, gates=()):
@@ -1046,7 +1042,7 @@
         keep, away, *rest = halve(
             mine, self.parts, self.blocks, 1 << place, self.columns, deps, gates
         )
-        self.parts = [(keep, 0), (swap(away, "blk", 1 << bit), 0)]
+        self.parts = [(keep, 0), (swap(away, BLK, 1 << bit), 0)]
         self.left.remove(bit)
         self.blocks //= 2
         return (away, *rest) if rest else away
@@ -1066,8 +1062,8 @@
 
 
 def butterfly_steps():
-    blocks = lax.axis_size("blk")
-    return [("dp", 1)] + [("blk", 1 << i) for i in range(blocks.bit_length() - 1)] + [("head", 1)]
+    blocks = lax.axis_size(BLK)
+    return [(DP, 1)] + [(BLK, 1 << i) for i in range(blocks.bit_length() - 1)] + [(HEAD, 1)]
 
 
 def butterfly_add(x, got, deps=()):
@@ -1078,7 +1074,6 @@
         in_specs=[whole, whole],
         out_shape=[jax.ShapeDtypeStruct(x.shape, F32)],
         cost_estimate=cost(TAIL),
-        name="small_sum",
     )(x, got)[0]
 
 
@@ -1104,14 +1099,14 @@
     used = 3 * slots
     padded = -(-slots // 16) * 16
     memory = CSEGS * slots
-    position = lax.axis_index("blk")
-    core = lax.axis_index("dp")
-    me = lax.axis_index("head")
+    position = lax.axis_index(BLK)
+    core = lax.axis_index(DP)
+    me = lax.axis_index(HEAD)
     ot = 1 - me
     scaling = hd ** (-0.5)
     half = model // 2
-    share = model // (lax.axis_size("blk") * lax.axis_size("dp"))
-    bits = lax.axis_size("blk").bit_length() - 1
+    share = model // (lax.axis_size(BLK) * lax.axis_size(DP))
+    bits = lax.axis_size(BLK).bit_length() - 1
     rising = list(range(bits))
     falling = [1, 0] + rising[2:]
     scalars = jnp.stack([core, me]).astype(jnp.int32)
@@ -1120,21 +1115,21 @@
     small = jnp.concatenate(
         [pick(recon_cot, ot), jnp.pad(slopes, (0, rows - heads)).reshape(1, rows)], 0
     )
-    small_got = swap(small, "head")
+    small_got = swap(small, HEAD)
     half_rows = model // 2
     qkv_part = lax.dynamic_slice_in_dim(w_qkv, core * half_rows, half_rows, 1)
     out_part = lax.dynamic_slice_in_dim(w_out, core * half_rows, half_rows, 1)
     far_part = jnp.concatenate([qkv_part, out_part[None]], 0)
-    far_got = swap(far_part, "head")
-    groups = ("own", "oth")
-
-    halo_raw = shift(pick(tokens, me), "blk", 1)
+    far_got = swap(far_part, HEAD)
+    groups = (OWN, OTH)
+
+    halo_raw = shift(pick(tokens, me), BLK, 1)
     normed, tri_own, tri_oth = front(
         me_arg, tokens, norm1_gain, norm1_bias, slots, padded, deps=(far_part, small)
     )
     packed = dot(tri_own, w_comp.reshape(3 * model, model)) + comp_bias
     packed = packed.astype(BF)
-    lag2, lag3 = shift(packed, "blk", 2), shift(packed, "blk", 3)
+    lag2, lag3 = shift(packed, BLK, 2), shift(packed, BLK, 3)
 
     docs = pick(doc_ids, me)
     query_doc = lax.dynamic_slice_in_dim(docs, position * rows, rows, 0).reshape(1, rows)
@@ -1145,54 +1140,54 @@
         position.reshape(1).astype(jnp.int32), window, query_doc, slots, deps=(packed,)
     )
 
-    weights, outs = {"own": w_qkv}, {"own": w_out}
-    cots = {"own": pick(recon_cot, me).reshape(heads, 1, rows)}
-    slope = {"own": slopes}
+    weights, outs = {OWN: w_qkv}, {OWN: w_out}
+    cots = {OWN: pick(recon_cot, me).reshape(heads, 1, rows)}
+    slope = {OWN: slopes}
     q, ko, vo, kc, vc, rec, kf, vf, att, lse = ({} for _ in range(10))
-    q["own"], ko["own"], vo["own"], kc["own"], vc["own"], lag2 = project(
+    q[OWN], ko[OWN], vo[OWN], kc[OWN], vc[OWN], lag2 = project(
         normed, packed, w_qkv, deps=(far,), gates=(lag2,)
     )
-    lag4 = shift(lag2, "blk", 2)
-    cots["oth"] = small_got[:heads].reshape(heads, 1, rows)
-    slope["oth"] = small_got[heads, :heads]
-    rec["own"] = recon_both(
-        q["own"], ko["own"], vo["own"], kc["own"], vc["own"], cots["own"], slots, scaling,
+    lag4 = shift(lag2, BLK, 2)
+    cots[OTH] = small_got[:heads].reshape(heads, 1, rows)
+    slope[OTH] = small_got[heads, :heads]
+    rec[OWN] = recon_both(
+        q[OWN], ko[OWN], vo[OWN], kc[OWN], vc[OWN], cots[OWN], slots, scaling,
     )
     mem = jnp.zeros((rows, model), BF)
     for index, lag in enumerate((lag4, lag3, lag2)):
         place = (index * slots, rows - (index + 1) * slots)
         mem = mem + jnp.pad(lag[:slots], (place, (0, 0)))
-    halo = norm_halo(halo_raw, norm1_gain, norm1_bias, deps=(rec["own"][0],))[0]
-    kf["own"], vf["own"], far_got = project_distant(halo, mem, w_qkv, gates=(far_got,))
-    near_got = swap(far_got, "dp")
-    att["own"], lse["own"] = attend_forward(
-        slope["own"], q["own"], kf["own"], vf["own"], ko["own"], vo["own"], far, scaling
-    )
-    weights["oth"] = in_order(core, far_got[:3], near_got[:3], 1)
-    outs["oth"] = in_order(core, far_got[3], near_got[3], 1)
-    q["oth"], ko["oth"], vo["oth"], kc["oth"], vc["oth"] = project(
-        normed, packed, weights["oth"], deps=(att["own"],)
-    )
-    kf["oth"], vf["oth"] = project_distant(halo, mem, weights["oth"], deps=(q["oth"],))
-    att["oth"], lse["oth"] = attend_forward(
-        slope["oth"], q["oth"], kf["oth"], vf["oth"], ko["oth"], vo["oth"], far, scaling
+    halo = norm_halo(halo_raw, norm1_gain, norm1_bias, deps=(rec[OWN][0],))[0]
+    kf[OWN], vf[OWN], far_got = project_distant(halo, mem, w_qkv, gates=(far_got,))
+    near_got = swap(far_got, DP)
+    att[OWN], lse[OWN] = attend_forward(
+        slope[OWN], q[OWN], kf[OWN], vf[OWN], ko[OWN], vo[OWN], far, scaling
+    )
+    weights[OTH] = in_order(core, far_got[:3], near_got[:3], 1)
+    outs[OTH] = in_order(core, far_got[3], near_got[3], 1)
+    q[OTH], ko[OTH], vo[OTH], kc[OTH], vc[OTH] = project(
+        normed, packed, weights[OTH], deps=(att[OWN],)
+    )
+    kf[OTH], vf[OTH] = project_distant(halo, mem, weights[OTH], deps=(q[OTH],))
+    att[OTH], lse[OTH] = attend_forward(
+        slope[OTH], q[OTH], kf[OTH], vf[OTH], ko[OTH], vo[OTH], far, scaling
     )
 
     middle, n2_own = middle_norm(
-        me_arg, tokens, att["own"], att["oth"], w_out, outs["oth"], norm2_gain, norm2_bias
-    )
-    n2_oth = swap(n2_own, "head")
-    rec["oth"] = recon_both(
-        q["oth"], ko["oth"], vo["oth"], kc["oth"], vc["oth"], cots["oth"], slots, scaling,
+        me_arg, tokens, att[OWN], att[OTH], w_out, outs[OTH], norm2_gain, norm2_bias
+    )
+    n2_oth = swap(n2_own, HEAD)
+    rec[OTH] = recon_both(
+        q[OTH], ko[OTH], vo[OTH], kc[OTH], vc[OTH], cots[OTH], slots, scaling,
         deps=(n2_own,),
     )
     hid_own, din_own, dn_own = mlp(
-        me_arg, n2_own, out_cot, w_up, w_down, BF, deps=(rec["oth"][0],)
+        me_arg, n2_own, out_cot, w_up, w_down, BF, deps=(rec[OTH][0],)
     )
     hid_oth, din_oth, dn_oth = mlp(
         ot_arg, n2_oth, out_cot, w_up, w_down, BF, deps=(dn_own,)
     )
-    dn_got = swap(dn_oth, "head")
+    dn_got = swap(dn_oth, HEAD)
     units = w_up.shape[1]
     up_down, token = weight_grads(
         scalars,
@@ -1200,34 +1195,34 @@
             [(n2_own, 0, din_own, (0, 0), units), (n2_oth, 0, din_oth, (0, 0), units)],
             [(out_cot, 0, hid_own, (0, 0), units), (out_cot, 1, hid_oth, (0, 0), units)],
         ],
-        0, model, "mlp_grads", deps=(dn_oth,),
+        0, model, 27.7, deps=(dn_oth,),
     )
     ffn_own, ffn_oth = branches(hid_own, hid_oth, w_down, deps=(token,))
-    up_down = lax.psum_scatter(up_down, ("blk", "dp"), scatter_dimension=0, tiled=True)
+    up_down = lax.psum_scatter(up_down, (BLK, DP), scatter_dimension=0, tiled=True)
     (
         dbranch, datt_own, datt_oth, row_own, row_oth, sums2,
         ffn_oth, recon_oth,
     ) = turn(
-        me_arg, dn_own, dn_got, middle, out_cot, att["own"], att["oth"], w_out, outs["oth"],
-        norm2_gain, heads, gates=(ffn_oth, rec["oth"][0]),
-    )
-    ffn_got = swap(ffn_oth, "head")
-    recon_got = swap(recon_oth.reshape(heads, rows), "head")
-    datt = {"own": datt_own, "oth": datt_oth}
-    row = {"own": row_own, "oth": row_oth}
+        me_arg, dn_own, dn_got, middle, out_cot, att[OWN], att[OTH], w_out, outs[OTH],
+        norm2_gain, heads, gates=(ffn_oth, rec[OTH][0]),
+    )
+    ffn_got = swap(ffn_oth, HEAD)
+    recon_got = swap(recon_oth.reshape(heads, rows), HEAD)
+    datt = {OWN: datt_own, OTH: datt_oth}
+    row = {OWN: row_own, OTH: row_oth}
     back, near, grads = {}, {}, {}
 
     def far_back(g, *deps):
         back[g] = attend_backward(
             slope[g], q[g], datt[g], lse[g], row[g], far, kf[g], vf[g], False, [], scaling,
-            deps=deps, late=g == "own",
+            deps=deps, late=g == OWN,
         )
 
     def near_back(g, *deps, gates=()):
         r = rec[g]
         near[g] = attend_backward(
             slope[g], q[g], datt[g], lse[g], row[g], far, ko[g], vo[g], True,
-            [back[g][0], r[1], r[2], r[3]], scaling, deps=deps, gates=gates, late=g == "own",
+            [back[g][0], r[1], r[2], r[3]], scaling, deps=deps, gates=gates, late=g == OWN,
         )
 
     def group_grads(g, *deps, gates=()):
@@ -1244,41 +1239,41 @@
             )
         sections.append([(dbranch, 0, att[g], (0, 0), width)])
         grads[g] = weight_grads(
-            scalars, sections, share, model, "attention_grads", deps=deps, gates=gates
+            scalars, sections, share, model, 26.4, deps=deps, gates=gates
         )
 
-    far_back("oth", dbranch)
-    near_back("oth")
-    group_grads("oth")
-    cross = trade(grads["oth"][0])
-    far_back("own", grads["oth"][1])
-    (lo_own,) = add((middle, ffn_own, ffn_got), 1, "layer_sum", deps=(back["own"][3],))
-    (cross,) = add((cross,), 1, "cross_sum", deps=(lo_own,))
-    cross_got = swap(cross, "head")
+    far_back(OTH, dbranch)
+    near_back(OTH)
+    group_grads(OTH)
+    cross = trade(grads[OTH][0])
+    far_back(OWN, grads[OTH][1])
+    (lo_own,) = add((middle, ffn_own, ffn_got), 1, deps=(back[OWN][3],))
+    (cross,) = add((cross,), 1, deps=(lo_own,))
+    cross_got = swap(cross, HEAD)
     halo_part, back4, back3, back2 = spread(
-        back["oth"][1], back["oth"][2], back["own"][1], back["own"][2], weights["oth"], w_qkv,
+        back[OTH][1], back[OTH][2], back[OWN][1], back[OWN][2], weights[OTH], w_qkv,
         slots, padded, deps=(cross,),
     )
     slot_gots = [
-        shift(part, "blk", -lag)
+        shift(part, BLK, -lag)
         for part, lag in zip((back4, back3, back2), range(CSEGS + 1, 1, -1))
     ]
-    near_back("own", halo_part)
-    group_grads("own")
-    own = trade(grads["own"][0])
+    near_back(OWN, halo_part)
+    group_grads(OWN)
+    own = trade(grads[OWN][0])
     base_oth = base_rows(
-        near["oth"][:3], rec["oth"][4:6], weights["oth"], [], deps=(grads["own"][1],)
-    )
-    base, slot_base = base_rows(near["own"][:3], rec["own"][4:6], w_qkv, base_oth)
+        near[OTH][:3], rec[OTH][4:6], weights[OTH], [], deps=(grads[OWN][1],)
+    )
+    base, slot_base = base_rows(near[OWN][:3], rec[OWN][4:6], w_qkv, base_oth)
     wide = 2 * width
     late = Halving([(own, 0, 0), (own, 0, 1), (cross_got, 0)], 2 * wide, rising, position)
     moved = late.step(base)
     dpacked, dp_mine, dp_away, bias_sum, halo_part, lo_own = packed_back(
         me_arg, slot_base, slot_gots, deps=(moved,), gates=(halo_part, lo_own)
     )
-    dp_got = swap(dp_away, "head")
-    halo_back = shift(halo_part, "blk", -1)
-    lo_got = swap(lo_own, "head")
+    dp_got = swap(dp_away, HEAD)
+    halo_back = shift(halo_part, BLK, -1)
+    lo_got = swap(lo_own, HEAD)
     send, token = weight_grads(
         scalars,
         [
@@ -1288,7 +1283,7 @@
             ]
             for tap in range(3)
         ],
-        share, model, "pack_grads",
+        share, model, 19.1,
     )
     comp = trade(send)
     comp = Halving([(comp, 0, 0), (comp, 0, 1)], 3 * half, falling, position)
@@ -1302,14 +1297,14 @@
     for g in groups:
         total = back[g][3] + near[g][3]
         dslopes[g] = -jnp.sum(total[:, 2] - total[:, 0] * total[:, 1], axis=1)
-    both = in_order(me, dslopes["own"], dslopes["oth"], 0)
+    both = in_order(me, dslopes[OWN], dslopes[OTH], 0)
     vector = jnp.concatenate(
         [sums1[0], sums1[1], sums2[0], sums2[1], bias_sum[0], jnp.pad(both, (0, 128 - 2 * heads))]
     ).reshape(-1, 128)
     rounds = butterfly_steps()
     vector_got = swap(vector, *rounds.pop(0))
     moved, grad_away = comp.step(sums1, gates=(grad_own,))
-    grad_got = swap(grad_away, "head")
+    grad_got = swap(grad_away, HEAD)
     vector = butterfly_add(vector, vector_got, deps=(moved,))
     vector_got = swap(vector, *rounds.pop(0))
     moved = vector
@@ -1335,14 +1330,14 @@
     comp = comp.last(vector, grad_tokens)
     vector = (vector + vector_got).reshape(-1)
     comp = comp.astype(BF)
-    comp_got = swap(comp, "head")
+    comp_got = swap(comp, HEAD)
     comp_all = in_order(
         me, comp.reshape(share, 3, half), comp_got.reshape(share, 3, half), 2
     ).astype(F32)
 
     slope_sum = lax.dynamic_slice_in_dim(vector, 5 * model + me * heads, heads, 0)
 
-    recon_own = rec["own"][0].reshape(heads, rows)
+    recon_own = rec[OWN][0].reshape(heads, rows)
     recon = in_order(me, recon_own[None], recon_got[None], 0)
     layer_out = in_order(me, lo_own[None], lo_got[None], 0)
     return (
@@ -1365,32 +1360,32 @@
 
 def solution(mesh):
     in_specs = (
-        P("dp", "blk", None),
-        P("dp", None),
-        P(None, None, "head"),
-        P("head", None),
-        P("head"),
-        P(None, "head"),
-        P("head", None),
+        P(DP, BLK, None),
+        P(DP, None),
+        P(None, None, HEAD),
+        P(HEAD, None),
+        P(HEAD),
+        P(None, HEAD),
+        P(HEAD, None),
         P(),
         P(),
         P(),
         P(),
         P(),
         P(),
-        P("dp", "blk", None),
-        P("dp", "head", "blk"),
+        P(DP, BLK, None),
+        P(DP, HEAD, BLK),
     )
     out_specs = (
-        P("dp", "blk", None),
-        P("dp", "head", "blk"),
-        P("dp", "blk", None),
-        P(None, ("blk", "dp"), "head"),
-        P("head", ("blk", "dp")),
-        P("head"),
-        P(("blk", "dp"), "head"),
-        P("head", ("blk", "dp")),
-        P(None, ("blk", "dp"), None),
+        P(DP, BLK, None),
+        P(DP, HEAD, BLK),
+        P(DP, BLK, None),
+        P(None, (BLK, DP), HEAD),
+        P(HEAD, (BLK, DP)),
+        P(HEAD),
+        P((BLK, DP), HEAD),
+        P(HEAD, (BLK, DP)),
+        P(None, (BLK, DP), None),
         P(),
         P(),
         P(),

time: 431 us -> 426 us (0.988)
  Pallas kernels: 195 us -> 188 us
    pallas_call x43, Pallas kernels: 195 us -> 188 us  [run(): return pl.pallas_call(body, **settings)(*operands, *deps, *gates)]
  transfers between devices with their start and end apart: 34 -> 34, of which waited for: 11 -> 11; matrix products, arithmetic and copies ran while one was open for 8% -> 8% of each run, Pallas kernels for 37% -> 36%
where the time goes in v5:
time: 426 us; the launch traced here: 419 us
  Pallas kernels  188 us (44%)
  starting transfers between devices  93.1 us (22%)
  local copies, waits for them, and re-layouts  59.3 us (14%)
  waiting for transfers between devices  34.6 us (8%)
  other arithmetic  17.8 us (4%)
  between operations  16.5 us (4%)
  blocking collectives  7.96 us (2%)
    pallas_call x43, Pallas kernels, run(): return pl.pallas_call(body, **settings)(*operands, *deps, *gates)  188 us
    ppermute x23, starting transfers between devices, swap(): return lax.ppermute(x, axis, [(i, i ^ step) for i in range(devices)])  61.9 us
    unnamed x318, local copies, waits for them, and re-layouts  42.5 us
    ppermute x23, waiting for transfers between devices, swap(): return lax.ppermute(x, axis, [(i, i ^ step) for i in range(devices)])  32.8 us
    ppermute x8, starting transfers between devices, shift(): return lax.ppermute(x, axis, pairs)  19.7 us
    all_to_all x2, starting transfers between devices, trade(): return lax.all_to_all(x, DP, 0, 0)  11.5 us
    select_n x6, other arithmetic, in_order(): jnp.where(mine == 0, jnp.concatenate([first, second], axis), jnp.concaten...  9.47 us
  transfers between devices with their start and end apart: 34, of which 11 were waited for; matrix products, arithmetic and copies ran while one was open for 8% of the time, Pallas kernels for 36%

profile of v5, /device:TPU:0, one launch (start us, length us, event | category | flops | bytes accessed | tf_op | source)
XLA Modules:
  0.0 418.8 jit_solution(11165198622490133175)
XLA Ops:
  40.3 11.0 %shard_map.257 = (f32[4,1,512]{2,1,0:T(1,128)}, bf16[512,512]{1,0:T(8,128)(2,1)}, bf16[512,512]{1,0:T(8,128)(2,1)}, bf16[512,512]{1,0:T(8,128)(2,1)}, bf16[176,5...) custom-call(bf16[512,512]{1,0:T(8,128)(2,1)S(1)} %get-tuple-element.122.refs_0_.refs_1_, ...), custom_call_target="tpu_custom_call" | custom-call | flops 72142032 | bytes 1024 | tf_op jit(solution)/shard_map/pallas_call | solution.py:106
  71.0 6.7 %shard_map.260 = (bf16[512,512]{1,0:T(8,128)(2,1)S(1)}, f32[4,1,512]{2,1,0:T(1,128)S(1)}) custom-call(f32[4]{0:T(128)S(1)} %copy-done.132, bf16[512,512]{1,0:T(8,128)(2,1)S(1)} %copy-done.56, bf16[1024,512]{1,0:T(8,128)(2,1)S(1)} %copy-done.81, bf16[1024,512]{1,0:T(8,128)(2,1)S(1)} %copy-done.83, bf16[512,512]{1,0:T(8,128)(2,1)S(1)} %copy-done.68, ...), custom_call_target="tpu_custom_call" | custom-call | flops 53687092 | bytes 1024 | tf_op jit(solution)/shard_map/pallas_call | solution.py:106
  88.8 6.7 %shard_map.263 = (bf16[512,512]{1,0:T(8,128)(2,1)S(1)}, f32[4,1,512]{2,1,0:T(1,128)S(1)}) custom-call(f32[4]{0:T(128)S(1)} %slice_bitcast_fusion.8.refs_0_, bf16[512,512]{1,0:T(8,128)(2,1)S(1)} %get-tuple-element.133.refs_3_.refs_1_.refs_0_, bf16[1024,512]{1,0:T(8,128)(2,1)S(1)} %get-tuple-element.134.refs_2_.refs_6_, ...), custom_call_target="tpu_custom_call" | custom-call | flops 53687092 | bytes 1024 | tf_op jit(solution)/shard_map/pallas_call | solution.py:106
  101.7 10.9 %shard_map.265 = (f32[4,1,512]{2,1,0:T(1,128)}, bf16[512,512]{1,0:T(8,128)(2,1)}, bf16[512,512]{1,0:T(8,128)(2,1)}, bf16[512,512]{1,0:T(8,128)(2,1)}, bf16[176,5...) custom-call(bf16[512,512]{1,0:T(8,128)(2,1)S(1)} %get-tuple-element.133.refs_3_.refs_1_.refs_0_, ...), custom_call_target="tpu_custom_call" | custom-call | flops 72142032 | bytes 1024 | tf_op jit(solution)/shard_map/pallas_call | solution.py:106
  113.3 9.2 %shard_map.266 = (bf16[512,2048]{1,0:T(8,128)(2,1)S(1)}, bf16[512,2048]{1,0:T(8,128)(2,1)S(1)}, bf16[512,1024]{1,0:T(8,128)(2,1)S(1)}) custom-call(s32[1]{0:T(128)} %bitcast.refs_0_, bf16[512,1024]{1,0:T(8,128)(2,1)S(1)} %get-tuple-element.139.refs_6_.refs_1_, bf16[2,512,1024]{2,1,0:T(8,128)(2,1)S(1)} %copy-done.5, bf16[1024,2048]{1,0:T(8,128)(2,1)S(1)} %copy-done.19, ...), custom_call_target="tpu_custom_call" | custom-call | flops 107374184 | bytes 1024 | tf_op jit(solution)/shard_map/pallas_call | solution.py:106
  123.5 8.8 %shard_map.267 = (bf16[512,2048]{1,0:T(8,128)(2,1)S(1)}, bf16[512,2048]{1,0:T(8,128)(2,1)S(1)}, bf16[512,1024]{1,0:T(8,128)(2,1)S(1)}) custom-call(s32[1]{0:T(128)} %bitcast.15.refs_0_, bf16[512,1024]{1,0:T(8,128)(2,1)S(1)} %collective-permute-done.7.refs_1_.refs_3_, bf16[2,512,1024]{2,1,0:T(8,128)(2,1)S(1)} %copy-done.5, bf16[1024,2048]{1,0:T(8,128)(2,1)S(1)} %copy-done.19, ...), custom_call_target="tpu_custom_call" | custom-call | flops 107374184 | bytes 1024 | tf_op jit(solution)/shard_map/pallas_call | solution.py:106
  132.3 12.2 %shard_map.268 = (bf16[1024,4096]{1,0:T(8,128)(2,1)}, f32[8,128]{1,0:T(8,128)}) custom-call(s32[2]{0:T(128)S(1)} %pad_add_fusion.1.refs_0_, bf16[512,1024]{1,0:T(8,128)(2,1)S(1)} %get-tuple-element.139.refs_6_.refs_1_, bf16[512,2048]{1,0:T(8,128)(2,1)S(1)} %get-tuple-element.148.refs_2_, bf16[512,1024]{1,0:T(8,128)(2,1)S(1)} %collective-permute-done.7.refs_1_.refs_3_, ...), custom_call_target="tpu_custom_call" | custom-call | flops 201761264 | bytes 1024 | tf_op jit(solution)/shard_map/pallas_call | solution.py:106
  146.4 10.1 %shard_map.269 = (bf16[512,1024]{1,0:T(8,128)(2,1)S(1)}, bf16[512,1024]{1,0:T(8,128)(2,1)}) custom-call(bf16[512,2048]{1,0:T(8,128)(2,1)} %copy-done.50, bf16[512,2048]{1,0:T(8,128)(2,1)} %copy-done.51, bf16[2048,1024]{1,0:T(8,128)(2,1)} %refs_2_.11, f32[8,128]{1,0:T(8,128)S(1)} %copy-done.135), custom_call_target="tpu_custom_call" | custom-call | flops 100663296 | bytes 1024 | tf_op jit(solution)/shard_map/pallas_call | solution.py:106
  157.5 10.9 %collective-permute-done.8.refs_2_ = bf16[512,1024]{1,0:T(8,128)(2,1)S(1)} collective-permute-done((bf16[512,1024]{1,0:T(8,128)(2,1)}, bf16[512,1024]{1,0:T(8,128)(2,1)S(1)}, u32[]{:S(2)}, u32[]{:S(2)}) %collective-permute-start.8) | collective-permute-done | bytes 1048608 | tf_op jit(solution)/shard_map/ppermute | solution.py:61
  174.0 7.7 %shard_map.271 = (bf16[512,512]{1,0:T(8,128)(2,1)S(1)}, bf16[1024,512]{1,0:T(8,128)(2,1)S(1)}, bf16[1024,512]{1,0:T(8,128)(2,1)S(1)}, f32[4,8,512]{2,1,0:T(8,128)S(1)}) custom-call(f32[4]{0:T(128)S(1)} %copy-done.134, bf16[512,512]{1,0:T(8,128)(2,1)S(1)} %copy-done.28, bf16[512,512]{1,0:T(8,128)(2,1)S(1)} %get-tuple-element.155.refs_2_, ...), custom_call_target="tpu_custom_call" | custom-call | flops 150994944 | bytes 1024 | tf_op jit(solution)/shard_map/pallas_call | solution.py:106
  187.3 7.6 %shard_map.273 = (bf16[2,512,2048]{2,1,0:T(8,128)(2,1)}, f32[8,128]{1,0:T(8,128)}) custom-call(s32[2]{0:T(128)S(1)} %pad_add_fusion.1.refs_0_, bf16[512,1024]{1,0:T(8,128)(2,1)S(1)} %copy-done.23, bf16[512,512]{1,0:T(8,128)(2,1)S(1)} %get-tuple-element.163.refs_2_.refs_0_, bf16[512,512]{1,0:T(8,128)(2,1)S(1)} %get-tuple-element.164.refs_3_.refs_1_, ...), custom_call_target="tpu_custom_call" | custom-call | flops 109550064 | bytes 1024 | tf_op jit(solution)/shard_map/pallas_call | solution.py:106
  194.9 5.8 %all-to-all-start = ((bf16[2,512,2048]{2,1,0:T(8,128)(2,1)}), bf16[2,512,2048]{2,1,0:T(8,128)(2,1)}, u32[]{:S(2)}, u32[]{:S(2)}) async-start(bf16[2,512,2048]{2,1,0:T(8,128)(2,1)} %get-tuple-element.177), calls=%async_computation | async-start | bytes 8388608 | tf_op jit(solution)/shard_map/all_to_all | solution.py:56
  200.7 9.4 %shard_map.274 = (bf16[512,512]{1,0:T(8,128)(2,1)S(1)}, bf16[1024,512]{1,0:T(8,128)(2,1)S(1)}, bf16[1024,512]{1,0:T(8,128)(2,1)S(1)}, f32[4,8,512]{2,1,0:T(8,128)S(1)}) custom-call(f32[4]{0:T(128)S(1)} %copy-done.132, bf16[512,512]{1,0:T(8,128)(2,1)} %copy-done.55, bf16[512,512]{1,0:T(8,128)(2,1)} %copy-done.93, f32[4,1,512]{2,1,0:T(1,128)} %copy-done.128, ...), custom_call_target="tpu_custom_call" | custom-call | flops 150994944 | bytes 1024 | tf_op jit(solution)/shard_map/pallas_call | solution.py:106
  223.0 6.5 %shard_map.277 = (bf16[512,1024]{1,0:T(8,128)(2,1)}, bf16[176,1024]{1,0:T(8,128)(2,1)}, bf16[176,1024]{1,0:T(8,128)(2,1)}, bf16[176,1024]{1,0:T(8,128)(2,1)}) custom-call(bf16[1024,512]{1,0:T(8,128)(2,1)S(1)} %copy-done.46, bf16[1024,512]{1,0:T(8,128)(2,1)S(1)} %copy-done.48, bf16[1024,512]{1,0:T(8,128)(2,1)S(1)} %copy-done.40, ...), custom_call_target="tpu_custom_call" | custom-call | flops 100663296 | bytes 1024 | tf_op jit(solution)/shard_map/pallas_call | solution.py:106
  233.4 5.8 %shard_map.278 = (bf16[512,512]{1,0:T(8,128)(2,1)S(1)}, bf16[512,512]{1,0:T(8,128)(2,1)S(1)}, bf16[512,512]{1,0:T(8,128)(2,1)S(1)}, f32[4,8,512]{2,1,0:T(8,128)S(1)}) custom-call(f32[4]{0:T(128)S(1)} %copy-done.132, bf16[512,512]{1,0:T(8,128)(2,1)} %copy-done.55, bf16[512,512]{1,0:T(8,128)(2,1)} %copy-done.93, f32[4,1,512]{2,1,0:T(1,128)} %copy-done.128, ...), custom_call_target="tpu_custom_call" | custom-call | flops 83886080 | bytes 1024 | tf_op jit(solution)/shard_map/pallas_call | solution.py:106
  239.9 7.6 %shard_map.279 = (bf16[2,512,2048]{2,1,0:T(8,128)(2,1)}, f32[8,128]{1,0:T(8,128)}) custom-call(s32[2]{0:T(128)S(1)} %pad_add_fusion.1.refs_0_, bf16[512,1024]{1,0:T(8,128)(2,1)S(1)} %copy-done.24, bf16[512,512]{1,0:T(8,128)(2,1)S(1)} %get-tuple-element.182.refs_2_.refs_0_, bf16[512,512]{1,0:T(8,128)(2,1)S(1)} %get-tuple-element.183.refs_3_.refs_1_, ...), custom_call_target="tpu_custom_call" | custom-call | flops 109550064 | bytes 1024 | tf_op jit(solution)/shard_map/pallas_call | solution.py:106
  247.5 5.7 %all-to-all-start.1 = ((bf16[2,512,2048]{2,1,0:T(8,128)(2,1)}), bf16[2,512,2048]{2,1,0:T(8,128)(2,1)}, u32[]{:S(2)}, u32[]{:S(2)}) async-start(bf16[2,512,2048]{2,1,0:T(8,128)(2,1)} %get-tuple-element.194), calls=%async_computation.1 | async-start | bytes 8388608 | tf_op jit(solution)/shard_map/all_to_all | solution.py:56
  253.3 5.3 %shard_map.280 = (bf16[512,1024]{1,0:T(8,128)(2,1)S(1)}, bf16[176,1024]{1,0:T(8,128)(2,1)S(1)}) custom-call(bf16[512,512]{1,0:T(8,128)(2,1)} %copy-done.90, bf16[512,512]{1,0:T(8,128)(2,1)} %copy-done.91, bf16[512,512]{1,0:T(8,128)(2,1)} %copy-done.92, bf16[176,512]{1,0:T(8,128)(2,1)} %get-tuple-element.165.refs_5_.refs_3_, ...), custom_call_target="tpu_custom_call" | custom-call | flops 50331648 | bytes 1024 | tf_op jit(solution)/shard_map/pallas_call | solution.py:106
  260.4 5.5 %shard_map.281 = (bf16[512,1024]{1,0:T(8,128)(2,1)S(1)}, bf16[176,1024]{1,0:T(8,128)(2,1)S(1)}) custom-call(bf16[512,512]{1,0:T(8,128)(2,1)} %copy-done.94, bf16[512,512]{1,0:T(8,128)(2,1)} %copy-done.95, bf16[512,512]{1,0:T(8,128)(2,1)} %copy-done.96, bf16[176,512]{1,0:T(8,128)(2,1)} %get-tuple-element.185.refs_5_.refs_3_, ...), custom_call_target="tpu_custom_call" | custom-call | flops 50331648 | bytes 1024 | tf_op jit(solution)/shard_map/pallas_call | solution.py:106
  274.5 12.8 %collective-permute-start.17 = (bf16[256,2048]{1,0:T(8,128)(2,1)}, bf16[256,2048]{1,0:T(8,128)(2,1)}, u32[]{:S(2)}, u32[]{:S(2)}) collective-permute-start(bf16[256,2048]{1,0:T(8,128)(2,1)} %get-tuple-element.196.refs_5_), channel_id=1, source_target_pairs={{0,4},{4,0},{8,12},{12,8},{16,20},{20,16},{24,28},{28,24},{1,5},{5... | collective-permute-start | bytes 3145736 | tf_op jit(solution)/shard_map/ppermute | solution.py:61
  302.3 8.0 %all_to_all.15.refs_1_.refs_2_ = bf16[2,512,1536]{2,1,0:T(8,128)(2,1)S(1)} all-to-all(bf16[2,512,1536]{2,1,0:T(8,128)(2,1)} %get-tuple-element.205), channel_id=1, replica_groups=mesh['blk'=8,'dp'=2,'head'=2] {'dp'}, dimensions={0} | all-to-all | bytes 6291456 | tf_op jit(solution)/shard_map/all_to_all | solution.py:56
  312.3 12.0 %collective-permute-start.19 = (bf16[256,1536]{1,0:T(8,128)(2,1)}, bf16[256,1536]{1,0:T(8,128)(2,1)}, u32[]{:S(2)}, u32[]{:S(2)}) collective-permute-start(bf16[256,1536]{1,0:T(8,128)(2,1)} %get-tuple-element.207.refs_3_), channel_id=1, source_target_pairs={{0,8},{4,12},{8,0},{12,4},{16,24},{20,28},{24,16},{28,20},{1,9},{5... | collective-permute-start | bytes 2359304 | tf_op jit(solution)/shard_map/ppermute | solution.py:61
  337.7 9.0 %collective-permute-start.21 = (bf16[128,2048]{1,0:T(8,128)(2,1)}, bf16[128,2048]{1,0:T(8,128)(2,1)}, u32[]{:S(2)}, u32[]{:S(2)}) collective-permute-start(bf16[128,2048]{1,0:T(8,128)(2,1)} %get-tuple-element.208.refs_9_), channel_id=1, source_target_pairs={{0,8},{4,12},{8,0},{12,4},{16,24},{20,28},{24,16},{28,20},{1,9},{5... | collective-permute-start | bytes 1572872 | tf_op jit(solution)/shard_map/ppermute | solution.py:61
  349.5 4.7 %shard_map.287 = (bf16[512,1024]{1,0:T(8,128)(2,1)S(1)}, f32[8,1024]{1,0:T(8,128)S(1)}) custom-call(s32[1]{0:T(128)} %bitcast.refs_0_, bf16[512,1024]{1,0:T(8,128)(2,1)S(1)} %copy-done.77, bf16[512,1024]{1,0:T(8,128)(2,1)} %collective-permute-done.16.refs_2_, bf16[176,1024]{1,0:T(8,128)(2,1)S(1)} %get-tuple-element.200.refs_3_, ...), custom_call_target="tpu_custom_call" | custom-call | flops 67108864 | bytes 1024 | tf_op jit(solution)/shard_map/pallas_call | solution.py:106
  (458 shorter events, 202.5 us)
Async XLA Ops:
  7.2 369.7 %reduce-scatter.4.cloned.1.call-start = ((), (), s32[]{:S(2)}) async-start(), calls=%async_computation.4 | async-start | bytes 8912896 | tf_op jit(solution)/shard_map/reduce_scatter | solution.py:1201
  10.5 48.9 %collective-permute-start.4 = (bf16[4,512,512]{2,1,0:T(8,128)(2,1)}, bf16[4,512,512]{2,1,0:T(8,128)(2,1)}, u32[]{:S(2)}, u32[]{:S(2)}) collective-permute-start(bf16[4,512,512]{2,1,0:T(8,128)(2,1)} %pad_maximum_fusion.refs_5_), channel_id=1, source_target_pairs={{0,1},{1,0},{2,3},{3,2},{4,5},{5,4},{6,7},{7,6},{8,9},{9,8},{10,11... | collective-permute-start | bytes 6291464 | tf_op jit(solution)/shard_map/ppermute | solution.py:61
  19.3 15.8 %collective-permute-start = (bf16[176,1024]{1,0:T(8,128)(2,1)S(1)}, bf16[176,1024]{1,0:T(8,128)(2,1)}, u32[]{:S(2)}, u32[]{:S(2)}) collective-permute-start(bf16[176,1024]{1,0:T(8,128)(2,1)S(1)} %fusion.refs_3_.refs_1_.refs_4_), channel_id=1, source_target_pairs={{0,8},{4,12},{8,16},{12,20},{16,24},{20,28},{1,9},{5,13},{9,17},{1... | collective-permute-start | bytes 1081352 | tf_op jit(solution)/shard_map/ppermute | solution.py:52
  23.6 27.6 %collective-permute-start.3 = (bf16[176,1024]{1,0:T(8,128)(2,1)S(1)}, bf16[176,1024]{1,0:T(8,128)(2,1)}, u32[]{:S(2)}, u32[]{:S(2)}) collective-permute-start(bf16[176,1024]{1,0:T(8,128)(2,1)S(1)} %fusion.refs_3_.refs_1_.refs_4_), channel_id=1, source_target_pairs={{0,12},{4,16},{8,20},{12,24},{16,28},{1,13},{5,17},{9,21},{13,25},... | collective-permute-start | bytes 1081352 | tf_op jit(solution)/shard_map/ppermute | solution.py:52
  29.1 25.3 %collective-permute-start.1 = (bf16[512,1024]{1,0:T(8,128)(2,1)}, bf16[512,1024]{1,0:T(8,128)(2,1)}, u32[]{:S(2)}, u32[]{:S(2)}) collective-permute-start(bf16[512,1024]{1,0:T(8,128)(2,1)} %dynamic-slice_bitcast_fusion), channel_id=1, source_target_pairs={{0,4},{4,8},{8,12},{12,16},{16,20},{20,24},{24,28},{1,5},{5,9},{9,... | collective-permute-start | bytes 3145736 | tf_op jit(solution)/shard_map/ppermute | solution.py:52
  63.7 15.3 %collective-permute-start.6 = (bf16[4,512,512]{2,1,0:T(8,128)(2,1)}, bf16[4,512,512]{2,1,0:T(8,128)(2,1)}, u32[]{:S(2)}, u32[]{:S(2)}) collective-permute-start(bf16[4,512,512]{2,1,0:T(8,128)(2,1)} %get-tuple-element.132), channel_id=1, source_target_pairs={{0,2},{2,0},{1,3},{3,1},{4,6},{6,4},{5,7},{7,5},{8,10},{10,8},{9,1... | collective-permute-start | bytes 6291464 | tf_op jit(solution)/shard_map/ppermute | solution.py:61
  99.1 24.4 %collective-permute-start.7 = (bf16[512,1024]{1,0:T(8,128)(2,1)S(1)}, bf16[512,1024]{1,0:T(8,128)(2,1)S(1)}, u32[]{:S(2)}, u32[]{:S(2)}) collective-permute-start(bf16[512,1024]{1,0:T(8,128)(2,1)S(1)} %get-tuple-element.139.refs_6_.refs_1_), channel_id=1, source_target_pairs={{0,1},{1,0},{2,3},{3,2},{4,5},{5,4},{6,7},{7,6},{8,9},{9,8},{10,11... | collective-permute-start | bytes 3145736 | tf_op jit(solution)/shard_map/ppermute | solution.py:61
  144.6 23.8 %collective-permute-start.8 = (bf16[512,1024]{1,0:T(8,128)(2,1)}, bf16[512,1024]{1,0:T(8,128)(2,1)S(1)}, u32[]{:S(2)}, u32[]{:S(2)}) collective-permute-start(bf16[512,1024]{1,0:T(8,128)(2,1)} %copy-done.99), channel_id=1, source_target_pairs={{0,1},{1,0},{2,3},{3,2},{4,5},{5,4},{6,7},{7,6},{8,9},{9,8},{10,11... | collective-permute-start | bytes 3145736 | tf_op jit(solution)/shard_map/ppermute | solution.py:61
  172.2 39.8 %collective-permute-start.9 = (bf16[512,1024]{1,0:T(8,128)(2,1)}, bf16[512,1024]{1,0:T(8,128)(2,1)}, u32[]{:S(2)}, u32[]{:S(2)}) collective-permute-start(bf16[512,1024]{1,0:T(8,128)(2,1)} %get-tuple-element.179), channel_id=1, source_target_pairs={{0,1},{1,0},{2,3},{3,2},{4,5},{5,4},{6,7},{7,6},{8,9},{9,8},{10,11... | collective-permute-start | bytes 3145736 | tf_op jit(solution)/shard_map/ppermute | solution.py:61
  194.9 20.7 %all-to-all-start = ((bf16[2,512,2048]{2,1,0:T(8,128)(2,1)}), bf16[2,512,2048]{2,1,0:T(8,128)(2,1)}, u32[]{:S(2)}, u32[]{:S(2)}) async-start(bf16[2,512,2048]{2,1,0:T(8,128)(2,1)} %get-tuple-element.177), calls=%async_computation | async-start | bytes 8388608 | tf_op jit(solution)/shard_map/all_to_all | solution.py:56
  220.5 48.2 %collective-permute-start.13 = (bf16[512,2048]{1,0:T(8,128)(2,1)}, bf16[512,2048]{1,0:T(8,128)(2,1)}, u32[]{:S(2)}, u32[]{:S(2)}) collective-permute-start(bf16[512,2048]{1,0:T(8,128)(2,1)} %shard_map.276.refs_8_), channel_id=1, source_target_pairs={{0,1},{1,0},{2,3},{3,2},{4,5},{5,4},{6,7},{7,6},{8,9},{9,8},{10,11... | collective-permute-start | bytes 6291464 | tf_op jit(solution)/shard_map/ppermute | solution.py:61
  229.5 57.9 %collective-permute-start.10 = (bf16[176,1024]{1,0:T(8,128)(2,1)}, bf16[176,1024]{1,0:T(8,128)(2,1)}, u32[]{:S(2)}, u32[]{:S(2)}) collective-permute-start(bf16[176,1024]{1,0:T(8,128)(2,1)} %get-tuple-element.191), channel_id=1, source_target_pairs={{16,0},{20,4},{24,8},{28,12},{17,1},{21,5},{25,9},{29,13},{18,2},{... | collective-permute-start | bytes 1081352 | tf_op jit(solution)/shard_map/ppermute | solution.py:52
  230.8 56.6 %collective-permute-start.11 = (bf16[176,1024]{1,0:T(8,128)(2,1)}, bf16[176,1024]{1,0:T(8,128)(2,1)}, u32[]{:S(2)}, u32[]{:S(2)}) collective-permute-start(bf16[176,1024]{1,0:T(8,128)(2,1)} %get-tuple-element.192), channel_id=1, source_target_pairs={{12,0},{16,4},{20,8},{24,12},{28,16},{13,1},{17,5},{21,9},{25,13},... | collective-permute-start | bytes 1081352 | tf_op jit(solution)/shard_map/ppermute | solution.py:52
  232.1 55.3 %collective-permute-start.12 = (bf16[176,1024]{1,0:T(8,128)(2,1)}, bf16[176,1024]{1,0:T(8,128)(2,1)}, u32[]{:S(2)}, u32[]{:S(2)}) collective-permute-start(bf16[176,1024]{1,0:T(8,128)(2,1)} %get-tuple-element.193), channel_id=1, source_target_pairs={{8,0},{12,4},{16,8},{20,12},{24,16},{28,20},{9,1},{13,5},{17,9},{2... | collective-permute-start | bytes 1081352 | tf_op jit(solution)/shard_map/ppermute | solution.py:52
  247.5 20.1 %all-to-all-start.1 = ((bf16[2,512,2048]{2,1,0:T(8,128)(2,1)}), bf16[2,512,2048]{2,1,0:T(8,128)(2,1)}, u32[]{:S(2)}, u32[]{:S(2)}) async-start(bf16[2,512,2048]{2,1,0:T(8,128)(2,1)} %get-tuple-element.194), calls=%async_computation.1 | async-start | bytes 8388608 | tf_op jit(solution)/shard_map/all_to_all | solution.py:56
  274.5 59.0 %collective-permute-start.17 = (bf16[256,2048]{1,0:T(8,128)(2,1)}, bf16[256,2048]{1,0:T(8,128)(2,1)}, u32[]{:S(2)}, u32[]{:S(2)}) collective-permute-start(bf16[256,2048]{1,0:T(8,128)(2,1)} %get-tuple-element.196.refs_5_), channel_id=1, source_target_pairs={{0,4},{4,0},{8,12},{12,8},{16,20},{20,16},{24,28},{28,24},{1,5},{5... | collective-permute-start | bytes 3145736 | tf_op jit(solution)/shard_map/ppermute | solution.py:61
  290.0 56.7 %collective-permute-start.16 = (bf16[512,1024]{1,0:T(8,128)(2,1)}, bf16[512,1024]{1,0:T(8,128)(2,1)}, u32[]{:S(2)}, u32[]{:S(2)}) collective-permute-start(bf16[512,1024]{1,0:T(8,128)(2,1)} %get-tuple-element.199), channel_id=1, source_target_pairs={{4,0},{8,4},{12,8},{16,12},{20,16},{24,20},{28,24},{5,1},{9,5},{13... | collective-permute-start | bytes 3145736 | tf_op jit(solution)/shard_map/ppermute | solution.py:52
  312.3 43.0 %collective-permute-start.19 = (bf16[256,1536]{1,0:T(8,128)(2,1)}, bf16[256,1536]{1,0:T(8,128)(2,1)}, u32[]{:S(2)}, u32[]{:S(2)}) collective-permute-start(bf16[256,1536]{1,0:T(8,128)(2,1)} %get-tuple-element.207.refs_3_), channel_id=1, source_target_pairs={{0,8},{4,12},{8,0},{12,4},{16,24},{20,28},{24,16},{28,20},{1,9},{5... | collective-permute-start | bytes 2359304 | tf_op jit(solution)/shard_map/ppermute | solution.py:61
  325.4 21.3 %collective-permute-start.15 = (f32[4,512]{1,0:T(4,128)S(1)}, f32[4,512]{1,0:T(4,128)S(1)}, u32[]{:S(2)}, u32[]{:S(2)}) collective-permute-start(f32[4,512]{1,0:T(4,128)S(1)} %bitcast.91), channel_id=1, source_target_pairs={{0,1},{1,0},{2,3},{3,2},{4,5},{5,4},{6,7},{7,6},{8,9},{9,8},{10,11... | collective-permute-start | bytes 24584 | tf_op jit(solution)/shard_map/ppermute | solution.py:61
  328.8 35.3 %collective-permute-start.14 = (bf16[512,1024]{1,0:T(8,128)(2,1)}, bf16[512,1024]{1,0:T(8,128)(2,1)}, u32[]{:S(2)}, u32[]{:S(2)}) collective-permute-start(bf16[512,1024]{1,0:T(8,128)(2,1)} %copy-done.36), channel_id=1, source_target_pairs={{0,1},{1,0},{2,3},{3,2},{4,5},{5,4},{6,7},{7,6},{8,9},{9,8},{10,11... | collective-permute-start | bytes 3145736 | tf_op jit(solution)/shard_map/ppermute | solution.py:61
  337.7 30.4 %collective-permute-start.21 = (bf16[128,2048]{1,0:T(8,128)(2,1)}, bf16[128,2048]{1,0:T(8,128)(2,1)}, u32[]{:S(2)}, u32[]{:S(2)}) collective-permute-start(bf16[128,2048]{1,0:T(8,128)(2,1)} %get-tuple-element.208.refs_9_), channel_id=1, source_target_pairs={{0,8},{4,12},{8,0},{12,4},{16,24},{20,28},{24,16},{28,20},{1,9},{5... | collective-permute-start | bytes 1572872 | tf_op jit(solution)/shard_map/ppermute | solution.py:61
  360.6 26.9 %collective-permute-start.20 = (bf16[512,1024]{1,0:T(8,128)(2,1)}, bf16[512,1024]{1,0:T(8,128)(2,1)}, u32[]{:S(2)}, u32[]{:S(2)}) collective-permute-start(bf16[512,1024]{1,0:T(8,128)(2,1)} %get-tuple-element.212), channel_id=1, source_target_pairs={{0,1},{1,0},{2,3},{3,2},{4,5},{5,4},{6,7},{7,6},{8,9},{9,8},{10,11... | collective-permute-start | bytes 3145736 | tf_op jit(solution)/shard_map/ppermute | solution.py:61
  369.3 21.4 %collective-permute-start.23 = (bf16[64,2048]{1,0:T(8,128)(2,1)S(1)}, bf16[64,2048]{1,0:T(8,128)(2,1)}, u32[]{:S(2)}, u32[]{:S(2)}) collective-permute-start(bf16[64,2048]{1,0:T(8,128)(2,1)S(1)} %get-tuple-element.221.refs_3_), channel_id=1, source_target_pairs={{0,16},{4,20},{8,24},{12,28},{16,0},{20,4},{24,8},{28,12},{1,17},{... | collective-permute-start | bytes 786440 | tf_op jit(solution)/shard_map/ppermute | solution.py:61
  372.2 31.3 %collective-permute-start.29 = (bf16[64,1536]{1,0:T(8,128)(2,1)S(1)}, bf16[64,1536]{1,0:T(8,128)(2,1)S(1)}, u32[]{:S(2)}, u32[]{:S(2)}) collective-permute-start(bf16[64,1536]{1,0:T(8,128)(2,1)S(1)} %get-tuple-element.223.refs_2_), channel_id=1, source_target_pairs={{0,16},{4,20},{8,24},{12,28},{16,0},{20,4},{24,8},{28,12},{1,17},{... | collective-permute-start | bytes 589832 | tf_op jit(solution)/shard_map/ppermute | solution.py:61
  (164 other events, 1301.9 us)
Sparse Core Ops, SparseCore 0:
  144.7 141.9 reduce-scatter.3

commit v6 on v5

--- a/solution.py
+++ b/solution.py
@@ -15,7 +15,7 @@
 BF = jnp.bfloat16
 F32 = jnp.float32
 TILE = 256
-GROUP = 2
+GROUP = 4
 OWN, OTH = 0, 1
 BLK, DP, HEAD = "blk", "dp", "head"
 SHARE = 1 << 24
@@ -487,7 +487,7 @@
         in_specs=[near, near, near, small, small, lane],
         out_specs=[lane, near, near, near, small, small],
         out_shape=[jax.ShapeDtypeStruct((heads, 1, rows), F32), big, big, big, little, little],
-        compiler_params=pltpu.CompilerParams(vmem_limit_bytes=mib(10.3)),
+        compiler_params=pltpu.CompilerParams(vmem_limit_bytes=mib(16)),
         cost_estimate=cost(4.3),
         to_hbm=True,
     )(q, ko, vo, kc, vc, cot)
@@ -982,7 +982,6 @@
         out_shape=[jax.ShapeDtypeStruct((rows, wide), BF)] * split,
         compiler_params=pltpu.CompilerParams(vmem_limit_bytes=mib(14)),
         cost_estimate=cost(TAIL * 2),
-        from_hbm=True,
     )(*operands)
 
 

time: 426 us -> 424 us (level)
    unnamed x318 -> x322, local copies, waits for them, and re-layouts: 42.5 us -> 42.7 us
where the time goes in v6:
time: 424 us; the launch traced here: 417 us
  Pallas kernels  185 us (44%)
  starting transfers between devices  93.1 us (22%)
  local copies, waits for them, and re-layouts  59.4 us (14%)
  waiting for transfers between devices  35.7 us (8%)
  other arithmetic  18.1 us (4%)
  between operations  16.4 us (4%)
  blocking collectives  7.92 us (2%)
    pallas_call x43, Pallas kernels, run(): return pl.pallas_call(body, **settings)(*operands, *deps, *gates)  185 us
    ppermute x23, starting transfers between devices, swap(): return lax.ppermute(x, axis, [(i, i ^ step) for i in range(devices)])  61.1 us
    unnamed x322, local copies, waits for them, and re-layouts  42.7 us
    ppermute x23, waiting for transfers between devices, swap(): return lax.ppermute(x, axis, [(i, i ^ step) for i in range(devices)])  33.7 us
    ppermute x8, starting transfers between devices, shift(): return lax.ppermute(x, axis, pairs)  19.9 us
    all_to_all x2, starting transfers between devices, trade(): return lax.all_to_all(x, DP, 0, 0)  12 us
    select_n x6, other arithmetic, in_order(): jnp.where(mine == 0, jnp.concatenate([first, second], axis), jnp.concaten...  9.75 us
  transfers between devices with their start and end apart: 34, of which 11 were waited for; matrix products, arithmetic and copies ran while one was open for 8% of the time, Pallas kernels for 36%

profile of v6, /device:TPU:0, one launch (start us, length us, event | category | flops | bytes accessed | tf_op | source)
XLA Modules:
  0.0 416.7 jit_solution(8703909999799001940)
XLA Ops:
  40.3 10.7 %shard_map.257 = (f32[4,1,512]{2,1,0:T(1,128)}, bf16[512,512]{1,0:T(8,128)(2,1)}, bf16[512,512]{1,0:T(8,128)(2,1)}, bf16[512,512]{1,0:T(8,128)(2,1)}, bf16[176,5...) custom-call(bf16[512,512]{1,0:T(8,128)(2,1)S(1)} %get-tuple-element.122.refs_0_.refs_1_, ...), custom_call_target="tpu_custom_call" | custom-call | flops 72142032 | bytes 1024 | tf_op jit(solution)/shard_map/pallas_call | solution.py:106
  71.0 6.4 %shard_map.260 = (bf16[512,512]{1,0:T(8,128)(2,1)S(1)}, f32[4,1,512]{2,1,0:T(1,128)S(1)}) custom-call(f32[4]{0:T(128)S(1)} %copy-done.134, bf16[512,512]{1,0:T(8,128)(2,1)S(1)} %copy-done.56, bf16[1024,512]{1,0:T(8,128)(2,1)S(1)} %copy-done.82, bf16[1024,512]{1,0:T(8,128)(2,1)S(1)} %copy-done.84, bf16[512,512]{1,0:T(8,128)(2,1)S(1)} %copy-done.69, ...), custom_call_target="tpu_custom_call" | custom-call | flops 53687092 | bytes 1024 | tf_op jit(solution)/shard_map/pallas_call | solution.py:106
  88.7 6.3 %shard_map.263 = (bf16[512,512]{1,0:T(8,128)(2,1)S(1)}, f32[4,1,512]{2,1,0:T(1,128)S(1)}) custom-call(f32[4]{0:T(128)S(1)} %slice_bitcast_fusion.8.refs_0_, bf16[512,512]{1,0:T(8,128)(2,1)S(1)} %get-tuple-element.133.refs_3_.refs_1_.refs_0_, bf16[1024,512]{1,0:T(8,128)(2,1)S(1)} %get-tuple-element.134.refs_2_.refs_6_, ...), custom_call_target="tpu_custom_call" | custom-call | flops 53687092 | bytes 1024 | tf_op jit(solution)/shard_map/pallas_call | solution.py:106
  101.2 10.7 %shard_map.265 = (f32[4,1,512]{2,1,0:T(1,128)}, bf16[512,512]{1,0:T(8,128)(2,1)}, bf16[512,512]{1,0:T(8,128)(2,1)}, bf16[512,512]{1,0:T(8,128)(2,1)}, bf16[176,5...) custom-call(bf16[512,512]{1,0:T(8,128)(2,1)S(1)} %get-tuple-element.133.refs_3_.refs_1_.refs_0_, ...), custom_call_target="tpu_custom_call" | custom-call | flops 72142032 | bytes 1024 | tf_op jit(solution)/shard_map/pallas_call | solution.py:106
  112.6 8.8 %shard_map.266 = (bf16[512,2048]{1,0:T(8,128)(2,1)S(1)}, bf16[512,2048]{1,0:T(8,128)(2,1)S(1)}, bf16[512,1024]{1,0:T(8,128)(2,1)S(1)}) custom-call(s32[1]{0:T(128)} %bitcast.refs_0_, bf16[512,1024]{1,0:T(8,128)(2,1)S(1)} %get-tuple-element.139.refs_6_.refs_1_, bf16[2,512,1024]{2,1,0:T(8,128)(2,1)S(1)} %copy-done.5, bf16[1024,2048]{1,0:T(8,128)(2,1)S(1)} %copy-done.19, ...), custom_call_target="tpu_custom_call" | custom-call | flops 107374184 | bytes 1024 | tf_op jit(solution)/shard_map/pallas_call | solution.py:106
  123.1 8.8 %shard_map.267 = (bf16[512,2048]{1,0:T(8,128)(2,1)S(1)}, bf16[512,2048]{1,0:T(8,128)(2,1)S(1)}, bf16[512,1024]{1,0:T(8,128)(2,1)S(1)}) custom-call(s32[1]{0:T(128)} %bitcast.15.refs_0_, bf16[512,1024]{1,0:T(8,128)(2,1)S(1)} %collective-permute-done.7.refs_1_.refs_3_, bf16[2,512,1024]{2,1,0:T(8,128)(2,1)S(1)} %copy-done.5, bf16[1024,2048]{1,0:T(8,128)(2,1)S(1)} %copy-done.19, ...), custom_call_target="tpu_custom_call" | custom-call | flops 107374184 | bytes 1024 | tf_op jit(solution)/shard_map/pallas_call | solution.py:106
  131.9 12.4 %shard_map.268 = (bf16[1024,4096]{1,0:T(8,128)(2,1)}, f32[8,128]{1,0:T(8,128)}) custom-call(s32[2]{0:T(128)S(1)} %pad_add_fusion.1.refs_0_, bf16[512,1024]{1,0:T(8,128)(2,1)S(1)} %get-tuple-element.139.refs_6_.refs_1_, bf16[512,2048]{1,0:T(8,128)(2,1)S(1)} %get-tuple-element.148.refs_2_, bf16[512,1024]{1,0:T(8,128)(2,1)S(1)} %collective-permute-done.7.refs_1_.refs_3_, ...), custom_call_target="tpu_custom_call" | custom-call | flops 201761264 | bytes 1024 | tf_op jit(solution)/shard_map/pallas_call | solution.py:106
  146.2 10.1 %shard_map.269 = (bf16[512,1024]{1,0:T(8,128)(2,1)S(1)}, bf16[512,1024]{1,0:T(8,128)(2,1)}) custom-call(bf16[512,2048]{1,0:T(8,128)(2,1)} %copy-done.50, bf16[512,2048]{1,0:T(8,128)(2,1)} %copy-done.51, bf16[2048,1024]{1,0:T(8,128)(2,1)} %refs_2_.11, f32[8,128]{1,0:T(8,128)S(1)} %copy-done.137), custom_call_target="tpu_custom_call" | custom-call | flops 100663296 | bytes 1024 | tf_op jit(solution)/shard_map/pallas_call | solution.py:106
  157.3 10.9 %collective-permute-done.8.refs_2_ = bf16[512,1024]{1,0:T(8,128)(2,1)S(1)} collective-permute-done((bf16[512,1024]{1,0:T(8,128)(2,1)}, bf16[512,1024]{1,0:T(8,128)(2,1)S(1)}, u32[]{:S(2)}, u32[]{:S(2)}) %collective-permute-start.8) | collective-permute-done | bytes 1048608 | tf_op jit(solution)/shard_map/ppermute | solution.py:61
  174.2 7.1 %shard_map.271 = (bf16[512,512]{1,0:T(8,128)(2,1)S(1)}, bf16[1024,512]{1,0:T(8,128)(2,1)S(1)}, bf16[1024,512]{1,0:T(8,128)(2,1)S(1)}, f32[4,8,512]{2,1,0:T(8,128)S(1)}) custom-call(f32[4]{0:T(128)S(1)} %copy-done.136, bf16[512,512]{1,0:T(8,128)(2,1)S(1)} %copy-done.28, bf16[512,512]{1,0:T(8,128)(2,1)S(1)} %get-tuple-element.155.refs_2_, ...), custom_call_target="tpu_custom_call" | custom-call | flops 150994944 | bytes 1024 | tf_op jit(solution)/shard_map/pallas_call | solution.py:106
  186.5 7.6 %shard_map.273 = (bf16[2,512,2048]{2,1,0:T(8,128)(2,1)}, f32[8,128]{1,0:T(8,128)}) custom-call(s32[2]{0:T(128)S(1)} %pad_add_fusion.1.refs_0_, bf16[512,1024]{1,0:T(8,128)(2,1)S(1)} %copy-done.23, bf16[512,512]{1,0:T(8,128)(2,1)S(1)} %get-tuple-element.163.refs_2_.refs_0_, bf16[512,512]{1,0:T(8,128)(2,1)S(1)} %get-tuple-element.164.refs_3_.refs_1_, ...), custom_call_target="tpu_custom_call" | custom-call | flops 109550064 | bytes 1024 | tf_op jit(solution)/shard_map/pallas_call | solution.py:106
  194.1 6.2 %all-to-all-start = ((bf16[2,512,2048]{2,1,0:T(8,128)(2,1)}), bf16[2,512,2048]{2,1,0:T(8,128)(2,1)}, u32[]{:S(2)}, u32[]{:S(2)}) async-start(bf16[2,512,2048]{2,1,0:T(8,128)(2,1)} %get-tuple-element.177), calls=%async_computation | async-start | bytes 8388608 | tf_op jit(solution)/shard_map/all_to_all | solution.py:56
  200.3 9.0 %shard_map.274 = (bf16[512,512]{1,0:T(8,128)(2,1)S(1)}, bf16[1024,512]{1,0:T(8,128)(2,1)S(1)}, bf16[1024,512]{1,0:T(8,128)(2,1)S(1)}, f32[4,8,512]{2,1,0:T(8,128)S(1)}) custom-call(f32[4]{0:T(128)S(1)} %copy-done.134, bf16[512,512]{1,0:T(8,128)(2,1)} %copy-done.55, bf16[512,512]{1,0:T(8,128)(2,1)} %copy-done.94, f32[4,1,512]{2,1,0:T(1,128)} %copy-done.130, ...), custom_call_target="tpu_custom_call" | custom-call | flops 150994944 | bytes 1024 | tf_op jit(solution)/shard_map/pallas_call | solution.py:106
  221.3 6.5 %shard_map.277 = (bf16[512,1024]{1,0:T(8,128)(2,1)}, bf16[176,1024]{1,0:T(8,128)(2,1)}, bf16[176,1024]{1,0:T(8,128)(2,1)}, bf16[176,1024]{1,0:T(8,128)(2,1)}) custom-call(bf16[1024,512]{1,0:T(8,128)(2,1)S(1)} %copy-done.46, bf16[1024,512]{1,0:T(8,128)(2,1)S(1)} %copy-done.48, bf16[1024,512]{1,0:T(8,128)(2,1)S(1)} %copy-done.40, ...), custom_call_target="tpu_custom_call" | custom-call | flops 100663296 | bytes 1024 | tf_op jit(solution)/shard_map/pallas_call | solution.py:106
  231.9 5.7 %shard_map.278 = (bf16[512,512]{1,0:T(8,128)(2,1)S(1)}, bf16[512,512]{1,0:T(8,128)(2,1)S(1)}, bf16[512,512]{1,0:T(8,128)(2,1)S(1)}, f32[4,8,512]{2,1,0:T(8,128)S(1)}) custom-call(f32[4]{0:T(128)S(1)} %copy-done.134, bf16[512,512]{1,0:T(8,128)(2,1)} %copy-done.55, bf16[512,512]{1,0:T(8,128)(2,1)} %copy-done.94, f32[4,1,512]{2,1,0:T(1,128)} %copy-done.130, ...), custom_call_target="tpu_custom_call" | custom-call | flops 83886080 | bytes 1024 | tf_op jit(solution)/shard_map/pallas_call | solution.py:106
  238.3 7.6 %shard_map.279 = (bf16[2,512,2048]{2,1,0:T(8,128)(2,1)}, f32[8,128]{1,0:T(8,128)}) custom-call(s32[2]{0:T(128)S(1)} %pad_add_fusion.1.refs_0_, bf16[512,1024]{1,0:T(8,128)(2,1)S(1)} %copy-done.24, bf16[512,512]{1,0:T(8,128)(2,1)S(1)} %get-tuple-element.182.refs_2_.refs_0_, bf16[512,512]{1,0:T(8,128)(2,1)S(1)} %get-tuple-element.183.refs_3_.refs_1_, ...), custom_call_target="tpu_custom_call" | custom-call | flops 109550064 | bytes 1024 | tf_op jit(solution)/shard_map/pallas_call | solution.py:106
  245.9 5.8 %all-to-all-start.1 = ((bf16[2,512,2048]{2,1,0:T(8,128)(2,1)}), bf16[2,512,2048]{2,1,0:T(8,128)(2,1)}, u32[]{:S(2)}, u32[]{:S(2)}) async-start(bf16[2,512,2048]{2,1,0:T(8,128)(2,1)} %get-tuple-element.194), calls=%async_computation.1 | async-start | bytes 8388608 | tf_op jit(solution)/shard_map/all_to_all | solution.py:56
  251.8 5.1 %shard_map.280 = (bf16[512,1024]{1,0:T(8,128)(2,1)S(1)}, bf16[176,1024]{1,0:T(8,128)(2,1)S(1)}) custom-call(bf16[512,512]{1,0:T(8,128)(2,1)} %copy-done.91, bf16[512,512]{1,0:T(8,128)(2,1)} %copy-done.92, bf16[512,512]{1,0:T(8,128)(2,1)} %copy-done.93, bf16[176,512]{1,0:T(8,128)(2,1)} %get-tuple-element.165.refs_5_.refs_3_, ...), custom_call_target="tpu_custom_call" | custom-call | flops 50331648 | bytes 1024 | tf_op jit(solution)/shard_map/pallas_call | solution.py:106
  258.6 5.5 %shard_map.281 = (bf16[512,1024]{1,0:T(8,128)(2,1)S(1)}, bf16[176,1024]{1,0:T(8,128)(2,1)S(1)}) custom-call(bf16[512,512]{1,0:T(8,128)(2,1)} %copy-done.95, bf16[512,512]{1,0:T(8,128)(2,1)} %copy-done.96, bf16[512,512]{1,0:T(8,128)(2,1)} %copy-done.97, bf16[176,512]{1,0:T(8,128)(2,1)} %get-tuple-element.185.refs_5_.refs_3_, ...), custom_call_target="tpu_custom_call" | custom-call | flops 50331648 | bytes 1024 | tf_op jit(solution)/shard_map/pallas_call | solution.py:106
  273.0 12.4 %collective-permute-start.17 = (bf16[256,2048]{1,0:T(8,128)(2,1)}, bf16[256,2048]{1,0:T(8,128)(2,1)}, u32[]{:S(2)}, u32[]{:S(2)}) collective-permute-start(bf16[256,2048]{1,0:T(8,128)(2,1)} %get-tuple-element.196.refs_5_), channel_id=1, source_target_pairs={{0,4},{4,0},{8,12},{12,8},{16,20},{20,16},{24,28},{28,24},{1,5},{5... | collective-permute-start | bytes 3145736 | tf_op jit(solution)/shard_map/ppermute | solution.py:61
  300.5 7.9 %all_to_all.15.refs_1_.refs_2_ = bf16[2,512,1536]{2,1,0:T(8,128)(2,1)S(1)} all-to-all(bf16[2,512,1536]{2,1,0:T(8,128)(2,1)} %get-tuple-element.205), channel_id=1, replica_groups=mesh['blk'=8,'dp'=2,'head'=2] {'dp'}, dimensions={0} | all-to-all | bytes 6291456 | tf_op jit(solution)/shard_map/all_to_all | solution.py:56
  310.5 12.0 %collective-permute-start.19 = (bf16[256,1536]{1,0:T(8,128)(2,1)}, bf16[256,1536]{1,0:T(8,128)(2,1)}, u32[]{:S(2)}, u32[]{:S(2)}) collective-permute-start(bf16[256,1536]{1,0:T(8,128)(2,1)} %get-tuple-element.207.refs_3_), channel_id=1, source_target_pairs={{0,8},{4,12},{8,0},{12,4},{16,24},{20,28},{24,16},{28,20},{1,9},{5... | collective-permute-start | bytes 2359304 | tf_op jit(solution)/shard_map/ppermute | solution.py:61
  336.0 8.8 %collective-permute-start.21 = (bf16[128,2048]{1,0:T(8,128)(2,1)}, bf16[128,2048]{1,0:T(8,128)(2,1)}, u32[]{:S(2)}, u32[]{:S(2)}) collective-permute-start(bf16[128,2048]{1,0:T(8,128)(2,1)} %get-tuple-element.208.refs_9_), channel_id=1, source_target_pairs={{0,8},{4,12},{8,0},{12,4},{16,24},{20,28},{24,16},{28,20},{1,9},{5... | collective-permute-start | bytes 1572872 | tf_op jit(solution)/shard_map/ppermute | solution.py:61
  347.6 4.7 %shard_map.287 = (bf16[512,1024]{1,0:T(8,128)(2,1)S(1)}, f32[8,1024]{1,0:T(8,128)S(1)}) custom-call(s32[1]{0:T(128)} %bitcast.refs_0_, bf16[512,1024]{1,0:T(8,128)(2,1)S(1)} %copy-done.78, bf16[512,1024]{1,0:T(8,128)(2,1)} %collective-permute-done.16.refs_2_, bf16[176,1024]{1,0:T(8,128)(2,1)S(1)} %get-tuple-element.200.refs_3_, ...), custom_call_target="tpu_custom_call" | custom-call | flops 67108864 | bytes 1024 | tf_op jit(solution)/shard_map/pallas_call | solution.py:106
  (462 shorter events, 203.3 us)
Async XLA Ops:
  7.2 367.7 %reduce-scatter.4.cloned.1.call-start = ((), (), s32[]{:S(2)}) async-start(), calls=%async_computation.4 | async-start | bytes 8912896 | tf_op jit(solution)/shard_map/reduce_scatter | solution.py:1200
  10.5 48.9 %collective-permute-start.4 = (bf16[4,512,512]{2,1,0:T(8,128)(2,1)}, bf16[4,512,512]{2,1,0:T(8,128)(2,1)}, u32[]{:S(2)}, u32[]{:S(2)}) collective-permute-start(bf16[4,512,512]{2,1,0:T(8,128)(2,1)} %pad_maximum_fusion.refs_5_), channel_id=1, source_target_pairs={{0,1},{1,0},{2,3},{3,2},{4,5},{5,4},{6,7},{7,6},{8,9},{9,8},{10,11... | collective-permute-start | bytes 6291464 | tf_op jit(solution)/shard_map/ppermute | solution.py:61
  19.3 15.8 %collective-permute-start = (bf16[176,1024]{1,0:T(8,128)(2,1)S(1)}, bf16[176,1024]{1,0:T(8,128)(2,1)}, u32[]{:S(2)}, u32[]{:S(2)}) collective-permute-start(bf16[176,1024]{1,0:T(8,128)(2,1)S(1)} %fusion.refs_3_.refs_1_.refs_4_), channel_id=1, source_target_pairs={{0,8},{4,12},{8,16},{12,20},{16,24},{20,28},{1,9},{5,13},{9,17},{1... | collective-permute-start | bytes 1081352 | tf_op jit(solution)/shard_map/ppermute | solution.py:52
  23.6 27.4 %collective-permute-start.3 = (bf16[176,1024]{1,0:T(8,128)(2,1)S(1)}, bf16[176,1024]{1,0:T(8,128)(2,1)}, u32[]{:S(2)}, u32[]{:S(2)}) collective-permute-start(bf16[176,1024]{1,0:T(8,128)(2,1)S(1)} %fusion.refs_3_.refs_1_.refs_4_), channel_id=1, source_target_pairs={{0,12},{4,16},{8,20},{12,24},{16,28},{1,13},{5,17},{9,21},{13,25},... | collective-permute-start | bytes 1081352 | tf_op jit(solution)/shard_map/ppermute | solution.py:52
  29.0 25.3 %collective-permute-start.1 = (bf16[512,1024]{1,0:T(8,128)(2,1)}, bf16[512,1024]{1,0:T(8,128)(2,1)}, u32[]{:S(2)}, u32[]{:S(2)}) collective-permute-start(bf16[512,1024]{1,0:T(8,128)(2,1)} %dynamic-slice_bitcast_fusion), channel_id=1, source_target_pairs={{0,4},{4,8},{8,12},{12,16},{16,20},{20,24},{24,28},{1,5},{5,9},{9,... | collective-permute-start | bytes 3145736 | tf_op jit(solution)/shard_map/ppermute | solution.py:52
  63.7 15.0 %collective-permute-start.6 = (bf16[4,512,512]{2,1,0:T(8,128)(2,1)}, bf16[4,512,512]{2,1,0:T(8,128)(2,1)}, u32[]{:S(2)}, u32[]{:S(2)}) collective-permute-start(bf16[4,512,512]{2,1,0:T(8,128)(2,1)} %get-tuple-element.132), channel_id=1, source_target_pairs={{0,2},{2,0},{1,3},{3,1},{4,6},{6,4},{5,7},{7,5},{8,10},{10,8},{9,1... | collective-permute-start | bytes 6291464 | tf_op jit(solution)/shard_map/ppermute | solution.py:61
  98.7 24.4 %collective-permute-start.7 = (bf16[512,1024]{1,0:T(8,128)(2,1)S(1)}, bf16[512,1024]{1,0:T(8,128)(2,1)S(1)}, u32[]{:S(2)}, u32[]{:S(2)}) collective-permute-start(bf16[512,1024]{1,0:T(8,128)(2,1)S(1)} %get-tuple-element.139.refs_6_.refs_1_), channel_id=1, source_target_pairs={{0,1},{1,0},{2,3},{3,2},{4,5},{5,4},{6,7},{7,6},{8,9},{9,8},{10,11... | collective-permute-start | bytes 3145736 | tf_op jit(solution)/shard_map/ppermute | solution.py:61
  144.4 23.8 %collective-permute-start.8 = (bf16[512,1024]{1,0:T(8,128)(2,1)}, bf16[512,1024]{1,0:T(8,128)(2,1)S(1)}, u32[]{:S(2)}, u32[]{:S(2)}) collective-permute-start(bf16[512,1024]{1,0:T(8,128)(2,1)} %copy-done.100), channel_id=1, source_target_pairs={{0,1},{1,0},{2,3},{3,2},{4,5},{5,4},{6,7},{7,6},{8,9},{9,8},{10,11... | collective-permute-start | bytes 3145736 | tf_op jit(solution)/shard_map/ppermute | solution.py:61
  172.4 38.9 %collective-permute-start.9 = (bf16[512,1024]{1,0:T(8,128)(2,1)}, bf16[512,1024]{1,0:T(8,128)(2,1)}, u32[]{:S(2)}, u32[]{:S(2)}) collective-permute-start(bf16[512,1024]{1,0:T(8,128)(2,1)} %get-tuple-element.179), channel_id=1, source_target_pairs={{0,1},{1,0},{2,3},{3,2},{4,5},{5,4},{6,7},{7,6},{8,9},{9,8},{10,11... | collective-permute-start | bytes 3145736 | tf_op jit(solution)/shard_map/ppermute | solution.py:61
  194.1 19.9 %all-to-all-start = ((bf16[2,512,2048]{2,1,0:T(8,128)(2,1)}), bf16[2,512,2048]{2,1,0:T(8,128)(2,1)}, u32[]{:S(2)}, u32[]{:S(2)}) async-start(bf16[2,512,2048]{2,1,0:T(8,128)(2,1)} %get-tuple-element.177), calls=%async_computation | async-start | bytes 8388608 | tf_op jit(solution)/shard_map/all_to_all | solution.py:56
  218.7 48.4 %collective-permute-start.13 = (bf16[512,2048]{1,0:T(8,128)(2,1)}, bf16[512,2048]{1,0:T(8,128)(2,1)}, u32[]{:S(2)}, u32[]{:S(2)}) collective-permute-start(bf16[512,2048]{1,0:T(8,128)(2,1)} %shard_map.276.refs_8_), channel_id=1, source_target_pairs={{0,1},{1,0},{2,3},{3,2},{4,5},{5,4},{6,7},{7,6},{8,9},{9,8},{10,11... | collective-permute-start | bytes 6291464 | tf_op jit(solution)/shard_map/ppermute | solution.py:61
  227.7 57.7 %collective-permute-start.10 = (bf16[176,1024]{1,0:T(8,128)(2,1)}, bf16[176,1024]{1,0:T(8,128)(2,1)}, u32[]{:S(2)}, u32[]{:S(2)}) collective-permute-start(bf16[176,1024]{1,0:T(8,128)(2,1)} %get-tuple-element.191), channel_id=1, source_target_pairs={{16,0},{20,4},{24,8},{28,12},{17,1},{21,5},{25,9},{29,13},{18,2},{... | collective-permute-start | bytes 1081352 | tf_op jit(solution)/shard_map/ppermute | solution.py:52
  229.0 56.4 %collective-permute-start.11 = (bf16[176,1024]{1,0:T(8,128)(2,1)}, bf16[176,1024]{1,0:T(8,128)(2,1)}, u32[]{:S(2)}, u32[]{:S(2)}) collective-permute-start(bf16[176,1024]{1,0:T(8,128)(2,1)} %get-tuple-element.192), channel_id=1, source_target_pairs={{12,0},{16,4},{20,8},{24,12},{28,16},{13,1},{17,5},{21,9},{25,13},... | collective-permute-start | bytes 1081352 | tf_op jit(solution)/shard_map/ppermute | solution.py:52
  230.3 55.1 %collective-permute-start.12 = (bf16[176,1024]{1,0:T(8,128)(2,1)}, bf16[176,1024]{1,0:T(8,128)(2,1)}, u32[]{:S(2)}, u32[]{:S(2)}) collective-permute-start(bf16[176,1024]{1,0:T(8,128)(2,1)} %get-tuple-element.193), channel_id=1, source_target_pairs={{8,0},{12,4},{16,8},{20,12},{24,16},{28,20},{9,1},{13,5},{17,9},{2... | collective-permute-start | bytes 1081352 | tf_op jit(solution)/shard_map/ppermute | solution.py:52
  245.9 20.0 %all-to-all-start.1 = ((bf16[2,512,2048]{2,1,0:T(8,128)(2,1)}), bf16[2,512,2048]{2,1,0:T(8,128)(2,1)}, u32[]{:S(2)}, u32[]{:S(2)}) async-start(bf16[2,512,2048]{2,1,0:T(8,128)(2,1)} %get-tuple-element.194), calls=%async_computation.1 | async-start | bytes 8388608 | tf_op jit(solution)/shard_map/all_to_all | solution.py:56
  273.0 58.8 %collective-permute-start.17 = (bf16[256,2048]{1,0:T(8,128)(2,1)}, bf16[256,2048]{1,0:T(8,128)(2,1)}, u32[]{:S(2)}, u32[]{:S(2)}) collective-permute-start(bf16[256,2048]{1,0:T(8,128)(2,1)} %get-tuple-element.196.refs_5_), channel_id=1, source_target_pairs={{0,4},{4,0},{8,12},{12,8},{16,20},{20,16},{24,28},{28,24},{1,5},{5... | collective-permute-start | bytes 3145736 | tf_op jit(solution)/shard_map/ppermute | solution.py:61
  288.1 56.7 %collective-permute-start.16 = (bf16[512,1024]{1,0:T(8,128)(2,1)}, bf16[512,1024]{1,0:T(8,128)(2,1)}, u32[]{:S(2)}, u32[]{:S(2)}) collective-permute-start(bf16[512,1024]{1,0:T(8,128)(2,1)} %get-tuple-element.199), channel_id=1, source_target_pairs={{4,0},{8,4},{12,8},{16,12},{20,16},{24,20},{28,24},{5,1},{9,5},{13... | collective-permute-start | bytes 3145736 | tf_op jit(solution)/shard_map/ppermute | solution.py:52
  310.5 42.9 %collective-permute-start.19 = (bf16[256,1536]{1,0:T(8,128)(2,1)}, bf16[256,1536]{1,0:T(8,128)(2,1)}, u32[]{:S(2)}, u32[]{:S(2)}) collective-permute-start(bf16[256,1536]{1,0:T(8,128)(2,1)} %get-tuple-element.207.refs_3_), channel_id=1, source_target_pairs={{0,8},{4,12},{8,0},{12,4},{16,24},{20,28},{24,16},{28,20},{1,9},{5... | collective-permute-start | bytes 2359304 | tf_op jit(solution)/shard_map/ppermute | solution.py:61
  323.6 21.2 %collective-permute-start.15 = (f32[4,512]{1,0:T(4,128)S(1)}, f32[4,512]{1,0:T(4,128)S(1)}, u32[]{:S(2)}, u32[]{:S(2)}) collective-permute-start(f32[4,512]{1,0:T(4,128)S(1)} %bitcast.91), channel_id=1, source_target_pairs={{0,1},{1,0},{2,3},{3,2},{4,5},{5,4},{6,7},{7,6},{8,9},{9,8},{10,11... | collective-permute-start | bytes 24584 | tf_op jit(solution)/shard_map/ppermute | solution.py:61
  326.9 35.3 %collective-permute-start.14 = (bf16[512,1024]{1,0:T(8,128)(2,1)}, bf16[512,1024]{1,0:T(8,128)(2,1)}, u32[]{:S(2)}, u32[]{:S(2)}) collective-permute-start(bf16[512,1024]{1,0:T(8,128)(2,1)} %copy-done.36), channel_id=1, source_target_pairs={{0,1},{1,0},{2,3},{3,2},{4,5},{5,4},{6,7},{7,6},{8,9},{9,8},{10,11... | collective-permute-start | bytes 3145736 | tf_op jit(solution)/shard_map/ppermute | solution.py:61
  336.0 30.3 %collective-permute-start.21 = (bf16[128,2048]{1,0:T(8,128)(2,1)}, bf16[128,2048]{1,0:T(8,128)(2,1)}, u32[]{:S(2)}, u32[]{:S(2)}) collective-permute-start(bf16[128,2048]{1,0:T(8,128)(2,1)} %get-tuple-element.208.refs_9_), channel_id=1, source_target_pairs={{0,8},{4,12},{8,0},{12,4},{16,24},{20,28},{24,16},{28,20},{1,9},{5... | collective-permute-start | bytes 1572872 | tf_op jit(solution)/shard_map/ppermute | solution.py:61
  358.7 26.8 %collective-permute-start.20 = (bf16[512,1024]{1,0:T(8,128)(2,1)}, bf16[512,1024]{1,0:T(8,128)(2,1)}, u32[]{:S(2)}, u32[]{:S(2)}) collective-permute-start(bf16[512,1024]{1,0:T(8,128)(2,1)} %get-tuple-element.212), channel_id=1, source_target_pairs={{0,1},{1,0},{2,3},{3,2},{4,5},{5,4},{6,7},{7,6},{8,9},{9,8},{10,11... | collective-permute-start | bytes 3145736 | tf_op jit(solution)/shard_map/ppermute | solution.py:61
  367.5 21.3 %collective-permute-start.23 = (bf16[64,2048]{1,0:T(8,128)(2,1)S(1)}, bf16[64,2048]{1,0:T(8,128)(2,1)}, u32[]{:S(2)}, u32[]{:S(2)}) collective-permute-start(bf16[64,2048]{1,0:T(8,128)(2,1)S(1)} %get-tuple-element.221.refs_3_), channel_id=1, source_target_pairs={{0,16},{4,20},{8,24},{12,28},{16,0},{20,4},{24,8},{28,12},{1,17},{... | collective-permute-start | bytes 786440 | tf_op jit(solution)/shard_map/ppermute | solution.py:61
  370.2 31.4 %collective-permute-start.29 = (bf16[64,1536]{1,0:T(8,128)(2,1)S(1)}, bf16[64,1536]{1,0:T(8,128)(2,1)S(1)}, u32[]{:S(2)}, u32[]{:S(2)}) collective-permute-start(bf16[64,1536]{1,0:T(8,128)(2,1)S(1)} %get-tuple-element.223.refs_2_), channel_id=1, source_target_pairs={{0,16},{4,20},{8,24},{12,28},{16,0},{20,4},{24,8},{28,12},{1,17},{... | collective-permute-start | bytes 589832 | tf_op jit(solution)/shard_map/ppermute | solution.py:61
  (166 other events, 1308.0 us)
Sparse Core Ops, SparseCore 0:
  144.5 141.8 reduce-scatter.3
